TPU v7x, 256 devices: a whole 4x4x8 slice. The times are simulated.
256 devices in a mesh: sample: 2 (over z_lo), seq: 128 (over x, y, z_hi, core).
Axes of the slice: x: 4, y: 4, z: 8 (z_hi: 4, z_lo: 2; z = z_hi * 2 + z_lo), core: 2. Of those that a mesh axis runs over, the one named last changes fastest.
Arguments:
- grad_out: bfloat16 [4, 64, 128, 1152], P('sample', None, 'seq'), may hold values from -6 to 6
- t_query: bfloat16 [4, 64, 128, 1152], P('sample', None, 'seq'), may hold values from -200 to 200
- t_key: bfloat16 [4, 64, 128, 1152], P('sample', None, 'seq'), may hold values from -4 to 4
- t_value: bfloat16 [4, 64, 128, 1152], P('sample', None, 'seq'), may hold values from -6 to 6
- t_out_weight: bfloat16 [1152, 1152], P('seq'), may hold values from -0.1875 to 0.1875
- t_qkv_weight: bfloat16 [1152, 3456], P('seq'), may hold values from -0.1875 to 0.1875
- frame_input: bfloat16 [256, 128, 1152], P(('sample', 'seq')), may hold values from -6 to 6
- cross_weights: bfloat16 [2, 1152, 1152], P(None, 'sample'), may hold values from -0.1875 to 0.1875
- cap_key: bfloat16 [300, 1152], replicated, may hold values from -160 to 160
- cap_value: bfloat16 [300, 1152], replicated, may hold values from -6 to 6
- cap_length: int32 [1], replicated, may hold values from 75 to 300
Outputs:
- grad_input: bfloat16 [256, 128, 1152], P(('sample', 'seq'))
- caption_grad: float32 [300, 2304], P(None, ('sample', 'seq'))
All inputs are finite; a program needn't handle non-finite values.
Results may differ from a plain program's by a relative error of at most 0.028.
The roundings to bfloat16 on the way count: a program that leaves them out, or rounds other values in their place, can miss the bound.
Values may be sent and summed in bfloat16 or wider, within the bound.
No kernel may reach another device: no remote copies, remote signals or barrier semaphores. Data moves between devices by JAX's collectives and lax.ppermute only.
A program may use at most 128 MiB of HBM per device.

v0:
```python
import math

import jax
import jax.numpy as jnp
from jax import lax
from jax.sharding import PartitionSpec as P

HEADS = 16
HEAD_DIM = 72


CONTRACT_LAST = (((1,), (1,)), ((), ()))


def split_heads(tensor):
    return tensor.reshape(tensor.shape[:-1] + (HEADS, HEAD_DIM))


def merge_heads(tensor):
    return tensor.reshape(tensor.shape[:-2] + (tensor.shape[-2] * tensor.shape[-1],))


def temporal_grads(grad_heads, query, key_rows, value):
    scaling = 1.0 / math.sqrt(HEAD_DIM)
    grad_split = split_heads(grad_heads)
    query_split = split_heads(query)
    key_split = split_heads(key_rows)
    value_split = split_heads(value)
    scores = (
        jnp.einsum("sfphd,sgphd->sphfg", query_split, key_split, preferred_element_type=jnp.float32)
        * scaling
    )
    attention = jax.nn.softmax(scores, axis=-1)
    attention_low = attention.astype(jnp.bfloat16)
    value_grad = jnp.einsum(
        "sphfg,sfphd->sgphd", attention_low, grad_split, preferred_element_type=jnp.float32
    ).astype(jnp.bfloat16)
    prob_grad = jnp.einsum(
        "sfphd,sgphd->sphfg", grad_split, value_split, preferred_element_type=jnp.float32
    )
    centred = prob_grad - jnp.sum(prob_grad * attention, axis=-1, keepdims=True)
    score_grad = (attention * centred * scaling).astype(jnp.bfloat16)
    query_grad = jnp.einsum(
        "sphfg,sgphd->sfphd", score_grad, key_split, preferred_element_type=jnp.float32
    ).astype(jnp.bfloat16)
    key_grad = jnp.einsum(
        "sphfg,sfphd->sgphd", score_grad, query_split, preferred_element_type=jnp.float32
    ).astype(jnp.bfloat16)
    return jnp.concatenate(
        [merge_heads(query_grad), merge_heads(key_grad), merge_heads(value_grad)], axis=-1
    )


def cross_grads(x_rows, d_rows, w_query, w_out, cap_key, cap_value, valid_keys):
    scaling = 1.0 / math.sqrt(HEAD_DIM)
    cross_query = jnp.dot(x_rows, w_query, preferred_element_type=jnp.float32).astype(jnp.bfloat16)
    out_grad = lax.dot_general(
        d_rows, w_out, CONTRACT_LAST, preferred_element_type=jnp.float32
    ).astype(jnp.bfloat16)
    query_split = split_heads(cross_query)
    output_split = split_heads(out_grad)
    key_split = split_heads(cap_key)
    value_split = split_heads(cap_value)
    scores = (
        jnp.einsum("nhd,chd->nhc", query_split, key_split, preferred_element_type=jnp.float32)
        * scaling
    )
    scores = jnp.where(valid_keys[None, None, :], scores, -1e30)
    attention = jax.nn.softmax(scores, axis=-1)
    attention_low = attention.astype(jnp.bfloat16)
    prob_grad = jnp.einsum(
        "nhd,chd->nhc", output_split, value_split, preferred_element_type=jnp.float32
    )
    centred = prob_grad - jnp.sum(prob_grad * attention, axis=-1, keepdims=True)
    score_grad = (attention * centred * scaling).astype(jnp.bfloat16)
    cq_grad = merge_heads(
        jnp.einsum(
            "nhc,chd->nhd", score_grad, key_split, preferred_element_type=jnp.float32
        ).astype(jnp.bfloat16)
    )
    result = (
        d_rows.astype(jnp.float32)
        + lax.dot_general(cq_grad, w_query, CONTRACT_LAST, preferred_element_type=jnp.float32)
    ).astype(jnp.bfloat16)
    key_term = merge_heads(
        jnp.einsum("nhc,nhd->chd", score_grad, query_split, preferred_element_type=jnp.float32)
    )
    value_term = merge_heads(
        jnp.einsum("nhc,nhd->chd", attention_low, output_split, preferred_element_type=jnp.float32)
    )
    return (result, jnp.concatenate([key_term, value_term], axis=-1))


def local(
    grad_out,
    t_query,
    t_key,
    t_value,
    t_out_weight,
    t_qkv_weight,
    frame_input,
    cross_weights,
    cap_key,
    cap_value,
    cap_length,
):
    samp_here, frames, patch_here, width = grad_out.shape
    slot_shape = (samp_here * frames, patch_here, width)
    full_cross = lax.all_gather(cross_weights, "sample", axis=1, tiled=True)
    grad_rows = grad_out.reshape(-1, width)
    grad_heads = lax.dot_general(
        grad_rows,
        lax.all_gather(t_out_weight, "seq", axis=0, tiled=True),
        CONTRACT_LAST,
        preferred_element_type=jnp.float32,
    ).astype(jnp.bfloat16)
    qkv_grad = temporal_grads(grad_heads.reshape(grad_out.shape), t_query, t_key, t_value).reshape(
        -1, 3 * width
    )
    residual_part = grad_rows.astype(jnp.float32)
    product = lax.dot_general(
        qkv_grad,
        lax.all_gather(t_qkv_weight, "seq", axis=0, tiled=True),
        CONTRACT_LAST,
        preferred_element_type=jnp.float32,
    )
    mixed_rows = (residual_part + product).astype(jnp.bfloat16)
    valid_keys = jnp.arange(cap_key.shape[0]) < cap_length[0]
    arrived = lax.all_to_all(
        mixed_rows.reshape(slot_shape), "seq", split_axis=0, concat_axis=1, tiled=True
    )
    result_rows, caption_term = cross_grads(
        frame_input.reshape(-1, width),
        arrived.reshape(-1, width),
        full_cross[0],
        full_cross[1],
        cap_key,
        cap_value,
        valid_keys,
    )
    grad_input = result_rows.reshape(frame_input.shape)
    caption_grad = lax.psum_scatter(
        caption_term, ("sample", "seq"), scatter_dimension=1, tiled=True
    )
    return (grad_input, caption_grad)


def solution(mesh):
    return jax.shard_map(
        local,
        mesh=mesh,
        in_specs=(
            P("sample", None, "seq", None),
            P("sample", None, "seq", None),
            P("sample", None, "seq", None),
            P("sample", None, "seq", None),
            P("seq", None),
            P("seq", None),
            P(("sample", "seq"), None, None),
            P(None, "sample", None),
            P(),
            P(),
            P(),
        ),
        out_specs=(P(("sample", "seq"), None, None), P(None, ("sample", "seq"))),
        check_vma=False,
    )
```

profile of v0, /device:TPU:1, one launch (start us, length us, event | category | flops | bytes accessed | tf_op | source)
XLA Modules:
  0.0 581.3 jit_solution(2423297437568069202)
XLA Ops:
  7.2 0.0 copy-start
  7.2 0.0 copy-start.11
  7.2 0.0 all-gather.8.cloned.1.call-start
  7.2 0.7 all-gather.8.cloned.1.call-update
  7.9 0.0 all-gather.10.cloned.1.call-start
  8.0 0.7 all-gather.10.cloned.1.call-update
  8.7 0.0 copy-start.4
  8.7 0.0 all-gather.6.cloned.1.call-start
  8.7 0.7 all-gather.6.cloned.1.call-update
  9.4 0.0 copy-start.5
  10.1 0.0 copy-done.11
  10.2 0.9 reshape.126
  11.1 0.0 copy-start.6
  11.1 2.1 reshape.127
  13.2 0.0 copy-start.8
  13.2 2.1 reshape.129
  15.3 0.0 copy-done.4
  15.3 1.3 copy.72
  16.6 1.3 copy.74
  17.9 1.6 fusion.82
  19.5 76.8 %all-gather.8.cloned.1.call-done = bf16[128,9,1152]{2,1,0:T(8,128)(2,1)} async-done(((bf16[1,9,1152]{2,1,0:T(8,128)(2,1)}), bf16[128,9,1152]{2,1,0:T(8,128)(2,1)}) %all-gather.8.cloned.1.call-update) | async-done | bytes 2654224 | tf_op jit(solution)/shard_map/all_gather | solution.py:113
  96.2 4.3 reshape.142
  100.6 2.6 convolution_convert_fusion.1
  103.2 1.9 reshape.128
  105.1 1.5 fusion.33
  106.6 0.3 copy.69
  107.0 1.2 concatenate.15
  108.2 0.4 fusion.45
  108.6 2.2 fusion.31
  110.8 0.3 copy.65
  111.2 0.5 concatenate.13
  111.7 2.1 fusion.32
  113.8 0.3 copy.67
  114.1 0.5 concatenate.14
  114.7 0.0 copy-start.12
  114.7 90.7 %all-gather.10.cloned.1.call-done = bf16[128,9,3456]{2,1,0:T(8,128)(2,1)} async-done(((bf16[1,9,3456]{2,1,0:T(8,128)(2,1)}), bf16[128,9,3456]{2,1,0:T(8,128)(2,1)}) %all-gather.10.cloned.1.call-update) | async-done | bytes 7962640 | tf_op jit(solution)/shard_map/all_gather | solution.py:123
  205.4 14.7 %reshape.144 = bf16[1152,3456]{1,0:T(8,128)(2,1)} reshape(bf16[128,9,3456]{2,1,0:T(8,128)(2,1)} %all-gather.10.cloned.1.call-done) | data formatting | bytes 15925248
  220.1 0.0 copy-done.10
  220.1 6.4 %fusion.13 = bf16[128,1,1152]{2,0,1:T(8,128)(2,1)S(1)} fusion(bf16[1152,3456]{1,0:T(8,128)(2,1)} %reshape.144, bf16[128,1152]{1,0:T(8,128)(2,1)S(1)} %copy-done.12, bf16[128,1152]{1,0:T(8,128)(2,1)S(1)} %concatenate.14, bf16[128,1152]{1,0:T(8,128)(2,1)S(1)} %concatenate.13, bf16[128,1152]{1,0:T(8,128)(2,1)S(1)} %bitcast.133), kind=kOutput, calls=%fused_computation.25 | convolution fusion | flops 1022312448 | bytes 9437184 | tf_op jit(solution)/shard_map/dot_general | solution.py:121
  226.5 0.5 broadcast.63
  227.0 0.8 reduce.6
  227.8 1.0 reshape.145
  228.9 10.7 %all-to-all-start = ((bf16[128,2,576]{2,1,0:T(2,128)(2,1)}), bf16[128,2,576]{2,1,0:T(2,128)(2,1)S(1)}, u32[]{:S(2)}, u32[]{:S(2)}) async-start(bf16[128,2,576]{2,1,0:T(2,128)(2,1)} %reshape.145), calls=%async_computation | async-start | bytes 655360 | tf_op jit(solution)/shard_map/all_to_all | solution.py:129
  239.5 0.0 all-reduce.3.cloned.1.call-start
  239.6 46.9 %all-gather.6.cloned.1.call-done = bf16[2,1152,1152]{2,1,0:T(8,128)(2,1)} async-done(((bf16[2,576,1152]{2,1,0:T(8,128)(2,1)}), bf16[2,1152,1152]{2,1,0:T(8,128)(2,1)}) %all-gather.6.cloned.1.call-update) | async-done | bytes 5308432 | tf_op jit(solution)/shard_map/all_gather | solution.py:109
  286.4 2.3 convolution_convert_fusion
  288.8 0.2 copy.71
  289.0 0.0 copy-done.3
  289.0 2.6 fusion.87
  291.6 0.0 all-to-all-done
  291.6 0.5 reshape.146
  292.2 2.8 fusion.12
  294.9 0.2 copy.73
  295.1 2.0 fusion.88
  297.2 0.1 copy-done.14
  297.2 0.9 fusion.23
  298.1 6.2 %fusion.28 = f32[16,72,300]{2,1,0:T(8,128)} fusion(bf16[128,16,72]{0,2,1:T(8,128)(2,1)} %bitcast.135, f32[16,128,300]{1,2,0:T(8,128)} %fusion.88, f32[128,16,300]{0,2,1:T(8,128)} %get-tuple-element.5, f32[128,16]{0,1:T(8,128)S(1)} %get-tuple-element.4), kind=kOutput, calls=%fused_computation.43 | convolution fusion | flops 92776744 | bytes 6600704 | tf_op jit(solution)/shard_map/nhc,nhd->chd/dot_general | solution.py:86
  304.3 3.5 pad_maximum_fusion
  307.7 0.0 all-reduce.3.cloned.1.call-update
  307.8 0.0 copy-start.1
  307.8 5.0 fusion.34
  312.8 3.4 fusion.14
  316.2 257.2 %all-reduce.3.cloned.1.call-done = f32[300,2304]{0,1:T(8,128)} async-done(((f32[300,2304]{0,1:T(8,128)}), f32[300,2304]{0,1:T(8,128)}) %all-reduce.3.cloned.1.call-update) | async-done | bytes 2764816
  573.4 1.4 constant_dynamic-slice_fusion
  (18 shorter events, 0.0 us)
Async XLA Ops:
  7.2 279.3 %copy-start = (bf16[1,128,1152]{2,1,0:T(8,128)(2,1)S(1)}, bf16[1,128,1152]{2,1,0:T(8,128)(2,1)}, u32[]{:S(2)}) copy-start(bf16[1,128,1152]{2,1,0:T(8,128)(2,1)} %param.17) | copy-start | bytes 884740
  7.2 3.0 copy-start.11
  7.2 89.1 %all-gather.8.cloned.1.call-start = ((), (), s32[]{:S(2)}) async-start(), calls=%async_computation.2 | async-start | bytes 4755456 | tf_op jit(solution)/shard_map/all_gather | solution.py:113
  7.9 197.4 %all-gather.10.cloned.1.call-start = ((), (), s32[]{:S(2)}) async-start(), calls=%async_computation.3 | async-start | bytes 14266368 | tf_op jit(solution)/shard_map/all_gather | solution.py:123
  8.7 6.6 %copy-start.4 = (bf16[300,1152]{1,0:T(8,128)(2,1)S(1)}, bf16[300,1152]{1,0:T(8,128)(2,1)}, u32[]{:S(2)}) copy-start(bf16[300,1152]{1,0:T(8,128)(2,1)} %param.19) | copy-start | bytes 2073604
  8.7 277.8 %all-gather.6.cloned.1.call-start = ((), (), s32[]{:S(2)}) async-start(), calls=%async_computation.1 | async-start | bytes 7962624 | tf_op jit(solution)/shard_map/all_gather | solution.py:109
  9.4 7.2 %copy-start.5 = (bf16[300,1152]{1,0:T(8,128)(2,1)S(1)}, bf16[300,1152]{1,0:T(8,128)(2,1)}, u32[]{:S(2)}) copy-start(bf16[300,1152]{1,0:T(8,128)(2,1)} %param.20) | copy-start | bytes 2073604
  11.1 8.4 %copy-start.6 = (bf16[2,64,16,72]{3,2,1,0:T(8,128)(2,1)}, bf16[2,64,16,72]{3,2,1,0:T(8,128)(2,1)S(1)}, u32[]{:S(2)}) copy-start(bf16[2,64,16,72]{3,2,1,0:T(8,128)(2,1)S(1)} %reshape.126) | copy-start | bytes 884740
  13.2 6.3 %copy-start.8 = (bf16[2,64,16,72]{3,2,1,0:T(8,128)(2,1)}, bf16[2,64,16,72]{3,2,1,0:T(8,128)(2,1)S(1)}, u32[]{:S(2)}) copy-start(bf16[2,64,16,72]{3,2,1,0:T(8,128)(2,1)S(1)} %reshape.127) | copy-start | bytes 884740
  106.6 2.0 copy-start.9
  108.6 3.0 copy-start.7
  114.6 105.4 %copy-start.10 = (bf16[2,64,1,1152]{3,1,2,0:T(8,128)(2,1)S(1)}, bf16[2,64,1,1152]{3,1,2,0:T(8,128)(2,1)}, u32[]{:S(2)}) copy-start(bf16[2,64,1,1152]{3,1,2,0:T(8,128)(2,1)} %param.11) | copy-start | bytes 884740
  114.7 105.4 %copy-start.12 = (bf16[128,1152]{1,0:T(8,128)(2,1)S(1)}, bf16[128,1152]{1,0:T(8,128)(2,1)}, u32[]{:S(2)}) copy-start(bf16[128,1152]{1,0:T(8,128)(2,1)} %concatenate.15) | copy-start | bytes 884740
  228.9 60.2 %copy-start.3 = (bf16[300,1152]{0,1:T(8,128)(2,1)S(1)}, bf16[300,1152]{0,1:T(8,128)(2,1)}, u32[]{:S(2)}) copy-start(bf16[300,1152]{0,1:T(8,128)(2,1)} %copy.72) | copy-start | bytes 2073604
  228.9 62.8 %all-to-all-start = ((bf16[128,2,576]{2,1,0:T(2,128)(2,1)}), bf16[128,2,576]{2,1,0:T(2,128)(2,1)S(1)}, u32[]{:S(2)}, u32[]{:S(2)}) async-start(bf16[128,2,576]{2,1,0:T(2,128)(2,1)} %reshape.145), calls=%async_computation | async-start | bytes 655360 | tf_op jit(solution)/shard_map/all_to_all | solution.py:129
  239.5 333.9 %all-reduce.3.cloned.1.call-start = ((), (), s32[]{:S(2)}) async-start(), calls=%async_computation.4 | async-start | bytes 7077888
  289.0 3.1 copy-start.13
  292.1 3.0 copy-start.2
  295.1 2.1 copy-start.14
  307.8 267.0 %copy-start.1 = (bf16[1,128,1152]{2,1,0:T(8,128)(2,1)S(1)}, bf16[1,128,1152]{2,1,0:T(8,128)(2,1)}, u32[]{:S(2)}) copy-start(bf16[1,128,1152]{2,1,0:T(8,128)(2,1)} %param.17) | copy-start | bytes 884740
Sparse Core Ops, SparseCore 0:
  11.5 84.7 all-gather.7
  99.7 105.6 all-gather.9
  207.2 79.2 all-gather.5
  307.9 265.4 all-reduce.2
where the time goes:
time: 583 us; the launch traced here: 581 us
  waiting for transfers between devices  474 us (81%)
  matrix products  42 us (7%)
  local copies, waits for them, and re-layouts  35.9 us (6%)
  between operations  14.8 us (3%)
  starting transfers between devices  10.8 us (2%)
    unnamed x5, waiting for transfers between devices  259 us
    all_gather x1, waiting for transfers between devices, local(): lax.all_gather(t_qkv_weight, 'seq', axis=0, tiled=True)  90.7 us
    all_gather x1, waiting for transfers between devices, local(): lax.all_gather(t_out_weight, 'seq', axis=0, tiled=True)  76.8 us
    all_gather x1, waiting for transfers between devices, local(): full_cross = lax.all_gather(cross_weights, 'sample', axis=1, tiled=True)  46.9 us
    unnamed x37, local copies, waits for them, and re-layouts  24.7 us
  transfers between devices with their start and end apart: 5, of which 4 were waited for; matrix products, arithmetic and copies ran while one was open for 11% of the time, Pallas kernels for 0%

commit v1 on v0

--- a/solution.py
+++ b/solution.py
@@ -3,7 +3,7 @@
 import jax
 import jax.numpy as jnp
 from jax import lax
-from jax.sharding import PartitionSpec as P
+from jax.sharding import Mesh, PartitionSpec as P
 
 HEADS = 16
 HEAD_DIM = 72
@@ -82,13 +82,78 @@
         d_rows.astype(jnp.float32)
         + lax.dot_general(cq_grad, w_query, CONTRACT_LAST, preferred_element_type=jnp.float32)
     ).astype(jnp.bfloat16)
-    key_term = merge_heads(
-        jnp.einsum("nhc,nhd->chd", score_grad, query_split, preferred_element_type=jnp.float32)
-    )
-    value_term = merge_heads(
-        jnp.einsum("nhc,nhd->chd", attention_low, output_split, preferred_element_type=jnp.float32)
-    )
-    return (result, jnp.concatenate([key_term, value_term], axis=-1))
+    key_term = jnp.einsum(
+        "nhc,nhd->hdc", score_grad, query_split, preferred_element_type=jnp.float32
+    )
+    value_term = jnp.einsum(
+        "nhc,nhd->hdc", attention_low, output_split, preferred_element_type=jnp.float32
+    )
+    return (result, jnp.concatenate([key_term, value_term], axis=1).astype(jnp.bfloat16))
+
+
+ALL = ("s", "x", "y", "z", "c")
+SEQ = ("x", "y", "z", "c")
+SHAPE = (2, 4, 4, 4, 2)
+
+
+def flat(s, x, y, z, c):
+    return (((s * 4 + x) * 4 + y) * 4 + z) * 2 + c
+
+
+def ring_groups(first):
+    groups = []
+    for s in range(2):
+        for z in range(4):
+            for fixed in range(4):
+                groups.append([flat(s, i, fixed, z, first) for i in range(4)])
+                groups.append([flat(s, fixed, i, z, 1 - first) for i in range(4)])
+    return groups
+
+
+def gather_groups(block, groups):
+    copies = jnp.broadcast_to(block[None], (4,) + block.shape)
+    return lax.all_to_all(copies, ALL, 0, 0, axis_index_groups=groups)
+
+
+def gather_rows(block):
+    core = lax.axis_index("c")
+    near = gather_groups(block, ring_groups(0))
+    whole = gather_groups(near, ring_groups(1))
+    return whole
+
+
+def both_cores(mine):
+    core = lax.axis_index("c")
+    other = lax.ppermute(mine, "c", [(0, 1), (1, 0)])
+    rows = mine.shape[2] * 16
+    first = jnp.where(core == 0, mine, other).transpose(1, 0, 2, 3)
+    second = jnp.where(core == 0, other, mine)
+    return first.reshape(rows, -1), second.reshape(rows, -1)
+
+
+def cross_halves(cross_weights):
+    core = lax.axis_index("c")
+    side = lax.axis_index("s")
+
+    def place(z):
+        return (z % 2, z // 2)
+
+    pairs = []
+    for x in range(4):
+        for y in range(4):
+            for z in range(8):
+                for c in range(2):
+                    to = (z + (1 if c == 0 else 7)) % 8
+                    s0, z0 = place(z)
+                    s1, z1 = place(to)
+                    pairs.append((flat(s0, x, y, z0, c), flat(s1, x, y, z1, c)))
+    part = lax.dynamic_index_in_dim(cross_weights, core, 0, keepdims=False)
+    got = lax.ppermute(part, ALL, pairs)
+    swapped = lax.ppermute(got, "c", [(0, 1), (1, 0)])
+    other = jnp.stack([jnp.where(core == 0, got, swapped), jnp.where(core == 0, swapped, got)])
+    low = jnp.where(side == 0, cross_weights, other)
+    high = jnp.where(side == 0, other, cross_weights)
+    return jnp.concatenate([low, high], axis=1)
 
 
 def local(
@@ -106,30 +171,45 @@
 ):
     samp_here, frames, patch_here, width = grad_out.shape
     slot_shape = (samp_here * frames, patch_here, width)
-    full_cross = lax.all_gather(cross_weights, "sample", axis=1, tiled=True)
+    core = lax.axis_index("c")
+    full_cross = cross_halves(cross_weights)
     grad_rows = grad_out.reshape(-1, width)
-    grad_heads = lax.dot_general(
-        grad_rows,
-        lax.all_gather(t_out_weight, "seq", axis=0, tiled=True),
+    shard = jnp.concatenate([t_out_weight, t_qkv_weight], axis=1).reshape(2, -1)
+    column = lax.all_to_all(
+        jnp.broadcast_to(shard[None], (8,) + shard.shape), ("z", "c"), 0, 0
+    ).reshape(72, 4 * width)
+    out_part = lax.dynamic_slice(column, (0, core * 512), (72, 640))
+    qkv_part = lax.dynamic_slice(column, (0, 1152 + core * 1664), (72, 1792))
+    out_first, out_second = both_cores(gather_rows(out_part))
+    qkv_first, qkv_second = both_cores(gather_rows(qkv_part))
+    grad_heads = (
+        lax.dot_general(
+            grad_rows[:, :640], out_first, CONTRACT_LAST, preferred_element_type=jnp.float32
+        )
+        + lax.dot_general(
+            grad_rows[:, 640:],
+            out_second[:, 128:],
+            CONTRACT_LAST,
+            preferred_element_type=jnp.float32,
+        )
+    ).astype(jnp.bfloat16)
+    qkv_grad = temporal_grads(grad_heads.reshape(grad_out.shape), t_query, t_key, t_value).reshape(
+        -1, 3 * width
+    )
+    product = lax.dot_general(
+        qkv_grad[:, :1792], qkv_first, CONTRACT_LAST, preferred_element_type=jnp.float32
+    ) + lax.dot_general(
+        qkv_grad[:, 1792:],
+        qkv_second[:, 128:],
         CONTRACT_LAST,
         preferred_element_type=jnp.float32,
-    ).astype(jnp.bfloat16)
-    qkv_grad = temporal_grads(grad_heads.reshape(grad_out.shape), t_query, t_key, t_value).reshape(
-        -1, 3 * width
-    )
-    residual_part = grad_rows.astype(jnp.float32)
-    product = lax.dot_general(
-        qkv_grad,
-        lax.all_gather(t_qkv_weight, "seq", axis=0, tiled=True),
-        CONTRACT_LAST,
-        preferred_element_type=jnp.float32,
-    )
-    mixed_rows = (residual_part + product).astype(jnp.bfloat16)
+    )
+    mixed_rows = (grad_rows.astype(jnp.float32) + product).astype(jnp.bfloat16)
     valid_keys = jnp.arange(cap_key.shape[0]) < cap_length[0]
     arrived = lax.all_to_all(
-        mixed_rows.reshape(slot_shape), "seq", split_axis=0, concat_axis=1, tiled=True
-    )
-    result_rows, caption_term = cross_grads(
+        mixed_rows.reshape(slot_shape), SEQ, split_axis=0, concat_axis=1, tiled=True
+    )
+    result_rows, terms = cross_grads(
         frame_input.reshape(-1, width),
         arrived.reshape(-1, width),
         full_cross[0],
@@ -139,29 +219,30 @@
         valid_keys,
     )
     grad_input = result_rows.reshape(frame_input.shape)
-    caption_grad = lax.psum_scatter(
-        caption_term, ("sample", "seq"), scatter_dimension=1, tiled=True
-    )
-    return (grad_input, caption_grad)
+    head = jnp.sum(lax.all_to_all(terms, ("x", "y"), 0, 0).astype(jnp.float32), axis=0)
+    pieces = head.astype(jnp.bfloat16).reshape(16, 9, -1)
+    piece = jnp.sum(lax.all_to_all(pieces, ("s", "z", "c"), 0, 0).astype(jnp.float32), axis=0)
+    return (grad_input, piece.T)
 
 
 def solution(mesh):
+    fine = Mesh(mesh.devices.reshape(SHAPE), ALL)
     return jax.shard_map(
         local,
-        mesh=mesh,
+        mesh=fine,
         in_specs=(
-            P("sample", None, "seq", None),
-            P("sample", None, "seq", None),
-            P("sample", None, "seq", None),
-            P("sample", None, "seq", None),
-            P("seq", None),
-            P("seq", None),
-            P(("sample", "seq"), None, None),
-            P(None, "sample", None),
+            P("s", None, SEQ, None),
+            P("s", None, SEQ, None),
+            P("s", None, SEQ, None),
+            P("s", None, SEQ, None),
+            P(SEQ, None),
+            P(SEQ, None),
+            P(ALL, None, None),
+            P(None, "s", None),
             P(),
             P(),
             P(),
         ),
-        out_specs=(P(("sample", "seq"), None, None), P(None, ("sample", "seq"))),
+        out_specs=(P(ALL, None, None), P(None, ALL)),
         check_vma=False,
     )

time: 583 us -> 244 us (0.42)
  waiting for transfers between devices: 474 us -> 73.5 us
  starting transfers between devices: 10.8 us -> 59.3 us
  other arithmetic: 4.23 us -> 17.8 us
  between operations: 14.8 us -> 1.69 us
  blocking collectives: 0 us -> 12.1 us
    unnamed x5 -> x0, waiting for transfers between devices: 259 us -> none
    all_gather x3 -> x0, waiting for transfers between devices: 214 us -> none  [the longest x1 90.7 us: local(): lax.all_gather(t_qkv_weight, 'seq', axis=0, tiled=True)]
    all_to_all x1 -> x7, waiting for transfers between devices: 0.01 us -> 54.6 us  [the longest x1 16.7 us: local(): lax.all_to_all(terms, ('x', 'y'), 0, 0).astype(jnp.float32)]
    all_to_all x1 -> x7, starting transfers between devices: 10.7 us -> 43.5 us  [the longest x3 12.8 us: gather_groups(): return lax.all_to_all(copies, ALL, 0, 0, axis_index_groups=groups)]
    ppermute x0 -> x4, waiting for transfers between devices: none -> 18.9 us  [the longest x1 18.9 us: cross_halves(): got = lax.ppermute(part, ALL, pairs)]
    ppermute x0 -> x4, starting transfers between devices: none -> 15.8 us  [the longest x2 8.31 us: both_cores(): other = lax.ppermute(mine, 'c', [(0, 1), (1, 0)])]
    unnamed x37 -> x34, local copies, waits for them, and re-layouts: 24.7 us -> 11 us
    all_to_all x0 -> x1, blocking collectives: none -> 12.1 us  [gather_groups(): return lax.all_to_all(copies, ALL, 0, 0, axis_index_groups=groups)]
  transfers between devices with their start and end apart: 5 -> 11, of which waited for: 4 -> 7; matrix products, arithmetic and copies ran while one was open for 11% -> 21% of each run, Pallas kernels for 0% -> 0%
where the time goes in v1:
time: 244 us; the launch traced here: 243 us
  waiting for transfers between devices  73.5 us (30%)
  starting transfers between devices  59.3 us (24%)
  matrix products  43.4 us (18%)
  local copies, waits for them, and re-layouts  35 us (14%)
  other arithmetic  17.8 us (7%)
  blocking collectives  12.1 us (5%)
    ppermute x1, waiting for transfers between devices, cross_halves(): got = lax.ppermute(part, ALL, pairs)  18.9 us
    all_to_all x1, waiting for transfers between devices, local(): lax.all_to_all(terms, ('x', 'y'), 0, 0).astype(jnp.float32)  16.7 us
    all_to_all x1, waiting for transfers between devices, local(): lax.all_to_all(jnp.broadcast_to(shard[None], (8,) + shard.shape), ('z', '...  16.3 us
    all_to_all x3, starting transfers between devices, gather_groups(): return lax.all_to_all(copies, ALL, 0, 0, axis_index_groups=groups)  12.8 us
    all_to_all x1, blocking collectives, gather_groups(): return lax.all_to_all(copies, ALL, 0, 0, axis_index_groups=groups)  12.1 us
    unnamed x34, local copies, waits for them, and re-layouts  11 us
    all_to_all x1, waiting for transfers between devices, local(): lax.all_to_all(mixed_rows.reshape(slot_shape), SEQ, split_axis=0, concat_...  10.1 us
    all_to_all x1, starting transfers between devices, local(): lax.all_to_all(jnp.broadcast_to(shard[None], (8,) + shard.shape), ('z', '...  9.97 us
  transfers between devices with their start and end apart: 11, of which 7 were waited for; matrix products, arithmetic and copies ran while one was open for 21% of the time, Pallas kernels for 0%

profile of v1, /device:TPU:1, one launch (start us, length us, event | category | flops | bytes accessed | tf_op | source)
XLA Modules:
  0.0 242.9 jit_solution(10095165625125458515)
XLA Ops:
  0.6 1.0 pad_maximum_fusion.7
  1.7 1.2 broadcast_in_dim.21
  2.9 10.0 %all-to-all-start = ((bf16[8,2,20736]{2,1,0:T(2,128)(2,1)}), bf16[8,2,20736]{2,1,0:T(2,128)(2,1)S(1)}, u32[]{:S(2)}, u32[]{:S(2)}) async-start(bf16[8,2,20736]{2,1,0:T(2,128)(2,1)} %broadcast_in_dim.21), calls=%async_computation | async-start | bytes 1327104 | tf_op jit(solution)/shard_map/all_to_all | solution.py:178
  12.9 16.3 %all-to-all-done = bf16[8,2,20736]{2,1,0:T(2,128)(2,1)S(1)} async-done(((bf16[8,2,20736]{2,1,0:T(2,128)(2,1)}), bf16[8,2,20736]{2,1,0:T(2,128)(2,1)S(1)}, u32[]{:S(2)}, u32[]{:S(2)}) %all-to-all-start) | async-done | bytes 663584 | tf_op jit(solution)/shard_map/all_to_all | solution.py:178
  29.1 0.4 reshape.145
  29.6 0.8 broadcast_in_dim.22
  30.4 4.2 %all-to-all-start.1 = ((bf16[4,72,640]{2,1,0:T(8,128)(2,1)}), bf16[4,72,640]{2,1,0:T(8,128)(2,1)S(1)}, u32[]{:S(2)}, u32[]{:S(2)}) async-start(bf16[4,72,640]{2,1,0:T(8,128)(2,1)} %broadcast_in_dim.22), calls=%async_computation.1 | async-start | bytes 737280 | tf_op jit(solution)/shard_map/all_to_all | solution.py:115
  34.6 6.1 %all-to-all-done.1 = bf16[4,72,640]{2,1,0:T(8,128)(2,1)S(1)} async-done(((bf16[4,72,640]{2,1,0:T(8,128)(2,1)}), bf16[4,72,640]{2,1,0:T(8,128)(2,1)S(1)}, u32[]{:S(2)}, u32[]{:S(2)}) %all-to-all-start.1) | async-done | bytes 368672 | tf_op jit(solution)/shard_map/all_to_all | solution.py:115
  40.7 12.1 %all_to_all.44 = bf16[4,72,1792]{2,1,0:T(8,128)(2,1)S(1)} all-to-all(bf16[4,72,1792]{2,1,0:T(8,128)(2,1)S(1)} %broadcast_in_dim.24), channel_id=1, replica_groups={{0,32,64,96},{1,9,17,25},{8,40,72,104},{33,41,49,57},{16,48,80,112},{65..., dimensions={0} | all-to-all | bytes 2064384 | tf_op jit(solution)/shard_map/all_to_all | solution.py:115
  52.8 2.2 broadcast_in_dim.25
  55.0 5.1 %all-to-all-start.4 = ((bf16[4,4,72,1792]{3,2,1,0:T(8,128)(2,1)}), bf16[4,4,72,1792]{3,2,1,0:T(8,128)(2,1)}, u32[]{:S(2)}, u32[]{:S(2)}) async-start(bf16[4,4,72,1792]{3,2,1,0:T(8,128)(2,1)} %broadcast_in_dim.25), calls=%async_computation.4 | async-start | bytes 8257536 | tf_op jit(solution)/shard_map/all_to_all | solution.py:115
  60.2 0.9 collective-permute-start.2
  61.1 18.9 %collective-permute-done.2 = bf16[576,1152]{1,0:T(8,128)(2,1)} collective-permute-done((bf16[576,1152]{1,0:T(8,128)(2,1)S(1)}, bf16[576,1152]{1,0:T(8,128)(2,1)}, u32[]{:S(2)}, u32[]{:S(2)}) %collective-permute-start.2) | collective-permute-done | bytes 1327136 | tf_op jit(solution)/shard_map/ppermute | solution.py:151
  80.0 6.6 %collective-permute-start.3 = (bf16[576,1152]{1,0:T(8,128)(2,1)}, bf16[576,1152]{1,0:T(8,128)(2,1)}, u32[]{:S(2)}, u32[]{:S(2)}) collective-permute-start(bf16[576,1152]{1,0:T(8,128)(2,1)} %collective-permute-done.2), channel_id=1, source_target_pairs={{0,1},{1,0},{2,3},{3,2},{4,5},{5,4},{6,7},{7,6},{8,9},{9,8},{10,11... | collective-permute-start | bytes 3981320 | tf_op jit(solution)/shard_map/ppermute | solution.py:152
  86.7 1.3 broadcast_in_dim.23
  88.0 3.6 %all-to-all-start.2 = ((bf16[4,4,72,640]{3,2,1,0:T(8,128)(2,1)}), bf16[4,4,72,640]{3,2,1,0:T(8,128)(2,1)S(1)}, u32[]{:S(2)}, u32[]{:S(2)}) async-start(bf16[4,4,72,640]{3,2,1,0:T(8,128)(2,1)} %broadcast_in_dim.23), calls=%async_computation.2 | async-start | bytes 2949120 | tf_op jit(solution)/shard_map/all_to_all | solution.py:115
  91.6 4.5 %copy.97 = bf16[4,4,72,1792]{3,2,0,1:T(8,128)(2,1)} copy(bf16[4,4,72,1792]{3,2,1,0:T(8,128)(2,1)} %all-to-all-done.4) | data formatting | bytes 8257536 | tf_op jit(solution)/shard_map/all_to_all | solution.py:115
  96.0 8.0 %collective-permute-start.1 = (bf16[4,4,72,1792]{3,2,0,1:T(8,128)(2,1)}, bf16[4,4,72,1792]{3,2,0,1:T(8,128)(2,1)}, u32[]{:S(2)}, u32[]{:S(2)}) collective-permute-start(bf16[4,4,72,1792]{3,2,0,1:T(8,128)(2,1)} %copy.97), channel_id=1, source_target_pairs={{0,1},{1,0},{2,3},{3,2},{4,5},{5,4},{6,7},{7,6},{8,9},{9,8},{10,11... | collective-permute-start | bytes 12386312 | tf_op jit(solution)/shard_map/ppermute | solution.py:127
  104.1 0.9 reshape.149
  105.0 2.7 %reshape.143 = bf16[2,64,16,72]{3,2,1,0:T(8,128)(2,1)} reshape(bf16[2,64,1,1152]{3,1,2,0:T(8,128)(2,1)} %param.12) | data formatting | bytes 589824 | tf_op jit(solution)/shard_map/reshape
  107.7 1.9 reshape.144
  109.7 1.3 copy.105
  111.0 2.2 copy.103
  113.8 2.6 %fusion.95 = (f32[2,16,64]{2,1,0:T(8,128)S(1)}, f32[2,16,64,64]{2,3,1,0:T(8,128)}) fusion(bf16[2,64,16,72]{3,2,1,0:T(8,128)(2,1)S(1)} %reshape.144, bf16[2,64,16,72]{3,2,1,0:T(8,128)(2,1)} %reshape.143), kind=kOutput, calls=%fused_computation.114 | convolution fusion | flops 19267648 | bytes 1122304 | tf_op jit(solution)/shard_map/sub | solution.py:33
  116.9 2.1 select_bitcast_fusion.1
  119.1 3.0 %broadcast_select_fusion.3 = (bf16[2,576,1152]{2,1,0:T(8,128)(2,1)}, bf16[2,576,1152]{2,1,0:T(8,128)(2,1)}) fusion(bf16[2,576,1152]{2,1,0:T(8,128)(2,1)S(1)} %copy-done.3, pred[]{:T(512)S(6)} %eq.5, bf16[1,576,1152]{2,1,0:T(8,128)(2,1)S(1)} %get-tuple-element.9, bf16[1,576,1152]{2,1,0:T(8,128)(2,1)S(1)} %get-tuple-element.8), kind=kLoop, calls=%fused_computation.18 | loop fusion | flops 3981312 | bytes 10616833 | tf_op jit(solution)/shard_map/jit(_where)/select_n | solution.py:154
  122.6 0.8 copy-done.6
  123.4 0.5 fusion.45
  123.9 0.6 fusion.25
  124.7 0.5 copy.89
  125.6 2.6 %fusion.42 = bf16[2,64,1,16,72]{4,1,3,0,2:T(8,128)(2,1)S(1)} fusion(f32[2,16,64,64]{2,3,1,0:T(8,128)S(1)} %fusion.52, bf16[2,64,16,72]{3,2,1,0:T(8,128)(2,1)} %reshape.143, f32[2,16,64,64]{2,3,1,0:T(8,128)} %get-tuple-element.11, f32[2,16,64]{2,1,0:T(8,128)S(1)} %get-tuple-element.10), kind=kOutput, calls=%fused_computation.67 | convolution fusion | flops 19941440 | bytes 1646592 | tf_op jit(solution)/shard_map/sphfg,sfphd->sgphd/dot_general | solution.py:46
  128.6 0.5 concatenate.26
  129.1 1.6 fusion.43
  131.0 0.5 concatenate.28
  131.5 2.7 %fusion.41 = bf16[2,64,1,16,72]{4,1,3,0,2:T(8,128)(2,1)S(1)} fusion(f32[2,16,64,64]{2,3,1,0:T(8,128)} %copy-done.5, bf16[2,64,16,72]{3,2,1,0:T(8,128)(2,1)S(1)} %copy-done.10, f32[2,16,64,64]{2,3,1,0:T(8,128)} %get-tuple-element.11, f32[2,16,64]{2,1,0:T(8,128)S(1)} %get-tuple-element.10), kind=kOutput, calls=%fused_computation.66 | convolution fusion | flops 19941440 | bytes 1646592 | tf_op jit(solution)/shard_map/sphfg,sgphd->sfphd/dot_general | solution.py:43
  134.6 0.5 concatenate.25
  135.1 3.7 %broadcast_select_fusion.1 = (bf16[4,4,72,1792]{3,2,0,1:T(8,128)(2,1)S(1)}, bf16[4,4,72,1792]{3,2,0,1:T(8,128)(2,1)S(1)}) fusion(bf16[4,4,72,1792]{3,2,0,1:T(8,128)(2,1)} %collective-permute-done.1, pred[]{:T(512)S(6)} %eq.4, bf16[4,4,72,1792]{3,2,1,0:T(8,128)(2,1)} %all-to-all-done.4), kind=kLoop, calls=%fused_computation.7 | loop fusion | flops 4128768 | bytes 16515073 | tf_op jit(solution)/shard_map/jit(_where)/select_n | solution.py:129
  139.2 1.2 fusion.4
  140.4 2.2 fusion.24
  142.6 0.5 broadcast.67
  143.1 1.7 reduce.7
  144.8 1.1 reshape.163
  145.9 7.7 %all-to-all-start.5 = ((bf16[128,2,576]{2,1,0:T(2,128)(2,1)}), bf16[128,2,576]{2,1,0:T(2,128)(2,1)}, u32[]{:S(2)}, u32[]{:S(2)}) async-start(bf16[128,2,576]{2,1,0:T(2,128)(2,1)} %reshape.163), calls=%async_computation.5 | async-start | bytes 655360 | tf_op jit(solution)/shard_map/all_to_all | solution.py:209
  153.6 2.2 convolution_convert_fusion
  155.8 3.8 %fusion.100 = (f32[128,16]{0,1:T(8,128)S(1)}, f32[128,16,300]{0,2,1:T(8,128)}) fusion(pred[300]{0:T(512)(128)(4,1)S(1)} %iota_compare_fusion, bf16[128,16,72]{0,2,1:T(8,128)(2,1)S(1)} %bitcast.153, bf16[300,16,72]{0,2,1:T(8,128)(2,1)} %bitcast.146), kind=kOutput, calls=%fused_computation.115 | convolution fusion | flops 90931496 | bytes 3452204 | tf_op jit(solution)/shard_map/sub | solution.py:69
  159.7 10.1 %all-to-all-done.5 = bf16[128,2,576]{2,1,0:T(2,128)(2,1)} async-done(((bf16[128,2,576]{2,1,0:T(2,128)(2,1)}), bf16[128,2,576]{2,1,0:T(2,128)(2,1)}, u32[]{:S(2)}, u32[]{:S(2)}) %all-to-all-start.5) | async-done | bytes 294944 | tf_op jit(solution)/shard_map/all_to_all | solution.py:209
  169.8 2.5 %reshape.164 = bf16[128,1,1152]{2,1,0:T(2,128)(2,1)S(1)} reshape(bf16[128,2,576]{2,1,0:T(2,128)(2,1)} %all-to-all-done.5) | data formatting | bytes 589824
  172.3 3.0 %fusion.21 = bf16[128,1152]{1,0:T(8,128)(2,1)} fusion(bf16[2,576,1152]{2,1,0:T(8,128)(2,1)} %get-tuple-element.5, bf16[2,576,1152]{2,1,0:T(8,128)(2,1)S(1)} %copy-done.1, bf16[128,1,1152]{2,1,0:T(2,128)(2,1)S(1)} %reshape.164), kind=kOutput, calls=%fused_computation.36 | convolution fusion | flops 345194496 | bytes 5898240 | tf_op jit(solution)/shard_map/dot_general | solution.py:57
  175.3 1.8 copy.104
  177.1 3.4 %fusion.101 = f32[16,128,300]{1,2,0:T(8,128)} fusion(bf16[128,16,72]{0,2,1:T(8,128)(2,1)} %bitcast.144, bf16[300,16,72]{0,2,1:T(8,128)(2,1)} %bitcast.142), kind=kOutput, calls=%fused_computation.116 | convolution fusion | flops 88473600 | bytes 3443712 | tf_op jit(solution)/shard_map/nhd,chd->nhc/dot_general | solution.py:71
  180.6 1.8 convolution_convert_fusion.1
  182.4 5.9 %convolution_convert_fusion.2 = bf16[16,72,300]{2,1,0:T(8,128)(2,1)} fusion(bf16[128,16,72]{0,2,1:T(8,128)(2,1)} %bitcast.154, f32[16,128,300]{1,2,0:T(8,128)} %fusion.101, f32[128,16,300]{0,2,1:T(8,128)} %get-tuple-element.13, f32[128,16]{0,1:T(8,128)S(1)} %get-tuple-element.12), kind=kOutput, calls=%fused_computation.46 | convolution fusion | flops 93122344 | bytes 5909504 | tf_op jit(solution)/shard_map/nhc,nhd->hdc/dot_general | solution.py:85
  188.2 2.9 %pad_maximum_fusion.2 = bf16[16,144,300]{2,1,0:T(8,128)(2,1)} fusion(bf16[16,72,300]{2,1,0:T(8,128)(2,1)} %convolution_convert_fusion.1, bf16[16,72,300]{2,1,0:T(8,128)(2,1)} %convolution_convert_fusion.2), kind=kLoop, calls=%fused_computation.41 | loop fusion | flops 2764800 | bytes 2764800 | tf_op jit(solution)/shard_map/concatenate | solution.py:91
  191.2 4.4 %all-to-all-start.6 = ((bf16[16,144,300]{2,1,0:T(8,128)(2,1)}), bf16[16,144,300]{2,1,0:T(8,128)(2,1)}, u32[]{:S(2)}, u32[]{:S(2)}) async-start(bf16[16,144,300]{2,1,0:T(8,128)(2,1)} %pad_maximum_fusion.2), calls=%async_computation.6 | async-start | bytes 3538944 | tf_op jit(solution)/shard_map/all_to_all | solution.py:222
  195.6 5.9 %fusion.44 = bf16[16,128,72]{1,2,0:T(8,128)(2,1)} fusion(bf16[300,16,72]{0,2,1:T(8,128)(2,1)} %bitcast.147, f32[16,128,300]{1,2,0:T(8,128)} %fusion.101, f32[128,16,300]{0,2,1:T(8,128)} %get-tuple-element.13, f32[128,16]{0,1:T(8,128)S(1)} %get-tuple-element.12), kind=kOutput, calls=%fused_computation.69 | convolution fusion | flops 92924200 | bytes 5909504 | tf_op jit(solution)/shard_map/nhc,chd->nhd/dot_general | solution.py:77
  201.5 16.7 %all-to-all-done.6 = bf16[16,144,300]{2,1,0:T(8,128)(2,1)} async-done(((bf16[16,144,300]{2,1,0:T(8,128)(2,1)}), bf16[16,144,300]{2,1,0:T(8,128)(2,1)}, u32[]{:S(2)}, u32[]{:S(2)}) %all-to-all-start.6) | async-done | bytes 1382432 | tf_op jit(solution)/shard_map/all_to_all | solution.py:222
  218.2 2.4 %reduce_sum.61 = bf16[144,300]{1,0:T(8,128)(2,1)} reduce(bf16[16,144,300]{2,1,0:T(8,128)(2,1)} %all-to-all-done.6, bf16[]{:T(256)} %constant.37.clone.1), dimensions={0}, to_apply=%region_6.7 | reduce | flops 648000 | bytes 1468802 | tf_op jit(solution)/shard_map/reduce_sum | solution.py:222
  220.6 1.6 reshape.161
  222.3 1.8 reshape.165
  224.0 8.6 %all-to-all-start.7 = ((bf16[16,2,1350]{2,1,0:T(2,128)(2,1)}), bf16[16,2,1350]{2,1,0:T(2,128)(2,1)}, u32[]{:S(2)}, u32[]{:S(2)}) async-start(bf16[16,2,1350]{2,1,0:T(2,128)(2,1)} %reshape.165), calls=%async_computation.7 | async-start | bytes 180224 | tf_op jit(solution)/shard_map/all_to_all | solution.py:224
  232.7 3.1 %fusion.26 = bf16[1,128,1152]{2,1,0:T(8,128)(2,1)} fusion(bf16[128,1152]{0,1:T(8,128)(2,1)} %bitcast.152, bf16[128,1,1152]{2,1,0:T(2,128)(2,1)S(1)} %reshape.164, bf16[2,576,1152]{2,1,0:T(8,128)(2,1)S(1)} %copy-done.1, bf16[2,576,1152]{2,1,0:T(8,128)(2,1)} %get-tuple-element.5), kind=kOutput, calls=%fused_computation.40 | convolution fusion | flops 345489408 | bytes 6193152 | tf_op jit(solution)/shard_map/dot_general | solution.py:83
  235.7 5.3 %all-to-all-done.7 = bf16[16,2,1350]{2,1,0:T(2,128)(2,1)} async-done(((bf16[16,2,1350]{2,1,0:T(2,128)(2,1)}), bf16[16,2,1350]{2,1,0:T(2,128)(2,1)}, u32[]{:S(2)}, u32[]{:S(2)}) %all-to-all-start.7) | async-done | bytes 86432 | tf_op jit(solution)/shard_map/all_to_all | solution.py:224
  241.1 1.1 reshape.166
  242.2 0.7 convert_reduce_fusion
  (48 shorter events, 3.5 us)
Async XLA Ops:
  0.6 152.9 %copy-start = (bf16[1,128,1152]{2,1,0:T(8,128)(2,1)S(1)}, bf16[1,128,1152]{2,1,0:T(8,128)(2,1)}, u32[]{:S(2)}) copy-start(bf16[1,128,1152]{2,1,0:T(8,128)(2,1)} %param.17) | copy-start | bytes 884740
  2.9 26.2 %all-to-all-start = ((bf16[8,2,20736]{2,1,0:T(2,128)(2,1)}), bf16[8,2,20736]{2,1,0:T(2,128)(2,1)S(1)}, u32[]{:S(2)}, u32[]{:S(2)}) async-start(bf16[8,2,20736]{2,1,0:T(2,128)(2,1)} %broadcast_in_dim.21), calls=%async_computation | async-start | bytes 1327104 | tf_op jit(solution)/shard_map/all_to_all | solution.py:178
  30.4 10.3 %all-to-all-start.1 = ((bf16[4,72,640]{2,1,0:T(8,128)(2,1)}), bf16[4,72,640]{2,1,0:T(8,128)(2,1)S(1)}, u32[]{:S(2)}, u32[]{:S(2)}) async-start(bf16[4,72,640]{2,1,0:T(8,128)(2,1)} %broadcast_in_dim.22), calls=%async_computation.1 | async-start | bytes 737280 | tf_op jit(solution)/shard_map/all_to_all | solution.py:115
  55.0 5.1 %copy-start.2 = (bf16[2,576,1152]{2,1,0:T(8,128)(2,1)S(1)}, bf16[2,576,1152]{2,1,0:T(8,128)(2,1)}, u32[]{:S(2)}) copy-start(bf16[2,576,1152]{2,1,0:T(8,128)(2,1)} %param.18) | copy-start | bytes 7962628
  55.0 31.7 %all-to-all-start.4 = ((bf16[4,4,72,1792]{3,2,1,0:T(8,128)(2,1)}), bf16[4,4,72,1792]{3,2,1,0:T(8,128)(2,1)}, u32[]{:S(2)}, u32[]{:S(2)}) async-start(bf16[4,4,72,1792]{3,2,1,0:T(8,128)(2,1)} %broadcast_in_dim.25), calls=%async_computation.4 | async-start | bytes 8257536 | tf_op jit(solution)/shard_map/all_to_all | solution.py:115
  60.2 19.7 %collective-permute-start.2 = (bf16[576,1152]{1,0:T(8,128)(2,1)S(1)}, bf16[576,1152]{1,0:T(8,128)(2,1)}, u32[]{:S(2)}, u32[]{:S(2)}) collective-permute-start(bf16[576,1152]{1,0:T(8,128)(2,1)S(1)} %dynamic-slice_bitcast_fusion), channel_id=1, source_target_pairs={{0,128},{1,135},{128,2},{129,1},{2,130},{3,129},{130,4},{131,3},{4... | collective-permute-start | bytes 3981320 | tf_op jit(solution)/shard_map/ppermute | solution.py:151
  80.0 36.9 %collective-permute-start.3 = (bf16[576,1152]{1,0:T(8,128)(2,1)}, bf16[576,1152]{1,0:T(8,128)(2,1)}, u32[]{:S(2)}, u32[]{:S(2)}) collective-permute-start(bf16[576,1152]{1,0:T(8,128)(2,1)} %collective-permute-done.2), channel_id=1, source_target_pairs={{0,1},{1,0},{2,3},{3,2},{4,5},{5,4},{6,7},{7,6},{8,9},{9,8},{10,11... | collective-permute-start | bytes 3981320 | tf_op jit(solution)/shard_map/ppermute | solution.py:152
  88.0 28.4 %all-to-all-start.2 = ((bf16[4,4,72,640]{3,2,1,0:T(8,128)(2,1)}), bf16[4,4,72,640]{3,2,1,0:T(8,128)(2,1)S(1)}, u32[]{:S(2)}, u32[]{:S(2)}) async-start(bf16[4,4,72,640]{3,2,1,0:T(8,128)(2,1)} %broadcast_in_dim.23), calls=%async_computation.2 | async-start | bytes 2949120 | tf_op jit(solution)/shard_map/all_to_all | solution.py:115
  91.6 12.5 %copy-start.11 = (bf16[2,64,1,1152]{3,1,2,0:T(8,128)(2,1)S(1)}, bf16[2,64,1,1152]{3,1,2,0:T(8,128)(2,1)}, u32[]{:S(2)}) copy-start(bf16[2,64,1,1152]{3,1,2,0:T(8,128)(2,1)} %param.14) | copy-start | bytes 884740
  96.0 13.6 %copy-start.8 = (bf16[300,1152]{1,0:T(8,128)(2,1)S(1)}, bf16[300,1152]{1,0:T(8,128)(2,1)}, u32[]{:S(2)}) copy-start(bf16[300,1152]{1,0:T(8,128)(2,1)} %param.20) | copy-start | bytes 2073604
  96.0 39.1 %collective-permute-start.1 = (bf16[4,4,72,1792]{3,2,0,1:T(8,128)(2,1)}, bf16[4,4,72,1792]{3,2,0,1:T(8,128)(2,1)}, u32[]{:S(2)}, u32[]{:S(2)}) collective-permute-start(bf16[4,4,72,1792]{3,2,0,1:T(8,128)(2,1)} %copy.97), channel_id=1, source_target_pairs={{0,1},{1,0},{2,3},{3,2},{4,5},{5,4},{6,7},{7,6},{8,9},{9,8},{10,11... | collective-permute-start | bytes 12386312 | tf_op jit(solution)/shard_map/ppermute | solution.py:127
  109.6 6.8 %copy-start.9 = (bf16[2,64,16,72]{3,2,1,0:T(8,128)(2,1)}, bf16[2,64,16,72]{3,2,1,0:T(8,128)(2,1)S(1)}, u32[]{:S(2)}) copy-start(bf16[2,64,16,72]{3,2,1,0:T(8,128)(2,1)S(1)} %reshape.144) | copy-start | bytes 884740
  116.6 2.6 %copy-start.3 = (bf16[2,576,1152]{2,1,0:T(8,128)(2,1)S(1)}, bf16[2,576,1152]{2,1,0:T(8,128)(2,1)}, u32[]{:S(2)}) copy-start(bf16[2,576,1152]{2,1,0:T(8,128)(2,1)} %param.18) | copy-start | bytes 7962628
  116.6 5.5 %collective-permute-start = (bf16[4,4,72,640]{3,2,0,1:T(8,128)(2,1)S(1)}, bf16[4,4,72,640]{3,2,0,1:T(8,128)(2,1)S(1)}, u32[]{:S(2)}, u32[]{:S(2)}) collective-permute-start(bf16[4,4,72,640]{3,2,0,1:T(8,128)(2,1)S(1)} %copy.85), channel_id=1, source_target_pairs={{0,1},{1,0},{2,3},{3,2},{4,5},{5,4},{6,7},{7,6},{8,9},{9,8},{10,11... | collective-permute-start | bytes 4423688 | tf_op jit(solution)/shard_map/ppermute | solution.py:127
  122.4 1.0 copy-start.6
  125.6 2.6 %copy-start.5 = (f32[2,16,64,64]{2,3,1,0:T(8,128)}, f32[2,16,64,64]{2,3,1,0:T(8,128)S(1)}, u32[]{:S(2)}) copy-start(f32[2,16,64,64]{2,3,1,0:T(8,128)S(1)} %fusion.52) | copy-start | bytes 1572868
  129.1 2.4 %copy-start.10 = (bf16[2,64,16,72]{3,2,1,0:T(8,128)(2,1)S(1)}, bf16[2,64,16,72]{3,2,1,0:T(8,128)(2,1)}, u32[]{:S(2)}) copy-start(bf16[2,64,16,72]{3,2,1,0:T(8,128)(2,1)} %copy-done.9) | copy-start | bytes 884740
  139.1 1.2 copy-start.7
  140.4 13.2 %copy-start.1 = (bf16[2,576,1152]{2,1,0:T(8,128)(2,1)S(1)}, bf16[2,576,1152]{2,1,0:T(8,128)(2,1)}, u32[]{:S(2)}) copy-start(bf16[2,576,1152]{2,1,0:T(8,128)(2,1)} %get-tuple-element.4) | copy-start | bytes 7962628
  145.9 23.9 %all-to-all-start.5 = ((bf16[128,2,576]{2,1,0:T(2,128)(2,1)}), bf16[128,2,576]{2,1,0:T(2,128)(2,1)}, u32[]{:S(2)}, u32[]{:S(2)}) async-start(bf16[128,2,576]{2,1,0:T(2,128)(2,1)} %reshape.163), calls=%async_computation.5 | async-start | bytes 655360 | tf_op jit(solution)/shard_map/all_to_all | solution.py:209
  155.8 3.8 %copy-start.12 = (bf16[1152,128]{1,0:T(8,128)(2,1)}, bf16[1152,128]{1,0:T(8,128)(2,1)S(1)}, u32[]{:S(2)}) copy-start(bf16[1152,128]{1,0:T(8,128)(2,1)S(1)} %convolution_convert_fusion) | copy-start | bytes 884740
  177.1 3.5 %copy-start.4 = (bf16[128,1152]{0,1:T(8,128)(2,1)S(1)}, bf16[128,1152]{0,1:T(8,128)(2,1)}, u32[]{:S(2)}) copy-start(bf16[128,1152]{0,1:T(8,128)(2,1)} %copy.104) | copy-start | bytes 884740
  177.1 3.5 %copy-start.13 = (f32[128,16,300]{0,2,1:T(8,128)S(1)}, f32[128,16,300]{0,2,1:T(8,128)}, u32[]{:S(2)}) copy-start(f32[128,16,300]{0,2,1:T(8,128)} %get-tuple-element.13) | copy-start | bytes 7372804
  191.2 27.1 %all-to-all-start.6 = ((bf16[16,144,300]{2,1,0:T(8,128)(2,1)}), bf16[16,144,300]{2,1,0:T(8,128)(2,1)}, u32[]{:S(2)}, u32[]{:S(2)}) async-start(bf16[16,144,300]{2,1,0:T(8,128)(2,1)} %pad_maximum_fusion.2), calls=%async_computation.6 | async-start | bytes 3538944 | tf_op jit(solution)/shard_map/all_to_all | solution.py:222
  224.0 17.1 %all-to-all-start.7 = ((bf16[16,2,1350]{2,1,0:T(2,128)(2,1)}), bf16[16,2,1350]{2,1,0:T(2,128)(2,1)}, u32[]{:S(2)}, u32[]{:S(2)}) async-start(bf16[16,2,1350]{2,1,0:T(2,128)(2,1)} %reshape.165), calls=%async_computation.7 | async-start | bytes 180224 | tf_op jit(solution)/shard_map/all_to_all | solution.py:224

commit v2 on v1

--- a/solution.py
+++ b/solution.py
@@ -88,7 +88,7 @@
     value_term = jnp.einsum(
         "nhc,nhd->hdc", attention_low, output_split, preferred_element_type=jnp.float32
     )
-    return (result, jnp.concatenate([key_term, value_term], axis=1).astype(jnp.bfloat16))
+    return (result, jnp.stack([key_term, value_term]).astype(jnp.bfloat16))
 
 
 ALL = ("s", "x", "y", "z", "c")
@@ -113,13 +113,6 @@
 def gather_groups(block, groups):
     copies = jnp.broadcast_to(block[None], (4,) + block.shape)
     return lax.all_to_all(copies, ALL, 0, 0, axis_index_groups=groups)
-
-
-def gather_rows(block):
-    core = lax.axis_index("c")
-    near = gather_groups(block, ring_groups(0))
-    whole = gather_groups(near, ring_groups(1))
-    return whole
 
 
 def both_cores(mine):
@@ -172,23 +165,34 @@
     samp_here, frames, patch_here, width = grad_out.shape
     slot_shape = (samp_here * frames, patch_here, width)
     core = lax.axis_index("c")
+    grad_rows = grad_out.reshape(-1, width)
+    halves = jnp.stack(
+        [
+            jnp.concatenate([t_out_weight[:, :640], t_qkv_weight[:, :1664]], axis=1),
+            jnp.concatenate([t_out_weight[:, 640:], t_qkv_weight[:, 1664:]], axis=1),
+        ]
+    ).reshape(2, 2, -1)
+    shard = lax.all_to_all(halves, "c", 0, 0)
+    column = lax.all_to_all(jnp.broadcast_to(shard[None], (4,) + shard.shape), "z", 0, 0).reshape(
+        72, 2 * width
+    )
+    cross_weights, column = lax.optimization_barrier((cross_weights, column))
     full_cross = cross_halves(cross_weights)
-    grad_rows = grad_out.reshape(-1, width)
-    shard = jnp.concatenate([t_out_weight, t_qkv_weight], axis=1).reshape(2, -1)
-    column = lax.all_to_all(
-        jnp.broadcast_to(shard[None], (8,) + shard.shape), ("z", "c"), 0, 0
-    ).reshape(72, 4 * width)
-    out_part = lax.dynamic_slice(column, (0, core * 512), (72, 640))
-    qkv_part = lax.dynamic_slice(column, (0, 1152 + core * 1664), (72, 1792))
-    out_first, out_second = both_cores(gather_rows(out_part))
-    qkv_first, qkv_second = both_cores(gather_rows(qkv_part))
+    out_near = gather_groups(column[:, :640], ring_groups(0))
+    qkv_part, out_near = lax.optimization_barrier((column[:, 640:], out_near))
+    qkv_near = gather_groups(qkv_part, ring_groups(0))
+    out_whole = gather_groups(out_near, ring_groups(1))
+    qkv_near, out_whole = lax.optimization_barrier((qkv_near, out_whole))
+    qkv_whole = gather_groups(qkv_near, ring_groups(1))
+    out_first, out_second = both_cores(out_whole)
+    qkv_first, qkv_second = both_cores(qkv_whole)
     grad_heads = (
         lax.dot_general(
             grad_rows[:, :640], out_first, CONTRACT_LAST, preferred_element_type=jnp.float32
         )
         + lax.dot_general(
             grad_rows[:, 640:],
-            out_second[:, 128:],
+            out_second[:, :512],
             CONTRACT_LAST,
             preferred_element_type=jnp.float32,
         )
@@ -196,13 +200,19 @@
     qkv_grad = temporal_grads(grad_heads.reshape(grad_out.shape), t_query, t_key, t_value).reshape(
         -1, 3 * width
     )
-    product = lax.dot_general(
-        qkv_grad[:, :1792], qkv_first, CONTRACT_LAST, preferred_element_type=jnp.float32
-    ) + lax.dot_general(
-        qkv_grad[:, 1792:],
-        qkv_second[:, 128:],
-        CONTRACT_LAST,
-        preferred_element_type=jnp.float32,
+    product = (
+        lax.dot_general(
+            qkv_grad[:, :1664], qkv_first, CONTRACT_LAST, preferred_element_type=jnp.float32
+        )
+        + lax.dot_general(
+            qkv_grad[:, 1664:1792],
+            out_second[:, 512:],
+            CONTRACT_LAST,
+            preferred_element_type=jnp.float32,
+        )
+        + lax.dot_general(
+            qkv_grad[:, 1792:], qkv_second, CONTRACT_LAST, preferred_element_type=jnp.float32
+        )
     )
     mixed_rows = (grad_rows.astype(jnp.float32) + product).astype(jnp.bfloat16)
     valid_keys = jnp.arange(cap_key.shape[0]) < cap_length[0]
@@ -219,9 +229,15 @@
         valid_keys,
     )
     grad_input = result_rows.reshape(frame_input.shape)
-    head = jnp.sum(lax.all_to_all(terms, ("x", "y"), 0, 0).astype(jnp.float32), axis=0)
-    pieces = head.astype(jnp.bfloat16).reshape(16, 9, -1)
-    piece = jnp.sum(lax.all_to_all(pieces, ("s", "z", "c"), 0, 0).astype(jnp.float32), axis=0)
+    chip = jnp.sum(lax.all_to_all(terms, "c", 0, 0).astype(jnp.float32), axis=0)
+    head = jnp.sum(
+        lax.all_to_all(chip.astype(jnp.bfloat16), ("x", "y"), 0, 0).astype(jnp.float32), axis=0
+    )
+    pieces = head.astype(jnp.bfloat16).reshape(1, 8, 9, -1)
+    targets = jnp.where(
+        jnp.arange(2)[:, None, None, None] == core, pieces, jnp.zeros_like(pieces)
+    ).reshape(16, 9, -1)
+    piece = jnp.sum(lax.all_to_all(targets, ("s", "z", "c"), 0, 0).astype(jnp.float32), axis=0)
     return (grad_input, piece.T)
 
 

time: 244 us -> 250 us (1.025)
  blocking collectives: 12.1 us -> 58.5 us
  waiting for transfers between devices: 73.5 us -> 46 us
  starting transfers between devices: 59.3 us -> 40.4 us
  local copies, waits for them, and re-layouts: 35 us -> 37.5 us
    all_to_all x0 -> x3, blocking collectives: none -> 30.7 us  [the longest x1 17.1 us: local(): lax.all_to_all(jnp.broadcast_to(shard[None], (4,) + shard.shape), 'z', 0, 0)]
    all_to_all x3 -> x2, waiting for transfers between devices: 38.3 us -> 13.6 us  [the longest x1 8.34 us: local(): lax.all_to_all(chip.astype(jnp.bfloat16), ('x', 'y'), 0, 0)]
    all_to_all x1 -> x2, blocking collectives: 12.1 us -> 27.8 us  [gather_groups(): return lax.all_to_all(copies, ALL, 0, 0, axis_index_groups=groups)]
    all_to_all x3 -> x2, starting transfers between devices: 23 us -> 10.6 us  [the longest x1 6.26 us: local(): lax.all_to_all(targets, ('s', 'z', 'c'), 0, 0).astype(jnp.float32)]
    all_to_all x3 -> x2, starting transfers between devices: 12.8 us -> 8.95 us  [gather_groups(): return lax.all_to_all(copies, ALL, 0, 0, axis_index_groups=groups)]
    concatenate x2, other arithmetic: 3.87 us -> 0.02 us  [the longest x1 0.01 us: local(): jnp.concatenate([t_out_weight[:, 640:], t_qkv_weight[:, 1664:]], axis=1)]
    reshape x3 -> x2, local copies, waits for them, and re-layouts: 4.76 us -> 1.15 us
    ppermute x2, starting transfers between devices: 8.31 us -> 4.8 us  [both_cores(): other = lax.ppermute(mine, 'c', [(0, 1), (1, 0)])]
  transfers between devices with their start and end apart: 11 -> 9, of which waited for: 7 -> 5; matrix products, arithmetic and copies ran while one was open for 21% -> 21% of each run, Pallas kernels for 0% -> 0%
where the time goes in v2:
time: 250 us; the launch traced here: 249 us
  blocking collectives  58.5 us (23%)
  waiting for transfers between devices  46 us (18%)
  matrix products  44.9 us (18%)
  starting transfers between devices  40.4 us (16%)
  local copies, waits for them, and re-layouts  37.5 us (15%)
  other arithmetic  19.9 us (8%)
    all_to_all x2, blocking collectives, gather_groups(): return lax.all_to_all(copies, ALL, 0, 0, axis_index_groups=groups)  27.8 us
    all_to_all x1, blocking collectives, local(): lax.all_to_all(jnp.broadcast_to(shard[None], (4,) + shard.shape), 'z', 0, 0)  17.1 us
    ppermute x1, waiting for transfers between devices, cross_halves(): got = lax.ppermute(part, ALL, pairs)  16.2 us
    unnamed x32, local copies, waits for them, and re-layouts  12 us
    all_to_all x1, waiting for transfers between devices, local(): lax.all_to_all(mixed_rows.reshape(slot_shape), SEQ, split_axis=0, concat_...  10.1 us
    all_to_all x2, starting transfers between devices, gather_groups(): return lax.all_to_all(copies, ALL, 0, 0, axis_index_groups=groups)  8.95 us
    ppermute x1, starting transfers between devices, cross_halves(): swapped = lax.ppermute(got, 'c', [(0, 1), (1, 0)])  8.56 us
    all_to_all x1, waiting for transfers between devices, local(): lax.all_to_all(chip.astype(jnp.bfloat16), ('x', 'y'), 0, 0)  8.34 us
  transfers between devices with their start and end apart: 9, of which 5 were waited for; matrix products, arithmetic and copies ran while one was open for 21% of the time, Pallas kernels for 0%

profile of v2, /device:TPU:1, one launch (start us, length us, event | category | flops | bytes accessed | tf_op | source)
XLA Modules:
  0.0 248.9 jit_solution(11096450304674741440)
XLA Ops:
  0.6 0.9 slice.49
  1.5 0.8 slice.51
  2.3 0.7 slice.48
  3.1 0.7 slice.50
  4.1 6.7 %all_to_all.54 = bf16[2,2,10368]{2,1,0:T(2,128)(2,1)S(1)} all-to-all(bf16[2,2,10368]{2,1,0:T(2,128)(2,1)S(1)} %pad_maximum_fusion.7), channel_id=1, replica_groups=mesh['s'=2,'x'=4,'y'=4,'z'=4,'c'=2] {'c'}, dimensions={0} | all-to-all | bytes 165888 | tf_op jit(solution)/shard_map/all_to_all | solution.py:175
  10.9 17.1 %all_to_all.55 = bf16[4,2,2,10368]{3,2,1,0:T(2,128)(2,1)S(1)} all-to-all(bf16[4,2,2,10368]{3,2,1,0:T(2,128)(2,1)S(1)} %broadcast_in_dim.45), channel_id=1, replica_groups=mesh['s'=2,'x'=4,'y'=4,'z'=4,'c'=2] {'z'}, dimensions={0} | all-to-all | bytes 663552 | tf_op jit(solution)/shard_map/all_to_all | solution.py:176
  28.2 0.8 broadcast_in_dim.84
  29.0 4.2 %all-to-all-start.2 = ((bf16[4,72,640]{2,1,0:T(8,128)(2,1)}), bf16[4,72,640]{2,1,0:T(8,128)(2,1)S(1)}, u32[]{:S(2)}, u32[]{:S(2)}) async-start(bf16[4,72,640]{2,1,0:T(8,128)(2,1)} %broadcast_in_dim.84), calls=%async_computation.2 | async-start | bytes 737280 | tf_op jit(solution)/shard_map/all_to_all | solution.py:115
  33.2 6.1 %all-to-all-done.2 = bf16[4,72,640]{2,1,0:T(8,128)(2,1)S(1)} async-done(((bf16[4,72,640]{2,1,0:T(8,128)(2,1)}), bf16[4,72,640]{2,1,0:T(8,128)(2,1)S(1)}, u32[]{:S(2)}, u32[]{:S(2)}) %all-to-all-start.2) | async-done | bytes 368672 | tf_op jit(solution)/shard_map/all_to_all | solution.py:115
  39.4 11.9 %all_to_all.56 = bf16[4,72,1664]{2,1,0:T(8,128)(2,1)S(1)} all-to-all(bf16[4,72,1664]{2,1,0:T(8,128)(2,1)S(1)} %broadcast_in_dim.85), channel_id=1, replica_groups={{0,32,64,96},{1,9,17,25},{8,40,72,104},{33,41,49,57},{16,48,80,112},{65..., dimensions={0} | all-to-all | bytes 1916928 | tf_op jit(solution)/shard_map/all_to_all | solution.py:115
  51.4 15.8 %all_to_all.57 = bf16[4,4,72,640]{3,2,1,0:T(8,128)(2,1)S(1)} all-to-all(bf16[4,4,72,640]{3,2,1,0:T(8,128)(2,1)S(1)} %broadcast_in_dim.86), channel_id=1, replica_groups={{1,33,65,97},{0,8,16,24},{9,41,73,105},{32,40,48,56},{17,49,81,113},{64..., dimensions={0} | all-to-all | bytes 2949120 | tf_op jit(solution)/shard_map/all_to_all | solution.py:115
  67.3 2.2 broadcast_in_dim.87
  69.4 4.8 %all-to-all-start.5 = ((bf16[4,4,72,1664]{3,2,1,0:T(8,128)(2,1)}), bf16[4,4,72,1664]{3,2,1,0:T(8,128)(2,1)}, u32[]{:S(2)}, u32[]{:S(2)}) async-start(bf16[4,4,72,1664]{3,2,1,0:T(8,128)(2,1)} %broadcast_in_dim.87), calls=%async_computation.5 | async-start | bytes 7667712 | tf_op jit(solution)/shard_map/all_to_all | solution.py:115
  74.2 1.4 dynamic-slice_bitcast_fusion
  75.6 0.9 collective-permute-start.2
  76.5 16.2 %collective-permute-done.2 = bf16[576,1152]{1,0:T(8,128)(2,1)} collective-permute-done((bf16[576,1152]{1,0:T(8,128)(2,1)S(1)}, bf16[576,1152]{1,0:T(8,128)(2,1)}, u32[]{:S(2)}, u32[]{:S(2)}) %collective-permute-start.2) | collective-permute-done | bytes 1327136 | tf_op jit(solution)/shard_map/ppermute | solution.py:144
  92.7 8.6 %collective-permute-start.3 = (bf16[576,1152]{1,0:T(8,128)(2,1)}, bf16[576,1152]{1,0:T(8,128)(2,1)}, u32[]{:S(2)}, u32[]{:S(2)}) collective-permute-start(bf16[576,1152]{1,0:T(8,128)(2,1)} %collective-permute-done.2), channel_id=1, source_target_pairs={{0,1},{1,0},{2,3},{3,2},{4,5},{5,4},{6,7},{7,6},{8,9},{9,8},{10,11... | collective-permute-start | bytes 3981320 | tf_op jit(solution)/shard_map/ppermute | solution.py:145
  102.0 4.4 %copy.171 = bf16[4,4,72,1664]{3,2,0,1:T(8,128)(2,1)} copy(bf16[4,4,72,1664]{3,2,1,0:T(8,128)(2,1)} %all-to-all-done.5) | data formatting | bytes 7667712 | tf_op jit(solution)/shard_map/all_to_all | solution.py:115
  106.4 4.5 %collective-permute-start.1 = (bf16[4,4,72,1664]{3,2,0,1:T(8,128)(2,1)}, bf16[4,4,72,1664]{3,2,0,1:T(8,128)(2,1)}, u32[]{:S(2)}, u32[]{:S(2)}) collective-permute-start(bf16[4,4,72,1664]{3,2,0,1:T(8,128)(2,1)} %copy.171), channel_id=1, source_target_pairs={{0,1},{1,0},{2,3},{3,2},{4,5},{5,4},{6,7},{7,6},{8,9},{9,8},{10,11... | collective-permute-start | bytes 11501576 | tf_op jit(solution)/shard_map/ppermute | solution.py:120
  110.9 0.9 reshape.162
  111.9 0.9 reshape.156
  112.8 2.1 reshape.157
  114.9 2.4 copy.179
  117.3 2.2 copy.177
  119.5 1.5 fusion.98
  121.5 2.1 select_bitcast_fusion.1
  123.7 2.9 %broadcast_select_fusion.3 = (bf16[2,576,1152]{2,1,0:T(8,128)(2,1)}, bf16[2,576,1152]{2,1,0:T(8,128)(2,1)}) fusion(bf16[2,576,1152]{2,1,0:T(8,128)(2,1)S(1)} %copy-done.2, pred[]{:T(512)S(6)} %eq.24, bf16[1,576,1152]{2,1,0:T(8,128)(2,1)S(1)} %get-tuple-element.21, bf16[1,576,1152]{2,1,0:T(8,128)(2,1)S(1)} %get-tuple-element.20), kind=kLoop, calls=%fused_computation.16 | loop fusion | flops 3981312 | bytes 10616833 | tf_op jit(solution)/shard_map/jit(_where)/select_n | solution.py:147
  127.1 0.8 copy-done.5
  128.4 0.6 fusion.24
  129.8 1.4 fusion.51
  131.2 3.0 %fusion.41 = bf16[2,64,1,16,72]{4,1,3,0,2:T(8,128)(2,1)S(1)} fusion(f32[2,16,64,64]{2,3,1,0:T(8,128)} %fusion.51, bf16[2,64,16,72]{3,2,1,0:T(8,128)(2,1)} %copy-done.8, f32[2,16,64,64]{2,3,1,0:T(8,128)} %get-tuple-element.23, f32[2,16,64]{2,1,0:T(8,128)S(1)} %get-tuple-element.22), kind=kOutput, calls=%fused_computation.66 | convolution fusion | flops 19941440 | bytes 1646592 | tf_op jit(solution)/shard_map/sphfg,sfphd->sgphd/dot_general | solution.py:46
  135.1 1.7 fusion.42
  137.6 3.8 %fusion.40 = bf16[2,64,1,16,72]{4,1,3,0,2:T(8,128)(2,1)} fusion(f32[2,16,64,64]{2,3,1,0:T(8,128)} %fusion.51, bf16[2,64,16,72]{3,2,1,0:T(8,128)(2,1)} %copy-done.7, f32[2,16,64,64]{2,3,1,0:T(8,128)} %get-tuple-element.23, f32[2,16,64]{2,1,0:T(8,128)S(1)} %get-tuple-element.22), kind=kOutput, calls=%fused_computation.65 | convolution fusion | flops 19941440 | bytes 1646592 | tf_op jit(solution)/shard_map/sphfg,sgphd->sfphd/dot_general | solution.py:43
  141.4 1.4 copy.167
  143.5 3.6 %broadcast_select_fusion.1 = (bf16[4,4,72,1664]{3,2,0,1:T(8,128)(2,1)S(1)}, bf16[4,4,72,1664]{3,2,0,1:T(8,128)(2,1)S(1)}) fusion(bf16[4,4,72,1664]{3,2,0,1:T(8,128)(2,1)} %collective-permute-done.1, pred[]{:T(512)S(6)} %eq.23, bf16[4,4,72,1664]{3,2,1,0:T(8,128)(2,1)} %all-to-all-done.5), kind=kLoop, calls=%fused_computation.7 | loop fusion | flops 3833856 | bytes 15335425 | tf_op jit(solution)/shard_map/jit(_where)/select_n | solution.py:122
  147.5 1.2 fusion.60
  148.7 2.0 fusion.23
  151.2 1.7 reduce.8
  152.9 1.1 reshape.175
  154.0 6.6 %all-to-all-start.6 = ((bf16[128,2,576]{2,1,0:T(2,128)(2,1)}), bf16[128,2,576]{2,1,0:T(2,128)(2,1)}, u32[]{:S(2)}, u32[]{:S(2)}) async-start(bf16[128,2,576]{2,1,0:T(2,128)(2,1)} %reshape.175), calls=%async_computation.6 | async-start | bytes 655360 | tf_op jit(solution)/shard_map/all_to_all | solution.py:219
  160.6 2.2 convolution_convert_fusion
  162.8 3.8 %fusion.103 = (f32[128,16]{0,1:T(8,128)S(1)}, f32[128,16,300]{0,2,1:T(8,128)}) fusion(pred[300]{0:T(512)(128)(4,1)S(1)} %iota_compare_fusion, bf16[128,16,72]{0,2,1:T(8,128)(2,1)S(1)} %bitcast.158, bf16[300,16,72]{0,2,1:T(8,128)(2,1)} %bitcast.151), kind=kOutput, calls=%fused_computation.121 | convolution fusion | flops 90931496 | bytes 3452204 | tf_op jit(solution)/shard_map/sub | solution.py:69
  166.7 10.1 %all-to-all-done.6 = bf16[128,2,576]{2,1,0:T(2,128)(2,1)} async-done(((bf16[128,2,576]{2,1,0:T(2,128)(2,1)}), bf16[128,2,576]{2,1,0:T(2,128)(2,1)}, u32[]{:S(2)}, u32[]{:S(2)}) %all-to-all-start.6) | async-done | bytes 294944 | tf_op jit(solution)/shard_map/all_to_all | solution.py:219
  176.7 2.5 %reshape.176 = bf16[128,1,1152]{2,1,0:T(2,128)(2,1)S(1)} reshape(bf16[128,2,576]{2,1,0:T(2,128)(2,1)} %all-to-all-done.6) | data formatting | bytes 589824
  179.2 3.0 %fusion.20 = bf16[128,1152]{1,0:T(8,128)(2,1)} fusion(bf16[2,576,1152]{2,1,0:T(8,128)(2,1)} %get-tuple-element.17, bf16[2,576,1152]{2,1,0:T(8,128)(2,1)S(1)} %copy-done.1, bf16[128,1,1152]{2,1,0:T(2,128)(2,1)S(1)} %reshape.176), kind=kOutput, calls=%fused_computation.35 | convolution fusion | flops 345194496 | bytes 5898240 | tf_op jit(solution)/shard_map/dot_general | solution.py:57
  182.2 1.8 copy.178
  184.0 3.4 %fusion.104 = f32[16,128,300]{1,2,0:T(8,128)} fusion(bf16[128,16,72]{0,2,1:T(8,128)(2,1)} %bitcast.149, bf16[300,16,72]{0,2,1:T(8,128)(2,1)} %bitcast.146), kind=kOutput, calls=%fused_computation.122 | convolution fusion | flops 88473600 | bytes 3443712 | tf_op jit(solution)/shard_map/nhd,chd->nhc/dot_general | solution.py:71
  187.5 1.8 fusion.34
  189.3 5.8 %fusion.33 = bf16[1,16,72,300]{3,2,1,0:T(8,128)(2,1)} fusion(bf16[128,16,72]{0,2,1:T(8,128)(2,1)} %bitcast.159, f32[16,128,300]{1,2,0:T(8,128)} %fusion.104, f32[128,16,300]{0,2,1:T(8,128)} %get-tuple-element.25, f32[128,16]{0,1:T(8,128)S(1)} %get-tuple-element.24), kind=kOutput, calls=%fused_computation.54 | convolution fusion | flops 93122344 | bytes 5909504 | tf_op jit(solution)/shard_map/nhc,nhd->hdc/dot_general | solution.py:85
  195.2 1.8 pad_maximum_fusion.2
  196.9 7.0 %all_to_all.58 = bf16[2,16,72,300]{3,2,1,0:T(8,128)(2,1)} all-to-all(bf16[2,16,72,300]{3,2,1,0:T(8,128)(2,1)S(1)} %pad_maximum_fusion.2), channel_id=1, replica_groups=mesh['s'=2,'x'=4,'y'=4,'z'=4,'c'=2] {'c'}, dimensions={0} | all-to-all | bytes 2764800 | tf_op jit(solution)/shard_map/all_to_all | solution.py:232
  203.9 3.0 %reduce_sum.73 = bf16[16,72,300]{2,1,0:T(8,128)(2,1)} reduce(bf16[2,16,72,300]{3,2,1,0:T(8,128)(2,1)} %all_to_all.58, bf16[]{:T(256)} %constant.29.clone.1), dimensions={0}, to_apply=%region_6.7 | reduce | flops 345600 | bytes 2073602 | tf_op jit(solution)/shard_map/reduce_sum | solution.py:232
  206.9 4.3 %all-to-all-start.8 = ((bf16[16,72,300]{2,1,0:T(8,128)(2,1)}), bf16[16,72,300]{2,1,0:T(8,128)(2,1)}, u32[]{:S(2)}, u32[]{:S(2)}) async-start(bf16[16,72,300]{2,1,0:T(8,128)(2,1)} %reduce_sum.73), calls=%async_computation.8 | async-start | bytes 1769472 | tf_op jit(solution)/shard_map/all_to_all | solution.py:234
  211.4 5.9 %convolution_convert_fusion.6 = bf16[16,128,72]{1,2,0:T(8,128)(2,1)} fusion(bf16[300,16,72]{0,2,1:T(8,128)(2,1)} %bitcast.152, f32[16,128,300]{1,2,0:T(8,128)} %fusion.104, f32[128,16,300]{0,2,1:T(8,128)} %get-tuple-element.25, f32[128,16]{0,1:T(8,128)S(1)} %get-tuple-element.24), kind=kOutput, calls=%fused_computation.68 | convolution fusion | flops 92924200 | bytes 5909504 | tf_op jit(solution)/shard_map/nhc,chd->nhd/dot_general | solution.py:77
  217.2 8.3 %all-to-all-done.8 = bf16[16,72,300]{2,1,0:T(8,128)(2,1)} async-done(((bf16[16,72,300]{2,1,0:T(8,128)(2,1)}), bf16[16,72,300]{2,1,0:T(8,128)(2,1)}, u32[]{:S(2)}, u32[]{:S(2)}) %all-to-all-start.8) | async-done | bytes 691232 | tf_op jit(solution)/shard_map/all_to_all | solution.py:234
  225.6 1.9 reduce_sum.74
  227.5 1.5 broadcast_in_dim.93
  229.0 1.7 bitcast_select_fusion
  230.7 1.8 reshape.177
  232.4 6.3 %all-to-all-start.9 = ((bf16[16,2,1350]{2,1,0:T(2,128)(2,1)}), bf16[16,2,1350]{2,1,0:T(2,128)(2,1)}, u32[]{:S(2)}, u32[]{:S(2)}) async-start(bf16[16,2,1350]{2,1,0:T(2,128)(2,1)} %reshape.177), calls=%async_computation.9 | async-start | bytes 180224 | tf_op jit(solution)/shard_map/all_to_all | solution.py:240
  238.7 3.1 %fusion.25 = bf16[1,128,1152]{2,1,0:T(8,128)(2,1)} fusion(bf16[128,1152]{0,1:T(8,128)(2,1)} %bitcast.157, bf16[128,1,1152]{2,1,0:T(2,128)(2,1)S(1)} %reshape.176, bf16[2,576,1152]{2,1,0:T(8,128)(2,1)S(1)} %copy-done.1, bf16[2,576,1152]{2,1,0:T(8,128)(2,1)} %get-tuple-element.17), kind=kOutput, calls=%fused_computation.39 | convolution fusion | flops 345489408 | bytes 6193152 | tf_op jit(solution)/shard_map/dot_general | solution.py:83
  241.8 5.3 %all-to-all-done.9 = bf16[16,2,1350]{2,1,0:T(2,128)(2,1)} async-done(((bf16[16,2,1350]{2,1,0:T(2,128)(2,1)}), bf16[16,2,1350]{2,1,0:T(2,128)(2,1)}, u32[]{:S(2)}, u32[]{:S(2)}) %all-to-all-start.9) | async-done | bytes 86432 | tf_op jit(solution)/shard_map/all_to_all | solution.py:240
  247.1 1.1 reshape.178
  248.2 0.7 convert_reduce_fusion
  (59 shorter events, 6.6 us)
Async XLA Ops:
  0.6 159.9 %copy-start = (bf16[1,128,1152]{2,1,0:T(8,128)(2,1)S(1)}, bf16[1,128,1152]{2,1,0:T(8,128)(2,1)}, u32[]{:S(2)}) copy-start(bf16[1,128,1152]{2,1,0:T(8,128)(2,1)} %param.17) | copy-start | bytes 884740
  29.0 10.3 %all-to-all-start.2 = ((bf16[4,72,640]{2,1,0:T(8,128)(2,1)}), bf16[4,72,640]{2,1,0:T(8,128)(2,1)S(1)}, u32[]{:S(2)}, u32[]{:S(2)}) async-start(bf16[4,72,640]{2,1,0:T(8,128)(2,1)} %broadcast_in_dim.84), calls=%async_computation.2 | async-start | bytes 737280 | tf_op jit(solution)/shard_map/all_to_all | solution.py:115
  69.4 32.6 %all-to-all-start.5 = ((bf16[4,4,72,1664]{3,2,1,0:T(8,128)(2,1)}), bf16[4,4,72,1664]{3,2,1,0:T(8,128)(2,1)}, u32[]{:S(2)}, u32[]{:S(2)}) async-start(bf16[4,4,72,1664]{3,2,1,0:T(8,128)(2,1)} %broadcast_in_dim.87), calls=%async_computation.5 | async-start | bytes 7667712 | tf_op jit(solution)/shard_map/all_to_all | solution.py:115
  75.6 17.1 %collective-permute-start.2 = (bf16[576,1152]{1,0:T(8,128)(2,1)S(1)}, bf16[576,1152]{1,0:T(8,128)(2,1)}, u32[]{:S(2)}, u32[]{:S(2)}) collective-permute-start(bf16[576,1152]{1,0:T(8,128)(2,1)S(1)} %dynamic-slice_bitcast_fusion), channel_id=1, source_target_pairs={{0,128},{1,135},{128,2},{129,1},{2,130},{3,129},{130,4},{131,3},{4... | collective-permute-start | bytes 3981320 | tf_op jit(solution)/shard_map/ppermute | solution.py:144
  92.7 28.7 %collective-permute-start.3 = (bf16[576,1152]{1,0:T(8,128)(2,1)}, bf16[576,1152]{1,0:T(8,128)(2,1)}, u32[]{:S(2)}, u32[]{:S(2)}) collective-permute-start(bf16[576,1152]{1,0:T(8,128)(2,1)} %collective-permute-done.2), channel_id=1, source_target_pairs={{0,1},{1,0},{2,3},{3,2},{4,5},{5,4},{6,7},{7,6},{8,9},{9,8},{10,11... | collective-permute-start | bytes 3981320 | tf_op jit(solution)/shard_map/ppermute | solution.py:145
  102.0 9.0 %copy-start.9 = (bf16[2,64,1,1152]{3,1,2,0:T(8,128)(2,1)S(1)}, bf16[2,64,1,1152]{3,1,2,0:T(8,128)(2,1)}, u32[]{:S(2)}) copy-start(bf16[2,64,1,1152]{3,1,2,0:T(8,128)(2,1)} %param.14) | copy-start | bytes 884740
  102.0 9.9 %copy-start.10 = (bf16[2,64,1,1152]{3,1,2,0:T(8,128)(2,1)S(1)}, bf16[2,64,1,1152]{3,1,2,0:T(8,128)(2,1)}, u32[]{:S(2)}) copy-start(bf16[2,64,1,1152]{3,1,2,0:T(8,128)(2,1)} %param.12) | copy-start | bytes 884740
  106.4 37.1 %collective-permute-start.1 = (bf16[4,4,72,1664]{3,2,0,1:T(8,128)(2,1)}, bf16[4,4,72,1664]{3,2,0,1:T(8,128)(2,1)}, u32[]{:S(2)}, u32[]{:S(2)}) collective-permute-start(bf16[4,4,72,1664]{3,2,0,1:T(8,128)(2,1)} %copy.171), channel_id=1, source_target_pairs={{0,1},{1,0},{2,3},{3,2},{4,5},{5,4},{6,7},{7,6},{8,9},{9,8},{10,11... | collective-permute-start | bytes 11501576 | tf_op jit(solution)/shard_map/ppermute | solution.py:120
  112.8 8.2 %copy-start.8 = (bf16[2,64,16,72]{3,2,1,0:T(8,128)(2,1)}, bf16[2,64,16,72]{3,2,1,0:T(8,128)(2,1)S(1)}, u32[]{:S(2)}) copy-start(bf16[2,64,16,72]{3,2,1,0:T(8,128)(2,1)S(1)} %reshape.156) | copy-start | bytes 884740
  114.9 6.1 %copy-start.7 = (bf16[2,64,16,72]{3,2,1,0:T(8,128)(2,1)}, bf16[2,64,16,72]{3,2,1,0:T(8,128)(2,1)S(1)}, u32[]{:S(2)}) copy-start(bf16[2,64,16,72]{3,2,1,0:T(8,128)(2,1)S(1)} %reshape.157) | copy-start | bytes 884740
  121.2 2.6 %copy-start.2 = (bf16[2,576,1152]{2,1,0:T(8,128)(2,1)S(1)}, bf16[2,576,1152]{2,1,0:T(8,128)(2,1)}, u32[]{:S(2)}) copy-start(bf16[2,576,1152]{2,1,0:T(8,128)(2,1)} %param.18) | copy-start | bytes 7962628
  121.2 5.5 %collective-permute-start = (bf16[4,4,72,640]{3,2,0,1:T(8,128)(2,1)S(1)}, bf16[4,4,72,640]{3,2,0,1:T(8,128)(2,1)S(1)}, u32[]{:S(2)}, u32[]{:S(2)}) collective-permute-start(bf16[4,4,72,640]{3,2,0,1:T(8,128)(2,1)S(1)} %copy.159), channel_id=1, source_target_pairs={{0,1},{1,0},{2,3},{3,2},{4,5},{5,4},{6,7},{7,6},{8,9},{9,8},{10,11... | collective-permute-start | bytes 4423688 | tf_op jit(solution)/shard_map/ppermute | solution.py:120
  127.0 1.0 copy-start.5
  129.8 4.4 %copy-start.3 = (bf16[2,64,16,72]{3,1,2,0:T(8,128)(2,1)}, bf16[2,64,16,72]{3,1,2,0:T(8,128)(2,1)S(1)}, u32[]{:S(2)}) copy-start(bf16[2,64,16,72]{3,1,2,0:T(8,128)(2,1)S(1)} %copy.163) | copy-start | bytes 884740
  147.5 1.2 copy-start.6
  148.7 11.9 %copy-start.1 = (bf16[2,576,1152]{2,1,0:T(8,128)(2,1)S(1)}, bf16[2,576,1152]{2,1,0:T(8,128)(2,1)}, u32[]{:S(2)}) copy-start(bf16[2,576,1152]{2,1,0:T(8,128)(2,1)} %get-tuple-element.16) | copy-start | bytes 7962628
  154.0 22.7 %all-to-all-start.6 = ((bf16[128,2,576]{2,1,0:T(2,128)(2,1)}), bf16[128,2,576]{2,1,0:T(2,128)(2,1)}, u32[]{:S(2)}, u32[]{:S(2)}) async-start(bf16[128,2,576]{2,1,0:T(2,128)(2,1)} %reshape.175), calls=%async_computation.6 | async-start | bytes 655360 | tf_op jit(solution)/shard_map/all_to_all | solution.py:219
  162.8 3.8 %copy-start.11 = (bf16[1152,128]{1,0:T(8,128)(2,1)}, bf16[1152,128]{1,0:T(8,128)(2,1)S(1)}, u32[]{:S(2)}) copy-start(bf16[1152,128]{1,0:T(8,128)(2,1)S(1)} %convolution_convert_fusion) | copy-start | bytes 884740
  184.0 3.4 %copy-start.4 = (bf16[128,1152]{0,1:T(8,128)(2,1)S(1)}, bf16[128,1152]{0,1:T(8,128)(2,1)}, u32[]{:S(2)}) copy-start(bf16[128,1152]{0,1:T(8,128)(2,1)} %copy.178) | copy-start | bytes 884740
  184.0 3.4 %copy-start.12 = (f32[128,16,300]{0,2,1:T(8,128)S(1)}, f32[128,16,300]{0,2,1:T(8,128)}, u32[]{:S(2)}) copy-start(f32[128,16,300]{0,2,1:T(8,128)} %get-tuple-element.25) | copy-start | bytes 7372804
  206.9 18.7 %all-to-all-start.8 = ((bf16[16,72,300]{2,1,0:T(8,128)(2,1)}), bf16[16,72,300]{2,1,0:T(8,128)(2,1)}, u32[]{:S(2)}, u32[]{:S(2)}) async-start(bf16[16,72,300]{2,1,0:T(8,128)(2,1)} %reduce_sum.73), calls=%async_computation.8 | async-start | bytes 1769472 | tf_op jit(solution)/shard_map/all_to_all | solution.py:234
  232.4 14.6 %all-to-all-start.9 = ((bf16[16,2,1350]{2,1,0:T(2,128)(2,1)}), bf16[16,2,1350]{2,1,0:T(2,128)(2,1)}, u32[]{:S(2)}, u32[]{:S(2)}) async-start(bf16[16,2,1350]{2,1,0:T(2,128)(2,1)} %reshape.177), calls=%async_computation.9 | async-start | bytes 180224 | tf_op jit(solution)/shard_map/all_to_all | solution.py:240

commit v3 on v1

--- a/solution.py
+++ b/solution.py
@@ -2,6 +2,7 @@
 
 import jax
 import jax.numpy as jnp
+import numpy as np
 from jax import lax
 from jax.sharding import Mesh, PartitionSpec as P
 
@@ -51,7 +52,7 @@
     )
 
 
-def cross_grads(x_rows, d_rows, w_query, w_out, cap_key, cap_value, valid_keys):
+def cross_grads(x_rows, d_rows, place, w_query, w_out, cap_key, cap_value, valid_keys):
     scaling = 1.0 / math.sqrt(HEAD_DIM)
     cross_query = jnp.dot(x_rows, w_query, preferred_element_type=jnp.float32).astype(jnp.bfloat16)
     out_grad = lax.dot_general(
@@ -79,7 +80,7 @@
         ).astype(jnp.bfloat16)
     )
     result = (
-        d_rows.astype(jnp.float32)
+        jnp.dot(d_rows, place, preferred_element_type=jnp.float32)
         + lax.dot_general(cq_grad, w_query, CONTRACT_LAST, preferred_element_type=jnp.float32)
     ).astype(jnp.bfloat16)
     key_term = jnp.einsum(
@@ -115,20 +116,24 @@
     return lax.all_to_all(copies, ALL, 0, 0, axis_index_groups=groups)
 
 
-def gather_rows(block):
+def swap_cores(block):
+    return lax.ppermute(block, "c", [(0, 1), (1, 0)])
+
+
+def in_core_order(mine, other):
     core = lax.axis_index("c")
-    near = gather_groups(block, ring_groups(0))
-    whole = gather_groups(near, ring_groups(1))
-    return whole
-
-
-def both_cores(mine):
-    core = lax.axis_index("c")
-    other = lax.ppermute(mine, "c", [(0, 1), (1, 0)])
-    rows = mine.shape[2] * 16
-    first = jnp.where(core == 0, mine, other).transpose(1, 0, 2, 3)
-    second = jnp.where(core == 0, other, mine)
-    return first.reshape(rows, -1), second.reshape(rows, -1)
+    return jnp.stack([jnp.where(core == 0, mine, other), jnp.where(core == 0, other, mine)])
+
+
+def feature_order():
+    order = np.full((2, 4, 4, 40), -1, np.int32)
+    for c in range(2):
+        for i in range(4):
+            for j in range(4):
+                x, y = (j, i) if c == 0 else (i, j)
+                for q in range(36):
+                    order[c, i, j, q] = 72 * (4 * x + y) + 18 * (q // 9) + 9 * c + q % 9
+    return order.reshape(1280)
 
 
 def cross_halves(cross_weights):
@@ -169,51 +174,61 @@
     cap_value,
     cap_length,
 ):
-    samp_here, frames, patch_here, width = grad_out.shape
-    slot_shape = (samp_here * frames, patch_here, width)
+    width = grad_out.shape[-1]
     core = lax.axis_index("c")
+    grad_rows = grad_out.reshape(-1, width)
+    rows = grad_rows.shape[0]
+    place = (jnp.asarray(feature_order())[:, None] == jnp.arange(width)[None, :]).astype(
+        jnp.bfloat16
+    )
+    place_mine = lax.dynamic_slice(place, (core * 640, 0), (640, width))
+    grad_both = in_core_order(grad_rows, swap_cores(grad_rows)).reshape(2 * rows, width)
+    shard = jnp.concatenate([t_out_weight, t_qkv_weight], axis=1).reshape(2, -1)
+    column = lax.all_to_all(jnp.broadcast_to(shard[None], (4,) + shard.shape), "z", 0, 0)
+    column = jnp.pad(column.reshape(36, 4 * width), ((0, 4), (0, 0)))
+    cross_weights, column = lax.optimization_barrier((cross_weights, column))
     full_cross = cross_halves(cross_weights)
-    grad_rows = grad_out.reshape(-1, width)
-    shard = jnp.concatenate([t_out_weight, t_qkv_weight], axis=1).reshape(2, -1)
-    column = lax.all_to_all(
-        jnp.broadcast_to(shard[None], (8,) + shard.shape), ("z", "c"), 0, 0
-    ).reshape(72, 4 * width)
-    out_part = lax.dynamic_slice(column, (0, core * 512), (72, 640))
-    qkv_part = lax.dynamic_slice(column, (0, 1152 + core * 1664), (72, 1792))
-    out_first, out_second = both_cores(gather_rows(out_part))
-    qkv_first, qkv_second = both_cores(gather_rows(qkv_part))
-    grad_heads = (
-        lax.dot_general(
-            grad_rows[:, :640], out_first, CONTRACT_LAST, preferred_element_type=jnp.float32
-        )
-        + lax.dot_general(
-            grad_rows[:, 640:],
-            out_second[:, 128:],
-            CONTRACT_LAST,
-            preferred_element_type=jnp.float32,
-        )
+    near = gather_groups(column, ring_groups(0))
+    out_mine = gather_groups(near[:, :, :width], ring_groups(1))
+    near, out_mine = lax.optimization_barrier((near, out_mine))
+    qkv_mine = gather_groups(near[:, :, width:], ring_groups(1)).reshape(640, 3 * width)
+    out_mine = out_mine.reshape(640, width)
+    heads_mine = (
+        lax.dot_general(grad_both, out_mine, CONTRACT_LAST, preferred_element_type=jnp.float32)
+        .astype(jnp.bfloat16)
+        .reshape(2, rows, 640)
+    )
+    kept = lax.dynamic_index_in_dim(heads_mine, core, 0, keepdims=False)
+    sent = lax.dynamic_index_in_dim(heads_mine, 1 - core, 0, keepdims=False)
+    heads_parts = in_core_order(kept, swap_cores(sent))
+    grad_heads = jnp.dot(
+        jnp.concatenate([heads_parts[0], heads_parts[1]], axis=1),
+        place,
+        preferred_element_type=jnp.float32,
     ).astype(jnp.bfloat16)
     qkv_grad = temporal_grads(grad_heads.reshape(grad_out.shape), t_query, t_key, t_value).reshape(
-        -1, 3 * width
+        rows, 3 * width
+    )
+    qkv_both = in_core_order(qkv_grad, swap_cores(qkv_grad)).reshape(2 * rows, 3 * width)
+    residual = lax.dot_general(
+        grad_both, place_mine, CONTRACT_LAST, preferred_element_type=jnp.float32
     )
     product = lax.dot_general(
-        qkv_grad[:, :1792], qkv_first, CONTRACT_LAST, preferred_element_type=jnp.float32
-    ) + lax.dot_general(
-        qkv_grad[:, 1792:],
-        qkv_second[:, 128:],
-        CONTRACT_LAST,
-        preferred_element_type=jnp.float32,
-    )
-    mixed_rows = (grad_rows.astype(jnp.float32) + product).astype(jnp.bfloat16)
+        qkv_both, qkv_mine, CONTRACT_LAST, preferred_element_type=jnp.float32
+    )
+    mixed = (residual + product).astype(jnp.bfloat16).reshape(2, rows, 640)
+    w_out_placed = lax.dot_general(
+        full_cross[1], place, CONTRACT_LAST, preferred_element_type=jnp.float32
+    ).astype(jnp.bfloat16)
     valid_keys = jnp.arange(cap_key.shape[0]) < cap_length[0]
-    arrived = lax.all_to_all(
-        mixed_rows.reshape(slot_shape), SEQ, split_axis=0, concat_axis=1, tiled=True
-    )
+    arrived = lax.all_to_all(mixed.transpose(1, 0, 2), SEQ, split_axis=0, concat_axis=0)
+    arrived = arrived.reshape(64, 2, 2, 640).transpose(0, 2, 1, 3).reshape(128, 1280)
     result_rows, terms = cross_grads(
         frame_input.reshape(-1, width),
-        arrived.reshape(-1, width),
+        arrived,
+        place,
         full_cross[0],
-        full_cross[1],
+        w_out_placed,
         cap_key,
         cap_value,
         valid_keys,

time: 244 us -> 225 us (0.922)
  waiting for transfers between devices: 73.5 us -> 47.1 us
  matrix products: 43.4 us -> 57.2 us
  blocking collectives: 12.1 us -> 0 us
    ppermute x1, waiting for transfers between devices: 18.9 us -> 2.43 us  [cross_halves(): got = lax.ppermute(part, ALL, pairs)]
    all_to_all x2, waiting for transfers between devices: 26.4 us -> 13.7 us  [the longest x1 8.31 us: local(): lax.all_to_all(mixed.transpose(1, 0, 2), SEQ, split_axis=0, concat_axis=0)]
    all_to_all x1 -> x0, blocking collectives: 12.1 us -> none  [gather_groups(): return lax.all_to_all(copies, ALL, 0, 0, axis_index_groups=groups)]
    dot_general x4 -> x5, matrix products: 4.4 us -> 12.2 us  [the longest x1 3.87 us: local(): lax.dot_general(qkv_both, qkv_mine, CONTRACT_LAST, preferred_element_type...]
    dot_general x1, matrix products: 2.96 us -> 8.57 us  [cross_grads(): lax.dot_general(d_rows, w_out, CONTRACT_LAST, preferred_element_type=jnp....]
    all_to_all x2 -> x0, local copies, waits for them, and re-layouts: 4.58 us -> none  [gather_groups(): return lax.all_to_all(copies, ALL, 0, 0, axis_index_groups=groups)]
    concatenate x3 -> x4, local copies, waits for them, and re-layouts: 1.53 us -> 5.46 us  [temporal_grads(): jnp.concatenate([merge_heads(query_grad), merge_heads(key_grad), merge_he...]
    another operation x0 -> x4, other arithmetic: none -> 3.47 us  [in_core_order(): jnp.stack([jnp.where(core == 0, mine, other), jnp.where(core == 0, other,...]
  transfers between devices with their start and end apart: 11 -> 12, of which waited for: 7 -> 6; matrix products, arithmetic and copies ran while one was open for 21% -> 35% of each run, Pallas kernels for 0% -> 0%
where the time goes in v3:
time: 225 us; the launch traced here: 224 us
  starting transfers between devices  61.7 us (27%)
  matrix products  57.2 us (25%)
  waiting for transfers between devices  47.1 us (21%)
  local copies, waits for them, and re-layouts  36 us (16%)
  other arithmetic  19.9 us (9%)
    all_to_all x1, waiting for transfers between devices, local(): lax.all_to_all(terms, ('x', 'y'), 0, 0).astype(jnp.float32)  17.3 us
    all_to_all x3, starting transfers between devices, gather_groups(): return lax.all_to_all(copies, ALL, 0, 0, axis_index_groups=groups)  13.7 us
    all_to_all x1, starting transfers between devices, local(): lax.all_to_all(mixed.transpose(1, 0, 2), SEQ, split_axis=0, concat_axis=0)  10.4 us
    unnamed x43, local copies, waits for them, and re-layouts  9.3 us
    all_to_all x1, starting transfers between devices, local(): lax.all_to_all(jnp.broadcast_to(shard[None], (4,) + shard.shape), 'z', 0, 0)  9.01 us
    dot_general x1, matrix products, cross_grads(): lax.dot_general(d_rows, w_out, CONTRACT_LAST, preferred_element_type=jnp....  8.57 us
    all_to_all x1, waiting for transfers between devices, local(): lax.all_to_all(mixed.transpose(1, 0, 2), SEQ, split_axis=0, concat_axis=0)  8.31 us
    all_to_all x1, starting transfers between devices, local(): lax.all_to_all(pieces, ('s', 'z', 'c'), 0, 0).astype(jnp.float32)  7.69 us
  transfers between devices with their start and end apart: 12, of which 6 were waited for; matrix products, arithmetic and copies ran while one was open for 35% of the time, Pallas kernels for 0%

profile of v3, /device:TPU:1, one launch (start us, length us, event | category | flops | bytes accessed | tf_op | source)
XLA Modules:
  0.0 223.5 jit_solution(5791485209139751451)
XLA Ops:
  0.7 1.0 pad_maximum_fusion.5
  2.7 9.0 %all-to-all-start = ((bf16[4,2,20736]{2,1,0:T(2,128)(2,1)}), bf16[4,2,20736]{2,1,0:T(2,128)(2,1)S(1)}, u32[]{:S(2)}, u32[]{:S(2)}) async-start(bf16[4,2,20736]{2,1,0:T(2,128)(2,1)} %broadcast_in_dim.19), calls=%async_computation | async-start | bytes 663552 | tf_op jit(solution)/shard_map/all_to_all | solution.py:187
  11.7 1.0 collective-permute-start
  12.6 1.9 reshape.147
  14.5 0.9 reshape.146
  15.5 5.3 %all-to-all-done = bf16[4,2,20736]{2,1,0:T(2,128)(2,1)S(1)} async-done(((bf16[4,2,20736]{2,1,0:T(2,128)(2,1)}), bf16[4,2,20736]{2,1,0:T(2,128)(2,1)S(1)}, u32[]{:S(2)}, u32[]{:S(2)}) %all-to-all-start) | async-done | bytes 331808 | tf_op jit(solution)/shard_map/all_to_all | solution.py:187
  21.1 1.2 broadcast_in_dim.20
  22.3 4.3 %all-to-all-start.1 = ((bf16[4,40,4608]{2,1,0:T(8,128)(2,1)}), bf16[4,40,4608]{2,1,0:T(8,128)(2,1)S(1)}, u32[]{:S(2)}, u32[]{:S(2)}) async-start(bf16[4,40,4608]{2,1,0:T(8,128)(2,1)} %broadcast_in_dim.20), calls=%async_computation.1 | async-start | bytes 2949120 | tf_op jit(solution)/shard_map/all_to_all | solution.py:116
  26.6 1.6 fusion.92
  28.9 2.2 iota_compare_fusion
  31.0 7.6 %all-to-all-done.1 = bf16[4,40,4608]{2,1,0:T(8,128)(2,1)S(1)} async-done(((bf16[4,40,4608]{2,1,0:T(8,128)(2,1)}), bf16[4,40,4608]{2,1,0:T(8,128)(2,1)S(1)}, u32[]{:S(2)}, u32[]{:S(2)}) %all-to-all-start.1) | async-done | bytes 1474592 | tf_op jit(solution)/shard_map/all_to_all | solution.py:116
  38.7 1.4 broadcast_in_dim.21
  40.2 4.3 %all-to-all-start.2 = ((bf16[4,4,40,1152]{3,2,1,0:T(8,128)(2,1)}), bf16[4,4,40,1152]{3,2,1,0:T(8,128)(2,1)}, u32[]{:S(2)}, u32[]{:S(2)}) async-start(bf16[4,4,40,1152]{3,2,1,0:T(8,128)(2,1)} %broadcast_in_dim.21), calls=%async_computation.2 | async-start | bytes 2949120 | tf_op jit(solution)/shard_map/all_to_all | solution.py:116
  44.6 2.3 %copy.54 = bf16[300,1152]{0,1:T(8,128)(2,1)} copy(bf16[300,1152]{1,0:T(8,128)(2,1)} %param.20) | data formatting | bytes 1382400 | tf_op args[8]
  46.9 1.9 reshape.152
  48.8 2.2 copy.56
  51.0 1.2 dynamic-slice_bitcast_fusion
  52.2 2.9 %collective-permute-start.3 = (bf16[576,1152]{1,0:T(8,128)(2,1)}, bf16[576,1152]{1,0:T(8,128)(2,1)}, u32[]{:S(2)}, u32[]{:S(2)}) collective-permute-start(bf16[576,1152]{1,0:T(8,128)(2,1)} %dynamic-slice_bitcast_fusion), channel_id=1, source_target_pairs={{0,128},{1,135},{128,2},{129,1},{2,130},{3,129},{130,4},{131,3},{4... | collective-permute-start | bytes 3981320 | tf_op jit(solution)/shard_map/ppermute | solution.py:156
  55.1 1.0 select_bitcast_fusion.5
  57.0 2.4 %convolution_convert_fusion.8 = bf16[256,640]{1,0:T(8,128)(2,1)S(1)} fusion(bf16[256,1152]{1,0:T(8,128)(2,1)} %bitcast.162, bf16[640,1152]{1,0:T(8,128)(2,1)} %bitcast.4), kind=kOutput, calls=%fused_computation.68 | convolution fusion | flops 377651200 | bytes 2392064 | tf_op jit(solution)/shard_map/dot_general | solution.py:197
  60.1 6.0 %collective-permute-start.1 = (bf16[128,640]{1,0:T(8,128)(2,1)}, bf16[128,640]{1,0:T(8,128)(2,1)}, u32[]{:S(2)}, u32[]{:S(2)}) collective-permute-start(bf16[128,640]{1,0:T(8,128)(2,1)} %dynamic-slice_bitcast_fusion.1), channel_id=1, source_target_pairs={{0,1},{1,0},{2,3},{3,2},{4,5},{5,4},{6,7},{7,6},{8,9},{9,8},{10,11... | collective-permute-start | bytes 491528 | tf_op jit(solution)/shard_map/ppermute | solution.py:120
  66.2 1.6 fusion.9
  67.7 2.4 %collective-permute-done.3 = bf16[576,1152]{1,0:T(8,128)(2,1)} collective-permute-done((bf16[576,1152]{1,0:T(8,128)(2,1)}, bf16[576,1152]{1,0:T(8,128)(2,1)}, u32[]{:S(2)}, u32[]{:S(2)}) %collective-permute-start.3) | collective-permute-done | bytes 1327136 | tf_op jit(solution)/shard_map/ppermute | solution.py:156
  70.1 6.6 %collective-permute-start.4 = (bf16[576,1152]{1,0:T(8,128)(2,1)}, bf16[576,1152]{1,0:T(8,128)(2,1)}, u32[]{:S(2)}, u32[]{:S(2)}) collective-permute-start(bf16[576,1152]{1,0:T(8,128)(2,1)} %collective-permute-done.3), channel_id=1, source_target_pairs={{0,1},{1,0},{2,3},{3,2},{4,5},{5,4},{6,7},{7,6},{8,9},{9,8},{10,11... | collective-permute-start | bytes 3981320 | tf_op jit(solution)/shard_map/ppermute | solution.py:157
  76.7 2.4 %broadcast_in_dim.22 = bf16[4,4,40,3456]{3,2,1,0:T(8,128)(2,1)} broadcast(bf16[4,40,3456]{2,1,0:T(8,128)(2,1)S(1)} %slice-done), dimensions={1,2,3} | broadcast | bytes 5529600 | tf_op jit(solution)/shard_map/broadcast_in_dim | solution.py:115
  79.1 5.1 %all-to-all-start.3 = ((bf16[4,4,40,3456]{3,2,1,0:T(8,128)(2,1)}), bf16[4,4,40,3456]{3,2,1,0:T(8,128)(2,1)}, u32[]{:S(2)}, u32[]{:S(2)}) async-start(bf16[4,4,40,3456]{3,2,1,0:T(8,128)(2,1)} %broadcast_in_dim.22), calls=%async_computation.3 | async-start | bytes 8847360 | tf_op jit(solution)/shard_map/all_to_all | solution.py:116
  84.2 1.0 bitcast_select_fusion.1
  85.2 2.2 fusion.23
  87.4 2.7 %reshape.151 = bf16[2,64,16,72]{3,2,1,0:T(8,128)(2,1)} reshape(bf16[128,1152]{1,0:T(8,128)(2,1)} %fusion.23) | data formatting | bytes 589824 | tf_op jit(solution)/shard_map/reshape.5
  90.1 2.5 %fusion.51 = f32[2,16,64,64]{2,3,1,0:T(8,128)} fusion(bf16[2,64,16,72]{3,2,1,0:T(8,128)(2,1)S(1)} %reshape.152, bf16[2,64,16,72]{3,2,1,0:T(8,128)(2,1)} %reshape.151), kind=kOutput, calls=%fused_computation.75 | convolution fusion | flops 18874368 | bytes 1114112 | tf_op jit(solution)/shard_map/sfphd,sgphd->sphfg/dot_general | solution.py:39
  92.6 4.1 %fusion.39 = bf16[2,64,1,16,72]{4,1,3,0,2:T(8,128)(2,1)} fusion(f32[2,16,64,64]{2,3,1,0:T(8,128)} %fusion.51, bf16[2,64,16,72]{3,2,1,0:T(8,128)(2,1)} %copy-done.8, f32[2,16,64,64]{2,3,1,0:T(8,128)} %get-tuple-element.21, f32[2,16,64]{2,1,0:T(8,128)S(1)} %get-tuple-element.20), kind=kOutput, calls=%fused_computation.63 | convolution fusion | flops 19941440 | bytes 1646592 | tf_op jit(solution)/shard_map/sphfg,sgphd->sfphd/dot_general | solution.py:44
  96.7 1.4 copy.47
  98.1 1.2 concatenate.25
  99.3 4.1 %fusion.40 = bf16[2,64,1,16,72]{4,1,3,0,2:T(8,128)(2,1)} fusion(f32[2,16,64,64]{2,3,1,0:T(8,128)} %fusion.51, bf16[2,64,16,72]{3,2,1,0:T(8,128)(2,1)} %copy-done.7, f32[2,16,64,64]{2,3,1,0:T(8,128)} %get-tuple-element.21, f32[2,16,64]{2,1,0:T(8,128)S(1)} %get-tuple-element.20), kind=kOutput, calls=%fused_computation.64 | convolution fusion | flops 19941440 | bytes 1646592 | tf_op jit(solution)/shard_map/sphfg,sfphd->sgphd/dot_general | solution.py:47
  103.4 1.4 copy.49
  104.7 1.3 concatenate.26
  106.0 1.8 constant_dynamic-update-slice_fusion.2
  107.8 1.7 fusion.41
  110.6 1.2 concatenate.27
  111.8 1.7 constant_dynamic-update-slice_fusion
  113.5 2.0 select_bitcast_fusion.1
  115.5 3.0 %broadcast_select_fusion.1 = (bf16[2,576,1152]{2,1,0:T(8,128)(2,1)}, bf16[2,576,1152]{2,1,0:T(8,128)(2,1)}) fusion(bf16[2,576,1152]{2,1,0:T(8,128)(2,1)S(1)} %copy-done.2, pred[]{:T(512)S(6)} %eq.14, bf16[1,576,1152]{2,1,0:T(8,128)(2,1)S(1)} %get-tuple-element.13, bf16[1,576,1152]{2,1,0:T(8,128)(2,1)S(1)} %get-tuple-element.12), kind=kLoop, calls=%fused_computation.22 | loop fusion | flops 3981312 | bytes 10616833 | tf_op jit(solution)/shard_map/jit(_where)/select_n | solution.py:159
  118.5 1.4 select_bitcast_fusion.3
  121.0 3.9 %fusion.42 = bf16[256,640]{1,0:T(8,128)(2,1)S(1)} fusion(f32[256,640]{1,0:T(8,128)S(1)} %copy-done.16, bf16[256,3456]{1,0:T(8,128)(2,1)S(1)} %bitcast.155, bf16[640,3456]{1,0:T(8,128)(2,1)} %bitcast.19), kind=kOutput, calls=%fused_computation.67 | convolution fusion | flops 1132789760 | bytes 7176192 | tf_op jit(solution)/shard_map/dot_general | solution.py:216
  124.9 1.1 copy.86
  125.9 10.4 %all-to-all-start.4 = ((bf16[128,2,640]{2,1,0:T(2,128)(2,1)}), bf16[128,2,640]{2,1,0:T(2,128)(2,1)S(1)}, u32[]{:S(2)}, u32[]{:S(2)}) async-start(bf16[128,2,640]{2,1,0:T(2,128)(2,1)} %bitcast.152), calls=%async_computation.4 | async-start | bytes 655360 | tf_op jit(solution)/shard_map/all_to_all | solution.py:224
  136.4 1.9 fusion.12
  138.3 1.6 convolution_convert_fusion.2
  140.0 3.8 %fusion.97 = (f32[128,16]{0,1:T(8,128)S(1)}, f32[128,16,300]{0,2,1:T(8,128)}) fusion(pred[300]{0:T(512)(128)(4,1)S(1)} %iota_compare_fusion.14, bf16[128,16,72]{0,2,1:T(8,128)(2,1)} %bitcast.172, bf16[300,16,72]{0,2,1:T(8,128)(2,1)} %bitcast.160), kind=kOutput, calls=%fused_computation.120 | convolution fusion | flops 90931496 | bytes 3452204 | tf_op jit(solution)/shard_map/sub | solution.py:70
  143.8 8.3 %all-to-all-done.4 = bf16[128,2,640]{2,1,0:T(2,128)(2,1)S(1)} async-done(((bf16[128,2,640]{2,1,0:T(2,128)(2,1)}), bf16[128,2,640]{2,1,0:T(2,128)(2,1)S(1)}, u32[]{:S(2)}, u32[]{:S(2)}) %all-to-all-start.4) | async-done | bytes 327712 | tf_op jit(solution)/shard_map/all_to_all | solution.py:224
  152.4 8.6 %convolution_convert_fusion.1 = bf16[128,1152]{1,0:T(8,128)(2,1)} fusion(bf16[128,1280]{1,0:T(8,128)(2,1)S(1)} %bitcast.166, s32[1280]{0:T(1024)S(1)} %copy-done.14, bf16[2,576,1152]{2,1,0:T(8,128)(2,1)} %get-tuple-element.11, bf16[2,576,1152]{2,1,0:T(8,128)(2,1)} %get-tuple-element.10), kind=kOutput, calls=%fused_computation.36 | convolution fusion | flops 3783278592 | bytes 5936128 | tf_op jit(solution)/shard_map/dot_general | solution.py:58
  161.0 1.2 copy.55
  162.2 3.4 %fusion.98 = f32[16,128,300]{1,2,0:T(8,128)} fusion(bf16[128,16,72]{0,2,1:T(8,128)(2,1)S(1)} %bitcast.158, bf16[300,16,72]{0,2,1:T(8,128)(2,1)} %bitcast.154), kind=kOutput, calls=%fused_computation.121 | convolution fusion | flops 88473600 | bytes 3443712 | tf_op jit(solution)/shard_map/nhd,chd->nhc/dot_general | solution.py:72
  165.5 1.8 convolution_convert_fusion.3
  167.3 5.9 %convolution_convert_fusion.4 = bf16[16,72,300]{2,1,0:T(8,128)(2,1)} fusion(bf16[128,16,72]{0,2,1:T(8,128)(2,1)S(1)} %bitcast.173, f32[16,128,300]{1,2,0:T(8,128)} %fusion.98, f32[128,16,300]{0,2,1:T(8,128)} %get-tuple-element.23, f32[128,16]{0,1:T(8,128)S(1)} %get-tuple-element.22), kind=kOutput, calls=%fused_computation.43 | convolution fusion | flops 93122344 | bytes 5909504 | tf_op jit(solution)/shard_map/nhc,nhd->hdc/dot_general | solution.py:86
  173.2 2.9 %pad_maximum_fusion.3 = bf16[16,144,300]{2,1,0:T(8,128)(2,1)} fusion(bf16[16,72,300]{2,1,0:T(8,128)(2,1)} %convolution_convert_fusion.3, bf16[16,72,300]{2,1,0:T(8,128)(2,1)} %convolution_convert_fusion.4), kind=kLoop, calls=%fused_computation.40 | loop fusion | flops 2764800 | bytes 2764800 | tf_op jit(solution)/shard_map/concatenate | solution.py:92
  176.1 4.4 %all-to-all-start.5 = ((bf16[16,144,300]{2,1,0:T(8,128)(2,1)}), bf16[16,144,300]{2,1,0:T(8,128)(2,1)}, u32[]{:S(2)}, u32[]{:S(2)}) async-start(bf16[16,144,300]{2,1,0:T(8,128)(2,1)} %pad_maximum_fusion.3), calls=%async_computation.5 | async-start | bytes 3538944 | tf_op jit(solution)/shard_map/all_to_all | solution.py:237
  180.5 5.2 %fusion.43 = bf16[16,128,72]{1,2,0:T(8,128)(2,1)S(1)} fusion(bf16[300,16,72]{0,2,1:T(8,128)(2,1)} %bitcast.161, f32[16,128,300]{1,2,0:T(8,128)} %fusion.98, f32[128,16,300]{0,2,1:T(8,128)} %get-tuple-element.23, f32[128,16]{0,1:T(8,128)S(1)} %get-tuple-element.22), kind=kOutput, calls=%fused_computation.69 | convolution fusion | flops 92924200 | bytes 5909504 | tf_op jit(solution)/shard_map/nhc,chd->nhd/dot_general | solution.py:78
  185.7 0.9 fusion.99
  186.6 17.3 %all-to-all-done.5 = bf16[16,144,300]{2,1,0:T(8,128)(2,1)} async-done(((bf16[16,144,300]{2,1,0:T(8,128)(2,1)}), bf16[16,144,300]{2,1,0:T(8,128)(2,1)}, u32[]{:S(2)}, u32[]{:S(2)}) %all-to-all-start.5) | async-done | bytes 1382432 | tf_op jit(solution)/shard_map/all_to_all | solution.py:237
  203.9 1.8 reduce_sum.61
  206.6 7.7 %all-to-all-start.6 = ((bf16[16,2,1350]{2,1,0:T(2,128)(2,1)}), bf16[16,2,1350]{2,1,0:T(2,128)(2,1)S(1)}, u32[]{:S(2)}, u32[]{:S(2)}) async-start(bf16[16,2,1350]{2,1,0:T(2,128)(2,1)} %reshape.166), calls=%async_computation.6 | async-start | bytes 180224 | tf_op jit(solution)/shard_map/all_to_all | solution.py:239
  214.3 2.2 fusion.24
  216.5 6.1 %all-to-all-done.6 = bf16[16,2,1350]{2,1,0:T(2,128)(2,1)S(1)} async-done(((bf16[16,2,1350]{2,1,0:T(2,128)(2,1)}), bf16[16,2,1350]{2,1,0:T(2,128)(2,1)S(1)}, u32[]{:S(2)}, u32[]{:S(2)}) %all-to-all-start.6) | async-done | bytes 86432 | tf_op jit(solution)/shard_map/all_to_all | solution.py:239
  (62 shorter events, 7.4 us)
Async XLA Ops:
  0.6 137.7 %copy-start = (bf16[1,128,1152]{2,1,0:T(8,128)(2,1)S(1)}, bf16[1,128,1152]{2,1,0:T(8,128)(2,1)}, u32[]{:S(2)}) copy-start(bf16[1,128,1152]{2,1,0:T(8,128)(2,1)} %param.18) | copy-start | bytes 884740
  0.6 13.9 %copy-start.12 = (bf16[2,64,1,1152]{3,1,2,0:T(8,128)(2,1)S(1)}, bf16[2,64,1,1152]{3,1,2,0:T(8,128)(2,1)}, u32[]{:S(2)}) copy-start(bf16[2,64,1,1152]{3,1,2,0:T(8,128)(2,1)} %param.13) | copy-start | bytes 884740
  2.7 18.2 %all-to-all-start = ((bf16[4,2,20736]{2,1,0:T(2,128)(2,1)}), bf16[4,2,20736]{2,1,0:T(2,128)(2,1)S(1)}, u32[]{:S(2)}, u32[]{:S(2)}) async-start(bf16[4,2,20736]{2,1,0:T(2,128)(2,1)} %broadcast_in_dim.19), calls=%async_computation | async-start | bytes 663552 | tf_op jit(solution)/shard_map/all_to_all | solution.py:187
  11.7 43.4 %collective-permute-start = (bf16[128,1152]{1,0:T(8,128)(2,1)}, bf16[128,1152]{1,0:T(8,128)(2,1)}, u32[]{:S(2)}, u32[]{:S(2)}) collective-permute-start(bf16[128,1152]{1,0:T(8,128)(2,1)} %bitcast.170), channel_id=1, source_target_pairs={{0,1},{1,0},{2,3},{3,2},{4,5},{5,4},{6,7},{7,6},{8,9},{9,8},{10,11... | collective-permute-start | bytes 884744 | tf_op jit(solution)/shard_map/ppermute | solution.py:120
  14.5 12.1 %copy-start.8 = (bf16[2,64,16,72]{3,2,1,0:T(8,128)(2,1)}, bf16[2,64,16,72]{3,2,1,0:T(8,128)(2,1)S(1)}, u32[]{:S(2)}) copy-start(bf16[2,64,16,72]{3,2,1,0:T(8,128)(2,1)S(1)} %reshape.147) | copy-start | bytes 884740
  15.5 11.1 %copy-start.7 = (bf16[2,64,16,72]{3,2,1,0:T(8,128)(2,1)}, bf16[2,64,16,72]{3,2,1,0:T(8,128)(2,1)S(1)}, u32[]{:S(2)}) copy-start(bf16[2,64,16,72]{3,2,1,0:T(8,128)(2,1)S(1)} %reshape.146) | copy-start | bytes 884740
  22.3 6.5 %copy-start.14 = (s32[1280]{0:T(1024)S(1)}, s32[1280]{0:T(1024)}, u32[]{:S(2)}) copy-start(s32[1280]{0:T(1024)} %constant.45.clone) | copy-start | bytes 15364
  22.3 16.3 %all-to-all-start.1 = ((bf16[4,40,4608]{2,1,0:T(8,128)(2,1)}), bf16[4,40,4608]{2,1,0:T(8,128)(2,1)S(1)}, u32[]{:S(2)}, u32[]{:S(2)}) async-start(bf16[4,40,4608]{2,1,0:T(8,128)(2,1)} %broadcast_in_dim.20), calls=%async_computation.1 | async-start | bytes 2949120 | tf_op jit(solution)/shard_map/all_to_all | solution.py:116
  38.7 1.6 copy-start.3
  40.2 16.8 %all-to-all-start.2 = ((bf16[4,4,40,1152]{3,2,1,0:T(8,128)(2,1)}), bf16[4,4,40,1152]{3,2,1,0:T(8,128)(2,1)}, u32[]{:S(2)}, u32[]{:S(2)}) async-start(bf16[4,4,40,1152]{3,2,1,0:T(8,128)(2,1)} %broadcast_in_dim.21), calls=%async_computation.2 | async-start | bytes 2949120 | tf_op jit(solution)/shard_map/all_to_all | solution.py:116
  44.6 6.5 %copy-start.2 = (bf16[2,576,1152]{2,1,0:T(8,128)(2,1)S(1)}, bf16[2,576,1152]{2,1,0:T(8,128)(2,1)}, u32[]{:S(2)}) copy-start(bf16[2,576,1152]{2,1,0:T(8,128)(2,1)} %param.19) | copy-start | bytes 7962628
  51.0 4.1 %copy-start.13 = (bf16[2,64,1,1152]{3,1,2,0:T(8,128)(2,1)S(1)}, bf16[2,64,1,1152]{3,1,2,0:T(8,128)(2,1)}, u32[]{:S(2)}) copy-start(bf16[2,64,1,1152]{3,1,2,0:T(8,128)(2,1)} %param.12) | copy-start | bytes 884740
  52.2 17.9 %collective-permute-start.3 = (bf16[576,1152]{1,0:T(8,128)(2,1)}, bf16[576,1152]{1,0:T(8,128)(2,1)}, u32[]{:S(2)}, u32[]{:S(2)}) collective-permute-start(bf16[576,1152]{1,0:T(8,128)(2,1)} %dynamic-slice_bitcast_fusion), channel_id=1, source_target_pairs={{0,128},{1,135},{128,2},{129,1},{2,130},{3,129},{130,4},{131,3},{4... | collective-permute-start | bytes 3981320 | tf_op jit(solution)/shard_map/ppermute | solution.py:156
  57.0 9.1 %copy-start.4 = (pred[1280,1152]{1,0:T(32,128)(4,1)S(1)}, pred[1280,1152]{1,0:T(32,128)(4,1)}, u32[]{:S(2)}) copy-start(pred[1280,1152]{1,0:T(32,128)(4,1)} %iota_compare_fusion) | copy-start | bytes 4423684
  57.0 9.1 %copy-start.6 = (bf16[2,128,1152]{2,1,0:T(8,128)(2,1)S(1)}, bf16[2,128,1152]{2,1,0:T(8,128)(2,1)}, u32[]{:S(2)}) copy-start(bf16[2,128,1152]{2,1,0:T(8,128)(2,1)} %pad_maximum_fusion.4) | copy-start | bytes 1769476
  59.4 8.3 %copy-start.9 = (bf16[256,640]{1,0:T(8,128)(2,1)}, bf16[256,640]{1,0:T(8,128)(2,1)S(1)}, u32[]{:S(2)}) copy-start(bf16[256,640]{1,0:T(8,128)(2,1)S(1)} %convolution_convert_fusion.8) | copy-start | bytes 983044
  59.4 17.2 %slice-start = ((bf16[4,40,4608]{2,1,0:T(8,128)(2,1)}), bf16[4,40,3456]{2,1,0:T(8,128)(2,1)S(1)}, s32[]{:S(2)}) async-start(bf16[4,40,4608]{2,1,0:T(8,128)(2,1)} %copy-done.3), calls=%async_computation.7 | async-start | bytes 2211840 | tf_op jit(solution)/shard_map/slice | solution.py:194
  60.1 24.0 %collective-permute-start.1 = (bf16[128,640]{1,0:T(8,128)(2,1)}, bf16[128,640]{1,0:T(8,128)(2,1)}, u32[]{:S(2)}, u32[]{:S(2)}) collective-permute-start(bf16[128,640]{1,0:T(8,128)(2,1)} %dynamic-slice_bitcast_fusion.1), channel_id=1, source_target_pairs={{0,1},{1,0},{2,3},{3,2},{4,5},{5,4},{6,7},{7,6},{8,9},{9,8},{10,11... | collective-permute-start | bytes 491528 | tf_op jit(solution)/shard_map/ppermute | solution.py:120
  70.1 43.4 %collective-permute-start.4 = (bf16[576,1152]{1,0:T(8,128)(2,1)}, bf16[576,1152]{1,0:T(8,128)(2,1)}, u32[]{:S(2)}, u32[]{:S(2)}) collective-permute-start(bf16[576,1152]{1,0:T(8,128)(2,1)} %collective-permute-done.3), channel_id=1, source_target_pairs={{0,1},{1,0},{2,3},{3,2},{4,5},{5,4},{6,7},{7,6},{8,9},{9,8},{10,11... | collective-permute-start | bytes 3981320 | tf_op jit(solution)/shard_map/ppermute | solution.py:157
  79.1 41.0 %all-to-all-start.3 = ((bf16[4,4,40,3456]{3,2,1,0:T(8,128)(2,1)}), bf16[4,4,40,3456]{3,2,1,0:T(8,128)(2,1)}, u32[]{:S(2)}, u32[]{:S(2)}) async-start(bf16[4,4,40,3456]{3,2,1,0:T(8,128)(2,1)} %broadcast_in_dim.22), calls=%async_computation.3 | async-start | bytes 8847360 | tf_op jit(solution)/shard_map/all_to_all | solution.py:116
  106.0 3.5 %copy-start.5 = (bf16[128,1152]{1,0:T(8,128)(2,1)S(1)}, bf16[128,1152]{1,0:T(8,128)(2,1)}, u32[]{:S(2)}) copy-start(bf16[128,1152]{1,0:T(8,128)(2,1)} %concatenate.26) | copy-start | bytes 884740
  113.5 5.0 %collective-permute-start.2 = (bf16[128,3456]{1,0:T(8,128)(2,1)}, bf16[128,3456]{1,0:T(8,128)(2,1)S(1)}, u32[]{:S(2)}, u32[]{:S(2)}) collective-permute-start(bf16[128,3456]{1,0:T(8,128)(2,1)} %constant_dynamic-update-slice_fusion), channel_id=1, source_target_pairs={{0,1},{1,0},{2,3},{3,2},{4,5},{5,4},{6,7},{7,6},{8,9},{9,8},{10,11... | collective-permute-start | bytes 2654216 | tf_op jit(solution)/shard_map/ppermute | solution.py:120
  119.9 1.1 copy-start.16
  125.9 26.2 %all-to-all-start.4 = ((bf16[128,2,640]{2,1,0:T(2,128)(2,1)}), bf16[128,2,640]{2,1,0:T(2,128)(2,1)S(1)}, u32[]{:S(2)}, u32[]{:S(2)}) async-start(bf16[128,2,640]{2,1,0:T(2,128)(2,1)} %bitcast.152), calls=%async_computation.4 | async-start | bytes 655360 | tf_op jit(solution)/shard_map/all_to_all | solution.py:224
  152.4 8.6 %copy-start.10 = (bf16[16,8,2,640]{3,1,2,0:T(8,128)(2,1)}, bf16[16,8,2,640]{3,1,2,0:T(8,128)(2,1)S(1)}, u32[]{:S(2)}) copy-start(bf16[16,8,2,640]{3,1,2,0:T(8,128)(2,1)S(1)} %copy.58) | copy-start | bytes 983044
  162.2 3.4 %copy-start.17 = (f32[128,16,300]{0,2,1:T(8,128)S(1)}, f32[128,16,300]{0,2,1:T(8,128)}, u32[]{:S(2)}) copy-start(f32[128,16,300]{0,2,1:T(8,128)} %get-tuple-element.23) | copy-start | bytes 7372804
  165.5 1.8 copy-start.15
  176.1 27.8 %all-to-all-start.5 = ((bf16[16,144,300]{2,1,0:T(8,128)(2,1)}), bf16[16,144,300]{2,1,0:T(8,128)(2,1)}, u32[]{:S(2)}, u32[]{:S(2)}) async-start(bf16[16,144,300]{2,1,0:T(8,128)(2,1)} %pad_maximum_fusion.3), calls=%async_computation.5 | async-start | bytes 3538944 | tf_op jit(solution)/shard_map/all_to_all | solution.py:237
  186.6 27.7 %copy-start.11 = (bf16[16,8,2,640]{3,1,2,0:T(8,128)(2,1)S(1)}, bf16[16,8,2,640]{3,1,2,0:T(8,128)(2,1)}, u32[]{:S(2)}) copy-start(bf16[16,8,2,640]{3,1,2,0:T(8,128)(2,1)} %copy-done.10) | copy-start | bytes 983044
  203.9 19.6 %copy-start.1 = (bf16[1,128,1152]{2,1,0:T(8,128)(2,1)S(1)}, bf16[1,128,1152]{2,1,0:T(8,128)(2,1)}, u32[]{:S(2)}) copy-start(bf16[1,128,1152]{2,1,0:T(8,128)(2,1)} %param.18) | copy-start | bytes 884740
  206.6 16.0 %all-to-all-start.6 = ((bf16[16,2,1350]{2,1,0:T(2,128)(2,1)}), bf16[16,2,1350]{2,1,0:T(2,128)(2,1)S(1)}, u32[]{:S(2)}, u32[]{:S(2)}) async-start(bf16[16,2,1350]{2,1,0:T(2,128)(2,1)} %reshape.166), calls=%async_computation.6 | async-start | bytes 180224 | tf_op jit(solution)/shard_map/all_to_all | solution.py:239

commit v4 on v3

v4 whole, which is shorter than its diff:
```python
import math

import jax
import jax.numpy as jnp
import numpy as np
from jax import lax
from jax.experimental import pallas as pl
from jax.experimental.pallas import tpu as pltpu
from jax.sharding import Mesh, PartitionSpec as P

HEADS = 16
HEAD_DIM = 72


CONTRACT_LAST = (((1,), (1,)), ((), ()))


CONTRACT_FIRST = (((0,), (0,)), ((), ()))
SCALE = 1.0 / math.sqrt(HEAD_DIM)
CAP = 300
CAP_PAD = 384


def dot(a, b, dims=(((1,), (0,)), ((), ()))):
    return lax.dot_general(a, b, dims, preferred_element_type=jnp.float32)


def softmax(scores):
    weights = jnp.exp(scores - jnp.max(scores, axis=-1, keepdims=True))
    return weights / jnp.sum(weights, axis=-1, keepdims=True)


def score_grads(attention, prob_grad):
    centred = prob_grad - jnp.sum(prob_grad * attention, axis=-1, keepdims=True)
    return (attention * centred * SCALE).astype(jnp.bfloat16)


def temporal_kernel(grad_ref, query_ref, key_ref, value_ref, out_ref):
    rows, width = grad_ref.shape
    frames = rows // 2
    same = (lax.broadcasted_iota(jnp.int32, (rows, rows), 0) < frames) == (
        lax.broadcasted_iota(jnp.int32, (rows, rows), 1) < frames
    )
    for head in range(HEADS):
        at = slice(head * HEAD_DIM, (head + 1) * HEAD_DIM)
        grad, query, key_rows, value = (
            ref[:, at] for ref in (grad_ref, query_ref, key_ref, value_ref)
        )
        scores = jnp.where(same, dot(query, key_rows, CONTRACT_LAST) * SCALE, -jnp.inf)
        attention = softmax(scores)
        score_grad = score_grads(attention, dot(grad, value, CONTRACT_LAST))
        for part, result in enumerate(
            (
                dot(score_grad, key_rows),
                dot(score_grad, query, CONTRACT_FIRST),
                dot(attention.astype(jnp.bfloat16), grad, CONTRACT_FIRST),
            )
        ):
            start = part * width + head * HEAD_DIM
            out_ref[:, start : start + HEAD_DIM] = result.astype(jnp.bfloat16)


def temporal_grads(grad_heads, query, key_rows, value):
    rows, width = grad_heads.shape
    return pl.pallas_call(
        temporal_kernel,
        out_shape=jax.ShapeDtypeStruct((rows, 3 * width), jnp.bfloat16),
        compiler_params=pltpu.CompilerParams(vmem_limit_bytes=24 << 20),
        cost_estimate=pl.CostEstimate(
            flops=10 * rows * rows * width,
            bytes_accessed=14 * rows * width,
            transcendentals=HEADS * rows * rows,
        ),
        name="temporal_grads",
    )(grad_heads, query, key_rows, value)


def cross_kernel(
    length_ref, arrived_ref, w_out_ref, query_ref, key_ref, value_ref, cq_ref, terms_ref, og_ref
):
    og_ref[...] = dot(arrived_ref[...], w_out_ref[...]).astype(jnp.bfloat16)
    rows = query_ref.shape[0]
    valid = lax.broadcasted_iota(jnp.int32, (rows, CAP_PAD), 1) < length_ref[0]
    for head in range(HEADS):
        at = slice(head * HEAD_DIM, (head + 1) * HEAD_DIM)
        query, out_grad, key_rows, value = (
            ref[:, at] for ref in (query_ref, og_ref, key_ref, value_ref)
        )
        scores = jnp.where(valid, dot(query, key_rows, CONTRACT_LAST) * SCALE, -1e30)
        attention = softmax(scores)
        score_grad = score_grads(attention, dot(out_grad, value, CONTRACT_LAST))
        cq_ref[:, at] = dot(score_grad, key_rows).astype(jnp.bfloat16)
        key_term = dot(query, score_grad, CONTRACT_FIRST)
        value_term = dot(out_grad, attention.astype(jnp.bfloat16), CONTRACT_FIRST)
        rest = jnp.zeros((HEAD_DIM, 640 - CAP_PAD), jnp.float32)
        shifted = pltpu.roll(jnp.concatenate([value_term, rest], axis=1), CAP, 1)
        terms_ref[head] = (jnp.concatenate([key_term, rest], axis=1) + shifted).astype(
            jnp.bfloat16
        )


def cross_grads(cap_length, arrived, w_out, cross_query, cap_key, cap_value):
    rows, width = cross_query.shape
    in_vmem = pl.BlockSpec(memory_space=pltpu.VMEM)
    return pl.pallas_call(
        cross_kernel,
        in_specs=[pl.BlockSpec(memory_space=pltpu.SMEM)] + [in_vmem] * 5,
        out_specs=(in_vmem, in_vmem),
        out_shape=(
            jax.ShapeDtypeStruct((rows, width), jnp.bfloat16),
            jax.ShapeDtypeStruct((HEADS, HEAD_DIM, 640), jnp.bfloat16),
        ),
        scratch_shapes=[pltpu.VMEM((rows, width), jnp.bfloat16)],
        compiler_params=pltpu.CompilerParams(vmem_limit_bytes=32 << 20),
        cost_estimate=pl.CostEstimate(
            flops=10 * rows * CAP_PAD * width + 2 * rows * width * arrived.shape[1],
            bytes_accessed=8 << 20,
            transcendentals=HEADS * rows * CAP_PAD,
        ),
        name="cross_grads",
    )(cap_length, arrived, w_out, cross_query, cap_key, cap_value)


ALL = ("s", "x", "y", "z", "c")
SEQ = ("x", "y", "z", "c")
SHAPE = (2, 4, 4, 4, 2)


def flat(s, x, y, z, c):
    return (((s * 4 + x) * 4 + y) * 4 + z) * 2 + c


def ring_groups(first):
    groups = []
    for s in range(2):
        for z in range(4):
            for fixed in range(4):
                groups.append([flat(s, i, fixed, z, first) for i in range(4)])
                groups.append([flat(s, fixed, i, z, 1 - first) for i in range(4)])
    return groups


def gather_groups(block, groups):
    copies = jnp.broadcast_to(block[None], (4,) + block.shape)
    return lax.all_to_all(copies, ALL, 0, 0, axis_index_groups=groups)


def swap_cores(block):
    return lax.ppermute(block, "c", [(0, 1), (1, 0)])


def in_core_order(mine, other):
    core = lax.axis_index("c")
    return jnp.stack([jnp.where(core == 0, mine, other), jnp.where(core == 0, other, mine)])


def feature_order():
    order = np.full((2, 4, 4, 40), -1, np.int32)
    for c in range(2):
        for i in range(4):
            for j in range(4):
                x, y = (j, i) if c == 0 else (i, j)
                for q in range(36):
                    order[c, i, j, q] = 72 * (4 * x + y) + 18 * (q // 9) + 9 * c + q % 9
    return order.reshape(1280)


def cross_halves(cross_weights):
    core = lax.axis_index("c")
    side = lax.axis_index("s")

    def place(z):
        return (z % 2, z // 2)

    pairs = []
    for x in range(4):
        for y in range(4):
            for z in range(8):
                for c in range(2):
                    to = (z + (1 if c == 0 else 7)) % 8
                    s0, z0 = place(z)
                    s1, z1 = place(to)
                    pairs.append((flat(s0, x, y, z0, c), flat(s1, x, y, z1, c)))
    part = lax.dynamic_index_in_dim(cross_weights, core, 0, keepdims=False)
    got = lax.ppermute(part, ALL, pairs)
    swapped = lax.ppermute(got, "c", [(0, 1), (1, 0)])
    other = jnp.stack([jnp.where(core == 0, got, swapped), jnp.where(core == 0, swapped, got)])
    low = jnp.where(side == 0, cross_weights, other)
    high = jnp.where(side == 0, other, cross_weights)
    return jnp.concatenate([low, high], axis=1)


def local(
    grad_out,
    t_query,
    t_key,
    t_value,
    t_out_weight,
    t_qkv_weight,
    frame_input,
    cross_weights,
    cap_key,
    cap_value,
    cap_length,
):
    width = grad_out.shape[-1]
    core = lax.axis_index("c")
    grad_rows = grad_out.reshape(-1, width)
    rows = grad_rows.shape[0]
    place = (jnp.asarray(feature_order())[:, None] == jnp.arange(width)[None, :]).astype(
        jnp.bfloat16
    )
    place_mine = lax.dynamic_slice(place, (core * 640, 0), (640, width))
    grad_both = in_core_order(grad_rows, swap_cores(grad_rows)).reshape(2 * rows, width)
    shard = jnp.concatenate([t_out_weight, t_qkv_weight], axis=1).reshape(2, -1)
    column = lax.all_to_all(jnp.broadcast_to(shard[None], (4,) + shard.shape), "z", 0, 0)
    column = jnp.pad(column.reshape(36, 4 * width), ((0, 4), (0, 0)))
    near = gather_groups(column, ring_groups(0))
    out_mine = gather_groups(near[:, :, :width], ring_groups(1))
    near, out_mine, cross_weights = lax.optimization_barrier((near, out_mine, cross_weights))
    full_cross = cross_halves(cross_weights)
    qkv_mine = gather_groups(near[:, :, width:], ring_groups(1)).reshape(640, 3 * width)
    out_mine = out_mine.reshape(640, width)
    heads_mine = (
        lax.dot_general(grad_both, out_mine, CONTRACT_LAST, preferred_element_type=jnp.float32)
        .astype(jnp.bfloat16)
        .reshape(2, rows, 640)
    )
    kept = lax.dynamic_index_in_dim(heads_mine, core, 0, keepdims=False)
    sent = lax.dynamic_index_in_dim(heads_mine, 1 - core, 0, keepdims=False)
    heads_parts = in_core_order(kept, swap_cores(sent))
    grad_heads = jnp.dot(
        jnp.concatenate([heads_parts[0], heads_parts[1]], axis=1),
        place,
        preferred_element_type=jnp.float32,
    ).astype(jnp.bfloat16)
    qkv_grad = temporal_grads(
        grad_heads, *(saved.reshape(rows, width) for saved in (t_query, t_key, t_value))
    )
    qkv_both = in_core_order(qkv_grad, swap_cores(qkv_grad)).reshape(2 * rows, 3 * width)
    residual = lax.dot_general(
        grad_both, place_mine, CONTRACT_LAST, preferred_element_type=jnp.float32
    )
    product = lax.dot_general(
        qkv_both, qkv_mine, CONTRACT_LAST, preferred_element_type=jnp.float32
    )
    mixed = (residual + product).astype(jnp.bfloat16).reshape(2, rows, 640)
    w_out_placed = lax.dot_general(
        place, full_cross[1], CONTRACT_LAST, preferred_element_type=jnp.float32
    ).astype(jnp.bfloat16)
    cross_query = jnp.dot(
        frame_input.reshape(rows, width), full_cross[0], preferred_element_type=jnp.float32
    ).astype(jnp.bfloat16)
    padding = ((0, CAP_PAD - CAP), (0, 0))
    arrived = lax.all_to_all(mixed.transpose(1, 0, 2), SEQ, split_axis=0, concat_axis=0)
    arrived = arrived.reshape(64, 2, 2, 640).transpose(0, 2, 1, 3).reshape(128, 1280)
    cq_grad, terms = cross_grads(
        cap_length,
        arrived,
        w_out_placed,
        cross_query,
        jnp.pad(cap_key, padding),
        jnp.pad(cap_value, padding),
    )
    grad_input = (
        jnp.dot(arrived, place, preferred_element_type=jnp.float32)
        + lax.dot_general(cq_grad, full_cross[0], CONTRACT_LAST, preferred_element_type=jnp.float32)
    ).astype(jnp.bfloat16)
    head = jnp.sum(lax.all_to_all(terms, ("x", "y"), 0, 0).astype(jnp.float32), axis=0)
    head = head.astype(jnp.bfloat16)
    pieces = jnp.concatenate(
        [head[:, :CAP].reshape(8, 9, CAP), head[:, CAP : 2 * CAP].reshape(8, 9, CAP)]
    )
    piece = jnp.sum(lax.all_to_all(pieces, ("s", "z", "c"), 0, 0).astype(jnp.float32), axis=0)
    return (grad_input.reshape(frame_input.shape), piece.T)


def solution(mesh):
    fine = Mesh(mesh.devices.reshape(SHAPE), ALL)
    return jax.shard_map(
        local,
        mesh=fine,
        in_specs=(
            P("s", None, SEQ, None),
            P("s", None, SEQ, None),
            P("s", None, SEQ, None),
            P("s", None, SEQ, None),
            P(SEQ, None),
            P(SEQ, None),
            P(ALL, None, None),
            P(None, "s", None),
            P(),
            P(),
            P(),
        ),
        out_specs=(P(ALL, None, None), P(None, ALL)),
        check_vma=False,
    )
```

time: 225 us -> 199 us (0.88)
  blocking collectives: 0 us -> 35.4 us
  matrix products: 57.2 us -> 24.5 us
  local copies, waits for them, and re-layouts: 36 us -> 14.6 us
  starting transfers between devices: 61.7 us -> 40.8 us
  Pallas kernels: 0 us -> 18.9 us
  other arithmetic: 19.9 us -> 11.3 us
  waiting for transfers between devices: 47.1 us -> 50.8 us
    all_to_all x0 -> x2, blocking collectives: none -> 35.4 us  [the longest x1 19.1 us: local(): lax.all_to_all(jnp.broadcast_to(shard[None], (4,) + shard.shape), 'z', 0, 0)]
    dot_general x12 -> x4, matrix products: 41.8 us -> 14 us  [the longest x1 7.82 us: local(): lax.dot_general(place, full_cross[1], CONTRACT_LAST, preferred_element_ty...]
    pallas_call x0 -> x2, Pallas kernels: none -> 18.9 us  [the longest x1 10.9 us: cross_grads(): pl.pallas_call(cross_kernel, in_specs=[pl.BlockSpec(memory_space=pltpu.SM...]
    all_to_all x3 -> x2, waiting for transfers between devices: 7.63 us -> 19.7 us  [gather_groups(): return lax.all_to_all(copies, ALL, 0, 0, axis_index_groups=groups)]
    all_to_all x1 -> x0, starting transfers between devices: 9.01 us -> none  [local(): lax.all_to_all(jnp.broadcast_to(shard[None], (4,) + shard.shape), 'z', 0, 0)]
    ppermute x1, starting transfers between devices: 6.55 us -> 0.04 us  [cross_halves(): swapped = lax.ppermute(got, 'c', [(0, 1), (1, 0)])]
    another operation x3 -> x0, local copies, waits for them, and re-layouts: 6.5 us -> none
    concatenate x4 -> x0, local copies, waits for them, and re-layouts: 5.46 us -> none  [temporal_grads(): jnp.concatenate([merge_heads(query_grad), merge_heads(key_grad), merge_he...]
  transfers between devices with their start and end apart: 12 -> 10, of which waited for: 6 -> 6; matrix products, arithmetic and copies ran while one was open for 35% -> 16% of each run, Pallas kernels for 0% -> 4%
where the time goes in v4:
time: 199 us; the launch traced here: 198 us
  waiting for transfers between devices  50.8 us (26%)
  starting transfers between devices  40.8 us (21%)
  blocking collectives  35.4 us (18%)
  matrix products  24.5 us (12%)
  Pallas kernels  18.9 us (9%)
  local copies, waits for them, and re-layouts  14.6 us (7%)
  other arithmetic  11.3 us (6%)
    all_to_all x2, waiting for transfers between devices, gather_groups(): return lax.all_to_all(copies, ALL, 0, 0, axis_index_groups=groups)  19.7 us
    all_to_all x1, blocking collectives, local(): lax.all_to_all(jnp.broadcast_to(shard[None], (4,) + shard.shape), 'z', 0, 0)  19.1 us
    all_to_all x1, blocking collectives, gather_groups(): return lax.all_to_all(copies, ALL, 0, 0, axis_index_groups=groups)  16.3 us
    all_to_all x1, waiting for transfers between devices, local(): lax.all_to_all(terms, ('x', 'y'), 0, 0).astype(jnp.float32)  16.1 us
    ppermute x3, starting transfers between devices, swap_cores(): return lax.ppermute(block, 'c', [(0, 1), (1, 0)])  12 us
    pallas_call x1, Pallas kernels, cross_grads(): pl.pallas_call(cross_kernel, in_specs=[pl.BlockSpec(memory_space=pltpu.SM...  10.9 us
    all_to_all x2, starting transfers between devices, gather_groups(): return lax.all_to_all(copies, ALL, 0, 0, axis_index_groups=groups)  8.94 us
    all_to_all x1, waiting for transfers between devices, local(): lax.all_to_all(mixed.transpose(1, 0, 2), SEQ, split_axis=0, concat_axis=0)  8.43 us
  transfers between devices with their start and end apart: 10, of which 6 were waited for; matrix products, arithmetic and copies ran while one was open for 16% of the time, Pallas kernels for 4%

profile of v4, /device:TPU:1, one launch (start us, length us, event | category | flops | bytes accessed | tf_op | source)
XLA Modules:
  0.0 197.9 jit_solution(18365839157562908908)
XLA Ops:
  0.6 0.0 copy-start
  0.6 1.0 pad_maximum_fusion.5
  1.6 0.1 broadcast_in_dim.10
  1.7 0.2 broadcast_in_dim.11
  1.9 19.1 %all_to_all.35 = bf16[4,2,20736]{2,1,0:T(2,128)(2,1)S(1)} all-to-all(bf16[4,2,20736]{2,1,0:T(2,128)(2,1)S(1)} %broadcast_in_dim.11), channel_id=1, replica_groups=mesh['s'=2,'x'=4,'y'=4,'z'=4,'c'=2] {'z'}, dimensions={0} | all-to-all | bytes 663552 | tf_op jit(solution)/shard_map/all_to_all | solution.py:216
  21.0 0.2 reshape.62
  21.2 0.1 broadcast_in_dim.12
  21.3 16.3 %all_to_all.36 = bf16[4,40,4608]{2,1,0:T(8,128)(2,1)S(1)} all-to-all(bf16[4,40,4608]{2,1,0:T(8,128)(2,1)S(1)} %broadcast_in_dim.12), channel_id=1, replica_groups={{0,32,64,96},{1,9,17,25},{8,40,72,104},{33,41,49,57},{16,48,80,112},{65..., dimensions={0} | all-to-all | bytes 2949120 | tf_op jit(solution)/shard_map/all_to_all | solution.py:145
  37.6 1.1 copy-done.9
  38.8 1.2 broadcast_in_dim.13
  40.0 3.7 %all-to-all-start.2 = ((bf16[4,4,40,1152]{3,2,1,0:T(8,128)(2,1)}), bf16[4,4,40,1152]{3,2,1,0:T(8,128)(2,1)S(1)}, u32[]{:S(2)}, u32[]{:S(2)}) async-start(bf16[4,4,40,1152]{3,2,1,0:T(8,128)(2,1)} %broadcast_in_dim.13), calls=%async_computation.2 | async-start | bytes 2949120 | tf_op jit(solution)/shard_map/all_to_all | solution.py:145
  43.8 5.1 %collective-permute-start = (bf16[128,1152]{1,0:T(8,128)(2,1)}, bf16[128,1152]{1,0:T(8,128)(2,1)}, u32[]{:S(2)}, u32[]{:S(2)}) collective-permute-start(bf16[128,1152]{1,0:T(8,128)(2,1)} %bitcast), channel_id=1, source_target_pairs={{0,1},{1,0},{2,3},{3,2},{4,5},{5,4},{6,7},{7,6},{8,9},{9,8},{10,11... | collective-permute-start | bytes 884744 | tf_op jit(solution)/shard_map/ppermute | solution.py:149
  49.5 0.1 pad.12.key_ref
  49.6 1.2 pad.13.value_ref
  50.8 0.0 collective-permute-done
  50.8 1.1 select_bitcast_fusion.5
  51.9 0.9 pad_maximum_fusion.3
  52.8 3.0 %all-to-all-done.2 = bf16[4,4,40,1152]{3,2,1,0:T(8,128)(2,1)S(1)} async-done(((bf16[4,4,40,1152]{3,2,1,0:T(8,128)(2,1)}), bf16[4,4,40,1152]{3,2,1,0:T(8,128)(2,1)S(1)}, u32[]{:S(2)}, u32[]{:S(2)}) %all-to-all-start.2) | async-done | bytes 1474592 | tf_op jit(solution)/shard_map/all_to_all | solution.py:145
  55.8 1.9 convolution_convert_fusion.2
  57.7 0.0 copy-start.2
  57.8 0.0 copy-start.3
  57.8 0.0 copy-start.4
  57.8 6.3 %collective-permute-start.1 = (bf16[128,640]{1,0:T(8,128)(2,1)S(1)}, bf16[128,640]{1,0:T(8,128)(2,1)S(1)}, u32[]{:S(2)}, u32[]{:S(2)}) collective-permute-start(bf16[128,640]{1,0:T(8,128)(2,1)S(1)} %dynamic-slice_bitcast_fusion.1), channel_id=1, source_target_pairs={{0,1},{1,0},{2,3},{3,2},{4,5},{5,4},{6,7},{7,6},{8,9},{9,8},{10,11... | collective-permute-start | bytes 491528 | tf_op jit(solution)/shard_map/ppermute | solution.py:149
  64.1 1.2 dynamic-slice_bitcast_fusion
  65.3 0.5 collective-permute-start.3
  65.9 0.0 collective-permute-done.1
  65.9 1.4 fusion.13.grad_ref
  67.4 0.0 slice-start
  67.4 8.0 %temporal_grads.1 = bf16[128,3456]{1,0:T(8,128)(2,1)S(1)} custom-call(bf16[128,1152]{1,0:T(8,128)(2,1)S(1)} %fusion.13.grad_ref, bf16[128,1152]{1,0:T(8,128)(2,1)S(1)} %bitcast.64, bf16[128,1152]{1,0:T(8,128)(2,1)S(1)} %bitcast.65, bf16[128,1152]{1,0:T(8,128)(2,1)S(1)} %bitcast.66), custom_call_target="tpu_custom_call" | custom-call | flops 188743680 | bytes 2064384 | tf_op jit(solution)/shard_map/temporal_grads/pallas_call | solution.py:65
  75.4 0.6 collective-permute-start.2
  76.0 2.2 %iota_compare_fusion = pred[1280,1152]{1,0:T(32,128)(4,1)} fusion(s32[1280]{0:T(1024)S(1)} %copy-done.13), kind=kLoop, calls=%fused_computation.1 | loop fusion | flops 1474560 | bytes 1479680 | tf_op jit(solution)/shard_map/eq | solution.py:210
  78.2 2.4 %broadcast_in_dim.14 = bf16[4,4,40,3456]{3,2,1,0:T(8,128)(2,1)} broadcast(bf16[4,40,3456]{2,1,0:T(8,128)(2,1)S(1)} %slice-done), dimensions={1,2,3} | broadcast | bytes 5529600 | tf_op jit(solution)/shard_map/broadcast_in_dim | solution.py:144
  80.5 5.2 %all-to-all-start.3 = ((bf16[4,4,40,3456]{3,2,1,0:T(8,128)(2,1)}), bf16[4,4,40,3456]{3,2,1,0:T(8,128)(2,1)}, u32[]{:S(2)}, u32[]{:S(2)}) async-start(bf16[4,4,40,3456]{3,2,1,0:T(8,128)(2,1)} %broadcast_in_dim.14), calls=%async_computation.3 | async-start | bytes 8847360 | tf_op jit(solution)/shard_map/all_to_all | solution.py:145
  85.8 2.7 %fusion.5 = f32[256,640]{1,0:T(8,128)} fusion(bf16[256,1152]{1,0:T(8,128)(2,1)S(1)} %bitcast.72, pred[1280,1152]{1,0:T(32,128)(4,1)} %iota_compare_fusion, s32[]{:T(128)S(6)} %select_n.75), kind=kOutput, calls=%fused_computation.9 | convolution fusion | flops 377487360 | bytes 1982468 | tf_op jit(solution)/shard_map/dot_general | solution.py:241
  88.4 0.0 collective-permute-done.3
  88.4 0.0 collective-permute-start.4
  88.5 1.3 select_bitcast_fusion.3
  89.8 1.4 pad_maximum_fusion.2
  91.2 0.5 collective-permute-done.4
  91.7 1.9 select_bitcast_fusion.1
  93.6 0.5 broadcast_select_fusion
  94.2 1.5 copy-done.5
  95.7 0.7 copy-done.6
  96.5 0.6 fusion.14.query_ref
  97.1 16.7 %all-to-all-done.3 = bf16[4,4,40,3456]{3,2,1,0:T(8,128)(2,1)} async-done(((bf16[4,4,40,3456]{3,2,1,0:T(8,128)(2,1)}), bf16[4,4,40,3456]{3,2,1,0:T(8,128)(2,1)}, u32[]{:S(2)}, u32[]{:S(2)}) %all-to-all-start.3) | async-done | bytes 4423712 | tf_op jit(solution)/shard_map/all_to_all | solution.py:145
  113.7 4.4 %fusion.16 = bf16[256,640]{1,0:T(8,128)(2,1)S(1)} fusion(f32[256,640]{1,0:T(8,128)S(1)} %copy-done.14, bf16[256,3456]{1,0:T(8,128)(2,1)} %bitcast.67, bf16[640,3456]{1,0:T(8,128)(2,1)} %bitcast.14), kind=kOutput, calls=%fused_computation.29 | convolution fusion | flops 1132789760 | bytes 7176192 | tf_op jit(solution)/shard_map/dot_general | solution.py:244
  118.2 1.1 copy.21
  119.2 7.7 %all-to-all-start.4 = ((bf16[128,2,640]{2,1,0:T(2,128)(2,1)}), bf16[128,2,640]{2,1,0:T(2,128)(2,1)S(1)}, u32[]{:S(2)}, u32[]{:S(2)}) async-start(bf16[128,2,640]{2,1,0:T(2,128)(2,1)} %bitcast.61), calls=%async_computation.4 | async-start | bytes 655360 | tf_op jit(solution)/shard_map/all_to_all | solution.py:255
  127.0 7.8 %convolution_convert_fusion.w_out_ref = bf16[1280,1152]{1,0:T(8,128)(2,1)} fusion(s32[1280]{0:T(1024)S(1)} %copy-done.13, bf16[2,576,1152]{2,1,0:T(8,128)(2,1)} %copy-done.6, bf16[2,576,1152]{2,1,0:T(8,128)(2,1)} %copy-done.5), kind=kOutput, calls=%fused_computation | convolution fusion | flops 3405643776 | bytes 8262656 | tf_op jit(solution)/shard_map/dot_general | solution.py:248
  134.8 8.4 %all-to-all-done.4 = bf16[128,2,640]{2,1,0:T(2,128)(2,1)S(1)} async-done(((bf16[128,2,640]{2,1,0:T(2,128)(2,1)}), bf16[128,2,640]{2,1,0:T(2,128)(2,1)S(1)}, u32[]{:S(2)}, u32[]{:S(2)}) %all-to-all-start.4) | async-done | bytes 327712 | tf_op jit(solution)/shard_map/all_to_all | solution.py:255
  143.2 0.3 copy.16
  143.5 1.8 copy-done.1
  145.4 10.9 %cross_grads.1 = (bf16[128,1152]{1,0:T(8,128)(2,1)S(1)}, bf16[16,72,640]{2,1,0:T(8,128)(2,1)}) custom-call(s32[1]{0:T(128)S(6)} %copy.24.length_ref, bf16[128,1280]{1,0:T(8,128)(2,1)S(1)} %bitcast.62, bf16[1280,1152]{1,0:T(8,128)(2,1)S(1)} %copy-done.1, bf16[128,1152]{1,0:T(8,128)(2,1)S(1)} %fusion.14.query_ref, bf16[384,1152]{1,0:T(8,128)(2,1)S(1)} %pad.12.key_ref, ...), custom_call_target="tpu_custom_call" | custom-call | flops 943718400 | bytes 8388608 | tf_op jit(solution)/shard_map/cross_grads/pallas_call | solution.py:105
  156.3 3.9 %all-to-all-start.5 = ((bf16[16,72,640]{2,1,0:T(8,128)(2,1)}), bf16[16,72,640]{2,1,0:T(8,128)(2,1)S(1)}, u32[]{:S(2)}, u32[]{:S(2)}) async-start(bf16[16,72,640]{2,1,0:T(8,128)(2,1)} %get-tuple-element.11), calls=%async_computation.5 | async-start | bytes 2949120 | tf_op jit(solution)/shard_map/all_to_all | solution.py:269
  160.2 3.5 %fusion.17 = f32[128,1152]{1,0:T(8,128)} fusion(bf16[128,1152]{1,0:T(8,128)(2,1)S(1)} %get-tuple-element.10, bf16[2,576,1152]{2,1,0:T(8,128)(2,1)} %copy-done.5, bf16[2,576,1152]{2,1,0:T(8,128)(2,1)} %copy-done.6), kind=kOutput, calls=%fused_computation.35 | convolution fusion | flops 345047040 | bytes 6193152 | tf_op jit(solution)/shard_map/dot_general | solution.py:267
  163.7 16.1 %all-to-all-done.5 = bf16[16,72,640]{2,1,0:T(8,128)(2,1)S(1)} async-done(((bf16[16,72,640]{2,1,0:T(8,128)(2,1)}), bf16[16,72,640]{2,1,0:T(8,128)(2,1)S(1)}, u32[]{:S(2)}, u32[]{:S(2)}) %all-to-all-start.5) | async-done | bytes 1474592 | tf_op jit(solution)/shard_map/all_to_all | solution.py:269
  179.7 0.2 reduce_sum.21
  179.9 0.1 fusion.29
  180.1 0.9 reshape.77
  181.0 7.7 %all-to-all-start.6 = ((bf16[16,2,1350]{2,1,0:T(2,128)(2,1)}), bf16[16,2,1350]{2,1,0:T(2,128)(2,1)S(1)}, u32[]{:S(2)}, u32[]{:S(2)}) async-start(bf16[16,2,1350]{2,1,0:T(2,128)(2,1)} %reshape.77), calls=%async_computation.6 | async-start | bytes 180224 | tf_op jit(solution)/shard_map/all_to_all | solution.py:274
  188.7 2.2 %fusion.15 = bf16[1,128,1152]{2,1,0:T(8,128)(2,1)} fusion(f32[128,1152]{1,0:T(8,128)S(1)} %copy-done.11, bf16[128,1280]{1,0:T(8,128)(2,1)S(1)} %bitcast.63, s32[1280]{0:T(1024)S(1)} %copy-done.13), kind=kOutput, calls=%fused_computation.23 | convolution fusion | flops 379256832 | bytes 1217536 | tf_op jit(solution)/shard_map/dot_general | solution.py:266
  190.8 6.1 %all-to-all-done.6 = bf16[16,2,1350]{2,1,0:T(2,128)(2,1)S(1)} async-done(((bf16[16,2,1350]{2,1,0:T(2,128)(2,1)}), bf16[16,2,1350]{2,1,0:T(2,128)(2,1)S(1)}, u32[]{:S(2)}, u32[]{:S(2)}) %all-to-all-start.6) | async-done | bytes 86432 | tf_op jit(solution)/shard_map/all_to_all | solution.py:274
  197.0 0.2 reshape.78
  197.2 0.7 convert_reduce_fusion
  (32 shorter events, 0.3 us)
Async XLA Ops:
  0.6 95.8 %copy-start = (bf16[1,128,1152]{2,1,0:T(8,128)(2,1)S(1)}, bf16[1,128,1152]{2,1,0:T(8,128)(2,1)}, u32[]{:S(2)}) copy-start(bf16[1,128,1152]{2,1,0:T(8,128)(2,1)} %param.18) | copy-start | bytes 884740
  37.6 1.1 copy-start.9
  38.8 10.7 %copy-start.10 = (bf16[300,1152]{1,0:T(8,128)(2,1)S(1)}, bf16[300,1152]{1,0:T(8,128)(2,1)}, u32[]{:S(2)}) copy-start(bf16[300,1152]{1,0:T(8,128)(2,1)} %param.20) | copy-start | bytes 2073604
  40.0 15.8 %all-to-all-start.2 = ((bf16[4,4,40,1152]{3,2,1,0:T(8,128)(2,1)}), bf16[4,4,40,1152]{3,2,1,0:T(8,128)(2,1)S(1)}, u32[]{:S(2)}, u32[]{:S(2)}) async-start(bf16[4,4,40,1152]{3,2,1,0:T(8,128)(2,1)} %broadcast_in_dim.13), calls=%async_computation.2 | async-start | bytes 2949120 | tf_op jit(solution)/shard_map/all_to_all | solution.py:145
  43.8 7.0 %collective-permute-start = (bf16[128,1152]{1,0:T(8,128)(2,1)}, bf16[128,1152]{1,0:T(8,128)(2,1)}, u32[]{:S(2)}, u32[]{:S(2)}) collective-permute-start(bf16[128,1152]{1,0:T(8,128)(2,1)} %bitcast), channel_id=1, source_target_pairs={{0,1},{1,0},{2,3},{3,2},{4,5},{5,4},{6,7},{7,6},{8,9},{9,8},{10,11... | collective-permute-start | bytes 884744 | tf_op jit(solution)/shard_map/ppermute | solution.py:149
  55.8 8.3 %copy-start.7 = (bf16[2,576,1152]{2,1,0:T(8,128)(2,1)S(1)}, bf16[2,576,1152]{2,1,0:T(8,128)(2,1)}, u32[]{:S(2)}) copy-start(bf16[2,576,1152]{2,1,0:T(8,128)(2,1)} %param.19) | copy-start | bytes 7962628
  55.8 10.1 %copy-start.13 = (s32[1280]{0:T(1024)S(1)}, s32[1280]{0:T(1024)}, u32[]{:S(2)}) copy-start(s32[1280]{0:T(1024)} %constant.36.clone) | copy-start | bytes 15364
  57.7 9.6 %copy-start.2 = (bf16[2,64,1,1152]{3,1,2,0:T(8,128)(2,1)S(1)}, bf16[2,64,1,1152]{3,1,2,0:T(8,128)(2,1)}, u32[]{:S(2)}) copy-start(bf16[2,64,1,1152]{3,1,2,0:T(8,128)(2,1)} %param.13) | copy-start | bytes 884740
  57.8 9.6 %copy-start.3 = (bf16[2,64,1,1152]{3,1,2,0:T(8,128)(2,1)S(1)}, bf16[2,64,1,1152]{3,1,2,0:T(8,128)(2,1)}, u32[]{:S(2)}) copy-start(bf16[2,64,1,1152]{3,1,2,0:T(8,128)(2,1)} %param.14) | copy-start | bytes 884740
  57.8 9.6 %copy-start.4 = (bf16[2,64,1,1152]{3,1,2,0:T(8,128)(2,1)S(1)}, bf16[2,64,1,1152]{3,1,2,0:T(8,128)(2,1)}, u32[]{:S(2)}) copy-start(bf16[2,64,1,1152]{3,1,2,0:T(8,128)(2,1)} %param.15) | copy-start | bytes 884740
  57.8 8.1 %collective-permute-start.1 = (bf16[128,640]{1,0:T(8,128)(2,1)S(1)}, bf16[128,640]{1,0:T(8,128)(2,1)S(1)}, u32[]{:S(2)}, u32[]{:S(2)}) collective-permute-start(bf16[128,640]{1,0:T(8,128)(2,1)S(1)} %dynamic-slice_bitcast_fusion.1), channel_id=1, source_target_pairs={{0,1},{1,0},{2,3},{3,2},{4,5},{5,4},{6,7},{7,6},{8,9},{9,8},{10,11... | collective-permute-start | bytes 491528 | tf_op jit(solution)/shard_map/ppermute | solution.py:149
  65.3 23.1 %collective-permute-start.3 = (bf16[576,1152]{1,0:T(8,128)(2,1)}, bf16[576,1152]{1,0:T(8,128)(2,1)}, u32[]{:S(2)}, u32[]{:S(2)}) collective-permute-start(bf16[576,1152]{1,0:T(8,128)(2,1)} %dynamic-slice_bitcast_fusion), channel_id=1, source_target_pairs={{0,128},{1,135},{128,2},{129,1},{2,130},{3,129},{130,4},{131,3},{4... | collective-permute-start | bytes 3981320 | tf_op jit(solution)/shard_map/ppermute | solution.py:185
  67.4 10.8 %slice-start = ((bf16[4,40,4608]{2,1,0:T(8,128)(2,1)}), bf16[4,40,3456]{2,1,0:T(8,128)(2,1)S(1)}, s32[]{:S(2)}) async-start(bf16[4,40,4608]{2,1,0:T(8,128)(2,1)} %copy-done.9), calls=%async_computation.7 | async-start | bytes 2211840 | tf_op jit(solution)/shard_map/slice | solution.py:222
  75.4 13.1 %collective-permute-start.2 = (bf16[128,3456]{1,0:T(8,128)(2,1)S(1)}, bf16[128,3456]{1,0:T(8,128)(2,1)}, u32[]{:S(2)}, u32[]{:S(2)}) collective-permute-start(bf16[128,3456]{1,0:T(8,128)(2,1)S(1)} %temporal_grads.1), channel_id=1, source_target_pairs={{0,1},{1,0},{2,3},{3,2},{4,5},{5,4},{6,7},{7,6},{8,9},{9,8},{10,11... | collective-permute-start | bytes 2654216 | tf_op jit(solution)/shard_map/ppermute | solution.py:149
  80.5 5.2 %copy-start.12 = (bf16[2,128,1152]{2,1,0:T(8,128)(2,1)S(1)}, bf16[2,128,1152]{2,1,0:T(8,128)(2,1)}, u32[]{:S(2)}) copy-start(bf16[2,128,1152]{2,1,0:T(8,128)(2,1)} %pad_maximum_fusion.3) | copy-start | bytes 1769476
  80.5 33.2 %all-to-all-start.3 = ((bf16[4,4,40,3456]{3,2,1,0:T(8,128)(2,1)}), bf16[4,4,40,3456]{3,2,1,0:T(8,128)(2,1)}, u32[]{:S(2)}, u32[]{:S(2)}) async-start(bf16[4,4,40,3456]{3,2,1,0:T(8,128)(2,1)} %broadcast_in_dim.14), calls=%async_computation.3 | async-start | bytes 8847360 | tf_op jit(solution)/shard_map/all_to_all | solution.py:145
  88.4 3.3 %collective-permute-start.4 = (bf16[576,1152]{1,0:T(8,128)(2,1)}, bf16[576,1152]{1,0:T(8,128)(2,1)S(1)}, u32[]{:S(2)}, u32[]{:S(2)}) collective-permute-start(bf16[576,1152]{1,0:T(8,128)(2,1)} %collective-permute-done.3), channel_id=1, source_target_pairs={{0,1},{1,0},{2,3},{3,2},{4,5},{5,4},{6,7},{7,6},{8,9},{9,8},{10,11... | collective-permute-start | bytes 3981320 | tf_op jit(solution)/shard_map/ppermute | solution.py:186
  91.2 2.4 %copy-start.8 = (bf16[2,576,1152]{2,1,0:T(8,128)(2,1)S(1)}, bf16[2,576,1152]{2,1,0:T(8,128)(2,1)}, u32[]{:S(2)}) copy-start(bf16[2,576,1152]{2,1,0:T(8,128)(2,1)} %param.19) | copy-start | bytes 7962628
  94.2 1.6 copy-start.5
  94.2 2.3 %copy-start.6 = (bf16[2,576,1152]{2,1,0:T(8,128)(2,1)}, bf16[2,576,1152]{2,1,0:T(8,128)(2,1)S(1)}, u32[]{:S(2)}) copy-start(bf16[2,576,1152]{2,1,0:T(8,128)(2,1)S(1)} %get-tuple-element.13) | copy-start | bytes 7962628
  96.5 17.3 %copy-start.14 = (f32[256,640]{1,0:T(8,128)S(1)}, f32[256,640]{1,0:T(8,128)}, u32[]{:S(2)}) copy-start(f32[256,640]{1,0:T(8,128)} %fusion.5) | copy-start | bytes 1966084
  119.2 24.0 %all-to-all-start.4 = ((bf16[128,2,640]{2,1,0:T(2,128)(2,1)}), bf16[128,2,640]{2,1,0:T(2,128)(2,1)S(1)}, u32[]{:S(2)}, u32[]{:S(2)}) async-start(bf16[128,2,640]{2,1,0:T(2,128)(2,1)} %bitcast.61), calls=%async_computation.4 | async-start | bytes 655360 | tf_op jit(solution)/shard_map/all_to_all | solution.py:255
  143.5 1.8 copy-start.1
  156.3 23.5 %all-to-all-start.5 = ((bf16[16,72,640]{2,1,0:T(8,128)(2,1)}), bf16[16,72,640]{2,1,0:T(8,128)(2,1)S(1)}, u32[]{:S(2)}, u32[]{:S(2)}) async-start(bf16[16,72,640]{2,1,0:T(8,128)(2,1)} %get-tuple-element.11), calls=%async_computation.5 | async-start | bytes 2949120 | tf_op jit(solution)/shard_map/all_to_all | solution.py:269
  163.7 25.0 %copy-start.11 = (f32[128,1152]{1,0:T(8,128)S(1)}, f32[128,1152]{1,0:T(8,128)}, u32[]{:S(2)}) copy-start(f32[128,1152]{1,0:T(8,128)} %fusion.17) | copy-start | bytes 1769476
  181.0 16.0 %all-to-all-start.6 = ((bf16[16,2,1350]{2,1,0:T(2,128)(2,1)}), bf16[16,2,1350]{2,1,0:T(2,128)(2,1)S(1)}, u32[]{:S(2)}, u32[]{:S(2)}) async-start(bf16[16,2,1350]{2,1,0:T(2,128)(2,1)} %reshape.77), calls=%async_computation.6 | async-start | bytes 180224 | tf_op jit(solution)/shard_map/all_to_all | solution.py:274

commit v5 on v4

--- a/solution.py
+++ b/solution.py
@@ -73,6 +73,40 @@
         ),
         name="temporal_grads",
     )(grad_heads, query, key_rows, value)
+
+
+def mixed_kernel(slot_ref, qkv_ref, residual_ref, w0, w1, w2, w3, out_ref, held, arrived):
+    copies = [
+        pltpu.make_async_copy(block, held.at[slot_ref[i]], arrived.at[i])
+        for i, block in enumerate((w0, w1, w2, w3))
+    ]
+    for copy in copies:
+        copy.start()
+    for copy in copies:
+        copy.wait()
+    weight = held[...].reshape(-1, held.shape[2])
+    product = dot(qkv_ref[...], weight, CONTRACT_LAST)
+    out_ref[...] = (residual_ref[...] + product).astype(jnp.bfloat16)
+
+
+def mixed_half(slots, qkv_both, residual, blocks):
+    in_vmem = pl.BlockSpec(memory_space=pltpu.VMEM)
+    return pl.pallas_call(
+        mixed_kernel,
+        in_specs=[pl.BlockSpec(memory_space=pltpu.SMEM), in_vmem, in_vmem]
+        + [pl.BlockSpec(memory_space=pl.ANY)] * 4,
+        out_specs=in_vmem,
+        out_shape=jax.ShapeDtypeStruct(residual.shape, jnp.bfloat16),
+        scratch_shapes=[
+            pltpu.VMEM((4,) + blocks[0].shape, jnp.bfloat16),
+            pltpu.SemaphoreType.DMA((4,)),
+        ],
+        compiler_params=pltpu.CompilerParams(vmem_limit_bytes=32 << 20),
+        cost_estimate=pl.CostEstimate(
+            flops=2 * residual.size * qkv_both.shape[1], bytes_accessed=8 << 20, transcendentals=0
+        ),
+        name="mixed_half",
+    )(slots, qkv_both, residual, *blocks)
 
 
 def cross_kernel(
@@ -145,6 +179,17 @@
     return lax.all_to_all(copies, ALL, 0, 0, axis_index_groups=groups)
 
 
+def shift_last(block, step):
+    pairs = []
+    for s in range(2):
+        for x in range(4):
+            for y in range(4):
+                for z in range(4):
+                    pairs.append((flat(s, x, y, z, 0), flat(s, x, (y + step) % 4, z, 0)))
+                    pairs.append((flat(s, x, y, z, 1), flat(s, (x + step) % 4, y, z, 1)))
+    return lax.ppermute(block, ALL, pairs)
+
+
 def swap_cores(block):
     return lax.ppermute(block, "c", [(0, 1), (1, 0)])
 
@@ -216,11 +261,13 @@
     column = lax.all_to_all(jnp.broadcast_to(shard[None], (4,) + shard.shape), "z", 0, 0)
     column = jnp.pad(column.reshape(36, 4 * width), ((0, 4), (0, 0)))
     near = gather_groups(column, ring_groups(0))
-    out_mine = gather_groups(near[:, :, :width], ring_groups(1))
-    near, out_mine, cross_weights = lax.optimization_barrier((near, out_mine, cross_weights))
+    near, cross_weights = lax.optimization_barrier((near, cross_weights))
+    qkv_near = near[:, :, width:].reshape(160, 3 * width)
+    blocks = [qkv_near] + [shift_last(qkv_near, step) for step in (1, 3, 2)]
+    place_here = jnp.where(core == 0, lax.axis_index("y"), lax.axis_index("x"))
+    slots = (place_here - jnp.array([0, 1, 3, 2], jnp.int32)) % 4
+    out_mine = gather_groups(near[:, :, :width], ring_groups(1)).reshape(640, width)
     full_cross = cross_halves(cross_weights)
-    qkv_mine = gather_groups(near[:, :, width:], ring_groups(1)).reshape(640, 3 * width)
-    out_mine = out_mine.reshape(640, width)
     heads_mine = (
         lax.dot_general(grad_both, out_mine, CONTRACT_LAST, preferred_element_type=jnp.float32)
         .astype(jnp.bfloat16)
@@ -241,10 +288,7 @@
     residual = lax.dot_general(
         grad_both, place_mine, CONTRACT_LAST, preferred_element_type=jnp.float32
     )
-    product = lax.dot_general(
-        qkv_both, qkv_mine, CONTRACT_LAST, preferred_element_type=jnp.float32
-    )
-    mixed = (residual + product).astype(jnp.bfloat16).reshape(2, rows, 640)
+    mixed = mixed_half(slots, qkv_both, residual, blocks).reshape(2, rows, 640)
     w_out_placed = lax.dot_general(
         place, full_cross[1], CONTRACT_LAST, preferred_element_type=jnp.float32
     ).astype(jnp.bfloat16)

time: 199 us -> 198 us (level)
  matrix products: 24.5 us -> 17.8 us
  waiting for transfers between devices: 50.8 us -> 57.1 us
  Pallas kernels: 18.9 us -> 21.9 us
  other arithmetic: 11.3 us -> 8.37 us
  local copies, waits for them, and re-layouts: 14.6 us -> 12.2 us
    ppermute x0 -> x3, waiting for transfers between devices: none -> 22.8 us  [shift_last(): return lax.ppermute(block, ALL, pairs)]
    all_to_all x2 -> x1, waiting for transfers between devices: 19.7 us -> 6.2 us  [gather_groups(): return lax.all_to_all(copies, ALL, 0, 0, axis_index_groups=groups)]
    all_to_all x2 -> x1, starting transfers between devices: 8.94 us -> 4.36 us  [gather_groups(): return lax.all_to_all(copies, ALL, 0, 0, axis_index_groups=groups)]
    dot_general x1 -> x0, matrix products: 4.41 us -> none  [local(): lax.dot_general(qkv_both, qkv_mine, CONTRACT_LAST, preferred_element_type...]
    all_to_all x1, waiting for transfers between devices: 8.43 us -> 4.46 us  [local(): lax.all_to_all(mixed.transpose(1, 0, 2), SEQ, split_axis=0, concat_axis=0)]
    another operation x4, other arithmetic: 4.74 us -> 1.65 us  [in_core_order(): jnp.stack([jnp.where(core == 0, mine, other), jnp.where(core == 0, other,...]
    ppermute x0 -> x3, starting transfers between devices: none -> 2.94 us  [shift_last(): return lax.ppermute(block, ALL, pairs)]
    pallas_call x0 -> x1, Pallas kernels: none -> 2.81 us  [mixed_half(): pl.pallas_call(mixed_kernel, in_specs=[pl.BlockSpec(memory_space=pltpu.SM...]
  transfers between devices with their start and end apart: 10 -> 12, of which waited for: 6 -> 6; matrix products, arithmetic and copies ran while one was open for 16% -> 13% of each run, Pallas kernels for 4% -> 5%
where the time goes in v5:
time: 198 us; the launch traced here: 197 us
  waiting for transfers between devices  57.1 us (29%)
  starting transfers between devices  42.7 us (22%)
  blocking collectives  35.4 us (18%)
  Pallas kernels  21.9 us (11%)
  matrix products  17.8 us (9%)
  local copies, waits for them, and re-layouts  12.2 us (6%)
  other arithmetic  8.37 us (4%)
    ppermute x3, waiting for transfers between devices, shift_last(): return lax.ppermute(block, ALL, pairs)  22.8 us
    all_to_all x1, blocking collectives, local(): lax.all_to_all(jnp.broadcast_to(shard[None], (4,) + shard.shape), 'z', 0, 0)  19.1 us
    all_to_all x1, blocking collectives, gather_groups(): return lax.all_to_all(copies, ALL, 0, 0, axis_index_groups=groups)  16.3 us
    all_to_all x1, waiting for transfers between devices, local(): lax.all_to_all(terms, ('x', 'y'), 0, 0).astype(jnp.float32)  16.3 us
    pallas_call x1, Pallas kernels, cross_grads(): pl.pallas_call(cross_kernel, in_specs=[pl.BlockSpec(memory_space=pltpu.SM...  11.2 us
    ppermute x3, starting transfers between devices, swap_cores(): return lax.ppermute(block, 'c', [(0, 1), (1, 0)])  10.8 us
    all_to_all x1, starting transfers between devices, local(): lax.all_to_all(mixed.transpose(1, 0, 2), SEQ, split_axis=0, concat_axis=0)  10 us
    all_to_all x1, starting transfers between devices, local(): lax.all_to_all(pieces, ('s', 'z', 'c'), 0, 0).astype(jnp.float32)  9.66 us
  transfers between devices with their start and end apart: 12, of which 6 were waited for; matrix products, arithmetic and copies ran while one was open for 13% of the time, Pallas kernels for 5%

profile of v5, /device:TPU:1, one launch (start us, length us, event | category | flops | bytes accessed | tf_op | source)
XLA Modules:
  0.0 197.2 jit_solution(9913945065898616676)
XLA Ops:
  0.6 0.0 copy-start
  0.6 1.0 pad_maximum_fusion.5
  1.6 0.1 broadcast_in_dim.8
  1.7 0.2 broadcast_in_dim.9
  1.9 19.1 %all_to_all.30 = bf16[4,2,20736]{2,1,0:T(2,128)(2,1)S(1)} all-to-all(bf16[4,2,20736]{2,1,0:T(2,128)(2,1)S(1)} %broadcast_in_dim.9), channel_id=1, replica_groups=mesh['s'=2,'x'=4,'y'=4,'z'=4,'c'=2] {'z'}, dimensions={0} | all-to-all | bytes 663552 | tf_op jit(solution)/shard_map/all_to_all | solution.py:261
  21.0 0.2 reshape.61
  21.2 0.1 broadcast_in_dim.10
  21.3 16.3 %all_to_all.31 = bf16[4,40,4608]{2,1,0:T(8,128)(2,1)S(1)} all-to-all(bf16[4,40,4608]{2,1,0:T(8,128)(2,1)S(1)} %broadcast_in_dim.10), channel_id=1, replica_groups={{0,32,64,96},{1,9,17,25},{8,40,72,104},{33,41,49,57},{16,48,80,112},{65..., dimensions={0} | all-to-all | bytes 2949120 | tf_op jit(solution)/shard_map/all_to_all | solution.py:179
  37.6 1.1 copy-done.9
  38.8 1.2 broadcast_in_dim.11
  40.0 4.4 %all-to-all-start.2 = ((bf16[4,4,40,1152]{3,2,1,0:T(8,128)(2,1)}), bf16[4,4,40,1152]{3,2,1,0:T(8,128)(2,1)}, u32[]{:S(2)}, u32[]{:S(2)}) async-start(bf16[4,4,40,1152]{3,2,1,0:T(8,128)(2,1)} %broadcast_in_dim.11), calls=%async_computation.2 | async-start | bytes 2949120 | tf_op jit(solution)/shard_map/all_to_all | solution.py:179
  44.4 0.0 copy-start.7
  44.4 4.5 %collective-permute-start = (bf16[128,1152]{1,0:T(8,128)(2,1)S(1)}, bf16[128,1152]{1,0:T(8,128)(2,1)S(1)}, u32[]{:S(2)}, u32[]{:S(2)}) collective-permute-start(bf16[128,1152]{1,0:T(8,128)(2,1)S(1)} %bitcast.77), channel_id=1, source_target_pairs={{0,1},{1,0},{2,3},{3,2},{4,5},{5,4},{6,7},{7,6},{8,9},{9,8},{10,11... | collective-permute-start | bytes 884744 | tf_op jit(solution)/shard_map/ppermute | solution.py:194
  48.9 1.2 collective-permute-done
  50.1 0.1 select_bitcast_fusion.5
  50.2 0.1 pad_maximum_fusion.3
  50.3 6.2 %all-to-all-done.2 = bf16[4,4,40,1152]{3,2,1,0:T(8,128)(2,1)} async-done(((bf16[4,4,40,1152]{3,2,1,0:T(8,128)(2,1)}), bf16[4,4,40,1152]{3,2,1,0:T(8,128)(2,1)}, u32[]{:S(2)}, u32[]{:S(2)}) %all-to-all-start.2) | async-done | bytes 1474592 | tf_op jit(solution)/shard_map/all_to_all | solution.py:179
  56.5 2.1 %convolution_convert_fusion.2 = bf16[256,640]{1,0:T(8,128)(2,1)S(1)} fusion(bf16[256,1152]{1,0:T(8,128)(2,1)S(1)} %bitcast.73, bf16[640,1152]{1,0:T(8,128)(2,1)} %bitcast.4), kind=kOutput, calls=%fused_computation.28 | convolution fusion | flops 377651200 | bytes 2392064 | tf_op jit(solution)/shard_map/dot_general | solution.py:272
  58.6 0.0 copy-start.2
  58.6 0.0 copy-start.3
  58.6 0.0 copy-start.4
  58.7 5.7 %collective-permute-start.1 = (bf16[128,640]{1,0:T(8,128)(2,1)S(1)}, bf16[128,640]{1,0:T(8,128)(2,1)S(1)}, u32[]{:S(2)}, u32[]{:S(2)}) collective-permute-start(bf16[128,640]{1,0:T(8,128)(2,1)S(1)} %dynamic-slice_bitcast_fusion.1), channel_id=1, source_target_pairs={{0,1},{1,0},{2,3},{3,2},{4,5},{5,4},{6,7},{7,6},{8,9},{9,8},{10,11... | collective-permute-start | bytes 491528 | tf_op jit(solution)/shard_map/ppermute | solution.py:194
  64.4 1.2 dynamic-slice_bitcast_fusion
  65.6 0.5 collective-permute-start.6
  66.2 1.4 fusion.13.grad_ref
  67.7 8.0 %temporal_grads.1 = bf16[128,3456]{1,0:T(8,128)(2,1)S(1)} custom-call(bf16[128,1152]{1,0:T(8,128)(2,1)S(1)} %fusion.13.grad_ref, bf16[128,1152]{1,0:T(8,128)(2,1)S(1)} %bitcast.68, bf16[128,1152]{1,0:T(8,128)(2,1)S(1)} %bitcast.69, bf16[128,1152]{1,0:T(8,128)(2,1)S(1)} %bitcast.70), custom_call_target="tpu_custom_call" | custom-call | flops 188743680 | bytes 2064384 | tf_op jit(solution)/shard_map/temporal_grads/pallas_call | solution.py:65
  75.7 0.0 copy-start.15
  75.7 0.6 collective-permute-start.2
  76.3 2.1 %iota_compare_fusion = pred[1280,1152]{1,0:T(32,128)(4,1)} fusion(s32[1280]{0:T(1024)S(1)} %copy-done.14), kind=kLoop, calls=%fused_computation.1 | loop fusion | flops 1474560 | bytes 1479680 | tf_op jit(solution)/shard_map/eq | solution.py:255
  79.1 0.1 pad.12.key_ref
  79.2 1.2 pad.13.value_ref
  80.4 1.9 fusion.5.residual_ref
  82.3 0.1 slice.20
  82.4 0.5 collective-permute-start.3
  83.0 2.4 %collective-permute-start.4 = (bf16[160,3456]{1,0:T(8,128)(2,1)S(1)}, bf16[160,3456]{1,0:T(8,128)(2,1)S(1)}, u32[]{:S(2)}, u32[]{:S(2)}) collective-permute-start(bf16[160,3456]{1,0:T(8,128)(2,1)S(1)} %bitcast.62), channel_id=1, source_target_pairs={{0,24},{1,97},{2,26},{3,99},{4,28},{5,101},{6,30},{7,103},{8,0},{9... | collective-permute-start | bytes 3317768 | tf_op jit(solution)/shard_map/ppermute | solution.py:190
  85.4 0.6 collective-permute-start.7
  86.0 1.3 select_bitcast_fusion.3
  87.3 0.2 pad_maximum_fusion.2
  87.5 22.8 %collective-permute-done.3.w1 = bf16[160,3456]{1,0:T(8,128)(2,1)S(1)} collective-permute-done((bf16[160,3456]{1,0:T(8,128)(2,1)S(1)}, bf16[160,3456]{1,0:T(8,128)(2,1)S(1)}, u32[]{:S(2)}, u32[]{:S(2)}) %collective-permute-start.3) | collective-permute-done | bytes 1105952 | tf_op jit(solution)/shard_map/ppermute | solution.py:190
  110.3 2.8 %mixed_half.1 = bf16[256,640]{1,0:T(8,128)(2,1)S(1)} custom-call(s32[4]{0:T(128)S(1)} %and_select_fusion.slot_ref, bf16[256,3456]{1,0:T(8,128)(2,1)S(1)} %bitcast.60, f32[256,640]{1,0:T(8,128)S(1)} %fusion.5.residual_ref, bf16[160,3456]{1,0:T(8,128)(2,1)S(1)} %bitcast.64, bf16[160,3456]{1,0:T(8,128)(2,1)S(1)} %collective-permute-done.3.w1, ...), custom_call_target="tpu_custom_call" | custom-call | flops 1132462080 | bytes 8388608 | tf_op jit(solution)/shard_map/mixed_half/pallas_call | solution.py:94
  113.1 1.1 copy.22
  114.2 10.0 %all-to-all-start.3 = ((bf16[128,2,640]{2,1,0:T(2,128)(2,1)}), bf16[128,2,640]{2,1,0:T(2,128)(2,1)S(1)}, u32[]{:S(2)}, u32[]{:S(2)}) async-start(bf16[128,2,640]{2,1,0:T(2,128)(2,1)} %bitcast.59), calls=%async_computation.3 | async-start | bytes 655360 | tf_op jit(solution)/shard_map/all_to_all | solution.py:299
  124.3 2.1 %select_bitcast_fusion.1 = (bf16[1,576,1152]{2,1,0:T(8,128)(2,1)S(1)}, bf16[1,576,1152]{2,1,0:T(8,128)(2,1)S(1)}) fusion(bf16[576,1152]{1,0:T(8,128)(2,1)} %collective-permute-done.6, bf16[576,1152]{1,0:T(8,128)(2,1)} %collective-permute-done.7, pred[]{:T(512)S(6)} %eq.12), kind=kLoop, calls=%fused_computation.26 | loop fusion | flops 1327104 | bytes 5308417 | tf_op jit(solution)/shard_map/stack | solution.py:232
  126.4 0.4 copy-done.8
  126.8 0.5 broadcast_select_fusion
  127.4 0.6 fusion.14.query_ref
  128.0 0.9 copy-done.5
  128.9 0.8 copy-done.6
  129.7 6.1 %convolution_convert_fusion.w_out_ref = bf16[1280,1152]{1,0:T(8,128)(2,1)} fusion(s32[1280]{0:T(1024)S(1)} %copy-done.14, bf16[2,576,1152]{2,1,0:T(8,128)(2,1)S(1)} %get-tuple-element.11, bf16[2,576,1152]{2,1,0:T(8,128)(2,1)S(1)} %get-tuple-element.10), kind=kOutput, calls=%fused_computation | convolution fusion | flops 3405643776 | bytes 8262656 | tf_op jit(solution)/shard_map/dot_general | solution.py:292
  135.8 4.5 %all-to-all-done.3 = bf16[128,2,640]{2,1,0:T(2,128)(2,1)S(1)} async-done(((bf16[128,2,640]{2,1,0:T(2,128)(2,1)}), bf16[128,2,640]{2,1,0:T(2,128)(2,1)S(1)}, u32[]{:S(2)}, u32[]{:S(2)}) %all-to-all-start.3) | async-done | bytes 327712 | tf_op jit(solution)/shard_map/all_to_all | solution.py:299
  140.3 0.3 copy.17
  140.6 1.8 copy-done.1
  142.4 11.2 %cross_grads.1 = (bf16[128,1152]{1,0:T(8,128)(2,1)S(1)}, bf16[16,72,640]{2,1,0:T(8,128)(2,1)}) custom-call(s32[1]{0:T(128)S(6)} %copy.25.length_ref, bf16[128,1280]{1,0:T(8,128)(2,1)S(1)} %bitcast.66, bf16[1280,1152]{1,0:T(8,128)(2,1)S(1)} %copy-done.1, bf16[128,1152]{1,0:T(8,128)(2,1)S(1)} %fusion.14.query_ref, bf16[384,1152]{1,0:T(8,128)(2,1)S(1)} %pad.12.key_ref, ...), custom_call_target="tpu_custom_call" | custom-call | flops 943718400 | bytes 8388608 | tf_op jit(solution)/shard_map/cross_grads/pallas_call | solution.py:139
  153.6 3.7 %all-to-all-start.4 = ((bf16[16,72,640]{2,1,0:T(8,128)(2,1)}), bf16[16,72,640]{2,1,0:T(8,128)(2,1)S(1)}, u32[]{:S(2)}, u32[]{:S(2)}) async-start(bf16[16,72,640]{2,1,0:T(8,128)(2,1)} %get-tuple-element.9), calls=%async_computation.4 | async-start | bytes 2949120 | tf_op jit(solution)/shard_map/all_to_all | solution.py:313
  157.3 3.5 %fusion.16 = f32[128,1152]{1,0:T(8,128)} fusion(bf16[128,1152]{1,0:T(8,128)(2,1)S(1)} %get-tuple-element.8, bf16[2,576,1152]{2,1,0:T(8,128)(2,1)} %copy-done.5, bf16[2,576,1152]{2,1,0:T(8,128)(2,1)} %copy-done.6), kind=kOutput, calls=%fused_computation.33 | convolution fusion | flops 345047040 | bytes 6193152 | tf_op jit(solution)/shard_map/dot_general | solution.py:311
  160.8 16.3 %all-to-all-done.4 = bf16[16,72,640]{2,1,0:T(8,128)(2,1)S(1)} async-done(((bf16[16,72,640]{2,1,0:T(8,128)(2,1)}), bf16[16,72,640]{2,1,0:T(8,128)(2,1)S(1)}, u32[]{:S(2)}, u32[]{:S(2)}) %all-to-all-start.4) | async-done | bytes 1474592 | tf_op jit(solution)/shard_map/all_to_all | solution.py:313
  177.1 0.2 reduce_sum.21
  177.3 0.1 fusion.29
  177.5 0.9 reshape.76
  178.3 9.7 %all-to-all-start.5 = ((bf16[16,2,1350]{2,1,0:T(2,128)(2,1)}), bf16[16,2,1350]{2,1,0:T(2,128)(2,1)S(1)}, u32[]{:S(2)}, u32[]{:S(2)}) async-start(bf16[16,2,1350]{2,1,0:T(2,128)(2,1)} %reshape.76), calls=%async_computation.5 | async-start | bytes 180224 | tf_op jit(solution)/shard_map/all_to_all | solution.py:318
  188.0 2.2 %fusion.15 = bf16[1,128,1152]{2,1,0:T(8,128)(2,1)} fusion(f32[128,1152]{1,0:T(8,128)S(1)} %copy-done.12, bf16[128,1280]{1,0:T(8,128)(2,1)S(1)} %bitcast.67, s32[1280]{0:T(1024)S(1)} %copy-done.14), kind=kOutput, calls=%fused_computation.23 | convolution fusion | flops 379256832 | bytes 1217536 | tf_op jit(solution)/shard_map/dot_general | solution.py:310
  190.2 6.1 %all-to-all-done.5 = bf16[16,2,1350]{2,1,0:T(2,128)(2,1)S(1)} async-done(((bf16[16,2,1350]{2,1,0:T(2,128)(2,1)}), bf16[16,2,1350]{2,1,0:T(2,128)(2,1)S(1)}, u32[]{:S(2)}, u32[]{:S(2)}) %all-to-all-start.5) | async-done | bytes 86432 | tf_op jit(solution)/shard_map/all_to_all | solution.py:318
  196.3 0.2 reshape.77
  196.6 0.7 convert_reduce_fusion
  (37 shorter events, 0.3 us)
Async XLA Ops:
  0.6 126.8 %copy-start = (bf16[1,128,1152]{2,1,0:T(8,128)(2,1)S(1)}, bf16[1,128,1152]{2,1,0:T(8,128)(2,1)}, u32[]{:S(2)}) copy-start(bf16[1,128,1152]{2,1,0:T(8,128)(2,1)} %param.19) | copy-start | bytes 884740
  37.6 1.1 copy-start.9
  38.8 5.6 %copy-start.13 = (bf16[2,64,1,1152]{3,1,2,0:T(8,128)(2,1)S(1)}, bf16[2,64,1,1152]{3,1,2,0:T(8,128)(2,1)}, u32[]{:S(2)}) copy-start(bf16[2,64,1,1152]{3,1,2,0:T(8,128)(2,1)} %param.13) | copy-start | bytes 884740
  40.0 16.4 %all-to-all-start.2 = ((bf16[4,4,40,1152]{3,2,1,0:T(8,128)(2,1)}), bf16[4,4,40,1152]{3,2,1,0:T(8,128)(2,1)}, u32[]{:S(2)}, u32[]{:S(2)}) async-start(bf16[4,4,40,1152]{3,2,1,0:T(8,128)(2,1)} %broadcast_in_dim.11), calls=%async_computation.2 | async-start | bytes 2949120 | tf_op jit(solution)/shard_map/all_to_all | solution.py:179
  44.4 20.0 %copy-start.7 = (bf16[2,576,1152]{2,1,0:T(8,128)(2,1)S(1)}, bf16[2,576,1152]{2,1,0:T(8,128)(2,1)}, u32[]{:S(2)}) copy-start(bf16[2,576,1152]{2,1,0:T(8,128)(2,1)} %param.20) | copy-start | bytes 7962628
  44.4 5.7 %collective-permute-start = (bf16[128,1152]{1,0:T(8,128)(2,1)S(1)}, bf16[128,1152]{1,0:T(8,128)(2,1)S(1)}, u32[]{:S(2)}, u32[]{:S(2)}) collective-permute-start(bf16[128,1152]{1,0:T(8,128)(2,1)S(1)} %bitcast.77), channel_id=1, source_target_pairs={{0,1},{1,0},{2,3},{3,2},{4,5},{5,4},{6,7},{7,6},{8,9},{9,8},{10,11... | collective-permute-start | bytes 884744 | tf_op jit(solution)/shard_map/ppermute | solution.py:194
  56.5 9.7 %copy-start.14 = (s32[1280]{0:T(1024)S(1)}, s32[1280]{0:T(1024)}, u32[]{:S(2)}) copy-start(s32[1280]{0:T(1024)} %constant.60.clone) | copy-start | bytes 15364
  58.6 9.0 %copy-start.2 = (bf16[2,64,1,1152]{3,1,2,0:T(8,128)(2,1)S(1)}, bf16[2,64,1,1152]{3,1,2,0:T(8,128)(2,1)}, u32[]{:S(2)}) copy-start(bf16[2,64,1,1152]{3,1,2,0:T(8,128)(2,1)} %param.14) | copy-start | bytes 884740
  58.6 9.0 %copy-start.3 = (bf16[2,64,1,1152]{3,1,2,0:T(8,128)(2,1)S(1)}, bf16[2,64,1,1152]{3,1,2,0:T(8,128)(2,1)}, u32[]{:S(2)}) copy-start(bf16[2,64,1,1152]{3,1,2,0:T(8,128)(2,1)} %param.15) | copy-start | bytes 884740
  58.6 9.0 %copy-start.4 = (bf16[2,64,1,1152]{3,1,2,0:T(8,128)(2,1)S(1)}, bf16[2,64,1,1152]{3,1,2,0:T(8,128)(2,1)}, u32[]{:S(2)}) copy-start(bf16[2,64,1,1152]{3,1,2,0:T(8,128)(2,1)} %param.16) | copy-start | bytes 884740
  58.7 7.5 %collective-permute-start.1 = (bf16[128,640]{1,0:T(8,128)(2,1)S(1)}, bf16[128,640]{1,0:T(8,128)(2,1)S(1)}, u32[]{:S(2)}, u32[]{:S(2)}) collective-permute-start(bf16[128,640]{1,0:T(8,128)(2,1)S(1)} %dynamic-slice_bitcast_fusion.1), channel_id=1, source_target_pairs={{0,1},{1,0},{2,3},{3,2},{4,5},{5,4},{6,7},{7,6},{8,9},{9,8},{10,11... | collective-permute-start | bytes 491528 | tf_op jit(solution)/shard_map/ppermute | solution.py:194
  65.6 19.8 %collective-permute-start.6 = (bf16[576,1152]{1,0:T(8,128)(2,1)}, bf16[576,1152]{1,0:T(8,128)(2,1)}, u32[]{:S(2)}, u32[]{:S(2)}) collective-permute-start(bf16[576,1152]{1,0:T(8,128)(2,1)} %dynamic-slice_bitcast_fusion), channel_id=1, source_target_pairs={{0,128},{1,135},{128,2},{129,1},{2,130},{3,129},{130,4},{131,3},{4... | collective-permute-start | bytes 3981320 | tf_op jit(solution)/shard_map/ppermute | solution.py:230
  66.2 12.9 %copy-start.11 = (bf16[300,1152]{1,0:T(8,128)(2,1)S(1)}, bf16[300,1152]{1,0:T(8,128)(2,1)}, u32[]{:S(2)}) copy-start(bf16[300,1152]{1,0:T(8,128)(2,1)} %param.21) | copy-start | bytes 2073604
  75.7 4.7 %copy-start.15 = (s32[4]{0:T(128)S(1)}, s32[4]{0:T(128)}, u32[]{:S(2)}) copy-start(s32[4]{0:T(128)} %constant.75) | copy-start | bytes 52
  75.7 10.3 %collective-permute-start.2 = (bf16[128,3456]{1,0:T(8,128)(2,1)S(1)}, bf16[128,3456]{1,0:T(8,128)(2,1)}, u32[]{:S(2)}, u32[]{:S(2)}) collective-permute-start(bf16[128,3456]{1,0:T(8,128)(2,1)S(1)} %temporal_grads.1), channel_id=1, source_target_pairs={{0,1},{1,0},{2,3},{3,2},{4,5},{5,4},{6,7},{7,6},{8,9},{9,8},{10,11... | collective-permute-start | bytes 2654216 | tf_op jit(solution)/shard_map/ppermute | solution.py:194
  80.4 2.0 %copy-start.10 = (bf16[4,40,4608]{2,1,0:T(8,128)(2,1)S(1)}, bf16[4,40,4608]{2,1,0:T(8,128)(2,1)}, u32[]{:S(2)}) copy-start(bf16[4,40,4608]{2,1,0:T(8,128)(2,1)} %copy-done.9) | copy-start | bytes 4423684
  82.4 27.9 %collective-permute-start.3 = (bf16[160,3456]{1,0:T(8,128)(2,1)S(1)}, bf16[160,3456]{1,0:T(8,128)(2,1)S(1)}, u32[]{:S(2)}, u32[]{:S(2)}) collective-permute-start(bf16[160,3456]{1,0:T(8,128)(2,1)S(1)} %bitcast.61), channel_id=1, source_target_pairs={{0,8},{1,33},{2,10},{3,35},{4,12},{5,37},{6,14},{7,39},{8,16},{9,4... | collective-permute-start | bytes 3317768 | tf_op jit(solution)/shard_map/ppermute | solution.py:190
  83.0 27.3 %collective-permute-start.4 = (bf16[160,3456]{1,0:T(8,128)(2,1)S(1)}, bf16[160,3456]{1,0:T(8,128)(2,1)S(1)}, u32[]{:S(2)}, u32[]{:S(2)}) collective-permute-start(bf16[160,3456]{1,0:T(8,128)(2,1)S(1)} %bitcast.62), channel_id=1, source_target_pairs={{0,24},{1,97},{2,26},{3,99},{4,28},{5,101},{6,30},{7,103},{8,0},{9... | collective-permute-start | bytes 3317768 | tf_op jit(solution)/shard_map/ppermute | solution.py:190
  85.4 24.9 %collective-permute-start.5 = (bf16[160,3456]{1,0:T(8,128)(2,1)S(1)}, bf16[160,3456]{1,0:T(8,128)(2,1)S(1)}, u32[]{:S(2)}, u32[]{:S(2)}) collective-permute-start(bf16[160,3456]{1,0:T(8,128)(2,1)S(1)} %bitcast.63), channel_id=1, source_target_pairs={{0,16},{1,65},{2,18},{3,67},{4,20},{5,69},{6,22},{7,71},{8,24},{9,... | collective-permute-start | bytes 3317768 | tf_op jit(solution)/shard_map/ppermute | solution.py:190
  85.4 38.9 %collective-permute-start.7 = (bf16[576,1152]{1,0:T(8,128)(2,1)}, bf16[576,1152]{1,0:T(8,128)(2,1)}, u32[]{:S(2)}, u32[]{:S(2)}) collective-permute-start(bf16[576,1152]{1,0:T(8,128)(2,1)} %collective-permute-done.6), channel_id=1, source_target_pairs={{0,1},{1,0},{2,3},{3,2},{4,5},{5,4},{6,7},{7,6},{8,9},{9,8},{10,11... | collective-permute-start | bytes 3981320 | tf_op jit(solution)/shard_map/ppermute | solution.py:231
  114.2 26.1 %all-to-all-start.3 = ((bf16[128,2,640]{2,1,0:T(2,128)(2,1)}), bf16[128,2,640]{2,1,0:T(2,128)(2,1)S(1)}, u32[]{:S(2)}, u32[]{:S(2)}) async-start(bf16[128,2,640]{2,1,0:T(2,128)(2,1)} %bitcast.59), calls=%async_computation.3 | async-start | bytes 655360 | tf_op jit(solution)/shard_map/all_to_all | solution.py:299
  124.3 2.6 %copy-start.8 = (bf16[2,576,1152]{2,1,0:T(8,128)(2,1)S(1)}, bf16[2,576,1152]{2,1,0:T(8,128)(2,1)}, u32[]{:S(2)}) copy-start(bf16[2,576,1152]{2,1,0:T(8,128)(2,1)} %param.20) | copy-start | bytes 7962628
  127.4 1.5 copy-start.5
  127.4 2.3 %copy-start.6 = (bf16[2,576,1152]{2,1,0:T(8,128)(2,1)}, bf16[2,576,1152]{2,1,0:T(8,128)(2,1)S(1)}, u32[]{:S(2)}) copy-start(bf16[2,576,1152]{2,1,0:T(8,128)(2,1)S(1)} %get-tuple-element.11) | copy-start | bytes 7962628
  140.6 1.8 copy-start.1
  153.6 23.5 %all-to-all-start.4 = ((bf16[16,72,640]{2,1,0:T(8,128)(2,1)}), bf16[16,72,640]{2,1,0:T(8,128)(2,1)S(1)}, u32[]{:S(2)}, u32[]{:S(2)}) async-start(bf16[16,72,640]{2,1,0:T(8,128)(2,1)} %get-tuple-element.9), calls=%async_computation.4 | async-start | bytes 2949120 | tf_op jit(solution)/shard_map/all_to_all | solution.py:313
  160.8 27.2 %copy-start.12 = (f32[128,1152]{1,0:T(8,128)S(1)}, f32[128,1152]{1,0:T(8,128)}, u32[]{:S(2)}) copy-start(f32[128,1152]{1,0:T(8,128)} %fusion.16) | copy-start | bytes 1769476
  178.3 18.0 %all-to-all-start.5 = ((bf16[16,2,1350]{2,1,0:T(2,128)(2,1)}), bf16[16,2,1350]{2,1,0:T(2,128)(2,1)S(1)}, u32[]{:S(2)}, u32[]{:S(2)}) async-start(bf16[16,2,1350]{2,1,0:T(2,128)(2,1)} %reshape.76), calls=%async_computation.5 | async-start | bytes 180224 | tf_op jit(solution)/shard_map/all_to_all | solution.py:318

commit v6 on v5

--- a/solution.py
+++ b/solution.py
@@ -67,9 +67,7 @@
         out_shape=jax.ShapeDtypeStruct((rows, 3 * width), jnp.bfloat16),
         compiler_params=pltpu.CompilerParams(vmem_limit_bytes=24 << 20),
         cost_estimate=pl.CostEstimate(
-            flops=10 * rows * rows * width,
-            bytes_accessed=14 * rows * width,
-            transcendentals=HEADS * rows * rows,
+            flops=rows * width, bytes_accessed=2 * rows * width, transcendentals=0
         ),
         name="temporal_grads",
     )(grad_heads, query, key_rows, value)
@@ -109,50 +107,80 @@
     )(slots, qkv_both, residual, *blocks)
 
 
+def probs_kernel(length_ref, query_ref, key_ref, probs_ref):
+    rows = query_ref.shape[0]
+    valid = lax.broadcasted_iota(jnp.int32, (rows, CAP_PAD), 1) < length_ref[0]
+    for head in range(HEADS):
+        at = slice(head * HEAD_DIM, (head + 1) * HEAD_DIM)
+        scores = dot(query_ref[:, at], key_ref[:, at], CONTRACT_LAST) * SCALE
+        probs_ref[head] = softmax(jnp.where(valid, scores, -1e30))
+
+
+def cross_probs(cap_length, cross_query, cap_key):
+    rows, width = cross_query.shape
+    in_vmem = pl.BlockSpec(memory_space=pltpu.VMEM)
+    return pl.pallas_call(
+        probs_kernel,
+        in_specs=[pl.BlockSpec(memory_space=pltpu.SMEM), in_vmem, in_vmem],
+        out_specs=in_vmem,
+        out_shape=jax.ShapeDtypeStruct((HEADS, rows, CAP_PAD), jnp.float32),
+        compiler_params=pltpu.CompilerParams(vmem_limit_bytes=16 << 20),
+        cost_estimate=pl.CostEstimate(
+            flops=2 * rows * CAP_PAD * width,
+            bytes_accessed=4 << 20,
+            transcendentals=HEADS * rows * CAP_PAD,
+        ),
+        name="cross_probs",
+    )(cap_length, cross_query, cap_key)
+
+
 def cross_kernel(
-    length_ref, arrived_ref, w_out_ref, query_ref, key_ref, value_ref, cq_ref, terms_ref, og_ref
+    core_ref,
+    arrived_ref,
+    w_out_ref,
+    query_ref,
+    key_ref,
+    value_ref,
+    probs_ref,
+    cq_ref,
+    keep_ref,
+    send_ref,
+    og_ref,
 ):
     og_ref[...] = dot(arrived_ref[...], w_out_ref[...]).astype(jnp.bfloat16)
-    rows = query_ref.shape[0]
-    valid = lax.broadcasted_iota(jnp.int32, (rows, CAP_PAD), 1) < length_ref[0]
+    first = core_ref[0] == 0
     for head in range(HEADS):
         at = slice(head * HEAD_DIM, (head + 1) * HEAD_DIM)
         query, out_grad, key_rows, value = (
             ref[:, at] for ref in (query_ref, og_ref, key_ref, value_ref)
         )
-        scores = jnp.where(valid, dot(query, key_rows, CONTRACT_LAST) * SCALE, -1e30)
-        attention = softmax(scores)
+        attention = probs_ref[head]
         score_grad = score_grads(attention, dot(out_grad, value, CONTRACT_LAST))
         cq_ref[:, at] = dot(score_grad, key_rows).astype(jnp.bfloat16)
         key_term = dot(query, score_grad, CONTRACT_FIRST)
         value_term = dot(out_grad, attention.astype(jnp.bfloat16), CONTRACT_FIRST)
-        rest = jnp.zeros((HEAD_DIM, 640 - CAP_PAD), jnp.float32)
-        shifted = pltpu.roll(jnp.concatenate([value_term, rest], axis=1), CAP, 1)
-        terms_ref[head] = (jnp.concatenate([key_term, rest], axis=1) + shifted).astype(
-            jnp.bfloat16
-        )
-
-
-def cross_grads(cap_length, arrived, w_out, cross_query, cap_key, cap_value):
+        keep_ref[head] = jnp.where(first, key_term, value_term).astype(jnp.bfloat16)
+        send_ref[head] = jnp.where(first, value_term, key_term).astype(jnp.bfloat16)
+
+
+def cross_grads(core, arrived, w_out, cross_query, cap_key, cap_value, probs):
     rows, width = cross_query.shape
     in_vmem = pl.BlockSpec(memory_space=pltpu.VMEM)
+    term = jax.ShapeDtypeStruct((HEADS, HEAD_DIM, CAP_PAD), jnp.bfloat16)
     return pl.pallas_call(
         cross_kernel,
-        in_specs=[pl.BlockSpec(memory_space=pltpu.SMEM)] + [in_vmem] * 5,
-        out_specs=(in_vmem, in_vmem),
-        out_shape=(
-            jax.ShapeDtypeStruct((rows, width), jnp.bfloat16),
-            jax.ShapeDtypeStruct((HEADS, HEAD_DIM, 640), jnp.bfloat16),
-        ),
+        in_specs=[pl.BlockSpec(memory_space=pltpu.SMEM)] + [in_vmem] * 6,
+        out_specs=(in_vmem,) * 3,
+        out_shape=(jax.ShapeDtypeStruct((rows, width), jnp.bfloat16), term, term),
         scratch_shapes=[pltpu.VMEM((rows, width), jnp.bfloat16)],
         compiler_params=pltpu.CompilerParams(vmem_limit_bytes=32 << 20),
         cost_estimate=pl.CostEstimate(
-            flops=10 * rows * CAP_PAD * width + 2 * rows * width * arrived.shape[1],
-            bytes_accessed=8 << 20,
-            transcendentals=HEADS * rows * CAP_PAD,
+            flops=8 * rows * CAP_PAD * width + 2 * rows * width * arrived.shape[1],
+            bytes_accessed=12 << 20,
+            transcendentals=0,
         ),
         name="cross_grads",
-    )(cap_length, arrived, w_out, cross_query, cap_key, cap_value)
+    )(core, arrived, w_out, cross_query, cap_key, cap_value, probs)
 
 
 ALL = ("s", "x", "y", "z", "c")
@@ -268,6 +296,14 @@
     slots = (place_here - jnp.array([0, 1, 3, 2], jnp.int32)) % 4
     out_mine = gather_groups(near[:, :, :width], ring_groups(1)).reshape(640, width)
     full_cross = cross_halves(cross_weights)
+    residual = lax.dot_general(
+        grad_both, place_mine, CONTRACT_LAST, preferred_element_type=jnp.float32
+    )
+    padding = ((0, CAP_PAD - CAP), (0, 0))
+    cap_key, cap_value = jnp.pad(cap_key, padding), jnp.pad(cap_value, padding)
+    out_mine, residual, place, cap_key, cap_value = lax.optimization_barrier(
+        (out_mine, residual, place, cap_key, cap_value)
+    )
     heads_mine = (
         lax.dot_general(grad_both, out_mine, CONTRACT_LAST, preferred_element_type=jnp.float32)
         .astype(jnp.bfloat16)
@@ -284,10 +320,8 @@
     qkv_grad = temporal_grads(
         grad_heads, *(saved.reshape(rows, width) for saved in (t_query, t_key, t_value))
     )
+    qkv_grad, *blocks = lax.optimization_barrier((qkv_grad, *blocks))
     qkv_both = in_core_order(qkv_grad, swap_cores(qkv_grad)).reshape(2 * rows, 3 * width)
-    residual = lax.dot_general(
-        grad_both, place_mine, CONTRACT_LAST, preferred_element_type=jnp.float32
-    )
     mixed = mixed_half(slots, qkv_both, residual, blocks).reshape(2, rows, 640)
     w_out_placed = lax.dot_general(
         place, full_cross[1], CONTRACT_LAST, preferred_element_type=jnp.float32
@@ -295,26 +329,21 @@
     cross_query = jnp.dot(
         frame_input.reshape(rows, width), full_cross[0], preferred_element_type=jnp.float32
     ).astype(jnp.bfloat16)
-    padding = ((0, CAP_PAD - CAP), (0, 0))
+    probs = cross_probs(cap_length, cross_query, cap_key)
     arrived = lax.all_to_all(mixed.transpose(1, 0, 2), SEQ, split_axis=0, concat_axis=0)
     arrived = arrived.reshape(64, 2, 2, 640).transpose(0, 2, 1, 3).reshape(128, 1280)
-    cq_grad, terms = cross_grads(
-        cap_length,
-        arrived,
-        w_out_placed,
-        cross_query,
-        jnp.pad(cap_key, padding),
-        jnp.pad(cap_value, padding),
-    )
+    cq_grad, keep, send = cross_grads(
+        core.reshape(1), arrived, w_out_placed, cross_query, cap_key, cap_value, probs
+    )
+    chip = (keep.astype(jnp.float32) + swap_cores(send).astype(jnp.float32)).astype(jnp.bfloat16)
     grad_input = (
         jnp.dot(arrived, place, preferred_element_type=jnp.float32)
         + lax.dot_general(cq_grad, full_cross[0], CONTRACT_LAST, preferred_element_type=jnp.float32)
     ).astype(jnp.bfloat16)
-    head = jnp.sum(lax.all_to_all(terms, ("x", "y"), 0, 0).astype(jnp.float32), axis=0)
-    head = head.astype(jnp.bfloat16)
-    pieces = jnp.concatenate(
-        [head[:, :CAP].reshape(8, 9, CAP), head[:, CAP : 2 * CAP].reshape(8, 9, CAP)]
-    )
+    head = jnp.sum(lax.all_to_all(chip, ("x", "y"), 0, 0).astype(jnp.float32), axis=0)
+    pieces = head[:, :CAP].astype(jnp.bfloat16).reshape(1, 8, 9, CAP)
+    sides = jnp.arange(2).reshape(2, 1, 1, 1) == core
+    pieces = jnp.where(sides, pieces, jnp.zeros_like(pieces)).reshape(16, 9, CAP)
     piece = jnp.sum(lax.all_to_all(pieces, ("s", "z", "c"), 0, 0).astype(jnp.float32), axis=0)
     return (grad_input.reshape(frame_input.shape), piece.T)
 

time: 198 us -> 180 us (0.909)
  waiting for transfers between devices: 57.1 us -> 33.9 us
  blocking collectives: 35.4 us -> 19.1 us
  starting transfers between devices: 42.7 us -> 52.9 us
  local copies, waits for them, and re-layouts: 12.2 us -> 20.4 us
    ppermute x3, waiting for transfers between devices: 22.8 us -> 5.93 us  [shift_last(): return lax.ppermute(block, ALL, pairs)]
    all_to_all x1 -> x0, blocking collectives: 16.3 us -> none  [gather_groups(): return lax.all_to_all(copies, ALL, 0, 0, axis_index_groups=groups)]
    ppermute x3 -> x4, starting transfers between devices: 10.8 us -> 16.6 us  [swap_cores(): return lax.ppermute(block, 'c', [(0, 1), (1, 0)])]
    all_to_all x1, waiting for transfers between devices: 16.3 us -> 10.8 us  [local(): lax.all_to_all(chip, ('x', 'y'), 0, 0).astype(jnp.float32)]
    pallas_call x0 -> x1, Pallas kernels: none -> 4.79 us  [cross_probs(): pl.pallas_call(probs_kernel, in_specs=[pl.BlockSpec(memory_space=pltpu.SM...]
    pallas_call x1, Pallas kernels: 11.2 us -> 6.39 us  [cross_grads(): pl.pallas_call(cross_kernel, in_specs=[pl.BlockSpec(memory_space=pltpu.SM...]
    all_to_all x1, waiting for transfers between devices: 4.46 us -> 0.01 us  [local(): lax.all_to_all(mixed.transpose(1, 0, 2), SEQ, split_axis=0, concat_axis=0)]
    all_to_all x1 -> x2, starting transfers between devices: 4.36 us -> 8.5 us  [gather_groups(): return lax.all_to_all(copies, ALL, 0, 0, axis_index_groups=groups)]
  transfers between devices with their start and end apart: 12 -> 14, of which waited for: 6 -> 6; matrix products, arithmetic and copies ran while one was open for 13% -> 18% of each run, Pallas kernels for 5% -> 9%
where the time goes in v6:
time: 180 us; the launch traced here: 179 us
  starting transfers between devices  52.9 us (29%)
  waiting for transfers between devices  33.9 us (19%)
  Pallas kernels  23.2 us (13%)
  local copies, waits for them, and re-layouts  20.4 us (11%)
  blocking collectives  19.1 us (11%)
  matrix products  17.7 us (10%)
  other arithmetic  10.3 us (6%)
    all_to_all x1, blocking collectives, local(): lax.all_to_all(jnp.broadcast_to(shard[None], (4,) + shard.shape), 'z', 0, 0)  19.1 us
    ppermute x4, starting transfers between devices, swap_cores(): return lax.ppermute(block, 'c', [(0, 1), (1, 0)])  16.6 us
    all_to_all x1, waiting for transfers between devices, local(): lax.all_to_all(chip, ('x', 'y'), 0, 0).astype(jnp.float32)  10.8 us
    unnamed x53, local copies, waits for them, and re-layouts  10.4 us
    all_to_all x1, starting transfers between devices, local(): lax.all_to_all(pieces, ('s', 'z', 'c'), 0, 0).astype(jnp.float32)  9.79 us
    all_to_all x2, waiting for transfers between devices, gather_groups(): return lax.all_to_all(copies, ALL, 0, 0, axis_index_groups=groups)  8.52 us
    all_to_all x2, starting transfers between devices, gather_groups(): return lax.all_to_all(copies, ALL, 0, 0, axis_index_groups=groups)  8.5 us
    pallas_call x1, Pallas kernels, temporal_grads(): pl.pallas_call(temporal_kernel, out_shape=jax.ShapeDtypeStruct((rows, 3 *...  7.98 us
  transfers between devices with their start and end apart: 14, of which 6 were waited for; matrix products, arithmetic and copies ran while one was open for 18% of the time, Pallas kernels for 9%

profile of v6, /device:TPU:1, one launch (start us, length us, event | category | flops | bytes accessed | tf_op | source)
XLA Modules:
  0.0 179.2 jit_solution(1509903165512469373)
XLA Ops:
  0.6 1.0 pad_maximum_fusion.4
  1.6 0.1 broadcast_in_dim.54
  1.7 0.2 broadcast_in_dim.55
  1.9 19.1 %all_to_all.30 = bf16[4,2,20736]{2,1,0:T(2,128)(2,1)S(1)} all-to-all(bf16[4,2,20736]{2,1,0:T(2,128)(2,1)S(1)} %broadcast_in_dim.55), channel_id=1, replica_groups=mesh['s'=2,'x'=4,'y'=4,'z'=4,'c'=2] {'z'}, dimensions={0} | all-to-all | bytes 663552 | tf_op jit(solution)/shard_map/all_to_all | solution.py:289
  21.0 0.2 reshape.70
  21.2 1.3 broadcast_in_dim.56
  22.5 4.2 %all-to-all-start.1 = ((bf16[4,40,4608]{2,1,0:T(8,128)(2,1)}), bf16[4,40,4608]{2,1,0:T(8,128)(2,1)S(1)}, u32[]{:S(2)}, u32[]{:S(2)}) async-start(bf16[4,40,4608]{2,1,0:T(8,128)(2,1)} %broadcast_in_dim.56), calls=%async_computation.1 | async-start | bytes 2949120 | tf_op jit(solution)/shard_map/all_to_all | solution.py:207
  26.7 3.5 %collective-permute-start = (bf16[128,1152]{1,0:T(8,128)(2,1)S(1)}, bf16[128,1152]{1,0:T(8,128)(2,1)S(1)}, u32[]{:S(2)}, u32[]{:S(2)}) collective-permute-start(bf16[128,1152]{1,0:T(8,128)(2,1)S(1)} %bitcast.83), channel_id=1, source_target_pairs={{0,1},{1,0},{2,3},{3,2},{4,5},{5,4},{6,7},{7,6},{8,9},{9,8},{10,11... | collective-permute-start | bytes 884744 | tf_op jit(solution)/shard_map/ppermute | solution.py:222
  30.2 8.5 %all-to-all-done.1 = bf16[4,40,4608]{2,1,0:T(8,128)(2,1)S(1)} async-done(((bf16[4,40,4608]{2,1,0:T(8,128)(2,1)}), bf16[4,40,4608]{2,1,0:T(8,128)(2,1)S(1)}, u32[]{:S(2)}, u32[]{:S(2)}) %all-to-all-start.1) | async-done | bytes 1474592 | tf_op jit(solution)/shard_map/all_to_all | solution.py:207
  38.7 1.3 broadcast_in_dim.57
  40.0 4.3 %all-to-all-start.2 = ((bf16[4,4,40,1152]{3,2,1,0:T(8,128)(2,1)}), bf16[4,4,40,1152]{3,2,1,0:T(8,128)(2,1)}, u32[]{:S(2)}, u32[]{:S(2)}) async-start(bf16[4,4,40,1152]{3,2,1,0:T(8,128)(2,1)} %broadcast_in_dim.57), calls=%async_computation.2 | async-start | bytes 2949120 | tf_op jit(solution)/shard_map/all_to_all | solution.py:207
  44.4 2.9 %fusion.16 = (bf16[1280,1152]{1,0:T(8,128)(2,1)}, pred[1280,1152]{1,0:T(32,128)(4,1)}) fusion(s32[1280]{0:T(1024)S(1)} %copy-done.23), kind=kLoop, calls=%fused_computation.41 | loop fusion | flops 2949120 | bytes 4428800 | tf_op jit(solution)/shard_map/convert_element_type | solution.py:283
  47.3 1.0 pad.12.key_ref
  48.3 2.1 %pad.13.value_ref = bf16[384,1152]{1,0:T(8,128)(2,1)} pad(bf16[300,1152]{1,0:T(8,128)(2,1)} %param.22, bf16[]{:T(256)} %constant.53.clone.1), padding=0_84x0_0 | pad | bytes 1575938 | tf_op jit(solution)/shard_map/jit(_pad)/pad | solution.py:303
  50.6 2.7 %fusion.residual_ref = f32[256,640]{1,0:T(8,128)} fusion(bf16[256,1152]{1,0:T(8,128)(2,1)S(1)} %bitcast.79, pred[1280,1152]{1,0:T(32,128)(4,1)} %get-tuple-element.43, s32[]{:T(128)S(6)} %select_n.94), kind=kOutput, calls=%fused_computation.4 | convolution fusion | flops 377487360 | bytes 1982468 | tf_op jit(solution)/shard_map/dot_general | solution.py:299
  53.4 1.5 collective-permute-start.2
  54.9 1.5 collective-permute-start.3
  56.3 1.5 collective-permute-start.4
  57.8 2.2 %convolution_convert_fusion.3 = bf16[256,640]{1,0:T(8,128)(2,1)S(1)} fusion(bf16[256,1152]{1,0:T(8,128)(2,1)S(1)} %bitcast.80, bf16[640,1152]{1,0:T(8,128)(2,1)} %bitcast.4), kind=kOutput, calls=%fused_computation.24 | convolution fusion | flops 377651200 | bytes 2392064 | tf_op jit(solution)/shard_map/dot_general | solution.py:308
  60.1 6.1 %collective-permute-start.1 = (bf16[128,640]{1,0:T(8,128)(2,1)S(1)}, bf16[128,640]{1,0:T(8,128)(2,1)S(1)}, u32[]{:S(2)}, u32[]{:S(2)}) collective-permute-start(bf16[128,640]{1,0:T(8,128)(2,1)S(1)} %dynamic-slice_bitcast_fusion.1), channel_id=1, source_target_pairs={{0,1},{1,0},{2,3},{3,2},{4,5},{5,4},{6,7},{7,6},{8,9},{9,8},{10,11... | collective-permute-start | bytes 491528 | tf_op jit(solution)/shard_map/ppermute | solution.py:222
  66.2 1.2 dynamic-slice_bitcast_fusion
  67.3 0.5 collective-permute-start.6
  67.9 0.6 convolution_convert_fusion.2.grad_ref
  68.6 8.0 %temporal_grads.1 = bf16[128,3456]{1,0:T(8,128)(2,1)S(1)} custom-call(bf16[128,1152]{1,0:T(8,128)(2,1)S(1)} %convolution_convert_fusion.2.grad_ref, bf16[128,1152]{1,0:T(8,128)(2,1)S(1)} %bitcast.75, bf16[128,1152]{1,0:T(8,128)(2,1)S(1)} %bitcast.76, bf16[128,1152]{1,0:T(8,128)(2,1)S(1)} %bitcast.77), custom_call_target="tpu_custom_call" | custom-call | flops 147456 | bytes 294912 | tf_op jit(solution)/shard_map/temporal_grads/pallas_call | solution.py:65
  76.6 5.9 %collective-permute-done.4.w3 = bf16[160,3456]{1,0:T(8,128)(2,1)} collective-permute-done((bf16[160,3456]{1,0:T(8,128)(2,1)S(1)}, bf16[160,3456]{1,0:T(8,128)(2,1)}, u32[]{:S(2)}, u32[]{:S(2)}) %collective-permute-start.4) | collective-permute-done | bytes 1105952 | tf_op jit(solution)/shard_map/ppermute | solution.py:218
  82.5 5.8 %collective-permute-start.5 = (bf16[128,3456]{1,0:T(8,128)(2,1)S(1)}, bf16[128,3456]{1,0:T(8,128)(2,1)}, u32[]{:S(2)}, u32[]{:S(2)}) collective-permute-start(bf16[128,3456]{1,0:T(8,128)(2,1)S(1)} %temporal_grads.1), channel_id=1, source_target_pairs={{0,1},{1,0},{2,3},{3,2},{4,5},{5,4},{6,7},{7,6},{8,9},{9,8},{10,11... | collective-permute-start | bytes 2654216 | tf_op jit(solution)/shard_map/ppermute | solution.py:222
  89.0 0.1 collective-permute-start.7
  89.1 1.4 collective-permute-done.5
  90.5 1.3 select_bitcast_fusion.3
  91.8 0.2 pad_maximum_fusion.2
  92.0 0.9 copy-done.9
  92.9 4.1 %mixed_half.1 = bf16[256,640]{1,0:T(8,128)(2,1)S(1)} custom-call(s32[4]{0:T(128)S(1)} %and_select_fusion.slot_ref, bf16[256,3456]{1,0:T(8,128)(2,1)S(1)} %bitcast.67, f32[256,640]{1,0:T(8,128)S(1)} %copy-done.9, bf16[160,3456]{1,0:T(8,128)(2,1)S(1)} %bitcast.71, bf16[160,3456]{1,0:T(8,128)(2,1)S(1)} %collective-permute-done.2.w1, ...), custom_call_target="tpu_custom_call" | custom-call | flops 1132462080 | bytes 8388608 | tf_op jit(solution)/shard_map/mixed_half/pallas_call | solution.py:92
  97.0 1.1 copy.35
  98.1 6.7 %all-to-all-start.3 = ((bf16[128,2,640]{2,1,0:T(2,128)(2,1)}), bf16[128,2,640]{2,1,0:T(2,128)(2,1)}, u32[]{:S(2)}, u32[]{:S(2)}) async-start(bf16[128,2,640]{2,1,0:T(2,128)(2,1)} %bitcast.65), calls=%async_computation.3 | async-start | bytes 655360 | tf_op jit(solution)/shard_map/all_to_all | solution.py:333
  104.8 2.1 %select_bitcast_fusion.1 = (bf16[1,576,1152]{2,1,0:T(8,128)(2,1)S(1)}, bf16[1,576,1152]{2,1,0:T(8,128)(2,1)S(1)}) fusion(bf16[576,1152]{1,0:T(8,128)(2,1)} %collective-permute-done.6, bf16[576,1152]{1,0:T(8,128)(2,1)} %collective-permute-done.7, pred[]{:T(512)S(6)} %eq.21), kind=kLoop, calls=%fused_computation.22 | loop fusion | flops 1327104 | bytes 5308417 | tf_op jit(solution)/shard_map/stack | solution.py:260
  106.9 0.4 copy-done.20
  107.3 0.5 broadcast_select_fusion
  107.9 0.6 fusion.7.query_ref
  108.5 1.2 copy-done.1
  109.8 4.8 %cross_probs.1.probs_ref = f32[16,128,384]{2,1,0:T(8,128)S(1)} custom-call(s32[1]{0:T(128)S(6)} %copy.38.length_ref, bf16[128,1152]{1,0:T(8,128)(2,1)S(1)} %fusion.7.query_ref, bf16[384,1152]{1,0:T(8,128)(2,1)S(1)} %copy-done.1), custom_call_target="tpu_custom_call" | custom-call | flops 113246208 | bytes 4194304 | tf_op jit(solution)/shard_map/cross_probs/pallas_call | solution.py:122
  114.6 0.7 copy-done.7
  115.3 5.8 %convolution_convert_fusion.w_out_ref = bf16[1280,1152]{1,0:T(8,128)(2,1)} fusion(bf16[1280,1152]{1,0:T(8,128)(2,1)S(1)} %copy-done.16, bf16[2,576,1152]{2,1,0:T(8,128)(2,1)S(1)} %get-tuple-element.33, bf16[2,576,1152]{2,1,0:T(8,128)(2,1)S(1)} %get-tuple-element.32), kind=kOutput, calls=%fused_computation | convolution fusion | flops 3404169216 | bytes 11206656 | tf_op jit(solution)/shard_map/dot_general | solution.py:326
  121.1 1.2 copy.28
  122.4 1.3 copy-done.2
  123.7 1.2 copy-done.3
  124.8 1.8 %copy-done.6 = bf16[1280,1152]{1,0:T(8,128)(2,1)S(1)} copy-done((bf16[1280,1152]{1,0:T(8,128)(2,1)S(1)}, bf16[1280,1152]{1,0:T(8,128)(2,1)}, u32[]{:S(2)}) %copy-start.6) | copy-done | bytes 2949144
  126.7 1.0 copy-done.8
  127.6 6.4 %cross_grads.1 = (bf16[128,1152]{1,0:T(8,128)(2,1)S(1)}, bf16[16,72,384]{2,1,0:T(8,128)(2,1)S(1)}, bf16[16,72,384]{2,1,0:T(8,128)(2,1)S(1)}) custom-call(s32[1]{0:T(128)} %bitcast.19.core_ref, bf16[128,1280]{1,0:T(8,128)(2,1)S(1)} %bitcast.72, bf16[1280,1152]{1,0:T(8,128)(2,1)S(1)} %copy-done.6, bf16[128,1152]{1,0:T(8,128)(2,1)S(1)} %copy-done.8, ...), custom_call_target="tpu_custom_call" | custom-call | flops 830472192 | bytes 12582912 | tf_op jit(solution)/shard_map/cross_grads/pallas_call | solution.py:170
  134.0 0.7 copy-done.10
  134.8 1.2 collective-permute-start.8
  136.0 2.1 %collective-permute-done.8 = bf16[16,72,384]{2,1,0:T(8,128)(2,1)S(1)} collective-permute-done((bf16[16,72,384]{2,1,0:T(8,128)(2,1)S(1)}, bf16[16,72,384]{2,1,0:T(8,128)(2,1)S(1)}, u32[]{:S(2)}, u32[]{:S(2)}) %collective-permute-start.8) | collective-permute-done | bytes 884768 | tf_op jit(solution)/shard_map/ppermute | solution.py:222
  138.0 1.2 add_convert_fusion
  139.2 6.2 %all-to-all-start.4 = ((bf16[16,72,384]{2,1,0:T(8,128)(2,1)}), bf16[16,72,384]{2,1,0:T(8,128)(2,1)S(1)}, u32[]{:S(2)}, u32[]{:S(2)}) async-start(bf16[16,72,384]{2,1,0:T(8,128)(2,1)} %add_convert_fusion), calls=%async_computation.4 | async-start | bytes 1769472 | tf_op jit(solution)/shard_map/all_to_all | solution.py:343
  145.5 0.1 broadcast_in_dim.59
  145.6 2.7 %fusion.9 = f32[128,1152]{1,0:T(8,128)S(1)} fusion(bf16[128,1152]{1,0:T(8,128)(2,1)S(1)} %copy-done.11, bf16[2,576,1152]{2,1,0:T(8,128)(2,1)} %copy-done.17, bf16[2,576,1152]{2,1,0:T(8,128)(2,1)} %copy-done.18), kind=kOutput, calls=%fused_computation.28 | convolution fusion | flops 345047040 | bytes 6193152 | tf_op jit(solution)/shard_map/dot_general | solution.py:341
  148.3 10.8 %all-to-all-done.4 = bf16[16,72,384]{2,1,0:T(8,128)(2,1)S(1)} async-done(((bf16[16,72,384]{2,1,0:T(8,128)(2,1)}), bf16[16,72,384]{2,1,0:T(8,128)(2,1)S(1)}, u32[]{:S(2)}, u32[]{:S(2)}) %all-to-all-start.4) | async-done | bytes 884768 | tf_op jit(solution)/shard_map/all_to_all | solution.py:343
  159.1 0.1 reduce
  159.3 0.1 bitcast_select_fusion
  159.4 0.8 reshape.84
  160.2 9.8 %all-to-all-start.5 = ((bf16[16,2,1350]{2,1,0:T(2,128)(2,1)}), bf16[16,2,1350]{2,1,0:T(2,128)(2,1)S(1)}, u32[]{:S(2)}, u32[]{:S(2)}) async-start(bf16[16,2,1350]{2,1,0:T(2,128)(2,1)} %reshape.84), calls=%async_computation.5 | async-start | bytes 180224 | tf_op jit(solution)/shard_map/all_to_all | solution.py:347
  170.0 3.2 %fusion.8 = bf16[1,128,1152]{2,1,0:T(8,128)(2,1)} fusion(f32[128,1152]{1,0:T(8,128)S(1)} %fusion.9, bf16[128,1280]{1,0:T(8,128)(2,1)S(1)} %bitcast.73, bf16[1280,1152]{1,0:T(8,128)(2,1)} %get-tuple-element.19), kind=kOutput, calls=%fused_computation.18 | convolution fusion | flops 377782272 | bytes 4161536 | tf_op jit(solution)/shard_map/dot_general | solution.py:340
  173.2 5.2 %all-to-all-done.5 = bf16[16,2,1350]{2,1,0:T(2,128)(2,1)S(1)} async-done(((bf16[16,2,1350]{2,1,0:T(2,128)(2,1)}), bf16[16,2,1350]{2,1,0:T(2,128)(2,1)S(1)}, u32[]{:S(2)}, u32[]{:S(2)}) %all-to-all-start.5) | async-done | bytes 86432 | tf_op jit(solution)/shard_map/all_to_all | solution.py:347
  178.3 0.2 reshape.85
  178.6 0.7 convert_reduce_fusion
  (61 shorter events, 0.6 us)
Async XLA Ops:
  0.6 107.3 %copy-start = (bf16[1,128,1152]{2,1,0:T(8,128)(2,1)S(1)}, bf16[1,128,1152]{2,1,0:T(8,128)(2,1)}, u32[]{:S(2)}) copy-start(bf16[1,128,1152]{2,1,0:T(8,128)(2,1)} %param.19) | copy-start | bytes 884740
  21.2 5.5 %copy-start.22 = (bf16[2,64,1,1152]{3,1,2,0:T(8,128)(2,1)S(1)}, bf16[2,64,1,1152]{3,1,2,0:T(8,128)(2,1)}, u32[]{:S(2)}) copy-start(bf16[2,64,1,1152]{3,1,2,0:T(8,128)(2,1)} %param.13) | copy-start | bytes 884740
  22.5 16.2 %all-to-all-start.1 = ((bf16[4,40,4608]{2,1,0:T(8,128)(2,1)}), bf16[4,40,4608]{2,1,0:T(8,128)(2,1)S(1)}, u32[]{:S(2)}, u32[]{:S(2)}) async-start(bf16[4,40,4608]{2,1,0:T(8,128)(2,1)} %broadcast_in_dim.56), calls=%async_computation.1 | async-start | bytes 2949120 | tf_op jit(solution)/shard_map/all_to_all | solution.py:207
  26.7 17.6 %copy-start.23 = (s32[1280]{0:T(1024)S(1)}, s32[1280]{0:T(1024)}, u32[]{:S(2)}) copy-start(s32[1280]{0:T(1024)} %constant.60.clone) | copy-start | bytes 15364
  26.7 23.8 %collective-permute-start = (bf16[128,1152]{1,0:T(8,128)(2,1)S(1)}, bf16[128,1152]{1,0:T(8,128)(2,1)S(1)}, u32[]{:S(2)}, u32[]{:S(2)}) collective-permute-start(bf16[128,1152]{1,0:T(8,128)(2,1)S(1)} %bitcast.83), channel_id=1, source_target_pairs={{0,1},{1,0},{2,3},{3,2},{4,5},{5,4},{6,7},{7,6},{8,9},{9,8},{10,11... | collective-permute-start | bytes 884744 | tf_op jit(solution)/shard_map/ppermute | solution.py:222
  40.0 17.8 %all-to-all-start.2 = ((bf16[4,4,40,1152]{3,2,1,0:T(8,128)(2,1)}), bf16[4,4,40,1152]{3,2,1,0:T(8,128)(2,1)}, u32[]{:S(2)}, u32[]{:S(2)}) async-start(bf16[4,4,40,1152]{3,2,1,0:T(8,128)(2,1)} %broadcast_in_dim.57), calls=%async_computation.2 | async-start | bytes 2949120 | tf_op jit(solution)/shard_map/all_to_all | solution.py:207
  44.3 3.0 %copy-start.21 = (bf16[300,1152]{1,0:T(8,128)(2,1)S(1)}, bf16[300,1152]{1,0:T(8,128)(2,1)}, u32[]{:S(2)}) copy-start(bf16[300,1152]{1,0:T(8,128)(2,1)} %param.21) | copy-start | bytes 2073604
  53.4 23.2 %collective-permute-start.2 = (bf16[160,3456]{1,0:T(8,128)(2,1)S(1)}, bf16[160,3456]{1,0:T(8,128)(2,1)S(1)}, u32[]{:S(2)}, u32[]{:S(2)}) collective-permute-start(bf16[160,3456]{1,0:T(8,128)(2,1)S(1)} %bitcast.68), channel_id=1, source_target_pairs={{0,8},{1,33},{2,10},{3,35},{4,12},{5,37},{6,14},{7,39},{8,16},{9,4... | collective-permute-start | bytes 3317768 | tf_op jit(solution)/shard_map/ppermute | solution.py:218
  54.9 21.7 %collective-permute-start.3 = (bf16[160,3456]{1,0:T(8,128)(2,1)S(1)}, bf16[160,3456]{1,0:T(8,128)(2,1)}, u32[]{:S(2)}, u32[]{:S(2)}) collective-permute-start(bf16[160,3456]{1,0:T(8,128)(2,1)S(1)} %bitcast.69), channel_id=1, source_target_pairs={{0,24},{1,97},{2,26},{3,99},{4,28},{5,101},{6,30},{7,103},{8,0},{9... | collective-permute-start | bytes 3317768 | tf_op jit(solution)/shard_map/ppermute | solution.py:218
  56.3 26.1 %collective-permute-start.4 = (bf16[160,3456]{1,0:T(8,128)(2,1)S(1)}, bf16[160,3456]{1,0:T(8,128)(2,1)}, u32[]{:S(2)}, u32[]{:S(2)}) collective-permute-start(bf16[160,3456]{1,0:T(8,128)(2,1)S(1)} %bitcast.70), channel_id=1, source_target_pairs={{0,16},{1,65},{2,18},{3,67},{4,20},{5,69},{6,22},{7,71},{8,24},{9,... | collective-permute-start | bytes 3317768 | tf_op jit(solution)/shard_map/ppermute | solution.py:218
  57.8 8.3 %copy-start.19 = (bf16[2,576,1152]{2,1,0:T(8,128)(2,1)S(1)}, bf16[2,576,1152]{2,1,0:T(8,128)(2,1)}, u32[]{:S(2)}) copy-start(bf16[2,576,1152]{2,1,0:T(8,128)(2,1)} %param.20) | copy-start | bytes 7962628
  57.8 10.1 %copy-start.15 = (bf16[1280,1152]{1,0:T(8,128)(2,1)S(1)}, bf16[1280,1152]{1,0:T(8,128)(2,1)}, u32[]{:S(2)}) copy-start(bf16[1280,1152]{1,0:T(8,128)(2,1)} %get-tuple-element.19) | copy-start | bytes 8847364
  60.1 7.8 %collective-permute-start.1 = (bf16[128,640]{1,0:T(8,128)(2,1)S(1)}, bf16[128,640]{1,0:T(8,128)(2,1)S(1)}, u32[]{:S(2)}, u32[]{:S(2)}) collective-permute-start(bf16[128,640]{1,0:T(8,128)(2,1)S(1)} %dynamic-slice_bitcast_fusion.1), channel_id=1, source_target_pairs={{0,1},{1,0},{2,3},{3,2},{4,5},{5,4},{6,7},{7,6},{8,9},{9,8},{10,11... | collective-permute-start | bytes 491528 | tf_op jit(solution)/shard_map/ppermute | solution.py:222
  67.3 1.2 copy-start.12
  67.3 1.2 copy-start.13
  67.3 1.2 copy-start.14
  67.3 21.6 %collective-permute-start.6 = (bf16[576,1152]{1,0:T(8,128)(2,1)}, bf16[576,1152]{1,0:T(8,128)(2,1)}, u32[]{:S(2)}, u32[]{:S(2)}) collective-permute-start(bf16[576,1152]{1,0:T(8,128)(2,1)} %dynamic-slice_bitcast_fusion), channel_id=1, source_target_pairs={{0,128},{1,135},{128,2},{129,1},{2,130},{3,129},{130,4},{131,3},{4... | collective-permute-start | bytes 3981320 | tf_op jit(solution)/shard_map/ppermute | solution.py:258
  67.9 21.0 %copy-start.24 = (s32[4]{0:T(128)S(1)}, s32[4]{0:T(128)}, u32[]{:S(2)}) copy-start(s32[4]{0:T(128)} %constant.75) | copy-start | bytes 52
  82.5 8.0 %collective-permute-start.5 = (bf16[128,3456]{1,0:T(8,128)(2,1)S(1)}, bf16[128,3456]{1,0:T(8,128)(2,1)}, u32[]{:S(2)}, u32[]{:S(2)}) collective-permute-start(bf16[128,3456]{1,0:T(8,128)(2,1)S(1)} %temporal_grads.1), channel_id=1, source_target_pairs={{0,1},{1,0},{2,3},{3,2},{4,5},{5,4},{6,7},{7,6},{8,9},{9,8},{10,11... | collective-permute-start | bytes 2654216 | tf_op jit(solution)/shard_map/ppermute | solution.py:222
  89.0 15.8 %collective-permute-start.7 = (bf16[576,1152]{1,0:T(8,128)(2,1)}, bf16[576,1152]{1,0:T(8,128)(2,1)}, u32[]{:S(2)}, u32[]{:S(2)}) collective-permute-start(bf16[576,1152]{1,0:T(8,128)(2,1)} %collective-permute-done.6), channel_id=1, source_target_pairs={{0,1},{1,0},{2,3},{3,2},{4,5},{5,4},{6,7},{7,6},{8,9},{9,8},{10,11... | collective-permute-start | bytes 3981320 | tf_op jit(solution)/shard_map/ppermute | solution.py:259
  91.8 1.1 copy-start.9
  98.1 23.0 %all-to-all-start.3 = ((bf16[128,2,640]{2,1,0:T(2,128)(2,1)}), bf16[128,2,640]{2,1,0:T(2,128)(2,1)}, u32[]{:S(2)}, u32[]{:S(2)}) async-start(bf16[128,2,640]{2,1,0:T(2,128)(2,1)} %bitcast.65), calls=%async_computation.3 | async-start | bytes 655360 | tf_op jit(solution)/shard_map/all_to_all | solution.py:333
  104.8 2.6 %copy-start.20 = (bf16[2,576,1152]{2,1,0:T(8,128)(2,1)S(1)}, bf16[2,576,1152]{2,1,0:T(8,128)(2,1)}, u32[]{:S(2)}) copy-start(bf16[2,576,1152]{2,1,0:T(8,128)(2,1)} %param.20) | copy-start | bytes 7962628
  107.9 6.7 %copy-start.17 = (bf16[2,576,1152]{2,1,0:T(8,128)(2,1)}, bf16[2,576,1152]{2,1,0:T(8,128)(2,1)S(1)}, u32[]{:S(2)}) copy-start(bf16[2,576,1152]{2,1,0:T(8,128)(2,1)S(1)} %get-tuple-element.32) | copy-start | bytes 7962628
  107.9 6.7 %copy-start.18 = (bf16[2,576,1152]{2,1,0:T(8,128)(2,1)}, bf16[2,576,1152]{2,1,0:T(8,128)(2,1)S(1)}, u32[]{:S(2)}) copy-start(bf16[2,576,1152]{2,1,0:T(8,128)(2,1)S(1)} %get-tuple-element.33) | copy-start | bytes 7962628
  107.9 1.8 %copy-start.1 = (bf16[384,1152]{1,0:T(8,128)(2,1)S(1)}, bf16[384,1152]{1,0:T(8,128)(2,1)}, u32[]{:S(2)}) copy-start(bf16[384,1152]{1,0:T(8,128)(2,1)} %pad.12.key_ref) | copy-start | bytes 2654212
  109.8 5.5 %copy-start.16 = (bf16[1280,1152]{1,0:T(8,128)(2,1)S(1)}, bf16[1280,1152]{1,0:T(8,128)(2,1)}, u32[]{:S(2)}) copy-start(bf16[1280,1152]{1,0:T(8,128)(2,1)} %get-tuple-element.19) | copy-start | bytes 8847364
  114.6 0.7 copy-start.7
  122.4 11.6 %copy-start.4 = (bf16[16,8,2,640]{3,1,2,0:T(8,128)(2,1)}, bf16[16,8,2,640]{3,1,2,0:T(8,128)(2,1)S(1)}, u32[]{:S(2)}) copy-start(bf16[16,8,2,640]{3,1,2,0:T(8,128)(2,1)S(1)} %copy.32) | copy-start | bytes 983044
  122.4 1.3 copy-start.2
  123.7 1.2 copy-start.3
  124.8 1.8 %copy-start.6 = (bf16[1280,1152]{1,0:T(8,128)(2,1)S(1)}, bf16[1280,1152]{1,0:T(8,128)(2,1)}, u32[]{:S(2)}) copy-start(bf16[1280,1152]{1,0:T(8,128)(2,1)} %convolution_convert_fusion.w_out_ref) | copy-start | bytes 8847364
  126.7 1.0 copy-start.8
  134.0 0.7 copy-start.10
  134.7 10.9 %copy-start.11 = (bf16[128,1152]{1,0:T(8,128)(2,1)S(1)}, bf16[128,1152]{1,0:T(8,128)(2,1)}, u32[]{:S(2)}) copy-start(bf16[128,1152]{1,0:T(8,128)(2,1)} %copy-done.10) | copy-start | bytes 884740
  134.8 3.3 %collective-permute-start.8 = (bf16[16,72,384]{2,1,0:T(8,128)(2,1)S(1)}, bf16[16,72,384]{2,1,0:T(8,128)(2,1)S(1)}, u32[]{:S(2)}, u32[]{:S(2)}) collective-permute-start(bf16[16,72,384]{2,1,0:T(8,128)(2,1)S(1)} %get-tuple-element.31), channel_id=1, source_target_pairs={{0,1},{1,0},{2,3},{3,2},{4,5},{5,4},{6,7},{7,6},{8,9},{9,8},{10,11... | collective-permute-start | bytes 2654216 | tf_op jit(solution)/shard_map/ppermute | solution.py:222
  139.2 19.9 %all-to-all-start.4 = ((bf16[16,72,384]{2,1,0:T(8,128)(2,1)}), bf16[16,72,384]{2,1,0:T(8,128)(2,1)S(1)}, u32[]{:S(2)}, u32[]{:S(2)}) async-start(bf16[16,72,384]{2,1,0:T(8,128)(2,1)} %add_convert_fusion), calls=%async_computation.4 | async-start | bytes 1769472 | tf_op jit(solution)/shard_map/all_to_all | solution.py:343
  145.6 24.4 %copy-start.5 = (bf16[16,8,2,640]{3,1,2,0:T(8,128)(2,1)S(1)}, bf16[16,8,2,640]{3,1,2,0:T(8,128)(2,1)}, u32[]{:S(2)}) copy-start(bf16[16,8,2,640]{3,1,2,0:T(8,128)(2,1)} %copy-done.4) | copy-start | bytes 983044
  160.2 18.1 %all-to-all-start.5 = ((bf16[16,2,1350]{2,1,0:T(2,128)(2,1)}), bf16[16,2,1350]{2,1,0:T(2,128)(2,1)S(1)}, u32[]{:S(2)}, u32[]{:S(2)}) async-start(bf16[16,2,1350]{2,1,0:T(2,128)(2,1)} %reshape.84), calls=%async_computation.5 | async-start | bytes 180224 | tf_op jit(solution)/shard_map/all_to_all | solution.py:347

commit v7 on v6

--- a/solution.py
+++ b/solution.py
@@ -73,38 +73,48 @@
     )(grad_heads, query, key_rows, value)
 
 
-def mixed_kernel(slot_ref, qkv_ref, residual_ref, w0, w1, w2, w3, out_ref, held, arrived):
+def mixed_kernel(
+    place_ref, mine_ref, other_ref, residual_ref, w0, w1, w2, w3, out_ref, held, rows_ref, added, sems
+):
     copies = [
-        pltpu.make_async_copy(block, held.at[slot_ref[i]], arrived.at[i])
+        pltpu.make_async_copy(block, held.at[place_ref[i]], sems.at[i])
         for i, block in enumerate((w0, w1, w2, w3))
     ]
+    copies.append(pltpu.make_async_copy(residual_ref, added, sems.at[4]))
     for copy in copies:
         copy.start()
+    rows_ref[place_ref[4]] = mine_ref[...]
+    rows_ref[1 - place_ref[4]] = other_ref[...]
     for copy in copies:
         copy.wait()
-    weight = held[...].reshape(-1, held.shape[2])
-    product = dot(qkv_ref[...], weight, CONTRACT_LAST)
-    out_ref[...] = (residual_ref[...] + product).astype(jnp.bfloat16)
-
-
-def mixed_half(slots, qkv_both, residual, blocks):
+    depth = held.shape[2]
+    product = dot(
+        rows_ref[...].reshape(-1, depth), held[...].reshape(-1, depth), CONTRACT_LAST
+    )
+    out_ref[...] = (added[...] + product).astype(jnp.bfloat16)
+
+
+def mixed_half(places, mine, other, residual, blocks):
     in_vmem = pl.BlockSpec(memory_space=pltpu.VMEM)
+    rows, depth = mine.shape
     return pl.pallas_call(
         mixed_kernel,
         in_specs=[pl.BlockSpec(memory_space=pltpu.SMEM), in_vmem, in_vmem]
-        + [pl.BlockSpec(memory_space=pl.ANY)] * 4,
+        + [pl.BlockSpec(memory_space=pl.ANY)] * 5,
         out_specs=in_vmem,
         out_shape=jax.ShapeDtypeStruct(residual.shape, jnp.bfloat16),
         scratch_shapes=[
             pltpu.VMEM((4,) + blocks[0].shape, jnp.bfloat16),
-            pltpu.SemaphoreType.DMA((4,)),
+            pltpu.VMEM((2, rows, depth), jnp.bfloat16),
+            pltpu.VMEM(residual.shape, jnp.float32),
+            pltpu.SemaphoreType.DMA((5,)),
         ],
-        compiler_params=pltpu.CompilerParams(vmem_limit_bytes=32 << 20),
+        compiler_params=pltpu.CompilerParams(vmem_limit_bytes=24 << 20),
         cost_estimate=pl.CostEstimate(
-            flops=2 * residual.size * qkv_both.shape[1], bytes_accessed=8 << 20, transcendentals=0
+            flops=2 * residual.size * depth, bytes_accessed=8 << 20, transcendentals=0
         ),
         name="mixed_half",
-    )(slots, qkv_both, residual, *blocks)
+    )(places, mine, other, residual, *blocks)
 
 
 def probs_kernel(length_ref, query_ref, key_ref, probs_ref):
@@ -135,20 +145,37 @@
 
 
 def cross_kernel(
-    core_ref,
+    arrived_hbm,
+    w_out_hbm,
+    query_hbm,
+    key_hbm,
+    value_hbm,
+    probs_ref,
+    cq_ref,
+    terms_ref,
     arrived_ref,
     w_out_ref,
     query_ref,
     key_ref,
     value_ref,
-    probs_ref,
-    cq_ref,
-    keep_ref,
-    send_ref,
     og_ref,
+    sems,
 ):
+    held = (arrived_ref, w_out_ref, query_ref, key_ref, value_ref)
+    copies = [
+        pltpu.make_async_copy(source, target, sems.at[i])
+        for i, (source, target) in enumerate(
+            zip((arrived_hbm, w_out_hbm, query_hbm, key_hbm, value_hbm), held)
+        )
+    ]
+    for copy in copies:
+        copy.start()
+    for copy in copies[:2]:
+        copy.wait()
     og_ref[...] = dot(arrived_ref[...], w_out_ref[...]).astype(jnp.bfloat16)
-    first = core_ref[0] == 0
+    for copy in copies[2:]:
+        copy.wait()
+    rest = jnp.zeros((HEAD_DIM, 640 - CAP_PAD), jnp.float32)
     for head in range(HEADS):
         at = slice(head * HEAD_DIM, (head + 1) * HEAD_DIM)
         query, out_grad, key_rows, value = (
@@ -159,28 +186,34 @@
         cq_ref[:, at] = dot(score_grad, key_rows).astype(jnp.bfloat16)
         key_term = dot(query, score_grad, CONTRACT_FIRST)
         value_term = dot(out_grad, attention.astype(jnp.bfloat16), CONTRACT_FIRST)
-        keep_ref[head] = jnp.where(first, key_term, value_term).astype(jnp.bfloat16)
-        send_ref[head] = jnp.where(first, value_term, key_term).astype(jnp.bfloat16)
-
-
-def cross_grads(core, arrived, w_out, cross_query, cap_key, cap_value, probs):
+        shifted = pltpu.roll(jnp.concatenate([value_term, rest], axis=1), CAP, 1)
+        terms_ref[head] = (jnp.concatenate([key_term, rest], axis=1) + shifted).astype(
+            jnp.bfloat16
+        )
+
+
+def cross_grads(arrived, w_out, cross_query, cap_key, cap_value, probs):
     rows, width = cross_query.shape
     in_vmem = pl.BlockSpec(memory_space=pltpu.VMEM)
-    term = jax.ShapeDtypeStruct((HEADS, HEAD_DIM, CAP_PAD), jnp.bfloat16)
+    copied = (arrived, w_out, cross_query, cap_key, cap_value)
     return pl.pallas_call(
         cross_kernel,
-        in_specs=[pl.BlockSpec(memory_space=pltpu.SMEM)] + [in_vmem] * 6,
-        out_specs=(in_vmem,) * 3,
-        out_shape=(jax.ShapeDtypeStruct((rows, width), jnp.bfloat16), term, term),
-        scratch_shapes=[pltpu.VMEM((rows, width), jnp.bfloat16)],
-        compiler_params=pltpu.CompilerParams(vmem_limit_bytes=32 << 20),
+        in_specs=[pl.BlockSpec(memory_space=pl.ANY)] * 5 + [in_vmem],
+        out_specs=(in_vmem,) * 2,
+        out_shape=(
+            jax.ShapeDtypeStruct((rows, width), jnp.bfloat16),
+            jax.ShapeDtypeStruct((HEADS, HEAD_DIM, 640), jnp.bfloat16),
+        ),
+        scratch_shapes=[pltpu.VMEM(array.shape, array.dtype) for array in copied]
+        + [pltpu.VMEM((rows, width), jnp.bfloat16), pltpu.SemaphoreType.DMA((5,))],
+        compiler_params=pltpu.CompilerParams(vmem_limit_bytes=24 << 20),
         cost_estimate=pl.CostEstimate(
             flops=8 * rows * CAP_PAD * width + 2 * rows * width * arrived.shape[1],
             bytes_accessed=12 << 20,
             transcendentals=0,
         ),
         name="cross_grads",
-    )(core, arrived, w_out, cross_query, cap_key, cap_value, probs)
+    )(*copied, probs)
 
 
 ALL = ("s", "x", "y", "z", "c")
@@ -289,21 +322,23 @@
     column = lax.all_to_all(jnp.broadcast_to(shard[None], (4,) + shard.shape), "z", 0, 0)
     column = jnp.pad(column.reshape(36, 4 * width), ((0, 4), (0, 0)))
     near = gather_groups(column, ring_groups(0))
-    near, cross_weights = lax.optimization_barrier((near, cross_weights))
+    residual = lax.dot_general(
+        grad_both, place_mine, CONTRACT_LAST, preferred_element_type=jnp.float32
+    )
+    padding = ((0, CAP_PAD - CAP), (0, 0))
+    cap_key, cap_value = jnp.pad(cap_key, padding), jnp.pad(cap_value, padding)
+    near, cross_weights, grad_both, residual, place, cap_key, cap_value = (
+        lax.optimization_barrier(
+            (near, cross_weights, grad_both, residual, place, cap_key, cap_value)
+        )
+    )
     qkv_near = near[:, :, width:].reshape(160, 3 * width)
     blocks = [qkv_near] + [shift_last(qkv_near, step) for step in (1, 3, 2)]
     place_here = jnp.where(core == 0, lax.axis_index("y"), lax.axis_index("x"))
     slots = (place_here - jnp.array([0, 1, 3, 2], jnp.int32)) % 4
+    places = jnp.concatenate([slots, core.reshape(1)])
     out_mine = gather_groups(near[:, :, :width], ring_groups(1)).reshape(640, width)
     full_cross = cross_halves(cross_weights)
-    residual = lax.dot_general(
-        grad_both, place_mine, CONTRACT_LAST, preferred_element_type=jnp.float32
-    )
-    padding = ((0, CAP_PAD - CAP), (0, 0))
-    cap_key, cap_value = jnp.pad(cap_key, padding), jnp.pad(cap_value, padding)
-    out_mine, residual, place, cap_key, cap_value = lax.optimization_barrier(
-        (out_mine, residual, place, cap_key, cap_value)
-    )
     heads_mine = (
         lax.dot_general(grad_both, out_mine, CONTRACT_LAST, preferred_element_type=jnp.float32)
         .astype(jnp.bfloat16)
@@ -321,8 +356,9 @@
         grad_heads, *(saved.reshape(rows, width) for saved in (t_query, t_key, t_value))
     )
     qkv_grad, *blocks = lax.optimization_barrier((qkv_grad, *blocks))
-    qkv_both = in_core_order(qkv_grad, swap_cores(qkv_grad)).reshape(2 * rows, 3 * width)
-    mixed = mixed_half(slots, qkv_both, residual, blocks).reshape(2, rows, 640)
+    mixed = mixed_half(
+        places, qkv_grad, swap_cores(qkv_grad), residual, blocks
+    ).reshape(2, rows, 640)
     w_out_placed = lax.dot_general(
         place, full_cross[1], CONTRACT_LAST, preferred_element_type=jnp.float32
     ).astype(jnp.bfloat16)
@@ -332,18 +368,16 @@
     probs = cross_probs(cap_length, cross_query, cap_key)
     arrived = lax.all_to_all(mixed.transpose(1, 0, 2), SEQ, split_axis=0, concat_axis=0)
     arrived = arrived.reshape(64, 2, 2, 640).transpose(0, 2, 1, 3).reshape(128, 1280)
-    cq_grad, keep, send = cross_grads(
-        core.reshape(1), arrived, w_out_placed, cross_query, cap_key, cap_value, probs
-    )
-    chip = (keep.astype(jnp.float32) + swap_cores(send).astype(jnp.float32)).astype(jnp.bfloat16)
+    cq_grad, terms = cross_grads(arrived, w_out_placed, cross_query, cap_key, cap_value, probs)
     grad_input = (
         jnp.dot(arrived, place, preferred_element_type=jnp.float32)
         + lax.dot_general(cq_grad, full_cross[0], CONTRACT_LAST, preferred_element_type=jnp.float32)
     ).astype(jnp.bfloat16)
-    head = jnp.sum(lax.all_to_all(chip, ("x", "y"), 0, 0).astype(jnp.float32), axis=0)
-    pieces = head[:, :CAP].astype(jnp.bfloat16).reshape(1, 8, 9, CAP)
-    sides = jnp.arange(2).reshape(2, 1, 1, 1) == core
-    pieces = jnp.where(sides, pieces, jnp.zeros_like(pieces)).reshape(16, 9, CAP)
+    head = jnp.sum(lax.all_to_all(terms, ("x", "y"), 0, 0).astype(jnp.float32), axis=0)
+    head = head.astype(jnp.bfloat16)
+    pieces = jnp.concatenate(
+        [head[:, :CAP].reshape(8, 9, CAP), head[:, CAP : 2 * CAP].reshape(8, 9, CAP)]
+    )
     piece = jnp.sum(lax.all_to_all(pieces, ("s", "z", "c"), 0, 0).astype(jnp.float32), axis=0)
     return (grad_input.reshape(frame_input.shape), piece.T)
 

time: 180 us -> 188 us (1.044)
  blocking collectives: 19.1 us -> 0 us
  starting transfers between devices: 52.9 us -> 67.1 us
  local copies, waits for them, and re-layouts: 20.4 us -> 27.9 us
  waiting for transfers between devices: 33.9 us -> 37.9 us
  Pallas kernels: 23.2 us -> 25.3 us
    all_to_all x1 -> x0, blocking collectives: 19.1 us -> none  [local(): lax.all_to_all(jnp.broadcast_to(shard[None], (4,) + shard.shape), 'z', 0, 0)]
    all_to_all x1 -> x2, waiting for transfers between devices: 10.8 us -> 26 us  [the longest x1 17.8 us: local(): lax.all_to_all(terms, ('x', 'y'), 0, 0).astype(jnp.float32)]
    all_to_all x1 -> x2, starting transfers between devices: 6.24 us -> 16.4 us  [the longest x1 9.01 us: local(): lax.all_to_all(jnp.broadcast_to(shard[None], (4,) + shard.shape), 'z', 0, 0)]
    all_to_all x2, waiting for transfers between devices: 8.52 us -> 3.69 us  [gather_groups(): return lax.all_to_all(copies, ALL, 0, 0, axis_index_groups=groups)]
    ppermute x1, starting transfers between devices: 0.09 us -> 4.84 us  [cross_halves(): swapped = lax.ppermute(got, 'c', [(0, 1), (1, 0)])]
    ppermute x3, waiting for transfers between devices: 5.93 us -> 1.68 us  [shift_last(): return lax.ppermute(block, ALL, pairs)]
    unnamed x53 -> x63, local copies, waits for them, and re-layouts: 10.4 us -> 13.7 us
    ppermute x4 -> x3, starting transfers between devices: 16.6 us -> 13.5 us  [swap_cores(): return lax.ppermute(block, 'c', [(0, 1), (1, 0)])]
  transfers between devices with their start and end apart: 14 -> 14, of which waited for: 6 -> 8; matrix products, arithmetic and copies ran while one was open for 18% -> 18% of each run, Pallas kernels for 9% -> 9%
where the time goes in v7:
time: 188 us; the launch traced here: 187 us
  starting transfers between devices  67.1 us (36%)
  waiting for transfers between devices  37.9 us (20%)
  local copies, waits for them, and re-layouts  27.9 us (15%)
  Pallas kernels  25.3 us (13%)
  matrix products  17 us (9%)
  other arithmetic  9.82 us (5%)
    all_to_all x1, waiting for transfers between devices, local(): lax.all_to_all(terms, ('x', 'y'), 0, 0).astype(jnp.float32)  17.8 us
    unnamed x63, local copies, waits for them, and re-layouts  13.7 us
    ppermute x3, starting transfers between devices, swap_cores(): return lax.ppermute(block, 'c', [(0, 1), (1, 0)])  13.5 us
    all_to_all x1, starting transfers between devices, local(): lax.all_to_all(pieces, ('s', 'z', 'c'), 0, 0).astype(jnp.float32)  9.84 us
    all_to_all x1, starting transfers between devices, local(): lax.all_to_all(jnp.broadcast_to(shard[None], (4,) + shard.shape), 'z', 0, 0)  9.01 us
    all_to_all x2, starting transfers between devices, gather_groups(): return lax.all_to_all(copies, ALL, 0, 0, axis_index_groups=groups)  8.52 us
    all_to_all x1, waiting for transfers between devices, local(): lax.all_to_all(jnp.broadcast_to(shard[None], (4,) + shard.shape), 'z', 0, 0)  8.23 us
    pallas_call x1, Pallas kernels, temporal_grads(): pl.pallas_call(temporal_kernel, out_shape=jax.ShapeDtypeStruct((rows, 3 *...  7.98 us
  transfers between devices with their start and end apart: 14, of which 8 were waited for; matrix products, arithmetic and copies ran while one was open for 18% of the time, Pallas kernels for 9%

profile of v7, /device:TPU:1, one launch (start us, length us, event | category | flops | bytes accessed | tf_op | source)
XLA Modules:
  0.0 186.8 jit_solution(9368946189723073280)
XLA Ops:
  0.6 1.0 pad_maximum_fusion.4
  1.7 0.9 broadcast_in_dim.9
  2.6 9.0 %all-to-all-start = ((bf16[4,2,20736]{2,1,0:T(2,128)(2,1)}), bf16[4,2,20736]{2,1,0:T(2,128)(2,1)S(1)}, u32[]{:S(2)}, u32[]{:S(2)}) async-start(bf16[4,2,20736]{2,1,0:T(2,128)(2,1)} %broadcast_in_dim.9), calls=%async_computation | async-start | bytes 663552 | tf_op jit(solution)/shard_map/all_to_all | solution.py:322
  11.6 1.0 collective-permute-start
  12.6 8.2 %all-to-all-done = bf16[4,2,20736]{2,1,0:T(2,128)(2,1)S(1)} async-done(((bf16[4,2,20736]{2,1,0:T(2,128)(2,1)}), bf16[4,2,20736]{2,1,0:T(2,128)(2,1)S(1)}, u32[]{:S(2)}, u32[]{:S(2)}) %all-to-all-start) | async-done | bytes 331808 | tf_op jit(solution)/shard_map/all_to_all | solution.py:322
  21.1 1.2 broadcast_in_dim.10
  22.3 4.2 %all-to-all-start.1 = ((bf16[4,40,4608]{2,1,0:T(8,128)(2,1)}), bf16[4,40,4608]{2,1,0:T(8,128)(2,1)S(1)}, u32[]{:S(2)}, u32[]{:S(2)}) async-start(bf16[4,40,4608]{2,1,0:T(8,128)(2,1)} %broadcast_in_dim.10), calls=%async_computation.1 | async-start | bytes 2949120 | tf_op jit(solution)/shard_map/all_to_all | solution.py:240
  26.5 2.7 %fusion.16 = (bf16[1280,1152]{1,0:T(8,128)(2,1)}, pred[1280,1152]{1,0:T(32,128)(4,1)S(1)}) fusion(s32[1280]{0:T(1024)S(1)} %copy-done.28), kind=kLoop, calls=%fused_computation.37 | loop fusion | flops 2949120 | bytes 4428800 | tf_op jit(solution)/shard_map/convert_element_type | solution.py:316
  29.2 2.1 %pad.12.key_ref.key_hbm = bf16[384,1152]{1,0:T(8,128)(2,1)} pad(bf16[300,1152]{1,0:T(8,128)(2,1)} %param.21, bf16[]{:T(256)} %constant.53.clone.1), padding=0_84x0_0 | pad | bytes 1575938 | tf_op jit(solution)/shard_map/jit(_pad)/pad | solution.py:329
  31.3 2.2 %pad.13.value_hbm = bf16[384,1152]{1,0:T(8,128)(2,1)} pad(bf16[300,1152]{1,0:T(8,128)(2,1)} %param.22, bf16[]{:T(256)} %constant.53.clone.1), padding=0_84x0_0 | pad | bytes 1575938 | tf_op jit(solution)/shard_map/jit(_pad)/pad | solution.py:329
  33.5 1.0 select_bitcast_fusion.3
  34.6 0.8 copy-done.25
  35.4 1.6 fusion.residual_ref
  37.0 1.5 all-to-all-done.1
  38.5 1.1 copy-done.23
  39.6 1.2 slice.19
  40.8 1.3 broadcast_in_dim.11
  42.1 4.3 %all-to-all-start.2 = ((bf16[4,4,40,1152]{3,2,1,0:T(8,128)(2,1)}), bf16[4,4,40,1152]{3,2,1,0:T(8,128)(2,1)}, u32[]{:S(2)}, u32[]{:S(2)}) async-start(bf16[4,4,40,1152]{3,2,1,0:T(8,128)(2,1)} %broadcast_in_dim.11), calls=%async_computation.2 | async-start | bytes 2949120 | tf_op jit(solution)/shard_map/all_to_all | solution.py:240
  46.4 1.2 dynamic-slice_bitcast_fusion
  47.6 2.9 %collective-permute-start.6 = (bf16[576,1152]{1,0:T(8,128)(2,1)}, bf16[576,1152]{1,0:T(8,128)(2,1)}, u32[]{:S(2)}, u32[]{:S(2)}) collective-permute-start(bf16[576,1152]{1,0:T(8,128)(2,1)} %dynamic-slice_bitcast_fusion), channel_id=1, source_target_pairs={{0,128},{1,135},{128,2},{129,1},{2,130},{3,129},{130,4},{131,3},{4... | collective-permute-start | bytes 3981320 | tf_op jit(solution)/shard_map/ppermute | solution.py:291
  50.5 1.3 slice.20
  51.9 3.0 %collective-permute-start.4 = (bf16[160,3456]{1,0:T(8,128)(2,1)S(1)}, bf16[160,3456]{1,0:T(8,128)(2,1)S(1)}, u32[]{:S(2)}, u32[]{:S(2)}) collective-permute-start(bf16[160,3456]{1,0:T(8,128)(2,1)S(1)} %bitcast.59), channel_id=1, source_target_pairs={{0,16},{1,65},{2,18},{3,67},{4,20},{5,69},{6,22},{7,71},{8,24},{9,... | collective-permute-start | bytes 3317768 | tf_op jit(solution)/shard_map/ppermute | solution.py:251
  54.8 0.9 collective-permute-start.3
  55.7 0.6 collective-permute-start.2
  56.3 2.2 %all-to-all-done.2 = bf16[4,4,40,1152]{3,2,1,0:T(8,128)(2,1)} async-done(((bf16[4,4,40,1152]{3,2,1,0:T(8,128)(2,1)}), bf16[4,4,40,1152]{3,2,1,0:T(8,128)(2,1)}, u32[]{:S(2)}, u32[]{:S(2)}) %all-to-all-start.2) | async-done | bytes 1474592 | tf_op jit(solution)/shard_map/all_to_all | solution.py:240
  58.5 2.2 %convolution_convert_fusion.3 = bf16[256,640]{1,0:T(8,128)(2,1)S(1)} fusion(bf16[256,1152]{1,0:T(8,128)(2,1)S(1)} %bitcast.71, bf16[640,1152]{1,0:T(8,128)(2,1)} %bitcast.5), kind=kOutput, calls=%fused_computation.22 | convolution fusion | flops 377651200 | bytes 2392064 | tf_op jit(solution)/shard_map/dot_general | solution.py:343
  60.8 6.5 %collective-permute-start.1 = (bf16[128,640]{1,0:T(8,128)(2,1)S(1)}, bf16[128,640]{1,0:T(8,128)(2,1)S(1)}, u32[]{:S(2)}, u32[]{:S(2)}) collective-permute-start(bf16[128,640]{1,0:T(8,128)(2,1)S(1)} %dynamic-slice_bitcast_fusion.1), channel_id=1, source_target_pairs={{0,1},{1,0},{2,3},{3,2},{4,5},{5,4},{6,7},{7,6},{8,9},{9,8},{10,11... | collective-permute-start | bytes 491528 | tf_op jit(solution)/shard_map/ppermute | solution.py:255
  67.3 4.8 %collective-permute-start.7 = (bf16[576,1152]{1,0:T(8,128)(2,1)}, bf16[576,1152]{1,0:T(8,128)(2,1)}, u32[]{:S(2)}, u32[]{:S(2)}) collective-permute-start(bf16[576,1152]{1,0:T(8,128)(2,1)} %collective-permute-done.6), channel_id=1, source_target_pairs={{0,1},{1,0},{2,3},{3,2},{4,5},{5,4},{6,7},{7,6},{8,9},{9,8},{10,11... | collective-permute-start | bytes 3981320 | tf_op jit(solution)/shard_map/ppermute | solution.py:292
  72.2 0.6 convolution_convert_fusion.2.grad_ref
  72.8 8.0 %temporal_grads.1.mine_ref = bf16[128,3456]{1,0:T(8,128)(2,1)S(1)} custom-call(bf16[128,1152]{1,0:T(8,128)(2,1)S(1)} %convolution_convert_fusion.2.grad_ref, bf16[128,1152]{1,0:T(8,128)(2,1)S(1)} %bitcast.66, bf16[128,1152]{1,0:T(8,128)(2,1)S(1)} %bitcast.67, bf16[128,1152]{1,0:T(8,128)(2,1)S(1)} %bitcast.68), custom_call_target="tpu_custom_call" | custom-call | flops 147456 | bytes 294912 | tf_op jit(solution)/shard_map/temporal_grads/pallas_call | solution.py:65
  80.8 0.2 collective-permute-done.3.w2
  81.0 1.5 collective-permute-done.2.w1
  82.5 6.1 %collective-permute-start.5 = (bf16[128,3456]{1,0:T(8,128)(2,1)S(1)}, bf16[128,3456]{1,0:T(8,128)(2,1)}, u32[]{:S(2)}, u32[]{:S(2)}) collective-permute-start(bf16[128,3456]{1,0:T(8,128)(2,1)S(1)} %temporal_grads.1.mine_ref), channel_id=1, source_target_pairs={{0,1},{1,0},{2,3},{3,2},{4,5},{5,4},{6,7},{7,6},{8,9},{9,8},{10,11... | collective-permute-start | bytes 2654216 | tf_op jit(solution)/shard_map/ppermute | solution.py:255
  89.3 1.4 collective-permute-done.5.other_ref
  90.8 1.1 copy-done.10
  91.9 4.6 %mixed_half.1 = bf16[256,640]{1,0:T(8,128)(2,1)S(1)} custom-call(s32[5]{0:T(128)S(1)} %pad_add_fusion.place_ref, bf16[128,3456]{1,0:T(8,128)(2,1)S(1)} %temporal_grads.1.mine_ref, bf16[128,3456]{1,0:T(8,128)(2,1)} %collective-permute-done.5.other_ref, f32[256,640]{1,0:T(8,128)S(1)} %copy-done.10, bf16[160,3456]{1,0:T(8,128)(2,1)S(1)} %bitcast.62, ...), custom_call_target="tpu_custom_call" | custom-call | flops 1132462080 | bytes 8388608 | tf_op jit(solution)/shard_map/mixed_half/pallas_call | solution.py:100
  96.4 1.1 copy.22
  97.5 6.6 %all-to-all-start.3 = ((bf16[128,2,640]{2,1,0:T(2,128)(2,1)}), bf16[128,2,640]{2,1,0:T(2,128)(2,1)}, u32[]{:S(2)}, u32[]{:S(2)}) async-start(bf16[128,2,640]{2,1,0:T(2,128)(2,1)} %bitcast.58), calls=%async_computation.3 | async-start | bytes 655360 | tf_op jit(solution)/shard_map/all_to_all | solution.py:369
  104.2 2.1 %select_bitcast_fusion.1 = (bf16[1,576,1152]{2,1,0:T(8,128)(2,1)S(1)}, bf16[1,576,1152]{2,1,0:T(8,128)(2,1)S(1)}) fusion(bf16[576,1152]{1,0:T(8,128)(2,1)} %collective-permute-done.6, bf16[576,1152]{1,0:T(8,128)(2,1)} %collective-permute-done.7, pred[]{:T(512)S(6)} %eq.12), kind=kLoop, calls=%fused_computation.20 | loop fusion | flops 1327104 | bytes 5308417 | tf_op jit(solution)/shard_map/stack | solution.py:293
  106.3 0.4 copy-done.22
  106.7 0.5 broadcast_select_fusion
  107.3 0.6 fusion.7.query_ref.query_hbm
  107.9 1.2 copy-done.1
  109.1 4.8 %cross_probs.1.probs_ref = f32[16,128,384]{2,1,0:T(8,128)S(1)} custom-call(s32[1]{0:T(128)S(6)} %copy.25.length_ref, bf16[128,1152]{1,0:T(8,128)(2,1)S(1)} %fusion.7.query_ref.query_hbm, bf16[384,1152]{1,0:T(8,128)(2,1)S(1)} %copy-done.1), custom_call_target="tpu_custom_call" | custom-call | flops 113246208 | bytes 4194304 | tf_op jit(solution)/shard_map/cross_probs/pallas_call | solution.py:132
  114.0 0.7 copy-done.7
  114.7 5.8 %convolution_convert_fusion.w_out_hbm = bf16[1280,1152]{1,0:T(8,128)(2,1)} fusion(bf16[1280,1152]{1,0:T(8,128)(2,1)S(1)} %copy-done.17, bf16[2,576,1152]{2,1,0:T(8,128)(2,1)S(1)} %get-tuple-element.31, bf16[2,576,1152]{2,1,0:T(8,128)(2,1)S(1)} %get-tuple-element.30), kind=kOutput, calls=%fused_computation | convolution fusion | flops 3404169216 | bytes 11206656 | tf_op jit(solution)/shard_map/dot_general | solution.py:362
  120.4 1.2 copy.17
  121.7 1.3 copy-done.2
  123.0 1.2 copy-done.3
  124.2 1.8 copy-done.6
  126.0 1.0 copy-done.8
  127.0 8.0 %cross_grads.1 = (bf16[128,1152]{1,0:T(8,128)(2,1)S(1)}, bf16[16,72,640]{2,1,0:T(8,128)(2,1)S(1)}) custom-call(bf16[128,1280]{1,0:T(8,128)(2,1)S(1)} %bitcast.63, bf16[1280,1152]{1,0:T(8,128)(2,1)S(1)} %copy-done.6, bf16[128,1152]{1,0:T(8,128)(2,1)S(1)} %copy-done.8, bf16[384,1152]{1,0:T(8,128)(2,1)S(1)} %copy-done.2, bf16[384,1152]{1,0:T(8,128)(2,1)S(1)} %copy-done.3, ...), custom_call_target="tpu_custom_call" | custom-call | flops 830472192 | bytes 12582912 | tf_op jit(solution)/shard_map/cross_grads/pallas_call | solution.py:199
  135.0 1.2 copy-done.9
  136.1 0.7 copy-done.11
  136.8 7.4 %all-to-all-start.4 = ((bf16[16,72,640]{2,1,0:T(8,128)(2,1)}), bf16[16,72,640]{2,1,0:T(8,128)(2,1)}, u32[]{:S(2)}, u32[]{:S(2)}) async-start(bf16[16,72,640]{2,1,0:T(8,128)(2,1)} %copy-done.9), calls=%async_computation.4 | async-start | bytes 2949120 | tf_op jit(solution)/shard_map/all_to_all | solution.py:376
  144.3 3.1 %fusion.9 = f32[128,1152]{1,0:T(8,128)} fusion(bf16[128,1152]{1,0:T(8,128)(2,1)S(1)} %copy-done.12, bf16[2,576,1152]{2,1,0:T(8,128)(2,1)S(1)} %copy-done.19, bf16[2,576,1152]{2,1,0:T(8,128)(2,1)} %copy-done.20), kind=kOutput, calls=%fused_computation.25 | convolution fusion | flops 345047040 | bytes 6193152 | tf_op jit(solution)/shard_map/dot_general | solution.py:374
  147.4 17.8 %all-to-all-done.4 = bf16[16,72,640]{2,1,0:T(8,128)(2,1)} async-done(((bf16[16,72,640]{2,1,0:T(8,128)(2,1)}), bf16[16,72,640]{2,1,0:T(8,128)(2,1)}, u32[]{:S(2)}, u32[]{:S(2)}) %all-to-all-start.4) | async-done | bytes 1474592 | tf_op jit(solution)/shard_map/all_to_all | solution.py:376
  165.1 1.6 reduce_sum.21
  166.9 0.8 reshape.76
  167.8 9.8 %all-to-all-start.5 = ((bf16[16,2,1350]{2,1,0:T(2,128)(2,1)}), bf16[16,2,1350]{2,1,0:T(2,128)(2,1)S(1)}, u32[]{:S(2)}, u32[]{:S(2)}) async-start(bf16[16,2,1350]{2,1,0:T(2,128)(2,1)} %reshape.76), calls=%async_computation.5 | async-start | bytes 180224 | tf_op jit(solution)/shard_map/all_to_all | solution.py:381
  177.6 3.2 %fusion.8 = bf16[1,128,1152]{2,1,0:T(8,128)(2,1)} fusion(f32[128,1152]{1,0:T(8,128)S(1)} %copy-done.24, bf16[128,1280]{1,0:T(8,128)(2,1)S(1)} %bitcast.64, bf16[1280,1152]{1,0:T(8,128)(2,1)} %get-tuple-element.18), kind=kOutput, calls=%fused_computation.18 | convolution fusion | flops 377782272 | bytes 4161536 | tf_op jit(solution)/shard_map/dot_general | solution.py:373
  180.8 5.1 %all-to-all-done.5 = bf16[16,2,1350]{2,1,0:T(2,128)(2,1)S(1)} async-done(((bf16[16,2,1350]{2,1,0:T(2,128)(2,1)}), bf16[16,2,1350]{2,1,0:T(2,128)(2,1)S(1)}, u32[]{:S(2)}, u32[]{:S(2)}) %all-to-all-start.5) | async-done | bytes 86432 | tf_op jit(solution)/shard_map/all_to_all | solution.py:381
  185.9 0.2 reshape.77
  186.2 0.7 convert_reduce_fusion
  (67 shorter events, 0.9 us)
Async XLA Ops:
  0.6 106.6 %copy-start = (bf16[1,128,1152]{2,1,0:T(8,128)(2,1)S(1)}, bf16[1,128,1152]{2,1,0:T(8,128)(2,1)}, u32[]{:S(2)}) copy-start(bf16[1,128,1152]{2,1,0:T(8,128)(2,1)} %param.19) | copy-start | bytes 884740
  2.6 18.2 %all-to-all-start = ((bf16[4,2,20736]{2,1,0:T(2,128)(2,1)}), bf16[4,2,20736]{2,1,0:T(2,128)(2,1)S(1)}, u32[]{:S(2)}, u32[]{:S(2)}) async-start(bf16[4,2,20736]{2,1,0:T(2,128)(2,1)} %broadcast_in_dim.9), calls=%async_computation | async-start | bytes 663552 | tf_op jit(solution)/shard_map/all_to_all | solution.py:322
  11.6 21.9 %collective-permute-start = (bf16[128,1152]{1,0:T(8,128)(2,1)}, bf16[128,1152]{1,0:T(8,128)(2,1)}, u32[]{:S(2)}, u32[]{:S(2)}) collective-permute-start(bf16[128,1152]{1,0:T(8,128)(2,1)} %bitcast.74), channel_id=1, source_target_pairs={{0,1},{1,0},{2,3},{3,2},{4,5},{5,4},{6,7},{7,6},{8,9},{9,8},{10,11... | collective-permute-start | bytes 884744 | tf_op jit(solution)/shard_map/ppermute | solution.py:255
  21.0 5.5 %copy-start.28 = (s32[1280]{0:T(1024)S(1)}, s32[1280]{0:T(1024)}, u32[]{:S(2)}) copy-start(s32[1280]{0:T(1024)} %constant.60.clone) | copy-start | bytes 15364
  22.3 16.2 %all-to-all-start.1 = ((bf16[4,40,4608]{2,1,0:T(8,128)(2,1)}), bf16[4,40,4608]{2,1,0:T(8,128)(2,1)S(1)}, u32[]{:S(2)}, u32[]{:S(2)}) async-start(bf16[4,40,4608]{2,1,0:T(8,128)(2,1)} %broadcast_in_dim.10), calls=%async_computation.1 | async-start | bytes 2949120 | tf_op jit(solution)/shard_map/all_to_all | solution.py:240
  29.2 4.3 %copy-start.27 = (bf16[2,64,1,1152]{3,1,2,0:T(8,128)(2,1)S(1)}, bf16[2,64,1,1152]{3,1,2,0:T(8,128)(2,1)}, u32[]{:S(2)}) copy-start(bf16[2,64,1,1152]{3,1,2,0:T(8,128)(2,1)} %param.13) | copy-start | bytes 884740
  34.6 0.8 copy-start.25
  38.5 1.1 copy-start.23
  39.6 6.8 %copy-start.21 = (bf16[2,576,1152]{2,1,0:T(8,128)(2,1)S(1)}, bf16[2,576,1152]{2,1,0:T(8,128)(2,1)}, u32[]{:S(2)}) copy-start(bf16[2,576,1152]{2,1,0:T(8,128)(2,1)} %param.20) | copy-start | bytes 7962628
  42.1 16.4 %all-to-all-start.2 = ((bf16[4,4,40,1152]{3,2,1,0:T(8,128)(2,1)}), bf16[4,4,40,1152]{3,2,1,0:T(8,128)(2,1)}, u32[]{:S(2)}, u32[]{:S(2)}) async-start(bf16[4,4,40,1152]{3,2,1,0:T(8,128)(2,1)} %broadcast_in_dim.11), calls=%async_computation.2 | async-start | bytes 2949120 | tf_op jit(solution)/shard_map/all_to_all | solution.py:240
  46.4 12.1 %copy-start.26 = (bf16[2,128,1152]{2,1,0:T(8,128)(2,1)S(1)}, bf16[2,128,1152]{2,1,0:T(8,128)(2,1)}, u32[]{:S(2)}) copy-start(bf16[2,128,1152]{2,1,0:T(8,128)(2,1)} %copy-done.25) | copy-start | bytes 1769476
  47.6 19.6 %collective-permute-start.6 = (bf16[576,1152]{1,0:T(8,128)(2,1)}, bf16[576,1152]{1,0:T(8,128)(2,1)}, u32[]{:S(2)}, u32[]{:S(2)}) collective-permute-start(bf16[576,1152]{1,0:T(8,128)(2,1)} %dynamic-slice_bitcast_fusion), channel_id=1, source_target_pairs={{0,128},{1,135},{128,2},{129,1},{2,130},{3,129},{130,4},{131,3},{4... | collective-permute-start | bytes 3981320 | tf_op jit(solution)/shard_map/ppermute | solution.py:291
  51.9 28.9 %collective-permute-start.4 = (bf16[160,3456]{1,0:T(8,128)(2,1)S(1)}, bf16[160,3456]{1,0:T(8,128)(2,1)S(1)}, u32[]{:S(2)}, u32[]{:S(2)}) collective-permute-start(bf16[160,3456]{1,0:T(8,128)(2,1)S(1)} %bitcast.59), channel_id=1, source_target_pairs={{0,16},{1,65},{2,18},{3,67},{4,20},{5,69},{6,22},{7,71},{8,24},{9,... | collective-permute-start | bytes 3317768 | tf_op jit(solution)/shard_map/ppermute | solution.py:251
  54.8 26.2 %collective-permute-start.3 = (bf16[160,3456]{1,0:T(8,128)(2,1)S(1)}, bf16[160,3456]{1,0:T(8,128)(2,1)}, u32[]{:S(2)}, u32[]{:S(2)}) collective-permute-start(bf16[160,3456]{1,0:T(8,128)(2,1)S(1)} %bitcast.60), channel_id=1, source_target_pairs={{0,24},{1,97},{2,26},{3,99},{4,28},{5,101},{6,30},{7,103},{8,0},{9... | collective-permute-start | bytes 3317768 | tf_op jit(solution)/shard_map/ppermute | solution.py:251
  55.7 26.8 %collective-permute-start.2 = (bf16[160,3456]{1,0:T(8,128)(2,1)S(1)}, bf16[160,3456]{1,0:T(8,128)(2,1)}, u32[]{:S(2)}, u32[]{:S(2)}) collective-permute-start(bf16[160,3456]{1,0:T(8,128)(2,1)S(1)} %bitcast.61), channel_id=1, source_target_pairs={{0,8},{1,33},{2,10},{3,35},{4,12},{5,37},{6,14},{7,39},{8,16},{9,4... | collective-permute-start | bytes 3317768 | tf_op jit(solution)/shard_map/ppermute | solution.py:251
  58.5 13.7 %copy-start.16 = (bf16[1280,1152]{1,0:T(8,128)(2,1)S(1)}, bf16[1280,1152]{1,0:T(8,128)(2,1)}, u32[]{:S(2)}) copy-start(bf16[1280,1152]{1,0:T(8,128)(2,1)} %get-tuple-element.18) | copy-start | bytes 8847364
  60.7 12.1 %copy-start.13 = (bf16[2,64,1,1152]{3,1,2,0:T(8,128)(2,1)S(1)}, bf16[2,64,1,1152]{3,1,2,0:T(8,128)(2,1)}, u32[]{:S(2)}) copy-start(bf16[2,64,1,1152]{3,1,2,0:T(8,128)(2,1)} %param.14) | copy-start | bytes 884740
  60.7 12.1 %copy-start.14 = (bf16[2,64,1,1152]{3,1,2,0:T(8,128)(2,1)S(1)}, bf16[2,64,1,1152]{3,1,2,0:T(8,128)(2,1)}, u32[]{:S(2)}) copy-start(bf16[2,64,1,1152]{3,1,2,0:T(8,128)(2,1)} %param.15) | copy-start | bytes 884740
  60.7 12.1 %copy-start.15 = (bf16[2,64,1,1152]{3,1,2,0:T(8,128)(2,1)S(1)}, bf16[2,64,1,1152]{3,1,2,0:T(8,128)(2,1)}, u32[]{:S(2)}) copy-start(bf16[2,64,1,1152]{3,1,2,0:T(8,128)(2,1)} %param.16) | copy-start | bytes 884740
  60.8 11.3 %collective-permute-start.1 = (bf16[128,640]{1,0:T(8,128)(2,1)S(1)}, bf16[128,640]{1,0:T(8,128)(2,1)S(1)}, u32[]{:S(2)}, u32[]{:S(2)}) collective-permute-start(bf16[128,640]{1,0:T(8,128)(2,1)S(1)} %dynamic-slice_bitcast_fusion.1), channel_id=1, source_target_pairs={{0,1},{1,0},{2,3},{3,2},{4,5},{5,4},{6,7},{7,6},{8,9},{9,8},{10,11... | collective-permute-start | bytes 491528 | tf_op jit(solution)/shard_map/ppermute | solution.py:255
  67.3 36.9 %collective-permute-start.7 = (bf16[576,1152]{1,0:T(8,128)(2,1)}, bf16[576,1152]{1,0:T(8,128)(2,1)}, u32[]{:S(2)}, u32[]{:S(2)}) collective-permute-start(bf16[576,1152]{1,0:T(8,128)(2,1)} %collective-permute-done.6), channel_id=1, source_target_pairs={{0,1},{1,0},{2,3},{3,2},{4,5},{5,4},{6,7},{7,6},{8,9},{9,8},{10,11... | collective-permute-start | bytes 3981320 | tf_op jit(solution)/shard_map/ppermute | solution.py:292
  72.2 17.1 %copy-start.29 = (s32[4]{0:T(128)S(1)}, s32[4]{0:T(128)}, u32[]{:S(2)}) copy-start(s32[4]{0:T(128)} %constant.75) | copy-start | bytes 52
  82.5 8.3 %collective-permute-start.5 = (bf16[128,3456]{1,0:T(8,128)(2,1)S(1)}, bf16[128,3456]{1,0:T(8,128)(2,1)}, u32[]{:S(2)}, u32[]{:S(2)}) collective-permute-start(bf16[128,3456]{1,0:T(8,128)(2,1)S(1)} %temporal_grads.1.mine_ref), channel_id=1, source_target_pairs={{0,1},{1,0},{2,3},{3,2},{4,5},{5,4},{6,7},{7,6},{8,9},{9,8},{10,11... | collective-permute-start | bytes 2654216 | tf_op jit(solution)/shard_map/ppermute | solution.py:255
  90.8 1.1 copy-start.10
  97.5 22.9 %all-to-all-start.3 = ((bf16[128,2,640]{2,1,0:T(2,128)(2,1)}), bf16[128,2,640]{2,1,0:T(2,128)(2,1)}, u32[]{:S(2)}, u32[]{:S(2)}) async-start(bf16[128,2,640]{2,1,0:T(2,128)(2,1)} %bitcast.58), calls=%async_computation.3 | async-start | bytes 655360 | tf_op jit(solution)/shard_map/all_to_all | solution.py:369
  104.1 2.6 %copy-start.22 = (bf16[2,576,1152]{2,1,0:T(8,128)(2,1)S(1)}, bf16[2,576,1152]{2,1,0:T(8,128)(2,1)}, u32[]{:S(2)}) copy-start(bf16[2,576,1152]{2,1,0:T(8,128)(2,1)} %param.20) | copy-start | bytes 7962628
  107.2 6.7 %copy-start.18 = (bf16[2,576,1152]{2,1,0:T(8,128)(2,1)}, bf16[2,576,1152]{2,1,0:T(8,128)(2,1)S(1)}, u32[]{:S(2)}) copy-start(bf16[2,576,1152]{2,1,0:T(8,128)(2,1)S(1)} %get-tuple-element.30) | copy-start | bytes 7962628
  107.3 6.7 %copy-start.20 = (bf16[2,576,1152]{2,1,0:T(8,128)(2,1)}, bf16[2,576,1152]{2,1,0:T(8,128)(2,1)S(1)}, u32[]{:S(2)}) copy-start(bf16[2,576,1152]{2,1,0:T(8,128)(2,1)S(1)} %get-tuple-element.31) | copy-start | bytes 7962628
  107.3 1.8 copy-start.1
  109.1 5.5 %copy-start.17 = (bf16[1280,1152]{1,0:T(8,128)(2,1)S(1)}, bf16[1280,1152]{1,0:T(8,128)(2,1)}, u32[]{:S(2)}) copy-start(bf16[1280,1152]{1,0:T(8,128)(2,1)} %get-tuple-element.18) | copy-start | bytes 8847364
  113.9 0.7 copy-start.7
  121.7 13.2 %copy-start.4 = (bf16[16,8,2,640]{3,1,2,0:T(8,128)(2,1)}, bf16[16,8,2,640]{3,1,2,0:T(8,128)(2,1)S(1)}, u32[]{:S(2)}) copy-start(bf16[16,8,2,640]{3,1,2,0:T(8,128)(2,1)S(1)} %copy.20) | copy-start | bytes 983044
  121.7 1.3 copy-start.2
  123.0 1.2 copy-start.3
  124.2 1.8 copy-start.6
  126.0 1.0 copy-start.8
  135.0 1.2 copy-start.9
  136.1 0.7 copy-start.11
  136.8 7.4 %copy-start.19 = (bf16[2,576,1152]{2,1,0:T(8,128)(2,1)S(1)}, bf16[2,576,1152]{2,1,0:T(8,128)(2,1)}, u32[]{:S(2)}) copy-start(bf16[2,576,1152]{2,1,0:T(8,128)(2,1)} %copy-done.18) | copy-start | bytes 7962628
  136.8 7.4 %copy-start.12 = (bf16[128,1152]{1,0:T(8,128)(2,1)S(1)}, bf16[128,1152]{1,0:T(8,128)(2,1)}, u32[]{:S(2)}) copy-start(bf16[128,1152]{1,0:T(8,128)(2,1)} %copy-done.11) | copy-start | bytes 884740
  136.8 28.3 %all-to-all-start.4 = ((bf16[16,72,640]{2,1,0:T(8,128)(2,1)}), bf16[16,72,640]{2,1,0:T(8,128)(2,1)}, u32[]{:S(2)}, u32[]{:S(2)}) async-start(bf16[16,72,640]{2,1,0:T(8,128)(2,1)} %copy-done.9), calls=%async_computation.4 | async-start | bytes 2949120 | tf_op jit(solution)/shard_map/all_to_all | solution.py:376
  147.3 30.3 %copy-start.5 = (bf16[16,8,2,640]{3,1,2,0:T(8,128)(2,1)S(1)}, bf16[16,8,2,640]{3,1,2,0:T(8,128)(2,1)}, u32[]{:S(2)}) copy-start(bf16[16,8,2,640]{3,1,2,0:T(8,128)(2,1)} %copy-done.4) | copy-start | bytes 983044
  147.4 30.3 %copy-start.24 = (f32[128,1152]{1,0:T(8,128)S(1)}, f32[128,1152]{1,0:T(8,128)}, u32[]{:S(2)}) copy-start(f32[128,1152]{1,0:T(8,128)} %fusion.9) | copy-start | bytes 1769476
  167.8 18.2 %all-to-all-start.5 = ((bf16[16,2,1350]{2,1,0:T(2,128)(2,1)}), bf16[16,2,1350]{2,1,0:T(2,128)(2,1)S(1)}, u32[]{:S(2)}, u32[]{:S(2)}) async-start(bf16[16,2,1350]{2,1,0:T(2,128)(2,1)} %reshape.76), calls=%async_computation.5 | async-start | bytes 180224 | tf_op jit(solution)/shard_map/all_to_all | solution.py:381

commit v8 on v7

--- a/solution.py
+++ b/solution.py
@@ -91,7 +91,9 @@
     product = dot(
         rows_ref[...].reshape(-1, depth), held[...].reshape(-1, depth), CONTRACT_LAST
     )
-    out_ref[...] = (added[...] + product).astype(jnp.bfloat16)
+    made = product.shape[1]
+    out_ref[:, :made] = (added[:, :made].astype(jnp.float32) + product).astype(jnp.bfloat16)
+    out_ref[:, made:] = jnp.zeros((out_ref.shape[0], out_ref.shape[1] - made), jnp.bfloat16)
 
 
 def mixed_half(places, mine, other, residual, blocks):
@@ -106,7 +108,7 @@
         scratch_shapes=[
             pltpu.VMEM((4,) + blocks[0].shape, jnp.bfloat16),
             pltpu.VMEM((2, rows, depth), jnp.bfloat16),
-            pltpu.VMEM(residual.shape, jnp.float32),
+            pltpu.VMEM(residual.shape, jnp.bfloat16),
             pltpu.SemaphoreType.DMA((5,)),
         ],
         compiler_params=pltpu.CompilerParams(vmem_limit_bytes=24 << 20),
@@ -145,28 +147,30 @@
 
 
 def cross_kernel(
+    core_ref,
     arrived_hbm,
     w_out_hbm,
     query_hbm,
+    value_hbm,
+    probs_hbm,
     key_hbm,
-    value_hbm,
-    probs_ref,
     cq_ref,
-    terms_ref,
+    keep_ref,
+    send_ref,
     arrived_ref,
     w_out_ref,
     query_ref,
+    value_ref,
+    probs_ref,
     key_ref,
-    value_ref,
     og_ref,
     sems,
 ):
-    held = (arrived_ref, w_out_ref, query_ref, key_ref, value_ref)
+    held = (arrived_ref, w_out_ref, query_ref, value_ref, probs_ref, key_ref)
+    given = (arrived_hbm, w_out_hbm, query_hbm, value_hbm, probs_hbm, key_hbm)
     copies = [
         pltpu.make_async_copy(source, target, sems.at[i])
-        for i, (source, target) in enumerate(
-            zip((arrived_hbm, w_out_hbm, query_hbm, key_hbm, value_hbm), held)
-        )
+        for i, (source, target) in enumerate(zip(given, held))
     ]
     for copy in copies:
         copy.start()
@@ -175,7 +179,7 @@
     og_ref[...] = dot(arrived_ref[...], w_out_ref[...]).astype(jnp.bfloat16)
     for copy in copies[2:]:
         copy.wait()
-    rest = jnp.zeros((HEAD_DIM, 640 - CAP_PAD), jnp.float32)
+    first = core_ref[0] == 0
     for head in range(HEADS):
         at = slice(head * HEAD_DIM, (head + 1) * HEAD_DIM)
         query, out_grad, key_rows, value = (
@@ -186,34 +190,31 @@
         cq_ref[:, at] = dot(score_grad, key_rows).astype(jnp.bfloat16)
         key_term = dot(query, score_grad, CONTRACT_FIRST)
         value_term = dot(out_grad, attention.astype(jnp.bfloat16), CONTRACT_FIRST)
-        shifted = pltpu.roll(jnp.concatenate([value_term, rest], axis=1), CAP, 1)
-        terms_ref[head] = (jnp.concatenate([key_term, rest], axis=1) + shifted).astype(
-            jnp.bfloat16
-        )
-
-
-def cross_grads(arrived, w_out, cross_query, cap_key, cap_value, probs):
+        keep_ref[head] = jnp.where(first, key_term, value_term).astype(jnp.bfloat16)
+        send_ref[head] = jnp.where(first, value_term, key_term).astype(jnp.bfloat16)
+
+
+def cross_grads(core, arrived, w_out, cross_query, cap_value, probs, cap_key):
     rows, width = cross_query.shape
     in_vmem = pl.BlockSpec(memory_space=pltpu.VMEM)
-    copied = (arrived, w_out, cross_query, cap_key, cap_value)
+    copied = (arrived, w_out, cross_query, cap_value, probs, cap_key)
+    term = jax.ShapeDtypeStruct((HEADS, HEAD_DIM, CAP_PAD), jnp.bfloat16)
     return pl.pallas_call(
         cross_kernel,
-        in_specs=[pl.BlockSpec(memory_space=pl.ANY)] * 5 + [in_vmem],
-        out_specs=(in_vmem,) * 2,
-        out_shape=(
-            jax.ShapeDtypeStruct((rows, width), jnp.bfloat16),
-            jax.ShapeDtypeStruct((HEADS, HEAD_DIM, 640), jnp.bfloat16),
-        ),
+        in_specs=[pl.BlockSpec(memory_space=pltpu.SMEM)]
+        + [pl.BlockSpec(memory_space=pl.ANY)] * 6,
+        out_specs=(in_vmem,) * 3,
+        out_shape=(jax.ShapeDtypeStruct((rows, width), jnp.bfloat16), term, term),
         scratch_shapes=[pltpu.VMEM(array.shape, array.dtype) for array in copied]
-        + [pltpu.VMEM((rows, width), jnp.bfloat16), pltpu.SemaphoreType.DMA((5,))],
-        compiler_params=pltpu.CompilerParams(vmem_limit_bytes=24 << 20),
+        + [pltpu.VMEM((rows, width), jnp.bfloat16), pltpu.SemaphoreType.DMA((6,))],
+        compiler_params=pltpu.CompilerParams(vmem_limit_bytes=56 << 20),
         cost_estimate=pl.CostEstimate(
             flops=8 * rows * CAP_PAD * width + 2 * rows * width * arrived.shape[1],
             bytes_accessed=12 << 20,
             transcendentals=0,
         ),
         name="cross_grads",
-    )(*copied, probs)
+    )(core, *copied)
 
 
 ALL = ("s", "x", "y", "z", "c")
@@ -261,13 +262,14 @@
 
 
 def feature_order():
-    order = np.full((2, 4, 4, 40), -1, np.int32)
+    order = np.full((2, 640), -1, np.int32)
     for c in range(2):
         for i in range(4):
             for j in range(4):
                 x, y = (j, i) if c == 0 else (i, j)
                 for q in range(36):
-                    order[c, i, j, q] = 72 * (4 * x + y) + 18 * (q // 9) + 9 * c + q % 9
+                    at = (4 * i + j) * 36 + q
+                    order[c, at] = 72 * (4 * x + y) + 18 * (q // 9) + 9 * c + q % 9
     return order.reshape(1280)
 
 
@@ -324,33 +326,33 @@
     near = gather_groups(column, ring_groups(0))
     residual = lax.dot_general(
         grad_both, place_mine, CONTRACT_LAST, preferred_element_type=jnp.float32
-    )
+    ).astype(jnp.bfloat16)
     padding = ((0, CAP_PAD - CAP), (0, 0))
     cap_key, cap_value = jnp.pad(cap_key, padding), jnp.pad(cap_value, padding)
-    near, cross_weights, grad_both, residual, place, cap_key, cap_value = (
+    out_near = near[:, :36, :width].reshape(144, width)
+    out_near, cross_weights, grad_both, residual, place, cap_key, cap_value = (
         lax.optimization_barrier(
-            (near, cross_weights, grad_both, residual, place, cap_key, cap_value)
+            (out_near, cross_weights, grad_both, residual, place, cap_key, cap_value)
         )
     )
-    qkv_near = near[:, :, width:].reshape(160, 3 * width)
+    qkv_near = near[:, :36, width:].reshape(144, 3 * width)
     blocks = [qkv_near] + [shift_last(qkv_near, step) for step in (1, 3, 2)]
     place_here = jnp.where(core == 0, lax.axis_index("y"), lax.axis_index("x"))
     slots = (place_here - jnp.array([0, 1, 3, 2], jnp.int32)) % 4
     places = jnp.concatenate([slots, core.reshape(1)])
-    out_mine = gather_groups(near[:, :, :width], ring_groups(1)).reshape(640, width)
+    out_mine = gather_groups(out_near, ring_groups(1)).reshape(576, width)
     full_cross = cross_halves(cross_weights)
     heads_mine = (
         lax.dot_general(grad_both, out_mine, CONTRACT_LAST, preferred_element_type=jnp.float32)
         .astype(jnp.bfloat16)
-        .reshape(2, rows, 640)
+        .reshape(2, rows, 576)
     )
     kept = lax.dynamic_index_in_dim(heads_mine, core, 0, keepdims=False)
     sent = lax.dynamic_index_in_dim(heads_mine, 1 - core, 0, keepdims=False)
     heads_parts = in_core_order(kept, swap_cores(sent))
-    grad_heads = jnp.dot(
-        jnp.concatenate([heads_parts[0], heads_parts[1]], axis=1),
-        place,
-        preferred_element_type=jnp.float32,
+    grad_heads = (
+        jnp.dot(heads_parts[0], place[:576], preferred_element_type=jnp.float32)
+        + jnp.dot(heads_parts[1], place[640:1216], preferred_element_type=jnp.float32)
     ).astype(jnp.bfloat16)
     qkv_grad = temporal_grads(
         grad_heads, *(saved.reshape(rows, width) for saved in (t_query, t_key, t_value))
@@ -368,16 +370,18 @@
     probs = cross_probs(cap_length, cross_query, cap_key)
     arrived = lax.all_to_all(mixed.transpose(1, 0, 2), SEQ, split_axis=0, concat_axis=0)
     arrived = arrived.reshape(64, 2, 2, 640).transpose(0, 2, 1, 3).reshape(128, 1280)
-    cq_grad, terms = cross_grads(arrived, w_out_placed, cross_query, cap_key, cap_value, probs)
+    cq_grad, keep, send = cross_grads(
+        core.reshape(1), arrived, w_out_placed, cross_query, cap_value, probs, cap_key
+    )
+    chip = (keep.astype(jnp.float32) + swap_cores(send).astype(jnp.float32)).astype(jnp.bfloat16)
     grad_input = (
         jnp.dot(arrived, place, preferred_element_type=jnp.float32)
         + lax.dot_general(cq_grad, full_cross[0], CONTRACT_LAST, preferred_element_type=jnp.float32)
     ).astype(jnp.bfloat16)
-    head = jnp.sum(lax.all_to_all(terms, ("x", "y"), 0, 0).astype(jnp.float32), axis=0)
-    head = head.astype(jnp.bfloat16)
-    pieces = jnp.concatenate(
-        [head[:, :CAP].reshape(8, 9, CAP), head[:, CAP : 2 * CAP].reshape(8, 9, CAP)]
-    )
+    head = jnp.sum(lax.all_to_all(chip, ("x", "y"), 0, 0).astype(jnp.float32), axis=0)
+    pieces = head[:, :CAP].astype(jnp.bfloat16).reshape(1, 8, 9, CAP)
+    sides = jnp.arange(2).reshape(2, 1, 1, 1) == core
+    pieces = jnp.where(sides, pieces, jnp.zeros_like(pieces)).reshape(16, 9, CAP)
     piece = jnp.sum(lax.all_to_all(pieces, ("s", "z", "c"), 0, 0).astype(jnp.float32), axis=0)
     return (grad_input.reshape(frame_input.shape), piece.T)
 

time: 188 us -> 178 us (0.947)
  waiting for transfers between devices: 37.9 us -> 29.2 us
  local copies, waits for them, and re-layouts: 27.9 us -> 21.1 us
  starting transfers between devices: 67.1 us -> 63.8 us
  Pallas kernels: 25.3 us -> 28.4 us
  matrix products: 17 us -> 20 us
  other arithmetic: 9.82 us -> 12.3 us
    unnamed x63 -> x38, local copies, waits for them, and re-layouts: 13.7 us -> 4.85 us
    all_to_all x1, waiting for transfers between devices: 17.8 us -> 9.92 us  [local(): lax.all_to_all(chip, ('x', 'y'), 0, 0).astype(jnp.float32)]
    ppermute x3 -> x4, starting transfers between devices: 13.5 us -> 8.58 us  [swap_cores(): return lax.ppermute(block, 'c', [(0, 1), (1, 0)])]
    dot_general x1 -> x2, matrix products: 0.61 us -> 3.54 us  [the longest x1 1.77 us: local(): jnp.dot(heads_parts[0], place[:576], preferred_element_type=jnp.float32)]
    pallas_call x1, Pallas kernels: 7.95 us -> 10.7 us  [cross_grads(): pl.pallas_call(cross_kernel, in_specs=[pl.BlockSpec(memory_space=pltpu.SM...]
    convert_element_type x0 -> x1, other arithmetic: none -> 2.35 us  [local(): (keep.astype(jnp.float32) + swap_cores(send).astype(jnp.float32)).astype(...]
    ppermute x3 -> x4, waiting for transfers between devices: 1.43 us -> 3.69 us  [swap_cores(): return lax.ppermute(block, 'c', [(0, 1), (1, 0)])]
    reshape x2 -> x3, local copies, waits for them, and re-layouts: 0.06 us -> 2.22 us  [the longest x1 1.34 us: local(): qkv_near = near[:, :36, width:].reshape(144, 3 * width)]
  transfers between devices with their start and end apart: 14 -> 15, of which waited for: 8 -> 6; matrix products, arithmetic and copies ran while one was open for 18% -> 22% of each run, Pallas kernels for 9% -> 10%
where the time goes in v8:
time: 178 us; the launch traced here: 177 us
  starting transfers between devices  63.8 us (36%)
  waiting for transfers between devices  29.2 us (16%)
  Pallas kernels  28.4 us (16%)
  local copies, waits for them, and re-layouts  21.1 us (12%)
  matrix products  20 us (11%)
  other arithmetic  12.3 us (7%)
    pallas_call x1, Pallas kernels, cross_grads(): pl.pallas_call(cross_kernel, in_specs=[pl.BlockSpec(memory_space=pltpu.SM...  10.7 us
    all_to_all x1, waiting for transfers between devices, local(): lax.all_to_all(chip, ('x', 'y'), 0, 0).astype(jnp.float32)  9.92 us
    all_to_all x1, starting transfers between devices, local(): lax.all_to_all(pieces, ('s', 'z', 'c'), 0, 0).astype(jnp.float32)  9.79 us
    all_to_all x1, starting transfers between devices, local(): lax.all_to_all(jnp.broadcast_to(shard[None], (4,) + shard.shape), 'z', 0, 0)  9.01 us
    ppermute x4, starting transfers between devices, swap_cores(): return lax.ppermute(block, 'c', [(0, 1), (1, 0)])  8.58 us
    all_to_all x2, starting transfers between devices, gather_groups(): return lax.all_to_all(copies, ALL, 0, 0, axis_index_groups=groups)  8.49 us
    all_to_all x1, waiting for transfers between devices, local(): lax.all_to_all(jnp.broadcast_to(shard[None], (4,) + shard.shape), 'z', 0, 0)  8.23 us
    pallas_call x1, Pallas kernels, temporal_grads(): pl.pallas_call(temporal_kernel, out_shape=jax.ShapeDtypeStruct((rows, 3 *...  7.97 us
  transfers between devices with their start and end apart: 15, of which 6 were waited for; matrix products, arithmetic and copies ran while one was open for 22% of the time, Pallas kernels for 10%

profile of v8, /device:TPU:1, one launch (start us, length us, event | category | flops | bytes accessed | tf_op | source)
XLA Modules:
  0.0 176.6 jit_solution(12887753453004573881)
XLA Ops:
  0.6 1.0 pad_maximum_fusion.3
  1.6 0.1 broadcast_in_dim.54
  1.7 0.9 broadcast_in_dim.55
  2.6 9.0 %all-to-all-start = ((bf16[4,2,20736]{2,1,0:T(2,128)(2,1)}), bf16[4,2,20736]{2,1,0:T(2,128)(2,1)S(1)}, u32[]{:S(2)}, u32[]{:S(2)}) async-start(bf16[4,2,20736]{2,1,0:T(2,128)(2,1)} %broadcast_in_dim.55), calls=%async_computation | async-start | bytes 663552 | tf_op jit(solution)/shard_map/all_to_all | solution.py:324
  11.6 1.0 collective-permute-start
  12.6 8.2 %all-to-all-done = bf16[4,2,20736]{2,1,0:T(2,128)(2,1)S(1)} async-done(((bf16[4,2,20736]{2,1,0:T(2,128)(2,1)}), bf16[4,2,20736]{2,1,0:T(2,128)(2,1)S(1)}, u32[]{:S(2)}, u32[]{:S(2)}) %all-to-all-start) | async-done | bytes 331808 | tf_op jit(solution)/shard_map/all_to_all | solution.py:324
  20.8 0.2 reshape.70
  21.1 1.3 broadcast_in_dim.56
  22.3 4.2 %all-to-all-start.1 = ((bf16[4,40,4608]{2,1,0:T(8,128)(2,1)}), bf16[4,40,4608]{2,1,0:T(8,128)(2,1)S(1)}, u32[]{:S(2)}, u32[]{:S(2)}) async-start(bf16[4,40,4608]{2,1,0:T(8,128)(2,1)} %broadcast_in_dim.56), calls=%async_computation.1 | async-start | bytes 2949120 | tf_op jit(solution)/shard_map/all_to_all | solution.py:241
  26.5 3.1 %fusion.20 = (bf16[1280,1152]{1,0:T(8,128)(2,1)}, pred[1280,1152]{1,0:T(32,128)(4,1)}) fusion(s32[1280]{0:T(1024)S(1)} %copy-done.15), kind=kLoop, calls=%fused_computation.37 | loop fusion | flops 2949120 | bytes 4428800 | tf_op jit(solution)/shard_map/convert_element_type | solution.py:318
  29.6 1.2 pad.12.key_ref.key_hbm
  30.8 2.4 %pad.13.value_hbm = bf16[384,1152]{1,0:T(8,128)(2,1)} pad(bf16[300,1152]{1,0:T(8,128)(2,1)} %param.22, bf16[]{:T(256)} %constant.53.clone.1), padding=0_84x0_0 | pad | bytes 1575938 | tf_op jit(solution)/shard_map/jit(_pad)/pad | solution.py:331
  33.3 1.0 select_bitcast_fusion.3
  34.4 0.8 copy-done.12
  35.2 1.8 %fusion.13.residual_ref = bf16[256,640]{1,0:T(8,128)(2,1)S(1)} fusion(bf16[256,1152]{1,0:T(8,128)(2,1)S(1)} %bitcast.75, pred[1280,1152]{1,0:T(32,128)(4,1)} %get-tuple-element.41, s32[]{:T(128)S(6)} %select_n.81), kind=kOutput, calls=%fused_computation.27 | convolution fusion | flops 377651200 | bytes 1654788 | tf_op jit(solution)/shard_map/dot_general | solution.py:327
  37.0 1.5 all-to-all-done.1
  38.6 0.8 reshape.71
  39.4 2.1 %broadcast_in_dim.57 = bf16[4,144,1152]{2,1,0:T(8,128)(2,1)} broadcast(bf16[144,1152]{1,0:T(8,128)(2,1)} %reshape.71), dimensions={1,2} | broadcast | bytes 1658880 | tf_op jit(solution)/shard_map/broadcast_in_dim | solution.py:240
  41.5 4.3 %all-to-all-start.2 = ((bf16[4,144,1152]{2,1,0:T(8,128)(2,1)}), bf16[4,144,1152]{2,1,0:T(8,128)(2,1)}, u32[]{:S(2)}, u32[]{:S(2)}) async-start(bf16[4,144,1152]{2,1,0:T(8,128)(2,1)} %broadcast_in_dim.57), calls=%async_computation.2 | async-start | bytes 2654208 | tf_op jit(solution)/shard_map/all_to_all | solution.py:241
  45.8 2.6 %dynamic-slice_bitcast_fusion = bf16[576,1152]{1,0:T(8,128)(2,1)} fusion(bf16[2,576,1152]{2,1,0:T(8,128)(2,1)} %param.20, s32[]{:T(128)S(6)} %select_n.82), kind=kLoop, calls=%fused_computation.23 | loop fusion | bytes 2654212 | tf_op jit(solution)/shard_map/jit(dynamic_index_in_dim)/squeeze | solution.py:292
  48.4 2.9 %collective-permute-start.6 = (bf16[576,1152]{1,0:T(8,128)(2,1)}, bf16[576,1152]{1,0:T(8,128)(2,1)}, u32[]{:S(2)}, u32[]{:S(2)}) collective-permute-start(bf16[576,1152]{1,0:T(8,128)(2,1)} %dynamic-slice_bitcast_fusion), channel_id=1, source_target_pairs={{0,128},{1,135},{128,2},{129,1},{2,130},{3,129},{130,4},{131,3},{4... | collective-permute-start | bytes 3981320 | tf_op jit(solution)/shard_map/ppermute | solution.py:293
  51.3 1.1 slice.31
  52.4 1.3 reshape.79.w0
  53.7 1.5 collective-permute-start.2
  55.2 1.3 collective-permute-start.3
  56.5 1.7 collective-permute-start.4
  58.2 2.1 %convolution_convert_fusion.2 = bf16[256,576]{0,1:T(8,128)(2,1)S(1)} fusion(bf16[256,1152]{1,0:T(8,128)(2,1)} %bitcast.76, bf16[576,1152]{1,0:T(8,128)(2,1)} %bitcast.5), kind=kOutput, calls=%fused_computation.28 | convolution fusion | flops 339886080 | bytes 2211840 | tf_op jit(solution)/shard_map/dot_general | solution.py:346
  60.4 0.6 constant_dynamic-slice_fusion.1
  61.1 5.5 %collective-permute-start.1 = (bf16[128,576]{0,1:T(8,128)(2,1)S(1)}, bf16[128,576]{0,1:T(8,128)(2,1)S(1)}, u32[]{:S(2)}, u32[]{:S(2)}) collective-permute-start(bf16[128,576]{0,1:T(8,128)(2,1)S(1)} %bitcast.79), channel_id=1, source_target_pairs={{0,1},{1,0},{2,3},{3,2},{4,5},{5,4},{6,7},{7,6},{8,9},{9,8},{10,11... | collective-permute-start | bytes 442376 | tf_op jit(solution)/shard_map/ppermute | solution.py:256
  66.6 6.3 %collective-permute-start.7 = (bf16[576,1152]{1,0:T(8,128)(2,1)}, bf16[576,1152]{1,0:T(8,128)(2,1)}, u32[]{:S(2)}, u32[]{:S(2)}) collective-permute-start(bf16[576,1152]{1,0:T(8,128)(2,1)} %collective-permute-done.6), channel_id=1, source_target_pairs={{0,1},{1,0},{2,3},{3,2},{4,5},{5,4},{6,7},{7,6},{8,9},{9,8},{10,11... | collective-permute-start | bytes 3981320 | tf_op jit(solution)/shard_map/ppermute | solution.py:294
  72.9 1.8 fusion.10
  74.7 1.8 %fusion.6.grad_ref = bf16[128,1152]{1,0:T(8,128)(2,1)S(1)} fusion(f32[128,1152]{1,0:T(8,128)S(1)} %fusion.10, bf16[1280,1152]{1,0:T(8,128)(2,1)} %get-tuple-element.19, bf16[128,576]{0,1:T(8,128)(2,1)S(1)} %collective-permute-done.1, pred[]{:T(512)S(6)} %eq.39, bf16[1,128,576]{1,0,2:T(2,128)(2,1)S(1)} %get-tuple-element.38), kind=kOutput, calls=%fused_computation.15 | convolution fusion | flops 170237952 | bytes 2506753 | tf_op jit(solution)/shard_map/dot_general | solution.py:354
  76.5 8.0 %temporal_grads.1.mine_ref = bf16[128,3456]{1,0:T(8,128)(2,1)S(1)} custom-call(bf16[128,1152]{1,0:T(8,128)(2,1)S(1)} %fusion.6.grad_ref, bf16[128,1152]{1,0:T(8,128)(2,1)S(1)} %bitcast.68, bf16[128,1152]{1,0:T(8,128)(2,1)S(1)} %bitcast.69, bf16[128,1152]{1,0:T(8,128)(2,1)S(1)} %bitcast.70), custom_call_target="tpu_custom_call" | custom-call | flops 147456 | bytes 294912 | tf_op jit(solution)/shard_map/temporal_grads/pallas_call | solution.py:65
  84.5 0.9 collective-permute-start.5
  86.1 0.1 pad_add_fusion.place_ref
  86.2 1.4 collective-permute-done.5.other_ref
  87.6 5.0 %mixed_half.1 = bf16[256,640]{1,0:T(8,128)(2,1)S(1)} custom-call(s32[5]{0:T(128)S(1)} %pad_add_fusion.place_ref, bf16[128,3456]{1,0:T(8,128)(2,1)S(1)} %temporal_grads.1.mine_ref, bf16[128,3456]{1,0:T(8,128)(2,1)} %collective-permute-done.5.other_ref, bf16[256,640]{1,0:T(8,128)(2,1)S(1)} %fusion.13.residual_ref, bf16[144,3456]{1,0:T(8,128)(2,1)S(1)} %reshape.79.w0, ...), custom_call_target="tpu_custom_call" | custom-call | flops 1132462080 | bytes 8388608 | tf_op jit(solution)/shard_map/mixed_half/pallas_call | solution.py:102
  92.6 1.1 copy.53
  93.6 7.8 %all-to-all-start.3 = ((bf16[128,2,640]{2,1,0:T(2,128)(2,1)}), bf16[128,2,640]{2,1,0:T(2,128)(2,1)S(1)}, u32[]{:S(2)}, u32[]{:S(2)}) async-start(bf16[128,2,640]{2,1,0:T(2,128)(2,1)} %bitcast.64), calls=%async_computation.3 | async-start | bytes 655360 | tf_op jit(solution)/shard_map/all_to_all | solution.py:371
  101.5 2.1 %select_bitcast_fusion.1 = (bf16[1,576,1152]{2,1,0:T(8,128)(2,1)S(1)}, bf16[1,576,1152]{2,1,0:T(8,128)(2,1)S(1)}) fusion(bf16[576,1152]{1,0:T(8,128)(2,1)} %collective-permute-done.6, bf16[576,1152]{1,0:T(8,128)(2,1)} %collective-permute-done.7, pred[]{:T(512)S(6)} %eq.39), kind=kLoop, calls=%fused_computation.22 | loop fusion | flops 1327104 | bytes 5308417 | tf_op jit(solution)/shard_map/stack | solution.py:295
  103.6 0.4 copy-done.11
  104.0 0.5 broadcast_select_fusion
  104.6 0.6 fusion.8.query_ref.query_hbm
  105.2 4.8 %cross_probs.1.probs_hbm = f32[16,128,384]{2,1,0:T(8,128)S(1)} custom-call(s32[1]{0:T(128)S(6)} %copy.57.length_ref, bf16[128,1152]{1,0:T(8,128)(2,1)S(1)} %fusion.8.query_ref.query_hbm, bf16[384,1152]{1,0:T(8,128)(2,1)S(1)} %pad.12.key_ref.key_hbm), custom_call_target="tpu_custom_call" | custom-call | flops 113246208 | bytes 4194304 | tf_op jit(solution)/shard_map/cross_probs/pallas_call | solution.py:134
  110.1 1.6 copy-done.1
  111.7 5.9 %convolution_convert_fusion.w_out_hbm = bf16[1280,1152]{1,0:T(8,128)(2,1)} fusion(bf16[1280,1152]{1,0:T(8,128)(2,1)S(1)} %copy-done.7, bf16[2,576,1152]{2,1,0:T(8,128)(2,1)S(1)} %get-tuple-element.33, bf16[2,576,1152]{2,1,0:T(8,128)(2,1)S(1)} %get-tuple-element.32), kind=kOutput, calls=%fused_computation | convolution fusion | flops 3404169216 | bytes 11206656 | tf_op jit(solution)/shard_map/dot_general | solution.py:364
  117.6 0.3 copy.36
  117.8 0.8 copy.42
  118.6 10.7 %cross_grads.1 = (bf16[128,1152]{1,0:T(8,128)(2,1)}, bf16[16,72,384]{2,1,0:T(8,128)(2,1)}, bf16[16,72,384]{2,1,0:T(8,128)(2,1)}) custom-call(s32[1]{0:T(128)} %bitcast.core_ref, bf16[128,1280]{1,0:T(8,128)(2,1)} %bitcast.71, bf16[1280,1152]{1,0:T(8,128)(2,1)} %convolution_convert_fusion.w_out_hbm, bf16[128,1152]{1,0:T(8,128)(2,1)} %copy-done.3, ...), custom_call_target="tpu_custom_call" | custom-call | flops 830472192 | bytes 12582912 | tf_op jit(solution)/shard_map/cross_grads/pallas_call | solution.py:202
  129.3 1.2 collective-permute-start.8
  130.5 2.3 %collective-permute-done.8 = bf16[16,72,384]{2,1,0:T(8,128)(2,1)S(1)} collective-permute-done((bf16[16,72,384]{2,1,0:T(8,128)(2,1)}, bf16[16,72,384]{2,1,0:T(8,128)(2,1)S(1)}, u32[]{:S(2)}, u32[]{:S(2)}) %collective-permute-start.8) | collective-permute-done | bytes 884768 | tf_op jit(solution)/shard_map/ppermute | solution.py:256
  132.8 2.3 %add_convert_fusion = bf16[16,72,384]{2,1,0:T(8,128)(2,1)} fusion(bf16[16,72,384]{2,1,0:T(8,128)(2,1)S(1)} %collective-permute-done.8, bf16[16,72,384]{2,1,0:T(8,128)(2,1)} %get-tuple-element.30), kind=kLoop, calls=%fused_computation.20 | loop fusion | flops 1769472 | bytes 2654208 | tf_op jit(solution)/shard_map/convert_element_type | solution.py:376
  135.1 6.4 %all-to-all-start.4 = ((bf16[16,72,384]{2,1,0:T(8,128)(2,1)}), bf16[16,72,384]{2,1,0:T(8,128)(2,1)}, u32[]{:S(2)}, u32[]{:S(2)}) async-start(bf16[16,72,384]{2,1,0:T(8,128)(2,1)} %add_convert_fusion), calls=%async_computation.4 | async-start | bytes 1769472 | tf_op jit(solution)/shard_map/all_to_all | solution.py:381
  141.6 0.1 broadcast_in_dim.59
  141.7 3.6 %fusion.16 = f32[128,1152]{1,0:T(8,128)} fusion(bf16[128,1152]{1,0:T(8,128)(2,1)S(1)} %copy-done.13, bf16[2,576,1152]{2,1,0:T(8,128)(2,1)} %copy-done.9, bf16[2,576,1152]{2,1,0:T(8,128)(2,1)} %copy-done.10), kind=kOutput, calls=%fused_computation.30 | convolution fusion | flops 345047040 | bytes 6193152 | tf_op jit(solution)/shard_map/dot_general | solution.py:379
  145.4 9.9 %all-to-all-done.4 = bf16[16,72,384]{2,1,0:T(8,128)(2,1)} async-done(((bf16[16,72,384]{2,1,0:T(8,128)(2,1)}), bf16[16,72,384]{2,1,0:T(8,128)(2,1)}, u32[]{:S(2)}, u32[]{:S(2)}) %all-to-all-start.4) | async-done | bytes 884768 | tf_op jit(solution)/shard_map/all_to_all | solution.py:381
  155.3 1.3 reduce
  156.6 0.1 bitcast_select_fusion
  156.7 0.9 reshape.85
  157.6 9.8 %all-to-all-start.5 = ((bf16[16,2,1350]{2,1,0:T(2,128)(2,1)}), bf16[16,2,1350]{2,1,0:T(2,128)(2,1)S(1)}, u32[]{:S(2)}, u32[]{:S(2)}) async-start(bf16[16,2,1350]{2,1,0:T(2,128)(2,1)} %reshape.85), calls=%async_computation.5 | async-start | bytes 180224 | tf_op jit(solution)/shard_map/all_to_all | solution.py:385
  167.4 2.5 %fusion.9 = bf16[1,128,1152]{2,1,0:T(8,128)(2,1)} fusion(f32[128,1152]{1,0:T(8,128)} %fusion.16, bf16[128,1280]{1,0:T(8,128)(2,1)} %bitcast.72, bf16[1280,1152]{1,0:T(8,128)(2,1)S(1)} %copy-done.8), kind=kOutput, calls=%fused_computation.19 | convolution fusion | flops 377782272 | bytes 4161536 | tf_op jit(solution)/shard_map/dot_general | solution.py:378
  169.9 5.8 %all-to-all-done.5 = bf16[16,2,1350]{2,1,0:T(2,128)(2,1)S(1)} async-done(((bf16[16,2,1350]{2,1,0:T(2,128)(2,1)}), bf16[16,2,1350]{2,1,0:T(2,128)(2,1)S(1)}, u32[]{:S(2)}, u32[]{:S(2)}) %all-to-all-start.5) | async-done | bytes 86432 | tf_op jit(solution)/shard_map/all_to_all | solution.py:385
  175.7 0.2 reshape.86
  175.9 0.7 convert_reduce_fusion
  (49 shorter events, 0.4 us)
Async XLA Ops:
  0.6 104.0 %copy-start = (bf16[1,128,1152]{2,1,0:T(8,128)(2,1)S(1)}, bf16[1,128,1152]{2,1,0:T(8,128)(2,1)}, u32[]{:S(2)}) copy-start(bf16[1,128,1152]{2,1,0:T(8,128)(2,1)} %param.19) | copy-start | bytes 884740
  2.6 18.2 %all-to-all-start = ((bf16[4,2,20736]{2,1,0:T(2,128)(2,1)}), bf16[4,2,20736]{2,1,0:T(2,128)(2,1)S(1)}, u32[]{:S(2)}, u32[]{:S(2)}) async-start(bf16[4,2,20736]{2,1,0:T(2,128)(2,1)} %broadcast_in_dim.55), calls=%async_computation | async-start | bytes 663552 | tf_op jit(solution)/shard_map/all_to_all | solution.py:324
  11.6 21.6 %collective-permute-start = (bf16[128,1152]{1,0:T(8,128)(2,1)}, bf16[128,1152]{1,0:T(8,128)(2,1)}, u32[]{:S(2)}, u32[]{:S(2)}) collective-permute-start(bf16[128,1152]{1,0:T(8,128)(2,1)} %bitcast.77), channel_id=1, source_target_pairs={{0,1},{1,0},{2,3},{3,2},{4,5},{5,4},{6,7},{7,6},{8,9},{9,8},{10,11... | collective-permute-start | bytes 884744 | tf_op jit(solution)/shard_map/ppermute | solution.py:256
  21.0 5.5 %copy-start.15 = (s32[1280]{0:T(1024)S(1)}, s32[1280]{0:T(1024)}, u32[]{:S(2)}) copy-start(s32[1280]{0:T(1024)} %constant.60.clone) | copy-start | bytes 15364
  22.3 16.2 %all-to-all-start.1 = ((bf16[4,40,4608]{2,1,0:T(8,128)(2,1)}), bf16[4,40,4608]{2,1,0:T(8,128)(2,1)S(1)}, u32[]{:S(2)}, u32[]{:S(2)}) async-start(bf16[4,40,4608]{2,1,0:T(8,128)(2,1)} %broadcast_in_dim.56), calls=%async_computation.1 | async-start | bytes 2949120 | tf_op jit(solution)/shard_map/all_to_all | solution.py:241
  29.6 3.7 %copy-start.14 = (bf16[2,64,1,1152]{3,1,2,0:T(8,128)(2,1)S(1)}, bf16[2,64,1,1152]{3,1,2,0:T(8,128)(2,1)}, u32[]{:S(2)}) copy-start(bf16[2,64,1,1152]{3,1,2,0:T(8,128)(2,1)} %param.13) | copy-start | bytes 884740
  30.8 74.4 %copy-start.2 = (bf16[384,1152]{1,0:T(8,128)(2,1)}, bf16[384,1152]{1,0:T(8,128)(2,1)S(1)}, u32[]{:S(2)}) copy-start(bf16[384,1152]{1,0:T(8,128)(2,1)S(1)} %pad.12.key_ref.key_hbm) | copy-start | bytes 2654212
  34.3 0.8 copy-start.12
  41.5 16.7 %all-to-all-start.2 = ((bf16[4,144,1152]{2,1,0:T(8,128)(2,1)}), bf16[4,144,1152]{2,1,0:T(8,128)(2,1)}, u32[]{:S(2)}, u32[]{:S(2)}) async-start(bf16[4,144,1152]{2,1,0:T(8,128)(2,1)} %broadcast_in_dim.57), calls=%async_computation.2 | async-start | bytes 2654208 | tf_op jit(solution)/shard_map/all_to_all | solution.py:241
  48.4 18.2 %collective-permute-start.6 = (bf16[576,1152]{1,0:T(8,128)(2,1)}, bf16[576,1152]{1,0:T(8,128)(2,1)}, u32[]{:S(2)}, u32[]{:S(2)}) collective-permute-start(bf16[576,1152]{1,0:T(8,128)(2,1)} %dynamic-slice_bitcast_fusion), channel_id=1, source_target_pairs={{0,128},{1,135},{128,2},{129,1},{2,130},{3,129},{130,4},{131,3},{4... | collective-permute-start | bytes 3981320 | tf_op jit(solution)/shard_map/ppermute | solution.py:293
  53.7 30.8 %collective-permute-start.2 = (bf16[144,3456]{1,0:T(8,128)(2,1)S(1)}, bf16[144,3456]{1,0:T(8,128)(2,1)}, u32[]{:S(2)}, u32[]{:S(2)}) collective-permute-start(bf16[144,3456]{1,0:T(8,128)(2,1)S(1)} %reshape.79.w0), channel_id=1, source_target_pairs={{0,8},{1,33},{2,10},{3,35},{4,12},{5,37},{6,14},{7,39},{8,16},{9,4... | collective-permute-start | bytes 2985992 | tf_op jit(solution)/shard_map/ppermute | solution.py:252
  55.2 29.3 %collective-permute-start.3 = (bf16[144,3456]{1,0:T(8,128)(2,1)S(1)}, bf16[144,3456]{1,0:T(8,128)(2,1)}, u32[]{:S(2)}, u32[]{:S(2)}) collective-permute-start(bf16[144,3456]{1,0:T(8,128)(2,1)S(1)} %reshape.79.w0), channel_id=1, source_target_pairs={{0,24},{1,97},{2,26},{3,99},{4,28},{5,101},{6,30},{7,103},{8,0},{9... | collective-permute-start | bytes 2985992 | tf_op jit(solution)/shard_map/ppermute | solution.py:252
  56.5 28.0 %collective-permute-start.4 = (bf16[144,3456]{1,0:T(8,128)(2,1)S(1)}, bf16[144,3456]{1,0:T(8,128)(2,1)}, u32[]{:S(2)}, u32[]{:S(2)}) collective-permute-start(bf16[144,3456]{1,0:T(8,128)(2,1)S(1)} %reshape.79.w0), channel_id=1, source_target_pairs={{0,16},{1,65},{2,18},{3,67},{4,20},{5,69},{6,22},{7,71},{8,24},{9,... | collective-permute-start | bytes 2985992 | tf_op jit(solution)/shard_map/ppermute | solution.py:252
  61.0 15.5 %copy-start.4 = (bf16[2,64,1,1152]{3,1,2,0:T(8,128)(2,1)S(1)}, bf16[2,64,1,1152]{3,1,2,0:T(8,128)(2,1)}, u32[]{:S(2)}) copy-start(bf16[2,64,1,1152]{3,1,2,0:T(8,128)(2,1)} %param.14) | copy-start | bytes 884740
  61.0 15.5 %copy-start.5 = (bf16[2,64,1,1152]{3,1,2,0:T(8,128)(2,1)S(1)}, bf16[2,64,1,1152]{3,1,2,0:T(8,128)(2,1)}, u32[]{:S(2)}) copy-start(bf16[2,64,1,1152]{3,1,2,0:T(8,128)(2,1)} %param.15) | copy-start | bytes 884740
  61.0 15.5 %copy-start.6 = (bf16[2,64,1,1152]{3,1,2,0:T(8,128)(2,1)S(1)}, bf16[2,64,1,1152]{3,1,2,0:T(8,128)(2,1)}, u32[]{:S(2)}) copy-start(bf16[2,64,1,1152]{3,1,2,0:T(8,128)(2,1)} %param.16) | copy-start | bytes 884740
  61.1 11.9 %collective-permute-start.1 = (bf16[128,576]{0,1:T(8,128)(2,1)S(1)}, bf16[128,576]{0,1:T(8,128)(2,1)S(1)}, u32[]{:S(2)}, u32[]{:S(2)}) collective-permute-start(bf16[128,576]{0,1:T(8,128)(2,1)S(1)} %bitcast.79), channel_id=1, source_target_pairs={{0,1},{1,0},{2,3},{3,2},{4,5},{5,4},{6,7},{7,6},{8,9},{9,8},{10,11... | collective-permute-start | bytes 442376 | tf_op jit(solution)/shard_map/ppermute | solution.py:256
  66.6 34.9 %collective-permute-start.7 = (bf16[576,1152]{1,0:T(8,128)(2,1)}, bf16[576,1152]{1,0:T(8,128)(2,1)}, u32[]{:S(2)}, u32[]{:S(2)}) collective-permute-start(bf16[576,1152]{1,0:T(8,128)(2,1)} %collective-permute-done.6), channel_id=1, source_target_pairs={{0,1},{1,0},{2,3},{3,2},{4,5},{5,4},{6,7},{7,6},{8,9},{9,8},{10,11... | collective-permute-start | bytes 3981320 | tf_op jit(solution)/shard_map/ppermute | solution.py:294
  74.7 11.4 %copy-start.16 = (s32[4]{0:T(128)S(1)}, s32[4]{0:T(128)}, u32[]{:S(2)}) copy-start(s32[4]{0:T(128)} %constant.75) | copy-start | bytes 52
  84.5 3.1 %collective-permute-start.5 = (bf16[128,3456]{1,0:T(8,128)(2,1)S(1)}, bf16[128,3456]{1,0:T(8,128)(2,1)}, u32[]{:S(2)}, u32[]{:S(2)}) collective-permute-start(bf16[128,3456]{1,0:T(8,128)(2,1)S(1)} %temporal_grads.1.mine_ref), channel_id=1, source_target_pairs={{0,1},{1,0},{2,3},{3,2},{4,5},{5,4},{6,7},{7,6},{8,9},{9,8},{10,11... | collective-permute-start | bytes 2654216 | tf_op jit(solution)/shard_map/ppermute | solution.py:256
  93.6 23.9 %all-to-all-start.3 = ((bf16[128,2,640]{2,1,0:T(2,128)(2,1)}), bf16[128,2,640]{2,1,0:T(2,128)(2,1)S(1)}, u32[]{:S(2)}, u32[]{:S(2)}) async-start(bf16[128,2,640]{2,1,0:T(2,128)(2,1)} %bitcast.64), calls=%async_computation.3 | async-start | bytes 655360 | tf_op jit(solution)/shard_map/all_to_all | solution.py:371
  101.5 2.6 %copy-start.11 = (bf16[2,576,1152]{2,1,0:T(8,128)(2,1)S(1)}, bf16[2,576,1152]{2,1,0:T(8,128)(2,1)}, u32[]{:S(2)}) copy-start(bf16[2,576,1152]{2,1,0:T(8,128)(2,1)} %param.20) | copy-start | bytes 7962628
  104.6 5.5 %copy-start.9 = (bf16[2,576,1152]{2,1,0:T(8,128)(2,1)}, bf16[2,576,1152]{2,1,0:T(8,128)(2,1)S(1)}, u32[]{:S(2)}) copy-start(bf16[2,576,1152]{2,1,0:T(8,128)(2,1)S(1)} %get-tuple-element.32) | copy-start | bytes 7962628
  104.6 5.5 %copy-start.10 = (bf16[2,576,1152]{2,1,0:T(8,128)(2,1)}, bf16[2,576,1152]{2,1,0:T(8,128)(2,1)S(1)}, u32[]{:S(2)}) copy-start(bf16[2,576,1152]{2,1,0:T(8,128)(2,1)S(1)} %get-tuple-element.33) | copy-start | bytes 7962628
  105.2 12.3 %copy-start.3 = (bf16[128,1152]{1,0:T(8,128)(2,1)}, bf16[128,1152]{1,0:T(8,128)(2,1)S(1)}, u32[]{:S(2)}) copy-start(bf16[128,1152]{1,0:T(8,128)(2,1)S(1)} %fusion.8.query_ref.query_hbm) | copy-start | bytes 884740
  105.2 6.5 %copy-start.7 = (bf16[1280,1152]{1,0:T(8,128)(2,1)S(1)}, bf16[1280,1152]{1,0:T(8,128)(2,1)}, u32[]{:S(2)}) copy-start(bf16[1280,1152]{1,0:T(8,128)(2,1)} %get-tuple-element.19) | copy-start | bytes 8847364
  110.0 1.6 copy-start.1
  129.3 12.4 %copy-start.13 = (bf16[128,1152]{1,0:T(8,128)(2,1)S(1)}, bf16[128,1152]{1,0:T(8,128)(2,1)}, u32[]{:S(2)}) copy-start(bf16[128,1152]{1,0:T(8,128)(2,1)} %get-tuple-element.29) | copy-start | bytes 884740
  129.3 3.5 %collective-permute-start.8 = (bf16[16,72,384]{2,1,0:T(8,128)(2,1)}, bf16[16,72,384]{2,1,0:T(8,128)(2,1)S(1)}, u32[]{:S(2)}, u32[]{:S(2)}) collective-permute-start(bf16[16,72,384]{2,1,0:T(8,128)(2,1)} %get-tuple-element.31), channel_id=1, source_target_pairs={{0,1},{1,0},{2,3},{3,2},{4,5},{5,4},{6,7},{7,6},{8,9},{9,8},{10,11... | collective-permute-start | bytes 2654216 | tf_op jit(solution)/shard_map/ppermute | solution.py:256
  135.1 20.1 %all-to-all-start.4 = ((bf16[16,72,384]{2,1,0:T(8,128)(2,1)}), bf16[16,72,384]{2,1,0:T(8,128)(2,1)}, u32[]{:S(2)}, u32[]{:S(2)}) async-start(bf16[16,72,384]{2,1,0:T(8,128)(2,1)} %add_convert_fusion), calls=%async_computation.4 | async-start | bytes 1769472 | tf_op jit(solution)/shard_map/all_to_all | solution.py:381
  141.7 25.6 %copy-start.8 = (bf16[1280,1152]{1,0:T(8,128)(2,1)S(1)}, bf16[1280,1152]{1,0:T(8,128)(2,1)}, u32[]{:S(2)}) copy-start(bf16[1280,1152]{1,0:T(8,128)(2,1)} %get-tuple-element.19) | copy-start | bytes 8847364
  157.6 18.1 %all-to-all-start.5 = ((bf16[16,2,1350]{2,1,0:T(2,128)(2,1)}), bf16[16,2,1350]{2,1,0:T(2,128)(2,1)S(1)}, u32[]{:S(2)}, u32[]{:S(2)}) async-start(bf16[16,2,1350]{2,1,0:T(2,128)(2,1)} %reshape.85), calls=%async_computation.5 | async-start | bytes 180224 | tf_op jit(solution)/shard_map/all_to_all | solution.py:385

commit v9 on v8

--- a/solution.py
+++ b/solution.py
@@ -35,8 +35,18 @@
     return (attention * centred * SCALE).astype(jnp.bfloat16)
 
 
-def temporal_kernel(grad_ref, query_ref, key_ref, value_ref, out_ref):
-    rows, width = grad_ref.shape
+def temporal_kernel(
+    core_ref, kept_ref, got_ref, order_ref, query_ref, key_ref, value_ref, out_ref, grad_ref
+):
+    rows, width = query_ref.shape
+    half = kept_ref.shape[1]
+    start = order_ref.shape[0] // 2
+    kept, got = kept_ref[...], got_ref[...]
+    first = core_ref[0] == 0
+    grad_ref[...] = (
+        dot(jnp.where(first, kept, got), order_ref[:half])
+        + dot(jnp.where(first, got, kept), order_ref[start : start + half])
+    ).astype(jnp.bfloat16)
     frames = rows // 2
     same = (lax.broadcasted_iota(jnp.int32, (rows, rows), 0) < frames) == (
         lax.broadcasted_iota(jnp.int32, (rows, rows), 1) < frames
@@ -60,17 +70,21 @@
             out_ref[:, start : start + HEAD_DIM] = result.astype(jnp.bfloat16)
 
 
-def temporal_grads(grad_heads, query, key_rows, value):
-    rows, width = grad_heads.shape
+def temporal_grads(core, kept, got, order, query, key_rows, value):
+    rows, width = query.shape
     return pl.pallas_call(
         temporal_kernel,
+        in_specs=[pl.BlockSpec(memory_space=pltpu.SMEM)]
+        + [pl.BlockSpec(memory_space=pltpu.VMEM)] * 6,
+        out_specs=pl.BlockSpec(memory_space=pltpu.VMEM),
         out_shape=jax.ShapeDtypeStruct((rows, 3 * width), jnp.bfloat16),
-        compiler_params=pltpu.CompilerParams(vmem_limit_bytes=24 << 20),
+        scratch_shapes=[pltpu.VMEM((rows, width), jnp.bfloat16)],
+        compiler_params=pltpu.CompilerParams(vmem_limit_bytes=16 << 20),
         cost_estimate=pl.CostEstimate(
             flops=rows * width, bytes_accessed=2 * rows * width, transcendentals=0
         ),
         name="temporal_grads",
-    )(grad_heads, query, key_rows, value)
+    )(core, kept, got, order, query, key_rows, value)
 
 
 def mixed_kernel(
@@ -152,8 +166,8 @@
     w_out_hbm,
     query_hbm,
     value_hbm,
-    probs_hbm,
     key_hbm,
+    probs_ref,
     cq_ref,
     keep_ref,
     send_ref,
@@ -161,13 +175,12 @@
     w_out_ref,
     query_ref,
     value_ref,
-    probs_ref,
     key_ref,
     og_ref,
     sems,
 ):
-    held = (arrived_ref, w_out_ref, query_ref, value_ref, probs_ref, key_ref)
-    given = (arrived_hbm, w_out_hbm, query_hbm, value_hbm, probs_hbm, key_hbm)
+    held = (arrived_ref, w_out_ref, query_ref, value_ref, key_ref)
+    given = (arrived_hbm, w_out_hbm, query_hbm, value_hbm, key_hbm)
     copies = [
         pltpu.make_async_copy(source, target, sems.at[i])
         for i, (source, target) in enumerate(zip(given, held))
@@ -194,27 +207,28 @@
         send_ref[head] = jnp.where(first, value_term, key_term).astype(jnp.bfloat16)
 
 
-def cross_grads(core, arrived, w_out, cross_query, cap_value, probs, cap_key):
+def cross_grads(core, arrived, w_out, cross_query, cap_value, cap_key, probs):
     rows, width = cross_query.shape
     in_vmem = pl.BlockSpec(memory_space=pltpu.VMEM)
-    copied = (arrived, w_out, cross_query, cap_value, probs, cap_key)
+    copied = (arrived, w_out, cross_query, cap_value, cap_key)
     term = jax.ShapeDtypeStruct((HEADS, HEAD_DIM, CAP_PAD), jnp.bfloat16)
     return pl.pallas_call(
         cross_kernel,
         in_specs=[pl.BlockSpec(memory_space=pltpu.SMEM)]
-        + [pl.BlockSpec(memory_space=pl.ANY)] * 6,
+        + [pl.BlockSpec(memory_space=pl.ANY)] * 5
+        + [in_vmem],
         out_specs=(in_vmem,) * 3,
         out_shape=(jax.ShapeDtypeStruct((rows, width), jnp.bfloat16), term, term),
         scratch_shapes=[pltpu.VMEM(array.shape, array.dtype) for array in copied]
-        + [pltpu.VMEM((rows, width), jnp.bfloat16), pltpu.SemaphoreType.DMA((6,))],
-        compiler_params=pltpu.CompilerParams(vmem_limit_bytes=56 << 20),
+        + [pltpu.VMEM((rows, width), jnp.bfloat16), pltpu.SemaphoreType.DMA((5,))],
+        compiler_params=pltpu.CompilerParams(vmem_limit_bytes=54 << 20),
         cost_estimate=pl.CostEstimate(
             flops=8 * rows * CAP_PAD * width + 2 * rows * width * arrived.shape[1],
             bytes_accessed=12 << 20,
             transcendentals=0,
         ),
         name="cross_grads",
-    )(core, *copied)
+    )(core, *copied, probs)
 
 
 ALL = ("s", "x", "y", "z", "c")
@@ -273,10 +287,7 @@
     return order.reshape(1280)
 
 
-def cross_halves(cross_weights):
-    core = lax.axis_index("c")
-    side = lax.axis_index("s")
-
+def cross_fetch(part):
     def place(z):
         return (z % 2, z // 2)
 
@@ -289,8 +300,12 @@
                     s0, z0 = place(z)
                     s1, z1 = place(to)
                     pairs.append((flat(s0, x, y, z0, c), flat(s1, x, y, z1, c)))
-    part = lax.dynamic_index_in_dim(cross_weights, core, 0, keepdims=False)
-    got = lax.ppermute(part, ALL, pairs)
+    return lax.ppermute(part, ALL, pairs)
+
+
+def cross_whole(cross_weights, got):
+    core = lax.axis_index("c")
+    side = lax.axis_index("s")
     swapped = lax.ppermute(got, "c", [(0, 1), (1, 0)])
     other = jnp.stack([jnp.where(core == 0, got, swapped), jnp.where(core == 0, swapped, got)])
     low = jnp.where(side == 0, cross_weights, other)
@@ -330,9 +345,10 @@
     padding = ((0, CAP_PAD - CAP), (0, 0))
     cap_key, cap_value = jnp.pad(cap_key, padding), jnp.pad(cap_value, padding)
     out_near = near[:, :36, :width].reshape(144, width)
-    out_near, cross_weights, grad_both, residual, place, cap_key, cap_value = (
+    cross_part = lax.dynamic_index_in_dim(cross_weights, core, 0, keepdims=False)
+    out_near, cross_part, grad_both, residual, place, cap_key, cap_value = (
         lax.optimization_barrier(
-            (out_near, cross_weights, grad_both, residual, place, cap_key, cap_value)
+            (out_near, cross_part, grad_both, residual, place, cap_key, cap_value)
         )
     )
     qkv_near = near[:, :36, width:].reshape(144, 3 * width)
@@ -341,7 +357,7 @@
     slots = (place_here - jnp.array([0, 1, 3, 2], jnp.int32)) % 4
     places = jnp.concatenate([slots, core.reshape(1)])
     out_mine = gather_groups(out_near, ring_groups(1)).reshape(576, width)
-    full_cross = cross_halves(cross_weights)
+    cross_part = cross_fetch(cross_part)
     heads_mine = (
         lax.dot_general(grad_both, out_mine, CONTRACT_LAST, preferred_element_type=jnp.float32)
         .astype(jnp.bfloat16)
@@ -349,15 +365,15 @@
     )
     kept = lax.dynamic_index_in_dim(heads_mine, core, 0, keepdims=False)
     sent = lax.dynamic_index_in_dim(heads_mine, 1 - core, 0, keepdims=False)
-    heads_parts = in_core_order(kept, swap_cores(sent))
-    grad_heads = (
-        jnp.dot(heads_parts[0], place[:576], preferred_element_type=jnp.float32)
-        + jnp.dot(heads_parts[1], place[640:1216], preferred_element_type=jnp.float32)
-    ).astype(jnp.bfloat16)
     qkv_grad = temporal_grads(
-        grad_heads, *(saved.reshape(rows, width) for saved in (t_query, t_key, t_value))
-    )
-    qkv_grad, *blocks = lax.optimization_barrier((qkv_grad, *blocks))
+        core.reshape(1),
+        kept,
+        swap_cores(sent),
+        place,
+        *(saved.reshape(rows, width) for saved in (t_query, t_key, t_value)),
+    )
+    qkv_grad, cross_part, *blocks = lax.optimization_barrier((qkv_grad, cross_part, *blocks))
+    full_cross = cross_whole(cross_weights, cross_part)
     mixed = mixed_half(
         places, qkv_grad, swap_cores(qkv_grad), residual, blocks
     ).reshape(2, rows, 640)
@@ -371,7 +387,7 @@
     arrived = lax.all_to_all(mixed.transpose(1, 0, 2), SEQ, split_axis=0, concat_axis=0)
     arrived = arrived.reshape(64, 2, 2, 640).transpose(0, 2, 1, 3).reshape(128, 1280)
     cq_grad, keep, send = cross_grads(
-        core.reshape(1), arrived, w_out_placed, cross_query, cap_value, probs, cap_key
+        core.reshape(1), arrived, w_out_placed, cross_query, cap_value, cap_key, probs
     )
     chip = (keep.astype(jnp.float32) + swap_cores(send).astype(jnp.float32)).astype(jnp.bfloat16)
     grad_input = (

time: 178 us -> 191 us (1.073)
  local copies, waits for them, and re-layouts: 21.1 us -> 37.8 us
  starting transfers between devices: 63.8 us -> 60.2 us
  Pallas kernels: 28.4 us -> 31 us
  matrix products: 20 us -> 17.7 us
    unnamed x38 -> x35, local copies, waits for them, and re-layouts: 4.85 us -> 10.1 us
    dot_general x2 -> x0, matrix products: 3.54 us -> none  [the longest x1 1.77 us: local(): jnp.dot(heads_parts[0], place[:576], preferred_element_type=jnp.float32)]
    ppermute x4, waiting for transfers between devices: 3.69 us -> 6.82 us  [swap_cores(): return lax.ppermute(block, 'c', [(0, 1), (1, 0)])]
    all_to_all x1, waiting for transfers between devices: 8.23 us -> 5.26 us  [local(): lax.all_to_all(jnp.broadcast_to(shard[None], (4,) + shard.shape), 'z', 0, 0)]
    ppermute x2, starting transfers between devices: 9.23 us -> 6.37 us  [the longest x1 3.39 us: cross_whole(): swapped = lax.ppermute(got, 'c', [(0, 1), (1, 0)])]
  transfers between devices with their start and end apart: 15 -> 15, of which waited for: 6 -> 7; matrix products, arithmetic and copies ran while one was open for 22% -> 23% of each run, Pallas kernels for 10% -> 10%
where the time goes in v9:
time: 191 us; the launch traced here: 189 us
  starting transfers between devices  60.2 us (32%)
  local copies, waits for them, and re-layouts  37.8 us (20%)
  Pallas kernels  31 us (16%)
  waiting for transfers between devices  28.7 us (15%)
  matrix products  17.7 us (9%)
  other arithmetic  12.3 us (6%)
    pallas_call x1, Pallas kernels, cross_grads(): pl.pallas_call(cross_kernel, in_specs=[pl.BlockSpec(memory_space=pltpu.SM...  11.7 us
    all_to_all x1, starting transfers between devices, local(): lax.all_to_all(pieces, ('s', 'z', 'c'), 0, 0).astype(jnp.float32)  10.1 us
    unnamed x35, local copies, waits for them, and re-layouts  10.1 us
    all_to_all x1, waiting for transfers between devices, local(): lax.all_to_all(chip, ('x', 'y'), 0, 0).astype(jnp.float32)  10.1 us
    pallas_call x1, Pallas kernels, temporal_grads(): pl.pallas_call(temporal_kernel, in_specs=[pl.BlockSpec(memory_space=pltpu...  9.25 us
    all_to_all x1, starting transfers between devices, local(): lax.all_to_all(jnp.broadcast_to(shard[None], (4,) + shard.shape), 'z', 0, 0)  9.01 us
    all_to_all x2, starting transfers between devices, gather_groups(): return lax.all_to_all(copies, ALL, 0, 0, axis_index_groups=groups)  8.62 us
    ppermute x4, starting transfers between devices, swap_cores(): return lax.ppermute(block, 'c', [(0, 1), (1, 0)])  8.25 us
  transfers between devices with their start and end apart: 15, of which 7 were waited for; matrix products, arithmetic and copies ran while one was open for 23% of the time, Pallas kernels for 10%

profile of v9, /device:TPU:1, one launch (start us, length us, event | category | flops | bytes accessed | tf_op | source)
XLA Modules:
  0.0 189.2 jit_solution(15579733305660659369)
XLA Ops:
  0.6 1.0 pad_maximum_fusion.3
  1.7 0.9 broadcast_in_dim.55
  2.6 9.0 %all-to-all-start = ((bf16[4,2,20736]{2,1,0:T(2,128)(2,1)}), bf16[4,2,20736]{2,1,0:T(2,128)(2,1)}, u32[]{:S(2)}, u32[]{:S(2)}) async-start(bf16[4,2,20736]{2,1,0:T(2,128)(2,1)} %broadcast_in_dim.55), calls=%async_computation | async-start | bytes 663552 | tf_op jit(solution)/shard_map/all_to_all | solution.py:339
  11.6 1.0 collective-permute-start
  12.6 3.1 %fusion.16 = (bf16[1280,1152]{1,0:T(8,128)(2,1)S(1)}, pred[1280,1152]{1,0:T(32,128)(4,1)}) fusion(s32[1280]{0:T(1024)} %constant.60.clone), kind=kLoop, calls=%fused_computation.34 | loop fusion | flops 2949120 | bytes 4428800 | tf_op jit(solution)/shard_map/convert_element_type | solution.py:333
  15.7 5.3 %all-to-all-done = bf16[4,2,20736]{2,1,0:T(2,128)(2,1)} async-done(((bf16[4,2,20736]{2,1,0:T(2,128)(2,1)}), bf16[4,2,20736]{2,1,0:T(2,128)(2,1)}, u32[]{:S(2)}, u32[]{:S(2)}) %all-to-all-start) | async-done | bytes 331808 | tf_op jit(solution)/shard_map/all_to_all | solution.py:339
  20.9 1.9 %reshape.71 = bf16[36,4608]{1,0:T(8,128)(2,1)} reshape(bf16[4,2,20736]{2,1,0:T(2,128)(2,1)} %all-to-all-done) | data formatting | bytes 663552 | tf_op jit(solution)/shard_map/reshape | solution.py:340
  22.9 1.0 pad.11
  23.9 1.2 broadcast_in_dim.56
  25.1 4.3 %all-to-all-start.1 = ((bf16[4,40,4608]{2,1,0:T(8,128)(2,1)}), bf16[4,40,4608]{2,1,0:T(8,128)(2,1)}, u32[]{:S(2)}, u32[]{:S(2)}) async-start(bf16[4,40,4608]{2,1,0:T(8,128)(2,1)} %broadcast_in_dim.56), calls=%async_computation.1 | async-start | bytes 2949120 | tf_op jit(solution)/shard_map/all_to_all | solution.py:255
  29.4 2.6 %dynamic-slice_bitcast_fusion = bf16[576,1152]{1,0:T(8,128)(2,1)} fusion(bf16[2,576,1152]{2,1,0:T(8,128)(2,1)} %param.20, s32[]{:T(128)S(6)} %select_n.65), kind=kLoop, calls=%fused_computation.21 | loop fusion | bytes 2654212 | tf_op jit(solution)/shard_map/jit(dynamic_index_in_dim)/squeeze | solution.py:348
  32.0 2.2 %pad.12.key_ref.key_hbm = bf16[384,1152]{1,0:T(8,128)(2,1)} pad(bf16[300,1152]{1,0:T(8,128)(2,1)} %param.21, bf16[]{:T(256)} %constant.53.clone.1), padding=0_84x0_0 | pad | bytes 1575938 | tf_op jit(solution)/shard_map/jit(_pad)/pad | solution.py:346
  34.1 2.1 %pad.13.value_hbm = bf16[384,1152]{1,0:T(8,128)(2,1)} pad(bf16[300,1152]{1,0:T(8,128)(2,1)} %param.22, bf16[]{:T(256)} %constant.53.clone.1), padding=0_84x0_0 | pad | bytes 1575938 | tf_op jit(solution)/shard_map/jit(_pad)/pad | solution.py:346
  36.3 1.0 select_bitcast_fusion.3
  37.4 0.8 copy-done.12
  38.2 2.5 %fusion.9.residual_ref = bf16[256,640]{1,0:T(8,128)(2,1)} fusion(bf16[256,1152]{1,0:T(8,128)(2,1)S(1)} %bitcast.68, pred[1280,1152]{1,0:T(32,128)(4,1)} %get-tuple-element.43, s32[]{:T(128)S(6)} %select_n.69), kind=kOutput, calls=%fused_computation.22 | convolution fusion | flops 377651200 | bytes 1654788 | tf_op jit(solution)/shard_map/dot_general | solution.py:342
  40.8 0.7 all-to-all-done.1
  41.5 1.8 slice.22
  43.3 1.8 reshape.72
  45.1 2.1 %broadcast_in_dim.57 = bf16[4,144,1152]{2,1,0:T(8,128)(2,1)} broadcast(bf16[144,1152]{1,0:T(8,128)(2,1)} %reshape.72), dimensions={1,2} | broadcast | bytes 1658880 | tf_op jit(solution)/shard_map/broadcast_in_dim | solution.py:254
  47.2 4.3 %all-to-all-start.2 = ((bf16[4,144,1152]{2,1,0:T(8,128)(2,1)}), bf16[4,144,1152]{2,1,0:T(8,128)(2,1)}, u32[]{:S(2)}, u32[]{:S(2)}) async-start(bf16[4,144,1152]{2,1,0:T(8,128)(2,1)} %broadcast_in_dim.57), calls=%async_computation.2 | async-start | bytes 2654208 | tf_op jit(solution)/shard_map/all_to_all | solution.py:255
  51.5 3.0 %collective-permute-start.2 = (bf16[576,1152]{1,0:T(8,128)(2,1)}, bf16[576,1152]{1,0:T(8,128)(2,1)}, u32[]{:S(2)}, u32[]{:S(2)}) collective-permute-start(bf16[576,1152]{1,0:T(8,128)(2,1)} %dynamic-slice_bitcast_fusion), channel_id=1, source_target_pairs={{0,128},{1,135},{128,2},{129,1},{2,130},{3,129},{130,4},{131,3},{4... | collective-permute-start | bytes 3981320 | tf_op jit(solution)/shard_map/ppermute | solution.py:303
  54.5 2.4 %slice.23 = bf16[4,36,3456]{2,1,0:T(8,128)(2,1)} slice(bf16[4,40,4608]{2,1,0:T(8,128)(2,1)} %all-to-all-done.1), slice={[0:4], [0:36], [1152:4608]} | slice | bytes 1990656 | tf_op jit(solution)/shard_map/slice | solution.py:354
  56.9 2.2 %reshape.80.w0 = bf16[144,3456]{1,0:T(8,128)(2,1)} reshape(bf16[4,36,3456]{2,1,0:T(8,128)(2,1)} %slice.23) | data formatting | bytes 1990656 | tf_op jit(solution)/shard_map/reshape | solution.py:354
  59.1 1.3 collective-permute-start.3
  60.5 1.3 collective-permute-start.4
  61.8 1.6 collective-permute-start.5
  63.4 2.8 %convolution_convert_fusion.2 = bf16[256,576]{0,1:T(8,128)(2,1)} fusion(bf16[256,1152]{1,0:T(8,128)(2,1)} %bitcast.69, bf16[576,1152]{1,0:T(8,128)(2,1)} %bitcast.6), kind=kOutput, calls=%fused_computation.23 | convolution fusion | flops 339886080 | bytes 2211840 | tf_op jit(solution)/shard_map/dot_general | solution.py:362
  66.3 1.9 copy.42
  68.1 1.0 dynamic-slice_bitcast_fusion.1
  69.1 6.0 %collective-permute-start.1 = (bf16[128,576]{1,0:T(8,128)(2,1)S(1)}, bf16[128,576]{1,0:T(8,128)(2,1)S(1)}, u32[]{:S(2)}, u32[]{:S(2)}) collective-permute-start(bf16[128,576]{1,0:T(8,128)(2,1)S(1)} %get-tuple-element.40), channel_id=1, source_target_pairs={{0,1},{1,0},{2,3},{3,2},{4,5},{5,4},{6,7},{7,6},{8,9},{9,8},{10,11... | collective-permute-start | bytes 442376 | tf_op jit(solution)/shard_map/ppermute | solution.py:270
  75.2 1.0 collective-permute-done.1.got_ref
  76.2 1.0 copy-done.7
  77.2 1.0 copy-done.8
  78.1 9.2 %temporal_grads.1.mine_ref = bf16[128,3456]{1,0:T(8,128)(2,1)} custom-call(s32[1]{0:T(128)} %bitcast.core_ref, bf16[128,576]{1,0:T(8,128)(2,1)S(1)} %get-tuple-element.41.kept_ref, bf16[128,576]{1,0:T(8,128)(2,1)S(1)} %collective-permute-done.1.got_ref, bf16[1280,1152]{1,0:T(8,128)(2,1)S(1)} %get-tuple-element.20.order_ref, bf16[128,1152]{1,0:T(8,128)(2,1)S(1)} %bitcast.60, ...), custom_call_target="tpu_custom_call" | custom-call | flops 147456 | bytes 294912 | tf_op jit(solution)/shard_map/temporal_grads/pallas_call | solution.py:75
  87.4 3.4 %collective-permute-start.7 = (bf16[576,1152]{1,0:T(8,128)(2,1)}, bf16[576,1152]{1,0:T(8,128)(2,1)}, u32[]{:S(2)}, u32[]{:S(2)}) collective-permute-start(bf16[576,1152]{1,0:T(8,128)(2,1)} %collective-permute-done.2), channel_id=1, source_target_pairs={{0,1},{1,0},{2,3},{3,2},{4,5},{5,4},{6,7},{7,6},{8,9},{9,8},{10,11... | collective-permute-start | bytes 3981320 | tf_op jit(solution)/shard_map/ppermute | solution.py:309
  91.6 3.5 %collective-permute-done.6.other_ref = bf16[128,3456]{1,0:T(8,128)(2,1)} collective-permute-done((bf16[128,3456]{1,0:T(8,128)(2,1)}, bf16[128,3456]{1,0:T(8,128)(2,1)}, u32[]{:S(2)}, u32[]{:S(2)}) %collective-permute-start.6) | collective-permute-done | bytes 884768 | tf_op jit(solution)/shard_map/ppermute | solution.py:270
  95.1 1.2 copy-done.3
  96.3 1.0 copy-done.5
  97.3 5.2 %mixed_half.1 = bf16[256,640]{1,0:T(8,128)(2,1)S(1)} custom-call(s32[5]{0:T(128)S(1)} %pad_add_fusion.place_ref, bf16[128,3456]{1,0:T(8,128)(2,1)} %temporal_grads.1.mine_ref, bf16[128,3456]{1,0:T(8,128)(2,1)} %collective-permute-done.6.other_ref, bf16[256,640]{1,0:T(8,128)(2,1)S(1)} %copy-done.5, bf16[144,3456]{1,0:T(8,128)(2,1)S(1)} %copy-done.3, ...), custom_call_target="tpu_custom_call" | custom-call | flops 1132462080 | bytes 8388608 | tf_op jit(solution)/shard_map/mixed_half/pallas_call | solution.py:116
  102.5 1.1 copy.46
  103.6 7.2 %all-to-all-start.3 = ((bf16[128,2,640]{2,1,0:T(2,128)(2,1)}), bf16[128,2,640]{2,1,0:T(2,128)(2,1)}, u32[]{:S(2)}, u32[]{:S(2)}) async-start(bf16[128,2,640]{2,1,0:T(2,128)(2,1)} %bitcast.65), calls=%async_computation.3 | async-start | bytes 655360 | tf_op jit(solution)/shard_map/all_to_all | solution.py:387
  110.7 2.1 %select_bitcast_fusion.1 = (bf16[1,576,1152]{2,1,0:T(8,128)(2,1)S(1)}, bf16[1,576,1152]{2,1,0:T(8,128)(2,1)S(1)}) fusion(bf16[576,1152]{1,0:T(8,128)(2,1)} %collective-permute-done.2, bf16[576,1152]{1,0:T(8,128)(2,1)} %collective-permute-done.7, pred[]{:T(512)S(6)} %eq.37), kind=kLoop, calls=%fused_computation.20 | loop fusion | flops 1327104 | bytes 5308417 | tf_op jit(solution)/shard_map/stack | solution.py:310
  113.3 0.5 broadcast_select_fusion
  113.9 0.6 fusion.7.query_ref.query_hbm
  114.5 1.2 copy-done.2
  115.7 4.8 %cross_probs.1.probs_ref = f32[16,128,384]{2,1,0:T(8,128)S(1)} custom-call(s32[1]{0:T(128)S(6)} %copy.49.length_ref, bf16[128,1152]{1,0:T(8,128)(2,1)S(1)} %fusion.7.query_ref.query_hbm, bf16[384,1152]{1,0:T(8,128)(2,1)S(1)} %copy-done.2), custom_call_target="tpu_custom_call" | custom-call | flops 113246208 | bytes 4194304 | tf_op jit(solution)/shard_map/cross_probs/pallas_call | solution.py:148
  120.5 1.6 copy-done.1
  122.2 5.8 %convolution_convert_fusion.w_out_hbm = bf16[1280,1152]{1,0:T(8,128)(2,1)} fusion(bf16[1280,1152]{1,0:T(8,128)(2,1)S(1)} %get-tuple-element.20.order_ref, bf16[2,576,1152]{2,1,0:T(8,128)(2,1)S(1)} %get-tuple-element.35, bf16[2,576,1152]{2,1,0:T(8,128)(2,1)S(1)} %get-tuple-element.34), kind=kOutput, calls=%fused_computation | convolution fusion | flops 3404169216 | bytes 11206656 | tf_op jit(solution)/shard_map/dot_general | solution.py:380
  127.9 1.2 copy.38
  129.2 0.8 copy.43
  129.9 11.7 %cross_grads.1 = (bf16[128,1152]{1,0:T(8,128)(2,1)}, bf16[16,72,384]{2,1,0:T(8,128)(2,1)}, bf16[16,72,384]{2,1,0:T(8,128)(2,1)}) custom-call(s32[1]{0:T(128)} %bitcast.core_ref, bf16[128,1280]{1,0:T(8,128)(2,1)} %bitcast.63, bf16[1280,1152]{1,0:T(8,128)(2,1)} %convolution_convert_fusion.w_out_hbm, bf16[128,1152]{1,0:T(8,128)(2,1)} %copy-done.4, ...), custom_call_target="tpu_custom_call" | custom-call | flops 830472192 | bytes 12582912 | tf_op jit(solution)/shard_map/cross_grads/pallas_call | solution.py:215
  141.7 1.2 collective-permute-start.8
  142.9 2.3 %collective-permute-done.8 = bf16[16,72,384]{2,1,0:T(8,128)(2,1)S(1)} collective-permute-done((bf16[16,72,384]{2,1,0:T(8,128)(2,1)}, bf16[16,72,384]{2,1,0:T(8,128)(2,1)S(1)}, u32[]{:S(2)}, u32[]{:S(2)}) %collective-permute-start.8) | collective-permute-done | bytes 884768 | tf_op jit(solution)/shard_map/ppermute | solution.py:270
  145.2 2.4 %add_convert_fusion = bf16[16,72,384]{2,1,0:T(8,128)(2,1)} fusion(bf16[16,72,384]{2,1,0:T(8,128)(2,1)S(1)} %collective-permute-done.8, bf16[16,72,384]{2,1,0:T(8,128)(2,1)} %get-tuple-element.32), kind=kLoop, calls=%fused_computation.18 | loop fusion | flops 1769472 | bytes 2654208 | tf_op jit(solution)/shard_map/convert_element_type | solution.py:392
  147.5 6.4 %all-to-all-start.4 = ((bf16[16,72,384]{2,1,0:T(8,128)(2,1)}), bf16[16,72,384]{2,1,0:T(8,128)(2,1)}, u32[]{:S(2)}, u32[]{:S(2)}) async-start(bf16[16,72,384]{2,1,0:T(8,128)(2,1)} %add_convert_fusion), calls=%async_computation.4 | async-start | bytes 1769472 | tf_op jit(solution)/shard_map/all_to_all | solution.py:397
  154.1 3.5 %fusion.12 = f32[128,1152]{1,0:T(8,128)} fusion(bf16[128,1152]{1,0:T(8,128)(2,1)S(1)} %copy-done.13, bf16[2,576,1152]{2,1,0:T(8,128)(2,1)} %copy-done.9, bf16[2,576,1152]{2,1,0:T(8,128)(2,1)} %copy-done.10), kind=kOutput, calls=%fused_computation.25 | convolution fusion | flops 345047040 | bytes 6193152 | tf_op jit(solution)/shard_map/dot_general | solution.py:395
  157.6 10.1 %all-to-all-done.4 = bf16[16,72,384]{2,1,0:T(8,128)(2,1)} async-done(((bf16[16,72,384]{2,1,0:T(8,128)(2,1)}), bf16[16,72,384]{2,1,0:T(8,128)(2,1)}, u32[]{:S(2)}, u32[]{:S(2)}) %all-to-all-start.4) | async-done | bytes 884768 | tf_op jit(solution)/shard_map/all_to_all | solution.py:397
  167.6 1.3 reduce
  169.1 0.8 reshape.86
  169.9 10.1 %all-to-all-start.5 = ((bf16[16,2,1350]{2,1,0:T(2,128)(2,1)}), bf16[16,2,1350]{2,1,0:T(2,128)(2,1)S(1)}, u32[]{:S(2)}, u32[]{:S(2)}) async-start(bf16[16,2,1350]{2,1,0:T(2,128)(2,1)} %reshape.86), calls=%async_computation.5 | async-start | bytes 180224 | tf_op jit(solution)/shard_map/all_to_all | solution.py:401
  180.0 2.5 %fusion.8 = bf16[1,128,1152]{2,1,0:T(8,128)(2,1)} fusion(f32[128,1152]{1,0:T(8,128)} %fusion.12, bf16[128,1280]{1,0:T(8,128)(2,1)} %bitcast.64, bf16[1280,1152]{1,0:T(8,128)(2,1)S(1)} %get-tuple-element.20.order_ref), kind=kOutput, calls=%fused_computation.17 | convolution fusion | flops 377782272 | bytes 4161536 | tf_op jit(solution)/shard_map/dot_general | solution.py:394
  182.5 5.8 %all-to-all-done.5 = bf16[16,2,1350]{2,1,0:T(2,128)(2,1)S(1)} async-done(((bf16[16,2,1350]{2,1,0:T(2,128)(2,1)}), bf16[16,2,1350]{2,1,0:T(2,128)(2,1)S(1)}, u32[]{:S(2)}, u32[]{:S(2)}) %all-to-all-start.5) | async-done | bytes 86432 | tf_op jit(solution)/shard_map/all_to_all | solution.py:401
  188.6 0.7 convert_reduce_fusion
  (44 shorter events, 1.3 us)
Async XLA Ops:
  0.6 113.2 %copy-start = (bf16[1,128,1152]{2,1,0:T(8,128)(2,1)S(1)}, bf16[1,128,1152]{2,1,0:T(8,128)(2,1)}, u32[]{:S(2)}) copy-start(bf16[1,128,1152]{2,1,0:T(8,128)(2,1)} %param.19) | copy-start | bytes 884740
  2.6 18.3 %all-to-all-start = ((bf16[4,2,20736]{2,1,0:T(2,128)(2,1)}), bf16[4,2,20736]{2,1,0:T(2,128)(2,1)}, u32[]{:S(2)}, u32[]{:S(2)}) async-start(bf16[4,2,20736]{2,1,0:T(2,128)(2,1)} %broadcast_in_dim.55), calls=%async_computation | async-start | bytes 663552 | tf_op jit(solution)/shard_map/all_to_all | solution.py:339
  11.6 24.6 %collective-permute-start = (bf16[128,1152]{1,0:T(8,128)(2,1)}, bf16[128,1152]{1,0:T(8,128)(2,1)}, u32[]{:S(2)}, u32[]{:S(2)}) collective-permute-start(bf16[128,1152]{1,0:T(8,128)(2,1)} %bitcast.70), channel_id=1, source_target_pairs={{0,1},{1,0},{2,3},{3,2},{4,5},{5,4},{6,7},{7,6},{8,9},{9,8},{10,11... | collective-permute-start | bytes 884744 | tf_op jit(solution)/shard_map/ppermute | solution.py:270
  25.1 16.4 %all-to-all-start.1 = ((bf16[4,40,4608]{2,1,0:T(8,128)(2,1)}), bf16[4,40,4608]{2,1,0:T(8,128)(2,1)}, u32[]{:S(2)}, u32[]{:S(2)}) async-start(bf16[4,40,4608]{2,1,0:T(8,128)(2,1)} %broadcast_in_dim.56), calls=%async_computation.1 | async-start | bytes 2949120 | tf_op jit(solution)/shard_map/all_to_all | solution.py:255
  29.4 6.9 %copy-start.14 = (bf16[2,64,1,1152]{3,1,2,0:T(8,128)(2,1)S(1)}, bf16[2,64,1,1152]{3,1,2,0:T(8,128)(2,1)}, u32[]{:S(2)}) copy-start(bf16[2,64,1,1152]{3,1,2,0:T(8,128)(2,1)} %param.13) | copy-start | bytes 884740
  37.4 0.8 copy-start.12
  47.2 16.2 %all-to-all-start.2 = ((bf16[4,144,1152]{2,1,0:T(8,128)(2,1)}), bf16[4,144,1152]{2,1,0:T(8,128)(2,1)}, u32[]{:S(2)}, u32[]{:S(2)}) async-start(bf16[4,144,1152]{2,1,0:T(8,128)(2,1)} %broadcast_in_dim.57), calls=%async_computation.2 | async-start | bytes 2654208 | tf_op jit(solution)/shard_map/all_to_all | solution.py:255
  51.5 35.9 %collective-permute-start.2 = (bf16[576,1152]{1,0:T(8,128)(2,1)}, bf16[576,1152]{1,0:T(8,128)(2,1)}, u32[]{:S(2)}, u32[]{:S(2)}) collective-permute-start(bf16[576,1152]{1,0:T(8,128)(2,1)} %dynamic-slice_bitcast_fusion), channel_id=1, source_target_pairs={{0,128},{1,135},{128,2},{129,1},{2,130},{3,129},{130,4},{131,3},{4... | collective-permute-start | bytes 3981320 | tf_op jit(solution)/shard_map/ppermute | solution.py:303
  56.9 19.3 %copy-start.6 = (bf16[2,64,1,1152]{3,1,2,0:T(8,128)(2,1)S(1)}, bf16[2,64,1,1152]{3,1,2,0:T(8,128)(2,1)}, u32[]{:S(2)}) copy-start(bf16[2,64,1,1152]{3,1,2,0:T(8,128)(2,1)} %param.14) | copy-start | bytes 884740
  59.1 28.3 %collective-permute-start.3 = (bf16[144,3456]{1,0:T(8,128)(2,1)}, bf16[144,3456]{1,0:T(8,128)(2,1)}, u32[]{:S(2)}, u32[]{:S(2)}) collective-permute-start(bf16[144,3456]{1,0:T(8,128)(2,1)} %reshape.80.w0), channel_id=1, source_target_pairs={{0,8},{1,33},{2,10},{3,35},{4,12},{5,37},{6,14},{7,39},{8,16},{9,4... | collective-permute-start | bytes 2985992 | tf_op jit(solution)/shard_map/ppermute | solution.py:266
  60.5 26.9 %collective-permute-start.4 = (bf16[144,3456]{1,0:T(8,128)(2,1)}, bf16[144,3456]{1,0:T(8,128)(2,1)}, u32[]{:S(2)}, u32[]{:S(2)}) collective-permute-start(bf16[144,3456]{1,0:T(8,128)(2,1)} %reshape.80.w0), channel_id=1, source_target_pairs={{0,24},{1,97},{2,26},{3,99},{4,28},{5,101},{6,30},{7,103},{8,0},{9... | collective-permute-start | bytes 2985992 | tf_op jit(solution)/shard_map/ppermute | solution.py:266
  61.8 25.6 %collective-permute-start.5 = (bf16[144,3456]{1,0:T(8,128)(2,1)}, bf16[144,3456]{1,0:T(8,128)(2,1)}, u32[]{:S(2)}, u32[]{:S(2)}) collective-permute-start(bf16[144,3456]{1,0:T(8,128)(2,1)} %reshape.80.w0), channel_id=1, source_target_pairs={{0,16},{1,65},{2,18},{3,67},{4,20},{5,69},{6,22},{7,71},{8,24},{9,... | collective-permute-start | bytes 2985992 | tf_op jit(solution)/shard_map/ppermute | solution.py:266
  69.1 22.3 %copy-start.15 = (s32[4]{0:T(128)S(1)}, s32[4]{0:T(128)}, u32[]{:S(2)}) copy-start(s32[4]{0:T(128)} %constant.75) | copy-start | bytes 52
  69.1 7.1 %collective-permute-start.1 = (bf16[128,576]{1,0:T(8,128)(2,1)S(1)}, bf16[128,576]{1,0:T(8,128)(2,1)S(1)}, u32[]{:S(2)}, u32[]{:S(2)}) collective-permute-start(bf16[128,576]{1,0:T(8,128)(2,1)S(1)} %get-tuple-element.40), channel_id=1, source_target_pairs={{0,1},{1,0},{2,3},{3,2},{4,5},{5,4},{6,7},{7,6},{8,9},{9,8},{10,11... | collective-permute-start | bytes 442376 | tf_op jit(solution)/shard_map/ppermute | solution.py:270
  76.2 1.0 copy-start.7
  77.2 1.0 copy-start.8
  87.4 23.3 %collective-permute-start.7 = (bf16[576,1152]{1,0:T(8,128)(2,1)}, bf16[576,1152]{1,0:T(8,128)(2,1)}, u32[]{:S(2)}, u32[]{:S(2)}) collective-permute-start(bf16[576,1152]{1,0:T(8,128)(2,1)} %collective-permute-done.2), channel_id=1, source_target_pairs={{0,1},{1,0},{2,3},{3,2},{4,5},{5,4},{6,7},{7,6},{8,9},{9,8},{10,11... | collective-permute-start | bytes 3981320 | tf_op jit(solution)/shard_map/ppermute | solution.py:309
  90.8 4.3 %collective-permute-start.6 = (bf16[128,3456]{1,0:T(8,128)(2,1)}, bf16[128,3456]{1,0:T(8,128)(2,1)}, u32[]{:S(2)}, u32[]{:S(2)}) collective-permute-start(bf16[128,3456]{1,0:T(8,128)(2,1)} %temporal_grads.1.mine_ref), channel_id=1, source_target_pairs={{0,1},{1,0},{2,3},{3,2},{4,5},{5,4},{6,7},{7,6},{8,9},{9,8},{10,11... | collective-permute-start | bytes 2654216 | tf_op jit(solution)/shard_map/ppermute | solution.py:270
  95.1 1.2 copy-start.3
  96.3 1.0 copy-start.5
  103.6 24.4 %all-to-all-start.3 = ((bf16[128,2,640]{2,1,0:T(2,128)(2,1)}), bf16[128,2,640]{2,1,0:T(2,128)(2,1)}, u32[]{:S(2)}, u32[]{:S(2)}) async-start(bf16[128,2,640]{2,1,0:T(2,128)(2,1)} %bitcast.65), calls=%async_computation.3 | async-start | bytes 655360 | tf_op jit(solution)/shard_map/all_to_all | solution.py:387
  110.7 2.6 %copy-start.11 = (bf16[2,576,1152]{2,1,0:T(8,128)(2,1)S(1)}, bf16[2,576,1152]{2,1,0:T(8,128)(2,1)}, u32[]{:S(2)}) copy-start(bf16[2,576,1152]{2,1,0:T(8,128)(2,1)} %param.20) | copy-start | bytes 7962628
  113.8 6.7 %copy-start.9 = (bf16[2,576,1152]{2,1,0:T(8,128)(2,1)}, bf16[2,576,1152]{2,1,0:T(8,128)(2,1)S(1)}, u32[]{:S(2)}) copy-start(bf16[2,576,1152]{2,1,0:T(8,128)(2,1)S(1)} %get-tuple-element.34) | copy-start | bytes 7962628
  113.8 6.7 %copy-start.10 = (bf16[2,576,1152]{2,1,0:T(8,128)(2,1)}, bf16[2,576,1152]{2,1,0:T(8,128)(2,1)S(1)}, u32[]{:S(2)}) copy-start(bf16[2,576,1152]{2,1,0:T(8,128)(2,1)S(1)} %get-tuple-element.35) | copy-start | bytes 7962628
  113.9 1.8 copy-start.2
  115.7 12.2 %copy-start.4 = (bf16[128,1152]{1,0:T(8,128)(2,1)}, bf16[128,1152]{1,0:T(8,128)(2,1)S(1)}, u32[]{:S(2)}) copy-start(bf16[128,1152]{1,0:T(8,128)(2,1)S(1)} %fusion.7.query_ref.query_hbm) | copy-start | bytes 884740
  120.5 1.6 copy-start.1
  141.7 12.4 %copy-start.13 = (bf16[128,1152]{1,0:T(8,128)(2,1)S(1)}, bf16[128,1152]{1,0:T(8,128)(2,1)}, u32[]{:S(2)}) copy-start(bf16[128,1152]{1,0:T(8,128)(2,1)} %get-tuple-element.31) | copy-start | bytes 884740
  141.7 3.5 %collective-permute-start.8 = (bf16[16,72,384]{2,1,0:T(8,128)(2,1)}, bf16[16,72,384]{2,1,0:T(8,128)(2,1)S(1)}, u32[]{:S(2)}, u32[]{:S(2)}) collective-permute-start(bf16[16,72,384]{2,1,0:T(8,128)(2,1)} %get-tuple-element.33), channel_id=1, source_target_pairs={{0,1},{1,0},{2,3},{3,2},{4,5},{5,4},{6,7},{7,6},{8,9},{9,8},{10,11... | collective-permute-start | bytes 2654216 | tf_op jit(solution)/shard_map/ppermute | solution.py:270
  147.5 20.1 %all-to-all-start.4 = ((bf16[16,72,384]{2,1,0:T(8,128)(2,1)}), bf16[16,72,384]{2,1,0:T(8,128)(2,1)}, u32[]{:S(2)}, u32[]{:S(2)}) async-start(bf16[16,72,384]{2,1,0:T(8,128)(2,1)} %add_convert_fusion), calls=%async_computation.4 | async-start | bytes 1769472 | tf_op jit(solution)/shard_map/all_to_all | solution.py:397
  169.9 18.4 %all-to-all-start.5 = ((bf16[16,2,1350]{2,1,0:T(2,128)(2,1)}), bf16[16,2,1350]{2,1,0:T(2,128)(2,1)S(1)}, u32[]{:S(2)}, u32[]{:S(2)}) async-start(bf16[16,2,1350]{2,1,0:T(2,128)(2,1)} %reshape.86), calls=%async_computation.5 | async-start | bytes 180224 | tf_op jit(solution)/shard_map/all_to_all | solution.py:401

commit v10 on v8

--- a/solution.py
+++ b/solution.py
@@ -273,10 +273,7 @@
     return order.reshape(1280)
 
 
-def cross_halves(cross_weights):
-    core = lax.axis_index("c")
-    side = lax.axis_index("s")
-
+def cross_fetch(part):
     def place(z):
         return (z % 2, z // 2)
 
@@ -289,8 +286,12 @@
                     s0, z0 = place(z)
                     s1, z1 = place(to)
                     pairs.append((flat(s0, x, y, z0, c), flat(s1, x, y, z1, c)))
-    part = lax.dynamic_index_in_dim(cross_weights, core, 0, keepdims=False)
-    got = lax.ppermute(part, ALL, pairs)
+    return lax.ppermute(part, ALL, pairs)
+
+
+def cross_whole(cross_weights, got):
+    core = lax.axis_index("c")
+    side = lax.axis_index("s")
     swapped = lax.ppermute(got, "c", [(0, 1), (1, 0)])
     other = jnp.stack([jnp.where(core == 0, got, swapped), jnp.where(core == 0, swapped, got)])
     low = jnp.where(side == 0, cross_weights, other)
@@ -330,9 +331,10 @@
     padding = ((0, CAP_PAD - CAP), (0, 0))
     cap_key, cap_value = jnp.pad(cap_key, padding), jnp.pad(cap_value, padding)
     out_near = near[:, :36, :width].reshape(144, width)
-    out_near, cross_weights, grad_both, residual, place, cap_key, cap_value = (
+    cross_part = lax.dynamic_index_in_dim(cross_weights, core, 0, keepdims=False)
+    out_near, cross_part, grad_both, residual, place, cap_key, cap_value = (
         lax.optimization_barrier(
-            (out_near, cross_weights, grad_both, residual, place, cap_key, cap_value)
+            (out_near, cross_part, grad_both, residual, place, cap_key, cap_value)
         )
     )
     qkv_near = near[:, :36, width:].reshape(144, 3 * width)
@@ -341,7 +343,7 @@
     slots = (place_here - jnp.array([0, 1, 3, 2], jnp.int32)) % 4
     places = jnp.concatenate([slots, core.reshape(1)])
     out_mine = gather_groups(out_near, ring_groups(1)).reshape(576, width)
-    full_cross = cross_halves(cross_weights)
+    cross_part = cross_fetch(cross_part)
     heads_mine = (
         lax.dot_general(grad_both, out_mine, CONTRACT_LAST, preferred_element_type=jnp.float32)
         .astype(jnp.bfloat16)
@@ -357,7 +359,8 @@
     qkv_grad = temporal_grads(
         grad_heads, *(saved.reshape(rows, width) for saved in (t_query, t_key, t_value))
     )
-    qkv_grad, *blocks = lax.optimization_barrier((qkv_grad, *blocks))
+    qkv_grad, cross_part, *blocks = lax.optimization_barrier((qkv_grad, cross_part, *blocks))
+    full_cross = cross_whole(cross_weights, cross_part)
     mixed = mixed_half(
         places, qkv_grad, swap_cores(qkv_grad), residual, blocks
     ).reshape(2, rows, 640)

time: 178 us -> 176 us (0.989)
  waiting for transfers between devices: 29.2 us -> 32.2 us
  starting transfers between devices: 63.8 us -> 61 us
    all_to_all x1, waiting for transfers between devices: 8.23 us -> 4.56 us  [local(): lax.all_to_all(jnp.broadcast_to(shard[None], (4,) + shard.shape), 'z', 0, 0)]
    all_to_all x2, waiting for transfers between devices: 1.54 us -> 4.76 us  [gather_groups(): return lax.all_to_all(copies, ALL, 0, 0, axis_index_groups=groups)]
    ppermute x4, waiting for transfers between devices: 3.69 us -> 6.46 us  [swap_cores(): return lax.ppermute(block, 'c', [(0, 1), (1, 0)])]
    all_to_all x1, starting transfers between devices: 7.82 us -> 5.85 us  [local(): lax.all_to_all(mixed.transpose(1, 0, 2), SEQ, split_axis=0, concat_axis=0)]
    unnamed x38 -> x42, local copies, waits for them, and re-layouts: 4.85 us -> 4.84 us
  transfers between devices with their start and end apart: 15 -> 15, of which waited for: 6 -> 9; matrix products, arithmetic and copies ran while one was open for 22% -> 22% of each run, Pallas kernels for 10% -> 10%
where the time goes in v10:
time: 176 us; the launch traced here: 175 us
  starting transfers between devices  61 us (35%)
  waiting for transfers between devices  32.2 us (18%)
  Pallas kernels  28.4 us (16%)
  local copies, waits for them, and re-layouts  20.4 us (12%)
  matrix products  18.7 us (11%)
  other arithmetic  12.9 us (7%)
  between operations  1.77 us (1%)
    pallas_call x1, Pallas kernels, cross_grads(): pl.pallas_call(cross_kernel, in_specs=[pl.BlockSpec(memory_space=pltpu.SM...  10.7 us
    all_to_all x1, waiting for transfers between devices, local(): lax.all_to_all(chip, ('x', 'y'), 0, 0).astype(jnp.float32)  9.93 us
    all_to_all x1, starting transfers between devices, local(): lax.all_to_all(pieces, ('s', 'z', 'c'), 0, 0).astype(jnp.float32)  9.79 us
    all_to_all x1, starting transfers between devices, local(): lax.all_to_all(jnp.broadcast_to(shard[None], (4,) + shard.shape), 'z', 0, 0)  9.01 us
    ppermute x4, starting transfers between devices, swap_cores(): return lax.ppermute(block, 'c', [(0, 1), (1, 0)])  8.93 us
    all_to_all x2, starting transfers between devices, gather_groups(): return lax.all_to_all(copies, ALL, 0, 0, axis_index_groups=groups)  8.78 us
    pallas_call x1, Pallas kernels, temporal_grads(): pl.pallas_call(temporal_kernel, out_shape=jax.ShapeDtypeStruct((rows, 3 *...  7.97 us
    ppermute x4, waiting for transfers between devices, swap_cores(): return lax.ppermute(block, 'c', [(0, 1), (1, 0)])  6.46 us
  transfers between devices with their start and end apart: 15, of which 9 were waited for; matrix products, arithmetic and copies ran while one was open for 22% of the time, Pallas kernels for 10%

profile of v10, /device:TPU:1, one launch (start us, length us, event | category | flops | bytes accessed | tf_op | source)
XLA Modules:
  0.0 175.3 jit_solution(10869195675046011981)
XLA Ops:
  0.6 1.0 pad_maximum_fusion.3
  1.6 0.1 broadcast_in_dim.54
  1.7 0.9 broadcast_in_dim.55
  2.6 9.0 %all-to-all-start = ((bf16[4,2,20736]{2,1,0:T(2,128)(2,1)}), bf16[4,2,20736]{2,1,0:T(2,128)(2,1)S(1)}, u32[]{:S(2)}, u32[]{:S(2)}) async-start(bf16[4,2,20736]{2,1,0:T(2,128)(2,1)} %broadcast_in_dim.55), calls=%async_computation | async-start | bytes 663552 | tf_op jit(solution)/shard_map/all_to_all | solution.py:325
  11.6 1.0 collective-permute-start
  12.6 3.7 %fusion.20 = (bf16[1280,1152]{1,0:T(8,128)(2,1)}, pred[1280,1152]{1,0:T(32,128)(4,1)}) fusion(s32[1280]{0:T(1024)} %constant.60.clone), kind=kLoop, calls=%fused_computation.37 | loop fusion | flops 2949120 | bytes 4428800 | tf_op jit(solution)/shard_map/convert_element_type | solution.py:319
  16.3 4.6 %all-to-all-done = bf16[4,2,20736]{2,1,0:T(2,128)(2,1)S(1)} async-done(((bf16[4,2,20736]{2,1,0:T(2,128)(2,1)}), bf16[4,2,20736]{2,1,0:T(2,128)(2,1)S(1)}, u32[]{:S(2)}, u32[]{:S(2)}) %all-to-all-start) | async-done | bytes 331808 | tf_op jit(solution)/shard_map/all_to_all | solution.py:325
  20.8 0.2 reshape.70
  21.1 1.2 broadcast_in_dim.56
  22.3 4.5 %all-to-all-start.1 = ((bf16[4,40,4608]{2,1,0:T(8,128)(2,1)}), bf16[4,40,4608]{2,1,0:T(8,128)(2,1)}, u32[]{:S(2)}, u32[]{:S(2)}) async-start(bf16[4,40,4608]{2,1,0:T(8,128)(2,1)} %broadcast_in_dim.56), calls=%async_computation.1 | async-start | bytes 2949120 | tf_op jit(solution)/shard_map/all_to_all | solution.py:241
  26.8 1.3 dynamic-slice_bitcast_fusion
  28.1 1.3 pad.12.key_ref.key_hbm
  29.4 2.4 %pad.13.value_hbm = bf16[384,1152]{1,0:T(8,128)(2,1)} pad(bf16[300,1152]{1,0:T(8,128)(2,1)} %param.22, bf16[]{:T(256)} %constant.53.clone.1), padding=0_84x0_0 | pad | bytes 1575938 | tf_op jit(solution)/shard_map/jit(_pad)/pad | solution.py:332
  31.8 1.0 select_bitcast_fusion.3
  32.9 0.8 copy-done.14
  33.7 0.7 fusion.13.residual_ref
  34.4 4.4 %all-to-all-done.1 = bf16[4,40,4608]{2,1,0:T(8,128)(2,1)} async-done(((bf16[4,40,4608]{2,1,0:T(8,128)(2,1)}), bf16[4,40,4608]{2,1,0:T(8,128)(2,1)}, u32[]{:S(2)}, u32[]{:S(2)}) %all-to-all-start.1) | async-done | bytes 1474592 | tf_op jit(solution)/shard_map/all_to_all | solution.py:241
  38.9 1.0 slice.30
  40.0 1.2 broadcast_in_dim.57
  41.1 4.3 %all-to-all-start.2 = ((bf16[4,144,1152]{2,1,0:T(8,128)(2,1)}), bf16[4,144,1152]{2,1,0:T(8,128)(2,1)}, u32[]{:S(2)}, u32[]{:S(2)}) async-start(bf16[4,144,1152]{2,1,0:T(8,128)(2,1)} %broadcast_in_dim.57), calls=%async_computation.2 | async-start | bytes 2654208 | tf_op jit(solution)/shard_map/all_to_all | solution.py:241
  45.5 3.0 %collective-permute-start.2 = (bf16[576,1152]{1,0:T(8,128)(2,1)}, bf16[576,1152]{1,0:T(8,128)(2,1)}, u32[]{:S(2)}, u32[]{:S(2)}) collective-permute-start(bf16[576,1152]{1,0:T(8,128)(2,1)} %dynamic-slice_bitcast_fusion), channel_id=1, source_target_pairs={{0,128},{1,135},{128,2},{129,1},{2,130},{3,129},{130,4},{131,3},{4... | collective-permute-start | bytes 3981320 | tf_op jit(solution)/shard_map/ppermute | solution.py:289
  48.4 2.3 %slice.31 = bf16[4,36,3456]{2,1,0:T(8,128)(2,1)} slice(bf16[4,40,4608]{2,1,0:T(8,128)(2,1)} %all-to-all-done.1), slice={[0:4], [0:36], [1152:4608]} | slice | bytes 1990656 | tf_op jit(solution)/shard_map/slice | solution.py:340
  50.8 1.3 reshape.79.w0
  52.1 1.4 collective-permute-start.3
  53.5 1.3 collective-permute-start.4
  54.9 1.6 collective-permute-start.5
  56.5 0.3 all-to-all-done.2
  56.8 1.9 %convolution_convert_fusion.2 = bf16[256,576]{0,1:T(8,128)(2,1)S(1)} fusion(bf16[256,1152]{1,0:T(8,128)(2,1)S(1)} %bitcast.76, bf16[576,1152]{1,0:T(8,128)(2,1)} %bitcast.6), kind=kOutput, calls=%fused_computation.28 | convolution fusion | flops 339886080 | bytes 2211840 | tf_op jit(solution)/shard_map/dot_general | solution.py:348
  58.8 0.6 constant_dynamic-slice_fusion.1
  59.5 6.6 %collective-permute-start.1 = (bf16[128,576]{0,1:T(8,128)(2,1)S(1)}, bf16[128,576]{0,1:T(8,128)(2,1)S(1)}, u32[]{:S(2)}, u32[]{:S(2)}) collective-permute-start(bf16[128,576]{0,1:T(8,128)(2,1)S(1)} %bitcast.79), channel_id=1, source_target_pairs={{0,1},{1,0},{2,3},{3,2},{4,5},{5,4},{6,7},{7,6},{8,9},{9,8},{10,11... | collective-permute-start | bytes 442376 | tf_op jit(solution)/shard_map/ppermute | solution.py:256
  66.1 1.0 collective-permute-done.1
  67.1 1.8 %fusion.10 = f32[128,1152]{1,0:T(8,128)S(1)} fusion(bf16[1280,1152]{1,0:T(8,128)(2,1)} %get-tuple-element.20, bf16[128,576]{0,1:T(8,128)(2,1)S(1)} %collective-permute-done.1, pred[]{:T(512)S(6)} %eq.39, bf16[1,128,576]{1,0,2:T(2,128)(2,1)S(1)} %get-tuple-element.40), kind=kOutput, calls=%fused_computation.23 | convolution fusion | flops 169943040 | bytes 2211841 | tf_op jit(solution)/shard_map/dot_general | solution.py:357
  68.9 1.8 %fusion.6.grad_ref = bf16[128,1152]{1,0:T(8,128)(2,1)S(1)} fusion(f32[128,1152]{1,0:T(8,128)S(1)} %fusion.10, bf16[1280,1152]{1,0:T(8,128)(2,1)} %get-tuple-element.20, bf16[128,576]{0,1:T(8,128)(2,1)S(1)} %collective-permute-done.1, pred[]{:T(512)S(6)} %eq.39, bf16[1,128,576]{1,0,2:T(2,128)(2,1)S(1)} %get-tuple-element.40), kind=kOutput, calls=%fused_computation.15 | convolution fusion | flops 170237952 | bytes 2506753 | tf_op jit(solution)/shard_map/dot_general | solution.py:356
  70.7 8.0 %temporal_grads.1.mine_ref = bf16[128,3456]{1,0:T(8,128)(2,1)S(1)} custom-call(bf16[128,1152]{1,0:T(8,128)(2,1)S(1)} %fusion.6.grad_ref, bf16[128,1152]{1,0:T(8,128)(2,1)S(1)} %bitcast.68, bf16[128,1152]{1,0:T(8,128)(2,1)S(1)} %bitcast.69, bf16[128,1152]{1,0:T(8,128)(2,1)S(1)} %bitcast.70), custom_call_target="tpu_custom_call" | custom-call | flops 147456 | bytes 294912 | tf_op jit(solution)/shard_map/temporal_grads/pallas_call | solution.py:65
  78.7 5.7 %collective-permute-start.7 = (bf16[576,1152]{1,0:T(8,128)(2,1)}, bf16[576,1152]{1,0:T(8,128)(2,1)}, u32[]{:S(2)}, u32[]{:S(2)}) collective-permute-start(bf16[576,1152]{1,0:T(8,128)(2,1)} %collective-permute-done.2), channel_id=1, source_target_pairs={{0,1},{1,0},{2,3},{3,2},{4,5},{5,4},{6,7},{7,6},{8,9},{9,8},{10,11... | collective-permute-start | bytes 3981320 | tf_op jit(solution)/shard_map/ppermute | solution.py:295
  85.2 3.2 %collective-permute-done.6.other_ref = bf16[128,3456]{1,0:T(8,128)(2,1)} collective-permute-done((bf16[128,3456]{1,0:T(8,128)(2,1)S(1)}, bf16[128,3456]{1,0:T(8,128)(2,1)}, u32[]{:S(2)}, u32[]{:S(2)}) %collective-permute-start.6) | collective-permute-done | bytes 884768 | tf_op jit(solution)/shard_map/ppermute | solution.py:256
  88.4 5.0 %mixed_half.1 = bf16[256,640]{1,0:T(8,128)(2,1)S(1)} custom-call(s32[5]{0:T(128)S(1)} %pad_add_fusion.place_ref, bf16[128,3456]{1,0:T(8,128)(2,1)S(1)} %temporal_grads.1.mine_ref, bf16[128,3456]{1,0:T(8,128)(2,1)} %collective-permute-done.6.other_ref, bf16[256,640]{1,0:T(8,128)(2,1)S(1)} %fusion.13.residual_ref, bf16[144,3456]{1,0:T(8,128)(2,1)S(1)} %reshape.79.w0, ...), custom_call_target="tpu_custom_call" | custom-call | flops 1132462080 | bytes 8388608 | tf_op jit(solution)/shard_map/mixed_half/pallas_call | solution.py:102
  93.3 1.1 copy.53
  94.4 5.8 %all-to-all-start.3 = ((bf16[128,2,640]{2,1,0:T(2,128)(2,1)}), bf16[128,2,640]{2,1,0:T(2,128)(2,1)S(1)}, u32[]{:S(2)}, u32[]{:S(2)}) async-start(bf16[128,2,640]{2,1,0:T(2,128)(2,1)} %bitcast.64), calls=%async_computation.3 | async-start | bytes 655360 | tf_op jit(solution)/shard_map/all_to_all | solution.py:374
  100.3 2.1 %select_bitcast_fusion.1 = (bf16[1,576,1152]{2,1,0:T(8,128)(2,1)S(1)}, bf16[1,576,1152]{2,1,0:T(8,128)(2,1)S(1)}) fusion(bf16[576,1152]{1,0:T(8,128)(2,1)} %collective-permute-done.2, bf16[576,1152]{1,0:T(8,128)(2,1)} %collective-permute-done.7, pred[]{:T(512)S(6)} %eq.39), kind=kLoop, calls=%fused_computation.22 | loop fusion | flops 1327104 | bytes 5308417 | tf_op jit(solution)/shard_map/stack | solution.py:296
  102.4 0.4 copy-done.12
  102.8 0.5 broadcast_select_fusion
  103.4 0.6 fusion.8.query_ref.query_hbm
  104.0 4.8 %cross_probs.1.probs_hbm = f32[16,128,384]{2,1,0:T(8,128)S(1)} custom-call(s32[1]{0:T(128)S(6)} %copy.57.length_ref, bf16[128,1152]{1,0:T(8,128)(2,1)S(1)} %fusion.8.query_ref.query_hbm, bf16[384,1152]{1,0:T(8,128)(2,1)S(1)} %pad.12.key_ref.key_hbm), custom_call_target="tpu_custom_call" | custom-call | flops 113246208 | bytes 4194304 | tf_op jit(solution)/shard_map/cross_probs/pallas_call | solution.py:134
  108.8 1.6 copy-done.1
  110.5 5.8 %convolution_convert_fusion.w_out_hbm = bf16[1280,1152]{1,0:T(8,128)(2,1)} fusion(bf16[1280,1152]{1,0:T(8,128)(2,1)S(1)} %copy-done.7, bf16[2,576,1152]{2,1,0:T(8,128)(2,1)S(1)} %get-tuple-element.35, bf16[2,576,1152]{2,1,0:T(8,128)(2,1)S(1)} %get-tuple-element.34), kind=kOutput, calls=%fused_computation | convolution fusion | flops 3404169216 | bytes 11206656 | tf_op jit(solution)/shard_map/dot_general | solution.py:367
  116.3 0.6 all-to-all-done.3
  116.9 0.3 copy.36
  117.2 0.8 copy.42
  118.0 10.7 %cross_grads.1 = (bf16[128,1152]{1,0:T(8,128)(2,1)}, bf16[16,72,384]{2,1,0:T(8,128)(2,1)}, bf16[16,72,384]{2,1,0:T(8,128)(2,1)}) custom-call(s32[1]{0:T(128)} %bitcast.core_ref, bf16[128,1280]{1,0:T(8,128)(2,1)} %bitcast.71, bf16[1280,1152]{1,0:T(8,128)(2,1)} %convolution_convert_fusion.w_out_hbm, bf16[128,1152]{1,0:T(8,128)(2,1)} %copy-done.3, ...), custom_call_target="tpu_custom_call" | custom-call | flops 830472192 | bytes 12582912 | tf_op jit(solution)/shard_map/cross_grads/pallas_call | solution.py:202
  128.7 1.4 collective-permute-start.8
  130.1 2.3 %collective-permute-done.8 = bf16[16,72,384]{2,1,0:T(8,128)(2,1)S(1)} collective-permute-done((bf16[16,72,384]{2,1,0:T(8,128)(2,1)}, bf16[16,72,384]{2,1,0:T(8,128)(2,1)S(1)}, u32[]{:S(2)}, u32[]{:S(2)}) %collective-permute-start.8) | collective-permute-done | bytes 884768 | tf_op jit(solution)/shard_map/ppermute | solution.py:256
  132.4 2.3 %add_convert_fusion = bf16[16,72,384]{2,1,0:T(8,128)(2,1)} fusion(bf16[16,72,384]{2,1,0:T(8,128)(2,1)S(1)} %collective-permute-done.8, bf16[16,72,384]{2,1,0:T(8,128)(2,1)} %get-tuple-element.32), kind=kLoop, calls=%fused_computation.20 | loop fusion | flops 1769472 | bytes 2654208 | tf_op jit(solution)/shard_map/convert_element_type | solution.py:379
  134.7 5.6 %all-to-all-start.4 = ((bf16[16,72,384]{2,1,0:T(8,128)(2,1)}), bf16[16,72,384]{2,1,0:T(8,128)(2,1)}, u32[]{:S(2)}, u32[]{:S(2)}) async-start(bf16[16,72,384]{2,1,0:T(8,128)(2,1)} %add_convert_fusion), calls=%async_computation.4 | async-start | bytes 1769472 | tf_op jit(solution)/shard_map/all_to_all | solution.py:384
  140.5 3.6 %fusion.16 = f32[128,1152]{1,0:T(8,128)} fusion(bf16[128,1152]{1,0:T(8,128)(2,1)S(1)} %copy-done.16, bf16[2,576,1152]{2,1,0:T(8,128)(2,1)} %copy-done.9, bf16[2,576,1152]{2,1,0:T(8,128)(2,1)} %copy-done.10), kind=kOutput, calls=%fused_computation.30 | convolution fusion | flops 345047040 | bytes 6193152 | tf_op jit(solution)/shard_map/dot_general | solution.py:382
  144.1 9.9 %all-to-all-done.4 = bf16[16,72,384]{2,1,0:T(8,128)(2,1)} async-done(((bf16[16,72,384]{2,1,0:T(8,128)(2,1)}), bf16[16,72,384]{2,1,0:T(8,128)(2,1)}, u32[]{:S(2)}, u32[]{:S(2)}) %all-to-all-start.4) | async-done | bytes 884768 | tf_op jit(solution)/shard_map/all_to_all | solution.py:384
  154.0 1.3 reduce
  155.3 0.1 bitcast_select_fusion
  155.4 0.9 reshape.85
  156.3 9.8 %all-to-all-start.5 = ((bf16[16,2,1350]{2,1,0:T(2,128)(2,1)}), bf16[16,2,1350]{2,1,0:T(2,128)(2,1)S(1)}, u32[]{:S(2)}, u32[]{:S(2)}) async-start(bf16[16,2,1350]{2,1,0:T(2,128)(2,1)} %reshape.85), calls=%async_computation.5 | async-start | bytes 180224 | tf_op jit(solution)/shard_map/all_to_all | solution.py:388
  166.1 2.5 %fusion.9 = bf16[1,128,1152]{2,1,0:T(8,128)(2,1)} fusion(f32[128,1152]{1,0:T(8,128)} %fusion.16, bf16[128,1280]{1,0:T(8,128)(2,1)} %bitcast.72, bf16[1280,1152]{1,0:T(8,128)(2,1)S(1)} %copy-done.8), kind=kOutput, calls=%fused_computation.19 | convolution fusion | flops 377782272 | bytes 4161536 | tf_op jit(solution)/shard_map/dot_general | solution.py:381
  168.6 5.8 %all-to-all-done.5 = bf16[16,2,1350]{2,1,0:T(2,128)(2,1)S(1)} async-done(((bf16[16,2,1350]{2,1,0:T(2,128)(2,1)}), bf16[16,2,1350]{2,1,0:T(2,128)(2,1)S(1)}, u32[]{:S(2)}, u32[]{:S(2)}) %all-to-all-start.5) | async-done | bytes 86432 | tf_op jit(solution)/shard_map/all_to_all | solution.py:388
  174.4 0.2 reshape.86
  174.7 0.7 convert_reduce_fusion
  (53 shorter events, 0.7 us)
Async XLA Ops:
  0.6 102.7 %copy-start = (bf16[1,128,1152]{2,1,0:T(8,128)(2,1)S(1)}, bf16[1,128,1152]{2,1,0:T(8,128)(2,1)}, u32[]{:S(2)}) copy-start(bf16[1,128,1152]{2,1,0:T(8,128)(2,1)} %param.19) | copy-start | bytes 884740
  2.6 18.2 %all-to-all-start = ((bf16[4,2,20736]{2,1,0:T(2,128)(2,1)}), bf16[4,2,20736]{2,1,0:T(2,128)(2,1)S(1)}, u32[]{:S(2)}, u32[]{:S(2)}) async-start(bf16[4,2,20736]{2,1,0:T(2,128)(2,1)} %broadcast_in_dim.55), calls=%async_computation | async-start | bytes 663552 | tf_op jit(solution)/shard_map/all_to_all | solution.py:325
  11.6 20.1 %collective-permute-start = (bf16[128,1152]{1,0:T(8,128)(2,1)}, bf16[128,1152]{1,0:T(8,128)(2,1)}, u32[]{:S(2)}, u32[]{:S(2)}) collective-permute-start(bf16[128,1152]{1,0:T(8,128)(2,1)} %bitcast.77), channel_id=1, source_target_pairs={{0,1},{1,0},{2,3},{3,2},{4,5},{5,4},{6,7},{7,6},{8,9},{9,8},{10,11... | collective-permute-start | bytes 884744 | tf_op jit(solution)/shard_map/ppermute | solution.py:256
  21.0 5.7 %copy-start.11 = (bf16[2,576,1152]{2,1,0:T(8,128)(2,1)S(1)}, bf16[2,576,1152]{2,1,0:T(8,128)(2,1)}, u32[]{:S(2)}) copy-start(bf16[2,576,1152]{2,1,0:T(8,128)(2,1)} %param.20) | copy-start | bytes 7962628
  22.3 16.6 %all-to-all-start.1 = ((bf16[4,40,4608]{2,1,0:T(8,128)(2,1)}), bf16[4,40,4608]{2,1,0:T(8,128)(2,1)}, u32[]{:S(2)}, u32[]{:S(2)}) async-start(bf16[4,40,4608]{2,1,0:T(8,128)(2,1)} %broadcast_in_dim.56), calls=%async_computation.1 | async-start | bytes 2949120 | tf_op jit(solution)/shard_map/all_to_all | solution.py:241
  26.8 5.0 %copy-start.17 = (bf16[2,64,1,1152]{3,1,2,0:T(8,128)(2,1)S(1)}, bf16[2,64,1,1152]{3,1,2,0:T(8,128)(2,1)}, u32[]{:S(2)}) copy-start(bf16[2,64,1,1152]{3,1,2,0:T(8,128)(2,1)} %param.13) | copy-start | bytes 884740
  28.1 5.7 %copy-start.13 = (pred[1280,1152]{1,0:T(32,128)(4,1)S(1)}, pred[1280,1152]{1,0:T(32,128)(4,1)}, u32[]{:S(2)}) copy-start(pred[1280,1152]{1,0:T(32,128)(4,1)} %get-tuple-element.43) | copy-start | bytes 4423684
  29.3 74.6 %copy-start.2 = (bf16[384,1152]{1,0:T(8,128)(2,1)}, bf16[384,1152]{1,0:T(8,128)(2,1)S(1)}, u32[]{:S(2)}) copy-start(bf16[384,1152]{1,0:T(8,128)(2,1)S(1)} %pad.12.key_ref.key_hbm) | copy-start | bytes 2654212
  32.9 0.8 copy-start.14
  41.1 15.7 %all-to-all-start.2 = ((bf16[4,144,1152]{2,1,0:T(8,128)(2,1)}), bf16[4,144,1152]{2,1,0:T(8,128)(2,1)}, u32[]{:S(2)}, u32[]{:S(2)}) async-start(bf16[4,144,1152]{2,1,0:T(8,128)(2,1)} %broadcast_in_dim.57), calls=%async_computation.2 | async-start | bytes 2654208 | tf_op jit(solution)/shard_map/all_to_all | solution.py:241
  45.4 11.4 %copy-start.15 = (bf16[2,128,1152]{2,1,0:T(8,128)(2,1)S(1)}, bf16[2,128,1152]{2,1,0:T(8,128)(2,1)}, u32[]{:S(2)}) copy-start(bf16[2,128,1152]{2,1,0:T(8,128)(2,1)} %copy-done.14) | copy-start | bytes 1769476
  45.5 33.3 %collective-permute-start.2 = (bf16[576,1152]{1,0:T(8,128)(2,1)}, bf16[576,1152]{1,0:T(8,128)(2,1)}, u32[]{:S(2)}, u32[]{:S(2)}) collective-permute-start(bf16[576,1152]{1,0:T(8,128)(2,1)} %dynamic-slice_bitcast_fusion), channel_id=1, source_target_pairs={{0,128},{1,135},{128,2},{129,1},{2,130},{3,129},{130,4},{131,3},{4... | collective-permute-start | bytes 3981320 | tf_op jit(solution)/shard_map/ppermute | solution.py:289
  52.1 26.6 %collective-permute-start.3 = (bf16[144,3456]{1,0:T(8,128)(2,1)S(1)}, bf16[144,3456]{1,0:T(8,128)(2,1)}, u32[]{:S(2)}, u32[]{:S(2)}) collective-permute-start(bf16[144,3456]{1,0:T(8,128)(2,1)S(1)} %reshape.79.w0), channel_id=1, source_target_pairs={{0,8},{1,33},{2,10},{3,35},{4,12},{5,37},{6,14},{7,39},{8,16},{9,4... | collective-permute-start | bytes 2985992 | tf_op jit(solution)/shard_map/ppermute | solution.py:252
  53.5 25.2 %collective-permute-start.4 = (bf16[144,3456]{1,0:T(8,128)(2,1)S(1)}, bf16[144,3456]{1,0:T(8,128)(2,1)}, u32[]{:S(2)}, u32[]{:S(2)}) collective-permute-start(bf16[144,3456]{1,0:T(8,128)(2,1)S(1)} %reshape.79.w0), channel_id=1, source_target_pairs={{0,24},{1,97},{2,26},{3,99},{4,28},{5,101},{6,30},{7,103},{8,0},{9... | collective-permute-start | bytes 2985992 | tf_op jit(solution)/shard_map/ppermute | solution.py:252
  54.9 23.9 %collective-permute-start.5 = (bf16[144,3456]{1,0:T(8,128)(2,1)S(1)}, bf16[144,3456]{1,0:T(8,128)(2,1)}, u32[]{:S(2)}, u32[]{:S(2)}) collective-permute-start(bf16[144,3456]{1,0:T(8,128)(2,1)S(1)} %reshape.79.w0), channel_id=1, source_target_pairs={{0,16},{1,65},{2,18},{3,67},{4,20},{5,69},{6,22},{7,71},{8,24},{9,... | collective-permute-start | bytes 2985992 | tf_op jit(solution)/shard_map/ppermute | solution.py:252
  59.4 11.2 %copy-start.4 = (bf16[2,64,1,1152]{3,1,2,0:T(8,128)(2,1)S(1)}, bf16[2,64,1,1152]{3,1,2,0:T(8,128)(2,1)}, u32[]{:S(2)}) copy-start(bf16[2,64,1,1152]{3,1,2,0:T(8,128)(2,1)} %param.14) | copy-start | bytes 884740
  59.5 11.2 %copy-start.5 = (bf16[2,64,1,1152]{3,1,2,0:T(8,128)(2,1)S(1)}, bf16[2,64,1,1152]{3,1,2,0:T(8,128)(2,1)}, u32[]{:S(2)}) copy-start(bf16[2,64,1,1152]{3,1,2,0:T(8,128)(2,1)} %param.15) | copy-start | bytes 884740
  59.5 11.2 %copy-start.6 = (bf16[2,64,1,1152]{3,1,2,0:T(8,128)(2,1)S(1)}, bf16[2,64,1,1152]{3,1,2,0:T(8,128)(2,1)}, u32[]{:S(2)}) copy-start(bf16[2,64,1,1152]{3,1,2,0:T(8,128)(2,1)} %param.16) | copy-start | bytes 884740
  59.5 7.6 %collective-permute-start.1 = (bf16[128,576]{0,1:T(8,128)(2,1)S(1)}, bf16[128,576]{0,1:T(8,128)(2,1)S(1)}, u32[]{:S(2)}, u32[]{:S(2)}) collective-permute-start(bf16[128,576]{0,1:T(8,128)(2,1)S(1)} %bitcast.79), channel_id=1, source_target_pairs={{0,1},{1,0},{2,3},{3,2},{4,5},{5,4},{6,7},{7,6},{8,9},{9,8},{10,11... | collective-permute-start | bytes 442376 | tf_op jit(solution)/shard_map/ppermute | solution.py:256
  68.9 16.2 %copy-start.18 = (s32[4]{0:T(128)S(1)}, s32[4]{0:T(128)}, u32[]{:S(2)}) copy-start(s32[4]{0:T(128)} %constant.75) | copy-start | bytes 52
  78.7 21.5 %collective-permute-start.7 = (bf16[576,1152]{1,0:T(8,128)(2,1)}, bf16[576,1152]{1,0:T(8,128)(2,1)}, u32[]{:S(2)}, u32[]{:S(2)}) collective-permute-start(bf16[576,1152]{1,0:T(8,128)(2,1)} %collective-permute-done.2), channel_id=1, source_target_pairs={{0,1},{1,0},{2,3},{3,2},{4,5},{5,4},{6,7},{7,6},{8,9},{9,8},{10,11... | collective-permute-start | bytes 3981320 | tf_op jit(solution)/shard_map/ppermute | solution.py:295
  84.4 3.9 %collective-permute-start.6 = (bf16[128,3456]{1,0:T(8,128)(2,1)S(1)}, bf16[128,3456]{1,0:T(8,128)(2,1)}, u32[]{:S(2)}, u32[]{:S(2)}) collective-permute-start(bf16[128,3456]{1,0:T(8,128)(2,1)S(1)} %temporal_grads.1.mine_ref), channel_id=1, source_target_pairs={{0,1},{1,0},{2,3},{3,2},{4,5},{5,4},{6,7},{7,6},{8,9},{9,8},{10,11... | collective-permute-start | bytes 2654216 | tf_op jit(solution)/shard_map/ppermute | solution.py:256
  94.4 22.5 %all-to-all-start.3 = ((bf16[128,2,640]{2,1,0:T(2,128)(2,1)}), bf16[128,2,640]{2,1,0:T(2,128)(2,1)S(1)}, u32[]{:S(2)}, u32[]{:S(2)}) async-start(bf16[128,2,640]{2,1,0:T(2,128)(2,1)} %bitcast.64), calls=%async_computation.3 | async-start | bytes 655360 | tf_op jit(solution)/shard_map/all_to_all | solution.py:374
  100.2 2.6 %copy-start.12 = (bf16[2,576,1152]{2,1,0:T(8,128)(2,1)S(1)}, bf16[2,576,1152]{2,1,0:T(8,128)(2,1)}, u32[]{:S(2)}) copy-start(bf16[2,576,1152]{2,1,0:T(8,128)(2,1)} %param.20) | copy-start | bytes 7962628
  103.3 5.5 %copy-start.9 = (bf16[2,576,1152]{2,1,0:T(8,128)(2,1)}, bf16[2,576,1152]{2,1,0:T(8,128)(2,1)S(1)}, u32[]{:S(2)}) copy-start(bf16[2,576,1152]{2,1,0:T(8,128)(2,1)S(1)} %get-tuple-element.34) | copy-start | bytes 7962628
  103.3 5.5 %copy-start.10 = (bf16[2,576,1152]{2,1,0:T(8,128)(2,1)}, bf16[2,576,1152]{2,1,0:T(8,128)(2,1)S(1)}, u32[]{:S(2)}) copy-start(bf16[2,576,1152]{2,1,0:T(8,128)(2,1)S(1)} %get-tuple-element.35) | copy-start | bytes 7962628
  104.0 12.3 %copy-start.3 = (bf16[128,1152]{1,0:T(8,128)(2,1)}, bf16[128,1152]{1,0:T(8,128)(2,1)S(1)}, u32[]{:S(2)}) copy-start(bf16[128,1152]{1,0:T(8,128)(2,1)S(1)} %fusion.8.query_ref.query_hbm) | copy-start | bytes 884740
  104.0 6.5 %copy-start.7 = (bf16[1280,1152]{1,0:T(8,128)(2,1)S(1)}, bf16[1280,1152]{1,0:T(8,128)(2,1)}, u32[]{:S(2)}) copy-start(bf16[1280,1152]{1,0:T(8,128)(2,1)} %get-tuple-element.20) | copy-start | bytes 8847364
  108.8 1.6 copy-start.1
  128.7 11.8 %copy-start.16 = (bf16[128,1152]{1,0:T(8,128)(2,1)S(1)}, bf16[128,1152]{1,0:T(8,128)(2,1)}, u32[]{:S(2)}) copy-start(bf16[128,1152]{1,0:T(8,128)(2,1)} %get-tuple-element.31) | copy-start | bytes 884740
  128.7 3.7 %collective-permute-start.8 = (bf16[16,72,384]{2,1,0:T(8,128)(2,1)}, bf16[16,72,384]{2,1,0:T(8,128)(2,1)S(1)}, u32[]{:S(2)}, u32[]{:S(2)}) collective-permute-start(bf16[16,72,384]{2,1,0:T(8,128)(2,1)} %get-tuple-element.33), channel_id=1, source_target_pairs={{0,1},{1,0},{2,3},{3,2},{4,5},{5,4},{6,7},{7,6},{8,9},{9,8},{10,11... | collective-permute-start | bytes 2654216 | tf_op jit(solution)/shard_map/ppermute | solution.py:256
  134.7 19.3 %all-to-all-start.4 = ((bf16[16,72,384]{2,1,0:T(8,128)(2,1)}), bf16[16,72,384]{2,1,0:T(8,128)(2,1)}, u32[]{:S(2)}, u32[]{:S(2)}) async-start(bf16[16,72,384]{2,1,0:T(8,128)(2,1)} %add_convert_fusion), calls=%async_computation.4 | async-start | bytes 1769472 | tf_op jit(solution)/shard_map/all_to_all | solution.py:384
  140.5 25.6 %copy-start.8 = (bf16[1280,1152]{1,0:T(8,128)(2,1)S(1)}, bf16[1280,1152]{1,0:T(8,128)(2,1)}, u32[]{:S(2)}) copy-start(bf16[1280,1152]{1,0:T(8,128)(2,1)} %get-tuple-element.20) | copy-start | bytes 8847364
  156.3 18.1 %all-to-all-start.5 = ((bf16[16,2,1350]{2,1,0:T(2,128)(2,1)}), bf16[16,2,1350]{2,1,0:T(2,128)(2,1)S(1)}, u32[]{:S(2)}, u32[]{:S(2)}) async-start(bf16[16,2,1350]{2,1,0:T(2,128)(2,1)} %reshape.85), calls=%async_computation.5 | async-start | bytes 180224 | tf_op jit(solution)/shard_map/all_to_all | solution.py:388

commit v11 on v10

--- a/solution.py
+++ b/solution.py
@@ -207,7 +207,7 @@
         out_shape=(jax.ShapeDtypeStruct((rows, width), jnp.bfloat16), term, term),
         scratch_shapes=[pltpu.VMEM(array.shape, array.dtype) for array in copied]
         + [pltpu.VMEM((rows, width), jnp.bfloat16), pltpu.SemaphoreType.DMA((6,))],
-        compiler_params=pltpu.CompilerParams(vmem_limit_bytes=56 << 20),
+        compiler_params=pltpu.CompilerParams(vmem_limit_bytes=50 << 20),
         cost_estimate=pl.CostEstimate(
             flops=8 * rows * CAP_PAD * width + 2 * rows * width * arrived.shape[1],
             bytes_accessed=12 << 20,

time: 176 us -> 172 us (0.977)
  starting transfers between devices: 61 us -> 56.7 us
  other arithmetic: 12.9 us -> 10.5 us
    ppermute x1, starting transfers between devices: 5.69 us -> 1.37 us  [cross_whole(): swapped = lax.ppermute(got, 'c', [(0, 1), (1, 0)])]
    unnamed x42 -> x32, local copies, waits for them, and re-layouts: 4.84 us -> 4.08 us
  transfers between devices with their start and end apart: 15 -> 15, of which waited for: 9 -> 9; matrix products, arithmetic and copies ran while one was open for 22% -> 24% of each run, Pallas kernels for 10% -> 11%
where the time goes in v11:
time: 172 us; the launch traced here: 171 us
  starting transfers between devices  56.7 us (33%)
  waiting for transfers between devices  32.6 us (19%)
  Pallas kernels  28 us (16%)
  local copies, waits for them, and re-layouts  21.3 us (12%)
  matrix products  20.4 us (12%)
  other arithmetic  10.5 us (6%)
  between operations  1.73 us (1%)
    all_to_all x1, waiting for transfers between devices, local(): lax.all_to_all(chip, ('x', 'y'), 0, 0).astype(jnp.float32)  10.9 us
    all_to_all x1, starting transfers between devices, local(): lax.all_to_all(pieces, ('s', 'z', 'c'), 0, 0).astype(jnp.float32)  9.78 us
    pallas_call x1, Pallas kernels, cross_grads(): pl.pallas_call(cross_kernel, in_specs=[pl.BlockSpec(memory_space=pltpu.SM...  9.22 us
    all_to_all x1, starting transfers between devices, local(): lax.all_to_all(jnp.broadcast_to(shard[None], (4,) + shard.shape), 'z', 0, 0)  9.01 us
    ppermute x4, starting transfers between devices, swap_cores(): return lax.ppermute(block, 'c', [(0, 1), (1, 0)])  8.88 us
    all_to_all x2, starting transfers between devices, gather_groups(): return lax.all_to_all(copies, ALL, 0, 0, axis_index_groups=groups)  8.75 us
    pallas_call x1, Pallas kernels, temporal_grads(): pl.pallas_call(temporal_kernel, out_shape=jax.ShapeDtypeStruct((rows, 3 *...  8.72 us
    ppermute x4, waiting for transfers between devices, swap_cores(): return lax.ppermute(block, 'c', [(0, 1), (1, 0)])  6.59 us
  transfers between devices with their start and end apart: 15, of which 9 were waited for; matrix products, arithmetic and copies ran while one was open for 24% of the time, Pallas kernels for 11%

profile of v11, /device:TPU:1, one launch (start us, length us, event | category | flops | bytes accessed | tf_op | source)
XLA Modules:
  0.0 171.2 jit_solution(15755739317611581332)
XLA Ops:
  0.6 1.0 pad_maximum_fusion.3
  1.6 0.1 broadcast_in_dim.54
  1.7 0.9 broadcast_in_dim.55
  2.6 9.0 %all-to-all-start = ((bf16[4,2,20736]{2,1,0:T(2,128)(2,1)}), bf16[4,2,20736]{2,1,0:T(2,128)(2,1)S(1)}, u32[]{:S(2)}, u32[]{:S(2)}) async-start(bf16[4,2,20736]{2,1,0:T(2,128)(2,1)} %broadcast_in_dim.55), calls=%async_computation | async-start | bytes 663552 | tf_op jit(solution)/shard_map/all_to_all | solution.py:325
  11.6 1.0 collective-permute-start
  12.6 3.7 %fusion.20 = (bf16[1280,1152]{1,0:T(8,128)(2,1)}, pred[1280,1152]{1,0:T(32,128)(4,1)}) fusion(s32[1280]{0:T(1024)} %constant.60.clone), kind=kLoop, calls=%fused_computation.37 | loop fusion | flops 2949120 | bytes 4428800 | tf_op jit(solution)/shard_map/convert_element_type | solution.py:319
  16.3 4.6 %all-to-all-done = bf16[4,2,20736]{2,1,0:T(2,128)(2,1)S(1)} async-done(((bf16[4,2,20736]{2,1,0:T(2,128)(2,1)}), bf16[4,2,20736]{2,1,0:T(2,128)(2,1)S(1)}, u32[]{:S(2)}, u32[]{:S(2)}) %all-to-all-start) | async-done | bytes 331808 | tf_op jit(solution)/shard_map/all_to_all | solution.py:325
  20.8 0.2 reshape.70
  21.1 1.2 broadcast_in_dim.56
  22.3 4.5 %all-to-all-start.1 = ((bf16[4,40,4608]{2,1,0:T(8,128)(2,1)}), bf16[4,40,4608]{2,1,0:T(8,128)(2,1)}, u32[]{:S(2)}, u32[]{:S(2)}) async-start(bf16[4,40,4608]{2,1,0:T(8,128)(2,1)} %broadcast_in_dim.56), calls=%async_computation.1 | async-start | bytes 2949120 | tf_op jit(solution)/shard_map/all_to_all | solution.py:241
  26.8 1.3 dynamic-slice_bitcast_fusion
  28.1 1.2 pad.12.key_ref.key_hbm
  29.2 1.5 pad.13.value_hbm
  30.7 1.0 select_bitcast_fusion.3
  31.9 0.8 copy-done.11
  32.7 1.8 %fusion.13.residual_ref = bf16[256,640]{1,0:T(8,128)(2,1)S(1)} fusion(bf16[256,1152]{1,0:T(8,128)(2,1)S(1)} %bitcast.75, pred[1280,1152]{1,0:T(32,128)(4,1)} %get-tuple-element.43, s32[]{:T(128)S(6)} %select_n.82), kind=kOutput, calls=%fused_computation.27 | convolution fusion | flops 377651200 | bytes 1654788 | tf_op jit(solution)/shard_map/dot_general | solution.py:328
  34.5 4.3 %all-to-all-done.1 = bf16[4,40,4608]{2,1,0:T(8,128)(2,1)} async-done(((bf16[4,40,4608]{2,1,0:T(8,128)(2,1)}), bf16[4,40,4608]{2,1,0:T(8,128)(2,1)}, u32[]{:S(2)}, u32[]{:S(2)}) %all-to-all-start.1) | async-done | bytes 1474592 | tf_op jit(solution)/shard_map/all_to_all | solution.py:241
  38.8 1.0 slice.30
  39.9 1.2 broadcast_in_dim.57
  41.1 4.3 %all-to-all-start.2 = ((bf16[4,144,1152]{2,1,0:T(8,128)(2,1)}), bf16[4,144,1152]{2,1,0:T(8,128)(2,1)}, u32[]{:S(2)}, u32[]{:S(2)}) async-start(bf16[4,144,1152]{2,1,0:T(8,128)(2,1)} %broadcast_in_dim.57), calls=%async_computation.2 | async-start | bytes 2654208 | tf_op jit(solution)/shard_map/all_to_all | solution.py:241
  45.4 3.0 %collective-permute-start.2 = (bf16[576,1152]{1,0:T(8,128)(2,1)}, bf16[576,1152]{1,0:T(8,128)(2,1)}, u32[]{:S(2)}, u32[]{:S(2)}) collective-permute-start(bf16[576,1152]{1,0:T(8,128)(2,1)} %dynamic-slice_bitcast_fusion), channel_id=1, source_target_pairs={{0,128},{1,135},{128,2},{129,1},{2,130},{3,129},{130,4},{131,3},{4... | collective-permute-start | bytes 3981320 | tf_op jit(solution)/shard_map/ppermute | solution.py:289
  48.4 2.3 %slice.31 = bf16[4,36,3456]{2,1,0:T(8,128)(2,1)} slice(bf16[4,40,4608]{2,1,0:T(8,128)(2,1)} %all-to-all-done.1), slice={[0:4], [0:36], [1152:4608]} | slice | bytes 1990656 | tf_op jit(solution)/shard_map/slice | solution.py:340
  50.7 1.3 reshape.79.w0
  52.0 1.4 collective-permute-start.3
  53.5 1.3 collective-permute-start.4
  54.8 1.6 collective-permute-start.5
  56.4 0.3 all-to-all-done.2
  56.8 2.8 %convolution_convert_fusion.2 = bf16[256,576]{0,1:T(8,128)(2,1)} fusion(bf16[256,1152]{1,0:T(8,128)(2,1)} %bitcast.76, bf16[576,1152]{1,0:T(8,128)(2,1)} %bitcast.6), kind=kOutput, calls=%fused_computation.28 | convolution fusion | flops 339886080 | bytes 2211840 | tf_op jit(solution)/shard_map/dot_general | solution.py:348
  59.6 1.7 %reshape.75 = bf16[2,128,576]{1,0,2:T(2,128)(2,1)} reshape(bf16[256,576]{0,1:T(8,128)(2,1)} %convolution_convert_fusion.2) | data formatting | bytes 589824 | tf_op jit(solution)/shard_map/reshape | solution.py:350
  61.3 1.7 constant_dynamic-slice_fusion.1
  63.1 6.6 %collective-permute-start.1 = (bf16[128,576]{0,1:T(8,128)(2,1)S(1)}, bf16[128,576]{0,1:T(8,128)(2,1)S(1)}, u32[]{:S(2)}, u32[]{:S(2)}) collective-permute-start(bf16[128,576]{0,1:T(8,128)(2,1)S(1)} %bitcast.79), channel_id=1, source_target_pairs={{0,1},{1,0},{2,3},{3,2},{4,5},{5,4},{6,7},{7,6},{8,9},{9,8},{10,11... | collective-permute-start | bytes 442376 | tf_op jit(solution)/shard_map/ppermute | solution.py:256
  69.7 1.0 collective-permute-done.1
  70.7 1.8 %fusion.10 = f32[128,1152]{1,0:T(8,128)S(1)} fusion(bf16[1280,1152]{1,0:T(8,128)(2,1)} %get-tuple-element.20, bf16[128,576]{0,1:T(8,128)(2,1)S(1)} %collective-permute-done.1, pred[]{:T(512)S(6)} %eq.39, bf16[1,128,576]{1,0,2:T(2,128)(2,1)S(1)} %get-tuple-element.40), kind=kOutput, calls=%fused_computation.23 | convolution fusion | flops 169943040 | bytes 2211841 | tf_op jit(solution)/shard_map/dot_general | solution.py:357
  72.5 1.8 %fusion.6.grad_ref = bf16[128,1152]{1,0:T(8,128)(2,1)S(1)} fusion(f32[128,1152]{1,0:T(8,128)S(1)} %fusion.10, bf16[1280,1152]{1,0:T(8,128)(2,1)} %get-tuple-element.20, bf16[128,576]{0,1:T(8,128)(2,1)S(1)} %collective-permute-done.1, pred[]{:T(512)S(6)} %eq.39, bf16[1,128,576]{1,0,2:T(2,128)(2,1)S(1)} %get-tuple-element.40), kind=kOutput, calls=%fused_computation.15 | convolution fusion | flops 170237952 | bytes 2506753 | tf_op jit(solution)/shard_map/dot_general | solution.py:356
  74.3 8.7 %temporal_grads.1.mine_ref = bf16[128,3456]{1,0:T(8,128)(2,1)} custom-call(bf16[128,1152]{1,0:T(8,128)(2,1)S(1)} %fusion.6.grad_ref, bf16[128,1152]{1,0:T(8,128)(2,1)S(1)} %bitcast.70, bf16[128,1152]{1,0:T(8,128)(2,1)S(1)} %bitcast.71, bf16[128,1152]{1,0:T(8,128)(2,1)S(1)} %bitcast.72), custom_call_target="tpu_custom_call" | custom-call | flops 147456 | bytes 294912 | tf_op jit(solution)/shard_map/temporal_grads/pallas_call | solution.py:65
  83.0 1.4 collective-permute-start.7
  85.2 3.5 %collective-permute-done.6.other_ref = bf16[128,3456]{1,0:T(8,128)(2,1)} collective-permute-done((bf16[128,3456]{1,0:T(8,128)(2,1)}, bf16[128,3456]{1,0:T(8,128)(2,1)}, u32[]{:S(2)}, u32[]{:S(2)}) %collective-permute-start.6) | collective-permute-done | bytes 884768 | tf_op jit(solution)/shard_map/ppermute | solution.py:256
  88.7 5.2 %mixed_half.1 = bf16[256,640]{1,0:T(8,128)(2,1)S(1)} custom-call(s32[5]{0:T(128)S(1)} %pad_add_fusion.place_ref, bf16[128,3456]{1,0:T(8,128)(2,1)} %temporal_grads.1.mine_ref, bf16[128,3456]{1,0:T(8,128)(2,1)} %collective-permute-done.6.other_ref, bf16[256,640]{1,0:T(8,128)(2,1)S(1)} %fusion.13.residual_ref, bf16[144,3456]{1,0:T(8,128)(2,1)S(1)} %reshape.79.w0, ...), custom_call_target="tpu_custom_call" | custom-call | flops 1132462080 | bytes 8388608 | tf_op jit(solution)/shard_map/mixed_half/pallas_call | solution.py:102
  93.9 1.1 copy.53
  95.0 6.1 %all-to-all-start.3 = ((bf16[128,2,640]{2,1,0:T(2,128)(2,1)}), bf16[128,2,640]{2,1,0:T(2,128)(2,1)S(1)}, u32[]{:S(2)}, u32[]{:S(2)}) async-start(bf16[128,2,640]{2,1,0:T(2,128)(2,1)} %bitcast.64), calls=%async_computation.3 | async-start | bytes 655360 | tf_op jit(solution)/shard_map/all_to_all | solution.py:374
  101.1 2.1 %select_bitcast_fusion.1 = (bf16[1,576,1152]{2,1,0:T(8,128)(2,1)S(1)}, bf16[1,576,1152]{2,1,0:T(8,128)(2,1)S(1)}) fusion(bf16[576,1152]{1,0:T(8,128)(2,1)} %collective-permute-done.2, bf16[576,1152]{1,0:T(8,128)(2,1)} %collective-permute-done.7, pred[]{:T(512)S(6)} %eq.39), kind=kLoop, calls=%fused_computation.22 | loop fusion | flops 1327104 | bytes 5308417 | tf_op jit(solution)/shard_map/stack | solution.py:296
  103.2 0.4 copy-done.10
  103.6 0.5 broadcast_select_fusion
  104.2 0.6 fusion.8.query_ref.query_hbm
  104.8 4.8 %cross_probs.1.probs_hbm = f32[16,128,384]{2,1,0:T(8,128)S(1)} custom-call(s32[1]{0:T(128)S(6)} %copy.57.length_ref, bf16[128,1152]{1,0:T(8,128)(2,1)S(1)} %fusion.8.query_ref.query_hbm, bf16[384,1152]{1,0:T(8,128)(2,1)S(1)} %pad.12.key_ref.key_hbm), custom_call_target="tpu_custom_call" | custom-call | flops 113246208 | bytes 4194304 | tf_op jit(solution)/shard_map/cross_probs/pallas_call | solution.py:134
  109.7 1.6 copy-done.1
  111.3 5.9 %convolution_convert_fusion.w_out_hbm = bf16[1280,1152]{1,0:T(8,128)(2,1)} fusion(bf16[1280,1152]{1,0:T(8,128)(2,1)S(1)} %copy-done.6, bf16[2,576,1152]{2,1,0:T(8,128)(2,1)S(1)} %get-tuple-element.35, bf16[2,576,1152]{2,1,0:T(8,128)(2,1)S(1)} %get-tuple-element.34), kind=kOutput, calls=%fused_computation | convolution fusion | flops 3404169216 | bytes 11206656 | tf_op jit(solution)/shard_map/dot_general | solution.py:367
  117.1 0.7 all-to-all-done.3
  117.9 0.3 copy.36
  118.2 9.2 %cross_grads.1 = (bf16[128,1152]{1,0:T(8,128)(2,1)S(1)}, bf16[16,72,384]{2,1,0:T(8,128)(2,1)S(1)}, bf16[16,72,384]{2,1,0:T(8,128)(2,1)S(1)}) custom-call(s32[1]{0:T(128)} %bitcast.core_ref, bf16[128,1280]{1,0:T(8,128)(2,1)S(1)} %bitcast.67, bf16[1280,1152]{1,0:T(8,128)(2,1)} %convolution_convert_fusion.w_out_hbm, ...), custom_call_target="tpu_custom_call" | custom-call | flops 830472192 | bytes 12582912 | tf_op jit(solution)/shard_map/cross_grads/pallas_call | solution.py:202
  127.4 1.3 collective-permute-start.8
  128.7 2.1 %collective-permute-done.8 = bf16[16,72,384]{2,1,0:T(8,128)(2,1)S(1)} collective-permute-done((bf16[16,72,384]{2,1,0:T(8,128)(2,1)S(1)}, bf16[16,72,384]{2,1,0:T(8,128)(2,1)S(1)}, u32[]{:S(2)}, u32[]{:S(2)}) %collective-permute-start.8) | collective-permute-done | bytes 884768 | tf_op jit(solution)/shard_map/ppermute | solution.py:256
  130.8 1.1 add_convert_fusion
  131.9 5.5 %all-to-all-start.4 = ((bf16[16,72,384]{2,1,0:T(8,128)(2,1)}), bf16[16,72,384]{2,1,0:T(8,128)(2,1)S(1)}, u32[]{:S(2)}, u32[]{:S(2)}) async-start(bf16[16,72,384]{2,1,0:T(8,128)(2,1)} %add_convert_fusion), calls=%async_computation.4 | async-start | bytes 1769472 | tf_op jit(solution)/shard_map/all_to_all | solution.py:384
  137.6 2.6 %fusion.16 = f32[128,1152]{1,0:T(8,128)S(1)} fusion(bf16[128,1152]{1,0:T(8,128)(2,1)S(1)} %get-tuple-element.31, bf16[2,576,1152]{2,1,0:T(8,128)(2,1)} %copy-done.7, bf16[2,576,1152]{2,1,0:T(8,128)(2,1)} %copy-done.8), kind=kOutput, calls=%fused_computation.30 | convolution fusion | flops 345047040 | bytes 6193152 | tf_op jit(solution)/shard_map/dot_general | solution.py:382
  140.3 10.9 %all-to-all-done.4 = bf16[16,72,384]{2,1,0:T(8,128)(2,1)S(1)} async-done(((bf16[16,72,384]{2,1,0:T(8,128)(2,1)}), bf16[16,72,384]{2,1,0:T(8,128)(2,1)S(1)}, u32[]{:S(2)}, u32[]{:S(2)}) %all-to-all-start.4) | async-done | bytes 884768 | tf_op jit(solution)/shard_map/all_to_all | solution.py:384
  151.1 0.1 reduce
  151.3 0.1 bitcast_select_fusion
  151.4 0.9 reshape.85
  152.2 9.8 %all-to-all-start.5 = ((bf16[16,2,1350]{2,1,0:T(2,128)(2,1)}), bf16[16,2,1350]{2,1,0:T(2,128)(2,1)S(1)}, u32[]{:S(2)}, u32[]{:S(2)}) async-start(bf16[16,2,1350]{2,1,0:T(2,128)(2,1)} %reshape.85), calls=%async_computation.5 | async-start | bytes 180224 | tf_op jit(solution)/shard_map/all_to_all | solution.py:388
  162.0 3.1 %fusion.9 = bf16[1,128,1152]{2,1,0:T(8,128)(2,1)} fusion(f32[128,1152]{1,0:T(8,128)S(1)} %fusion.16, bf16[128,1280]{1,0:T(8,128)(2,1)S(1)} %bitcast.68, bf16[1280,1152]{1,0:T(8,128)(2,1)} %get-tuple-element.20), kind=kOutput, calls=%fused_computation.19 | convolution fusion | flops 377782272 | bytes 4161536 | tf_op jit(solution)/shard_map/dot_general | solution.py:381
  165.2 5.2 %all-to-all-done.5 = bf16[16,2,1350]{2,1,0:T(2,128)(2,1)S(1)} async-done(((bf16[16,2,1350]{2,1,0:T(2,128)(2,1)}), bf16[16,2,1350]{2,1,0:T(2,128)(2,1)S(1)}, u32[]{:S(2)}, u32[]{:S(2)}) %all-to-all-start.5) | async-done | bytes 86432 | tf_op jit(solution)/shard_map/all_to_all | solution.py:388
  170.3 0.2 reshape.86
  170.6 0.7 convert_reduce_fusion
  (43 shorter events, 0.6 us)
Async XLA Ops:
  0.6 103.6 %copy-start = (bf16[1,128,1152]{2,1,0:T(8,128)(2,1)S(1)}, bf16[1,128,1152]{2,1,0:T(8,128)(2,1)}, u32[]{:S(2)}) copy-start(bf16[1,128,1152]{2,1,0:T(8,128)(2,1)} %param.19) | copy-start | bytes 884740
  2.6 18.2 %all-to-all-start = ((bf16[4,2,20736]{2,1,0:T(2,128)(2,1)}), bf16[4,2,20736]{2,1,0:T(2,128)(2,1)S(1)}, u32[]{:S(2)}, u32[]{:S(2)}) async-start(bf16[4,2,20736]{2,1,0:T(2,128)(2,1)} %broadcast_in_dim.55), calls=%async_computation | async-start | bytes 663552 | tf_op jit(solution)/shard_map/all_to_all | solution.py:325
  11.6 19.1 %collective-permute-start = (bf16[128,1152]{1,0:T(8,128)(2,1)}, bf16[128,1152]{1,0:T(8,128)(2,1)}, u32[]{:S(2)}, u32[]{:S(2)}) collective-permute-start(bf16[128,1152]{1,0:T(8,128)(2,1)} %bitcast.77), channel_id=1, source_target_pairs={{0,1},{1,0},{2,3},{3,2},{4,5},{5,4},{6,7},{7,6},{8,9},{9,8},{10,11... | collective-permute-start | bytes 884744 | tf_op jit(solution)/shard_map/ppermute | solution.py:256
  21.0 5.7 %copy-start.9 = (bf16[2,576,1152]{2,1,0:T(8,128)(2,1)S(1)}, bf16[2,576,1152]{2,1,0:T(8,128)(2,1)}, u32[]{:S(2)}) copy-start(bf16[2,576,1152]{2,1,0:T(8,128)(2,1)} %param.20) | copy-start | bytes 7962628
  22.3 16.5 %all-to-all-start.1 = ((bf16[4,40,4608]{2,1,0:T(8,128)(2,1)}), bf16[4,40,4608]{2,1,0:T(8,128)(2,1)}, u32[]{:S(2)}, u32[]{:S(2)}) async-start(bf16[4,40,4608]{2,1,0:T(8,128)(2,1)} %broadcast_in_dim.56), calls=%async_computation.1 | async-start | bytes 2949120 | tf_op jit(solution)/shard_map/all_to_all | solution.py:241
  26.8 4.0 %copy-start.12 = (bf16[2,64,1,1152]{3,1,2,0:T(8,128)(2,1)S(1)}, bf16[2,64,1,1152]{3,1,2,0:T(8,128)(2,1)}, u32[]{:S(2)}) copy-start(bf16[2,64,1,1152]{3,1,2,0:T(8,128)(2,1)} %param.13) | copy-start | bytes 884740
  29.2 75.6 %copy-start.2 = (bf16[384,1152]{1,0:T(8,128)(2,1)}, bf16[384,1152]{1,0:T(8,128)(2,1)S(1)}, u32[]{:S(2)}) copy-start(bf16[384,1152]{1,0:T(8,128)(2,1)S(1)} %pad.12.key_ref.key_hbm) | copy-start | bytes 2654212
  31.8 0.8 copy-start.11
  41.1 15.7 %all-to-all-start.2 = ((bf16[4,144,1152]{2,1,0:T(8,128)(2,1)}), bf16[4,144,1152]{2,1,0:T(8,128)(2,1)}, u32[]{:S(2)}, u32[]{:S(2)}) async-start(bf16[4,144,1152]{2,1,0:T(8,128)(2,1)} %broadcast_in_dim.57), calls=%async_computation.2 | async-start | bytes 2654208 | tf_op jit(solution)/shard_map/all_to_all | solution.py:241
  45.4 37.6 %collective-permute-start.2 = (bf16[576,1152]{1,0:T(8,128)(2,1)}, bf16[576,1152]{1,0:T(8,128)(2,1)}, u32[]{:S(2)}, u32[]{:S(2)}) collective-permute-start(bf16[576,1152]{1,0:T(8,128)(2,1)} %dynamic-slice_bitcast_fusion), channel_id=1, source_target_pairs={{0,128},{1,135},{128,2},{129,1},{2,130},{3,129},{130,4},{131,3},{4... | collective-permute-start | bytes 3981320 | tf_op jit(solution)/shard_map/ppermute | solution.py:289
  52.0 31.0 %collective-permute-start.3 = (bf16[144,3456]{1,0:T(8,128)(2,1)S(1)}, bf16[144,3456]{1,0:T(8,128)(2,1)}, u32[]{:S(2)}, u32[]{:S(2)}) collective-permute-start(bf16[144,3456]{1,0:T(8,128)(2,1)S(1)} %reshape.79.w0), channel_id=1, source_target_pairs={{0,8},{1,33},{2,10},{3,35},{4,12},{5,37},{6,14},{7,39},{8,16},{9,4... | collective-permute-start | bytes 2985992 | tf_op jit(solution)/shard_map/ppermute | solution.py:252
  53.5 29.5 %collective-permute-start.4 = (bf16[144,3456]{1,0:T(8,128)(2,1)S(1)}, bf16[144,3456]{1,0:T(8,128)(2,1)}, u32[]{:S(2)}, u32[]{:S(2)}) collective-permute-start(bf16[144,3456]{1,0:T(8,128)(2,1)S(1)} %reshape.79.w0), channel_id=1, source_target_pairs={{0,24},{1,97},{2,26},{3,99},{4,28},{5,101},{6,30},{7,103},{8,0},{9... | collective-permute-start | bytes 2985992 | tf_op jit(solution)/shard_map/ppermute | solution.py:252
  54.8 28.2 %collective-permute-start.5 = (bf16[144,3456]{1,0:T(8,128)(2,1)S(1)}, bf16[144,3456]{1,0:T(8,128)(2,1)}, u32[]{:S(2)}, u32[]{:S(2)}) collective-permute-start(bf16[144,3456]{1,0:T(8,128)(2,1)S(1)} %reshape.79.w0), channel_id=1, source_target_pairs={{0,16},{1,65},{2,18},{3,67},{4,20},{5,69},{6,22},{7,71},{8,24},{9,... | collective-permute-start | bytes 2985992 | tf_op jit(solution)/shard_map/ppermute | solution.py:252
  63.0 11.3 %copy-start.3 = (bf16[2,64,1,1152]{3,1,2,0:T(8,128)(2,1)S(1)}, bf16[2,64,1,1152]{3,1,2,0:T(8,128)(2,1)}, u32[]{:S(2)}) copy-start(bf16[2,64,1,1152]{3,1,2,0:T(8,128)(2,1)} %param.14) | copy-start | bytes 884740
  63.0 11.3 %copy-start.4 = (bf16[2,64,1,1152]{3,1,2,0:T(8,128)(2,1)S(1)}, bf16[2,64,1,1152]{3,1,2,0:T(8,128)(2,1)}, u32[]{:S(2)}) copy-start(bf16[2,64,1,1152]{3,1,2,0:T(8,128)(2,1)} %param.15) | copy-start | bytes 884740
  63.0 11.2 %copy-start.5 = (bf16[2,64,1,1152]{3,1,2,0:T(8,128)(2,1)S(1)}, bf16[2,64,1,1152]{3,1,2,0:T(8,128)(2,1)}, u32[]{:S(2)}) copy-start(bf16[2,64,1,1152]{3,1,2,0:T(8,128)(2,1)} %param.16) | copy-start | bytes 884740
  63.1 7.6 %collective-permute-start.1 = (bf16[128,576]{0,1:T(8,128)(2,1)S(1)}, bf16[128,576]{0,1:T(8,128)(2,1)S(1)}, u32[]{:S(2)}, u32[]{:S(2)}) collective-permute-start(bf16[128,576]{0,1:T(8,128)(2,1)S(1)} %bitcast.79), channel_id=1, source_target_pairs={{0,1},{1,0},{2,3},{3,2},{4,5},{5,4},{6,7},{7,6},{8,9},{9,8},{10,11... | collective-permute-start | bytes 442376 | tf_op jit(solution)/shard_map/ppermute | solution.py:256
  72.5 12.6 %copy-start.13 = (s32[4]{0:T(128)S(1)}, s32[4]{0:T(128)}, u32[]{:S(2)}) copy-start(s32[4]{0:T(128)} %constant.75) | copy-start | bytes 52
  83.0 18.1 %collective-permute-start.7 = (bf16[576,1152]{1,0:T(8,128)(2,1)}, bf16[576,1152]{1,0:T(8,128)(2,1)}, u32[]{:S(2)}, u32[]{:S(2)}) collective-permute-start(bf16[576,1152]{1,0:T(8,128)(2,1)} %collective-permute-done.2), channel_id=1, source_target_pairs={{0,1},{1,0},{2,3},{3,2},{4,5},{5,4},{6,7},{7,6},{8,9},{9,8},{10,11... | collective-permute-start | bytes 3981320 | tf_op jit(solution)/shard_map/ppermute | solution.py:295
  84.4 4.3 %collective-permute-start.6 = (bf16[128,3456]{1,0:T(8,128)(2,1)}, bf16[128,3456]{1,0:T(8,128)(2,1)}, u32[]{:S(2)}, u32[]{:S(2)}) collective-permute-start(bf16[128,3456]{1,0:T(8,128)(2,1)} %temporal_grads.1.mine_ref), channel_id=1, source_target_pairs={{0,1},{1,0},{2,3},{3,2},{4,5},{5,4},{6,7},{7,6},{8,9},{9,8},{10,11... | collective-permute-start | bytes 2654216 | tf_op jit(solution)/shard_map/ppermute | solution.py:256
  95.0 22.9 %all-to-all-start.3 = ((bf16[128,2,640]{2,1,0:T(2,128)(2,1)}), bf16[128,2,640]{2,1,0:T(2,128)(2,1)S(1)}, u32[]{:S(2)}, u32[]{:S(2)}) async-start(bf16[128,2,640]{2,1,0:T(2,128)(2,1)} %bitcast.64), calls=%async_computation.3 | async-start | bytes 655360 | tf_op jit(solution)/shard_map/all_to_all | solution.py:374
  101.1 2.6 %copy-start.10 = (bf16[2,576,1152]{2,1,0:T(8,128)(2,1)S(1)}, bf16[2,576,1152]{2,1,0:T(8,128)(2,1)}, u32[]{:S(2)}) copy-start(bf16[2,576,1152]{2,1,0:T(8,128)(2,1)} %param.20) | copy-start | bytes 7962628
  104.2 5.5 %copy-start.7 = (bf16[2,576,1152]{2,1,0:T(8,128)(2,1)}, bf16[2,576,1152]{2,1,0:T(8,128)(2,1)S(1)}, u32[]{:S(2)}) copy-start(bf16[2,576,1152]{2,1,0:T(8,128)(2,1)S(1)} %get-tuple-element.34) | copy-start | bytes 7962628
  104.2 5.5 %copy-start.8 = (bf16[2,576,1152]{2,1,0:T(8,128)(2,1)}, bf16[2,576,1152]{2,1,0:T(8,128)(2,1)S(1)}, u32[]{:S(2)}) copy-start(bf16[2,576,1152]{2,1,0:T(8,128)(2,1)S(1)} %get-tuple-element.35) | copy-start | bytes 7962628
  104.8 6.5 %copy-start.6 = (bf16[1280,1152]{1,0:T(8,128)(2,1)S(1)}, bf16[1280,1152]{1,0:T(8,128)(2,1)}, u32[]{:S(2)}) copy-start(bf16[1280,1152]{1,0:T(8,128)(2,1)} %get-tuple-element.20) | copy-start | bytes 8847364
  109.6 1.6 copy-start.1
  127.4 3.4 %collective-permute-start.8 = (bf16[16,72,384]{2,1,0:T(8,128)(2,1)S(1)}, bf16[16,72,384]{2,1,0:T(8,128)(2,1)S(1)}, u32[]{:S(2)}, u32[]{:S(2)}) collective-permute-start(bf16[16,72,384]{2,1,0:T(8,128)(2,1)S(1)} %get-tuple-element.33), channel_id=1, source_target_pairs={{0,1},{1,0},{2,3},{3,2},{4,5},{5,4},{6,7},{7,6},{8,9},{9,8},{10,11... | collective-permute-start | bytes 2654216 | tf_op jit(solution)/shard_map/ppermute | solution.py:256
  131.9 19.2 %all-to-all-start.4 = ((bf16[16,72,384]{2,1,0:T(8,128)(2,1)}), bf16[16,72,384]{2,1,0:T(8,128)(2,1)S(1)}, u32[]{:S(2)}, u32[]{:S(2)}) async-start(bf16[16,72,384]{2,1,0:T(8,128)(2,1)} %add_convert_fusion), calls=%async_computation.4 | async-start | bytes 1769472 | tf_op jit(solution)/shard_map/all_to_all | solution.py:384
  152.2 18.1 %all-to-all-start.5 = ((bf16[16,2,1350]{2,1,0:T(2,128)(2,1)}), bf16[16,2,1350]{2,1,0:T(2,128)(2,1)S(1)}, u32[]{:S(2)}, u32[]{:S(2)}) async-start(bf16[16,2,1350]{2,1,0:T(2,128)(2,1)} %reshape.85), calls=%async_computation.5 | async-start | bytes 180224 | tf_op jit(solution)/shard_map/all_to_all | solution.py:388
